TPU v7x, 32 devices: a whole 2x2x4 slice. The times are simulated.
32 devices in a mesh: wide: 8 (over z, core), blk: 4 (over y, x).
Axes of the slice: x: 2, y: 2, z: 4, core: 2. Of those that a mesh axis runs over, the one named last changes fastest.
Arguments:
- query_emb: bfloat16 [128, 4096], P(('wide', 'blk')), may hold values from -0.1875 to 0.1875
- passage_emb: bfloat16 [128, 4096], P(('wide', 'blk')), may hold values from -0.1875 to 0.1875
- row_lse: float32 [128], P('wide'), may hold values from 2.5 to 4.5
- positive: int32 [128], P('wide'), may hold values from 0 to 15
- token_lengths: int32 [8, 16], P('wide'), may hold values from 1 to 16, 192 in all within a row
- destination: int32 [1536, 1], P('wide'), may hold values from 0 to 7; in each aligned block of 192 rows (0 to 191, 192 to 383, ...) at most 36 rows name the same one
- mlp_act: bfloat16 [1536, 12288], P('wide', 'blk'), may hold values from -6 to 6
- resid: bfloat16 [1536, 4096], P('wide', 'blk'), may hold values from -6 to 6
- w_down: bfloat16 [12288, 4096], P('blk'), may hold values from -0.054126588 to 0.054126588
- gain: float32 [4096], P('blk'), may hold values from 0.1 to 1.9
Outputs:
- query_grad: bfloat16 [128, 4096], P(('wide', 'blk'))
- resid_grad: bfloat16 [2304, 4096], P('wide', 'blk')
- act_grad: bfloat16 [2304, 12288], P('wide', 'blk')
- normed_out: bfloat16 [2304, 4096], P('wide', 'blk')
Inputs may be any that keep to these rules, and one draw needn't show every extreme that they name: `token_lengths`: each row lists the token counts of the group's 16 passages in order and sums to 192. Among the token rows of one group, at most 36 name the same destination.
All inputs are finite; a program needn't handle non-finite values.
Results may differ from a plain program's by a relative error of at most 0.02.
Values may be sent and summed in bfloat16 or wider, within the bound.
No kernel may reach another device: no remote copies, remote signals or barrier semaphores. Data moves between devices by JAX's collectives and lax.ppermute only.
A program may use at most 64 MiB of HBM per device.

v0:
```python
import jax
import jax.numpy as jnp
from jax import lax
from jax.sharding import PartitionSpec as P

logit_scale = 24.0
norm_eps = 1e-06


def coefficients(scores, lse_part, pos_part):
    columns = lax.broadcasted_iota(jnp.int32, scores.shape, 1)
    target = (pos_part[:, None] == columns).astype(jnp.float32)
    return (jnp.exp(scores - lse_part[:, None]) - target).astype(jnp.bfloat16)


def norm_layer(act_rows, resid_rows, grad_rows, w_down, gain):
    feat_width = resid_rows.shape[1]
    features = w_down.shape[1]
    offset = lax.axis_index("blk") * feat_width
    partial_terms = jnp.dot(act_rows, w_down, preferred_element_type=jnp.float32)
    own_columns = lax.dynamic_slice_in_dim(
        partial_terms, offset, feat_width, 1
    ) + resid_rows.astype(jnp.float32)
    partial_terms = lax.dynamic_update_slice_in_dim(partial_terms, own_columns, offset, 1)
    hidden = lax.psum_scatter(
        partial_terms.astype(jnp.bfloat16), "blk", scatter_dimension=1, tiled=True
    ).astype(jnp.float32)
    gained = gain[None, :] * grad_rows.astype(jnp.float32)
    squares, inner_sum = lax.psum(
        (jnp.sum(hidden * hidden, axis=1), jnp.sum(gained * hidden, axis=1)), "blk"
    )
    inv_rms = lax.rsqrt(squares / features + norm_eps)[:, None]
    inner_sum = inner_sum[:, None]
    normed = (gain[None, :] * hidden * inv_rms).astype(jnp.bfloat16)
    resid_back = (
        inv_rms * gained - hidden * (inv_rms * inv_rms * inv_rms) * inner_sum / features
    ).astype(jnp.bfloat16)
    act_back = lax.dot_general(
        lax.all_gather(resid_back, "blk", axis=1, tiled=True),
        w_down,
        (((1,), (1,)), ((), ())),
        preferred_element_type=jnp.float32,
    )
    return (resid_back, act_back.astype(jnp.bfloat16), normed)


def shards(
    query_emb,
    passage_emb,
    row_lse,
    positive,
    token_lengths,
    destination,
    mlp_act,
    resid,
    w_down,
    gain,
):
    pair_rows = query_emb.shape[0]
    feat_width = resid.shape[1]
    hid_width = w_down.shape[0]
    blk_index = lax.axis_index("blk")
    first_row = blk_index * pair_rows
    query_all, passage_all = (
        lax.all_gather(query_emb, "blk", axis=0, tiled=True),
        lax.all_gather(passage_emb, "blk", axis=0, tiled=True),
    )
    scores = logit_scale * jnp.dot(query_all, passage_all.T, preferred_element_type=jnp.float32)
    coef_full = coefficients(scores, row_lse, positive)
    own_coef = lax.dynamic_slice_in_dim(coef_full, first_row, pair_rows, 0)
    query_grad = (
        logit_scale * jnp.dot(own_coef, passage_all, preferred_element_type=jnp.float32)
    ).astype(jnp.bfloat16)
    query_cols = lax.dynamic_slice_in_dim(query_all, blk_index * feat_width, feat_width, 1)
    grad_cols = logit_scale * lax.dot_general(
        query_cols, coef_full, (((0,), (0,)), ((), ())), preferred_element_type=jnp.float32
    )
    lengths_row = token_lengths[0]
    starts = jnp.cumsum(lengths_row) - lengths_row
    tok_count = resid.shape[0]
    positions = lax.broadcasted_iota(jnp.int32, (tok_count, lengths_row.shape[0]), 0)
    member = (positions >= starts[None, :]) & (positions < (starts + lengths_row)[None, :])
    weights = member.astype(jnp.float32) * (1.0 / lengths_row.astype(jnp.float32))[None, :]
    tok_grad = lax.dot_general(
        weights,
        grad_cols,
        (((1,), (1,)), ((), ())),
        precision=lax.Precision.HIGHEST,
        preferred_element_type=jnp.float32,
    ).astype(jnp.bfloat16)
    wide_count = lax.axis_size("wide")
    slot_count = 3 * tok_count // (2 * wide_count)
    dest_hot = (destination == lax.broadcasted_iota(jnp.int32, (tok_count, wide_count), 1)).astype(
        jnp.int32
    )
    rank_of = jnp.cumsum(dest_hot, axis=0) - dest_hot
    slot_of = jnp.sum(rank_of * dest_hot, axis=1) + destination[:, 0] * slot_count
    placer = (
        lax.broadcasted_iota(jnp.int32, (wide_count * slot_count, tok_count), 0) == slot_of[None, :]
    ).astype(jnp.bfloat16)
    payload = jnp.concatenate([mlp_act, resid, tok_grad], axis=1)
    packed = jnp.dot(placer, payload, preferred_element_type=jnp.float32).astype(jnp.bfloat16)
    packed = packed.reshape(wide_count, slot_count, hid_width + 2 * feat_width)
    arrived = lax.all_to_all(packed, "wide", split_axis=0, concat_axis=0, tiled=True).reshape(
        wide_count * slot_count, hid_width + 2 * feat_width
    )
    resid_grad, act_grad, normed_out = norm_layer(
        arrived[:, :hid_width],
        arrived[:, hid_width : hid_width + feat_width],
        arrived[:, hid_width + feat_width :],
        w_down,
        gain,
    )
    return (query_grad, resid_grad, act_grad, normed_out)


def solution(mesh):
    return jax.shard_map(
        shards,
        mesh=mesh,
        in_specs=(
            P(("wide", "blk"), None),
            P(("wide", "blk"), None),
            P("wide"),
            P("wide"),
            P("wide", None),
            P("wide", None),
            P("wide", "blk"),
            P("wide", "blk"),
            P("blk", None),
            P("blk"),
        ),
        out_specs=(P(("wide", "blk"), None), P("wide", "blk"), P("wide", "blk"), P("wide", "blk")),
        check_vma=False,
    )
```

profile of v0, /device:TPU:0, one launch (start us, length us, event | category | flops | bytes accessed | tf_op | source)
XLA Modules:
  0.0 242.7 jit_solution(7557931241313803358)
XLA Ops:
  7.2 0.0 reduce-scatter.2.cloned.1.call-start
  7.2 0.7 divide_bitcast_fusion
  7.9 0.7 iota_compare_fusion.5
  8.6 0.6 reduce-window.10
  9.2 0.2 slice_reduce_fusion
  9.4 0.1 add_bitcast_fusion
  9.5 0.7 fusion.30
  10.2 0.7 multiply_add_fusion
  10.9 0.7 copy.16
  11.7 0.1 reduce.1
  11.8 0.7 fusion.34
  12.4 10.1 %all-gather = bf16[4,4,4096]{2,1,0:T(4,128)(2,1)S(1)} all-gather(bf16[1,4,4096]{2,1,0:T(4,128)(2,1)} %bitcast.26), channel_id=1, replica_groups=mesh['wide'=8,'blk'=4] {'blk'}, dimensions={0}, use_global_device_ids=true | all-gather | bytes 163840 | tf_op jit(solution)/shard_map/all_gather | solution.py:65
  22.6 8.2 %all-gather.1 = bf16[4,4,4096]{2,1,0:T(4,128)(2,1)S(1)} all-gather(bf16[1,4,4096]{2,1,0:T(4,128)(2,1)} %bitcast.27), channel_id=1, replica_groups=mesh['wide'=8,'blk'=4] {'blk'}, dimensions={0}, use_global_device_ids=true | all-gather | bytes 163840 | tf_op jit(solution)/shard_map/all_gather | solution.py:66
  30.9 0.8 fusion.19
  31.7 0.2 convolution_multiply_fusion.1
  31.9 0.8 convolution_convert_fusion.2
  32.7 3.9 %convolution_convert_fusion = bf16[288,5120]{1,0:T(8,128)(2,1)} fusion(bf16[192,1024]{1,0:T(8,128)(2,1)S(1)} %convolution_convert_fusion.2, bf16[192,1024]{1,0:T(8,128)(2,1)} %param.17, bf16[192,3072]{1,0:T(8,128)(2,1)} %param.16, s32[192]{0:T(256)S(1)} %multiply_add_fusion), kind=kOutput, calls=%fused_computation | convolution fusion | flops 573659136 | bytes 4915968 | tf_op jit(solution)/shard_map/dot_general | solution.py:102
  36.6 2.8 %reshape.52 = bf16[8,36,5120]{2,1,0:T(8,128)(2,1)S(1)} reshape(bf16[288,5120]{1,0:T(8,128)(2,1)} %convolution_convert_fusion) | data formatting | bytes 5898240 | tf_op jit(solution)/shard_map/reshape | solution.py:103
  39.5 79.1 %all_to_all.5 = bf16[8,36,5120]{2,1,0:T(8,128)(2,1)} all-to-all(bf16[8,36,5120]{2,1,0:T(8,128)(2,1)S(1)} %reshape.52), channel_id=1, replica_groups=mesh['wide'=8,'blk'=4] {'wide'}, dimensions={0} | all-to-all | bytes 5898240 | tf_op jit(solution)/shard_map/all_to_all | solution.py:104
  118.6 2.9 %reshape.53 = bf16[288,5120]{1,0:T(8,128)(2,1)S(1)} reshape(bf16[8,36,5120]{2,1,0:T(8,128)(2,1)} %all_to_all.5) | data formatting | bytes 5898240 | tf_op jit(solution)/shard_map/reshape | solution.py:104
  121.5 12.3 %fusion.6 = f32[288,4096]{1,0:T(8,128)S(1)} fusion(bf16[3072,4096]{1,0:T(8,128)(2,1)} %param.18, bf16[288,5120]{1,0:T(8,128)(2,1)S(1)} %reshape.53), kind=kOutput, calls=%fused_computation.13 | convolution fusion | flops 7247757312 | bytes 31653888 | tf_op jit(solution)/shard_map/dot_general | solution.py:20
  133.9 0.2 add_dynamic-update-slice_fusion
  134.1 1.7 convert_element_type.54
  135.9 0.0 copy-start
  135.9 0.0 reduce-scatter.2.cloned.1.call-update
  135.9 0.0 all-gather.4.cloned.1.call-start
  135.9 35.4 %reduce-scatter.2.cloned.1.call-done = bf16[288,1024]{1,0:T(8,128)(2,1)} async-done(((bf16[288,4096]{1,0:T(8,128)(2,1)}), bf16[288,1024]{1,0:T(8,128)(2,1)}) %reduce-scatter.2.cloned.1.call-update) | async-done | bytes 589840 | tf_op jit(solution)/shard_map/reduce_scatter | solution.py:25
  171.4 0.0 copy-done
  171.4 1.4 fusion.8
  172.8 8.9 %all-reduce.1 = (f32[288]{0:T(512)S(1)}, f32[288]{0:T(512)S(1)}) all-reduce(f32[288]{0:T(512)S(1)} %get-tuple-element.5, f32[288]{0:T(512)S(1)} %get-tuple-element.4), channel_id=1, replica_groups=mesh['wide'=8,'blk'=4] {'blk'}, use_global_device_ids=true, to_apply=%region_8.9 | all-reduce | flops 576 | bytes 4608 | tf_op jit(solution)/shard_map/psum | solution.py:29
  181.7 2.6 %fusion.15 = (bf16[288,1024]{1,0:T(8,128)(2,1)}, bf16[288,1024]{1,0:T(8,128)(2,1)}) fusion(bf16[288,1024]{1,0:T(8,128)(2,1)} %reduce-scatter.2.cloned.1.call-done, f32[1024]{0:T(1024)S(1)} %copy-done, f32[288]{0:T(512)S(1)} %get-tuple-element.10, f32[288]{0:T(512)S(1)} %get-tuple-element.6, f32[288]{0:T(512)S(1)} %get-tuple-element.11, ...), kind=kLoop, calls=%fused_computation.23 | loop fusion | flops 3538944 | bytes 2366848 | tf_op jit(solution)/shard_map/convert_element_type | solution.py:34
  184.3 0.0 all-gather.4.cloned.1.call-update
  184.3 0.8 fusion
  185.1 36.8 %all-gather.4.cloned.1.call-done = bf16[288,4096]{1,0:T(8,128)(2,1)} async-done(((bf16[288,1024]{1,0:T(8,128)(2,1)}), bf16[288,4096]{1,0:T(8,128)(2,1)}) %all-gather.4.cloned.1.call-update) | async-done | bytes 2359312 | tf_op jit(solution)/shard_map/all_gather | solution.py:39
  221.9 13.9 %convolution_convert_fusion.1 = bf16[288,3072]{1,0:T(8,128)(2,1)} fusion(bf16[288,4096]{1,0:T(8,128)(2,1)} %all-gather.4.cloned.1.call-done, bf16[3072,4096]{1,0:T(8,128)(2,1)} %param.18), kind=kOutput, calls=%fused_computation.3 | convolution fusion | flops 7248642048 | bytes 29294592 | tf_op jit(solution)/shard_map/dot_general | solution.py:38
  (7 shorter events, 0.2 us)
Async XLA Ops:
  7.2 164.2 %reduce-scatter.2.cloned.1.call-start = ((), (), s32[]{:S(2)}) async-start(), calls=%async_computation.2 | async-start | bytes 2949120 | tf_op jit(solution)/shard_map/reduce_scatter | solution.py:25
  135.9 35.5 %copy-start = (f32[1024]{0:T(1024)S(1)}, f32[1024]{0:T(1024)}, u32[]{:S(2)}) copy-start(f32[1024]{0:T(1024)} %param.19) | copy-start | bytes 12292
  135.9 86.0 %all-gather.4.cloned.1.call-start = ((), (), s32[]{:S(2)}) async-start(), calls=%async_computation.3 | async-start | bytes 2949120 | tf_op jit(solution)/shard_map/all_gather | solution.py:39
Sparse Core Ops, SparseCore 0:
  136.0 35.3 reduce-scatter.1
  184.5 37.4 all-gather.3
where the time goes:
time: 243 us
  blocking collectives  106 us (44%)
  waiting for transfers between devices  72.3 us (30%)
  matrix products  32.7 us (13%)
  between operations  14.1 us (6%)
  other arithmetic  10.3 us (4%)
  local copies, waits for them, and re-layouts  6.79 us (3%)
    all_to_all x1, blocking collectives, shards(): lax.all_to_all(packed, 'wide', split_axis=0, concat_axis=0, tiled=True)  79.1 us
    all_gather x1, waiting for transfers between devices, norm_layer(): lax.all_gather(resid_back, 'blk', axis=1, tiled=True)  36.8 us
    reduce_scatter x1, waiting for transfers between devices, norm_layer(): lax.psum_scatter(partial_terms.astype(jnp.bfloat16), 'blk', scatter_dimen...  35.4 us
    dot_general x1, matrix products, norm_layer(): lax.dot_general(lax.all_gather(resid_back, 'blk', axis=1, tiled=True), w_...  13.9 us
    dot_general x1, matrix products, norm_layer(): jnp.dot(act_rows, w_down, preferred_element_type=jnp.float32)  12.3 us
    all_gather x1, blocking collectives, shards(): lax.all_gather(query_emb, 'blk', axis=0, tiled=True)  10.1 us
    psum x1, blocking collectives, norm_layer(): lax.psum((jnp.sum(hidden * hidden, axis=1), jnp.sum(gained * hidden, axis...  8.91 us
    all_gather x1, blocking collectives, shards(): lax.all_gather(passage_emb, 'blk', axis=0, tiled=True)  8.25 us
  transfers between devices with their start and end apart: 2, of which 2 were waited for; matrix products, arithmetic and copies ran while one was open for 0% of the time, Pallas kernels for 0%

commit v1 on v0

v1 whole, which is shorter than its diff:
```python
import jax
import jax.numpy as jnp
from jax import lax
from jax.experimental import pallas as pl
from jax.experimental.pallas import tpu as pltpu
from jax.sharding import PartitionSpec as P

logit_scale = 24.0
norm_eps = 1e-06
f32 = jnp.float32
bf16 = jnp.bfloat16
kernel_vmem = 24 * 1024 * 1024


def tile_of(extent, most):
    tile = most
    while extent % tile:
        tile //= 2
    return tile


def swap(rows, axis, count, k):
    return lax.ppermute(rows, axis, [(i, i ^ k) for i in range(count)])


def project_body(group_ref, act_ref, w_ref, out_ref):
    out_ref[...] = jnp.dot(act_ref[...], w_ref[...], preferred_element_type=f32).astype(
        out_ref.dtype
    )


def project_own_body(group_ref, act_ref, w_ref, resid_ref, out_ref):
    out_ref[...] = jnp.dot(act_ref[...], w_ref[...], preferred_element_type=f32) + resid_ref[
        ...
    ].astype(f32)


def project(group, act, w_down, width, resid=None):
    rows, depth = act.shape
    tile = tile_of(width, 256)
    per_group = width // tile
    column_spec = pl.BlockSpec((rows, tile), lambda j, g: (0, j))
    in_specs = [
        pl.BlockSpec((rows, depth), lambda j, g: (0, 0)),
        pl.BlockSpec((depth, tile), lambda j, g: (0, g[0] * per_group + j)),
    ]
    operands = [act, w_down]
    if resid is not None:
        in_specs.append(column_spec)
        operands.append(resid)
    return pl.pallas_call(
        project_body if resid is None else project_own_body,
        grid_spec=pltpu.PrefetchScalarGridSpec(
            num_scalar_prefetch=1, grid=(per_group,), in_specs=in_specs, out_specs=column_spec
        ),
        out_shape=jax.ShapeDtypeStruct((rows, width), bf16 if resid is None else f32),
        compiler_params=pltpu.CompilerParams(vmem_limit_bytes=kernel_vmem),
        cost_estimate=pl.CostEstimate(
            flops=2 * rows * depth * width,
            bytes_accessed=2 * depth * width + 2 * rows * (depth + width),
            transcendentals=0,
        ),
    )(group, *operands)


def dot_t(left, right):
    return lax.dot_general(left, right, (((1,), (1,)), ((), ())), preferred_element_type=f32)


def back_first_body(group_ref, hid_ref, w_ref, out_ref):
    out_ref[...] = dot_t(hid_ref[...], w_ref[...])


def back_next_body(group_ref, hid_ref, w_ref, acc_ref, out_ref):
    out_ref[...] = acc_ref[...] + dot_t(hid_ref[...], w_ref[...])


def back(group, hid, w_down, acc=None):
    rows, width = hid.shape
    depth = w_down.shape[0]
    tile = tile_of(depth, 512)
    unit_spec = pl.BlockSpec((rows, tile), lambda j, g: (0, j))
    in_specs = [
        pl.BlockSpec((rows, width), lambda j, g: (0, 0)),
        pl.BlockSpec((tile, width), lambda j, g: (j, g[0])),
    ]
    operands = [hid, w_down]
    if acc is not None:
        in_specs.append(unit_spec)
        operands.append(acc)
    return pl.pallas_call(
        back_first_body if acc is None else back_next_body,
        grid_spec=pltpu.PrefetchScalarGridSpec(
            num_scalar_prefetch=1, grid=(depth // tile,), in_specs=in_specs, out_specs=unit_spec
        ),
        out_shape=jax.ShapeDtypeStruct((rows, depth), f32),
        compiler_params=pltpu.CompilerParams(vmem_limit_bytes=kernel_vmem),
        cost_estimate=pl.CostEstimate(
            flops=2 * rows * depth * width,
            bytes_accessed=2 * depth * width + 2 * rows * width + 8 * rows * depth,
            transcendentals=0,
        ),
    )(group, *operands)


def finish_body(features, *refs):
    (
        group_ref,
        hid_ref,
        w_ref,
        acc_ref,
        cross_ref,
        square_ref,
        hot_ref,
        share_ref,
        low_ref,
        low_act_ref,
        own_hid_ref,
        own_low_ref,
        gain_ref,
        act_out,
        resid_out,
        normed_out,
        lead,
        back_off,
    ) = refs

    @pl.when(pl.program_id(0) == 0)
    def _():
        hid = hid_ref[...]
        wide_hid = hid.astype(f32)
        squares = square_ref[...] + jnp.sum(wide_hid * wide_hid, axis=1, keepdims=True)
        cross = cross_ref[...] + dot_t(hid, low_ref[...])
        weights = hot_ref[...].astype(f32) * share_ref[...]
        inner = jnp.sum(cross * weights, axis=1, keepdims=True)
        inv_rms = lax.rsqrt(squares / features + norm_eps)
        lead[...] = inv_rms * jnp.sum(weights, axis=1, keepdims=True)
        back_off[...] = inv_rms * inv_rms * inv_rms * inner / features
        own = own_hid_ref[...].astype(f32)
        own_low = jnp.dot(hot_ref[...], own_low_ref[...], preferred_element_type=f32)
        resid_out[...] = (lead[...] * own_low - own * back_off[...]).astype(bf16)
        normed_out[...] = (gain_ref[...] * own * inv_rms).astype(bf16)

    low_act = jnp.dot(hot_ref[...], low_act_ref[...], preferred_element_type=f32)
    hid_act = acc_ref[...] + dot_t(hid_ref[...], w_ref[...])
    act_out[...] = (lead[...] * low_act - back_off[...] * hid_act).astype(bf16)


def finish(groups, hid, w_down, acc, cross, squares, hot, share, low, low_act, own_hid, gain):
    rows, width = hid.shape
    depth, features = w_down.shape
    pairs = hot.shape[1]
    tile = tile_of(depth, 512)

    def whole(shape):
        return pl.BlockSpec(shape, lambda j, g: (0, 0))

    def body(*refs):
        finish_body(features, *refs)

    return pl.pallas_call(
        body,
        grid_spec=pltpu.PrefetchScalarGridSpec(
            num_scalar_prefetch=1,
            grid=(depth // tile,),
            in_specs=[
                whole((rows, width)),
                pl.BlockSpec((tile, width), lambda j, g: (j, g[0])),
                pl.BlockSpec((rows, tile), lambda j, g: (0, j)),
                whole((rows, pairs)),
                whole((rows, 1)),
                whole((rows, pairs)),
                whole((1, pairs)),
                pl.BlockSpec((pairs, width), lambda j, g: (0, g[0])),
                pl.BlockSpec((pairs, tile), lambda j, g: (0, j)),
                whole((rows, width)),
                pl.BlockSpec((pairs, width), lambda j, g: (0, g[1])),
                whole((1, width)),
            ],
            out_specs=[
                pl.BlockSpec((rows, tile), lambda j, g: (0, j)),
                whole((rows, width)),
                whole((rows, width)),
            ],
            scratch_shapes=[pltpu.VMEM((rows, 1), f32), pltpu.VMEM((rows, 1), f32)],
        ),
        out_shape=[
            jax.ShapeDtypeStruct((rows, depth), bf16),
            jax.ShapeDtypeStruct((rows, width), bf16),
            jax.ShapeDtypeStruct((rows, width), bf16),
        ],
        compiler_params=pltpu.CompilerParams(vmem_limit_bytes=kernel_vmem),
        cost_estimate=pl.CostEstimate(
            flops=2 * rows * depth * width,
            bytes_accessed=2 * depth * width + 8 * rows * width + 6 * rows * depth,
            transcendentals=0,
        ),
    )(groups, hid, w_down, acc, cross, squares, hot, share, low, low_act, own_hid, low, gain)


def group_gradients(query_emb, passage_emb, row_lse, positive, gain, blk, blk_count):
    pair_rows = query_emb.shape[0]
    pairs = row_lse.shape[0]
    width = gain.shape[0]
    both = jnp.concatenate([query_emb, passage_emb], axis=0)
    parts = [both] + [swap(both, "blk", blk_count, k) for k in range(1, blk_count)]
    gains = [gain[None]] + [swap(gain[None], "blk", blk_count, k) for k in range(1, blk_count)]
    queries = jnp.concatenate([part[:pair_rows] for part in parts], axis=0)
    passages = jnp.concatenate([part[pair_rows:] for part in parts], axis=0)
    place = lax.iota(jnp.int32, pairs)
    named = (blk ^ (place // pair_rows)) * pair_rows + place % pair_rows
    reorder = named[:, None] == place[None, :]
    lse = jnp.sum(jnp.where(reorder, row_lse[None, :], 0.0), axis=1)
    target = jnp.sum(jnp.where(reorder, positive[None, :], 0), axis=1)
    scores = logit_scale * dot_t(queries, passages)
    hit = (target[:, None] == named[None, :]).astype(f32)
    coef = (jnp.exp(scores - lse[:, None]) - hit).astype(bf16)
    query_grad = (
        logit_scale * jnp.dot(coef[:pair_rows], passages, preferred_element_type=f32)
    ).astype(bf16)
    coef_named = jnp.dot(coef, reorder.astype(bf16), preferred_element_type=f32).astype(bf16)
    pass_grad = logit_scale * lax.dot_general(
        coef_named, queries, (((0,), (0,)), ((), ())), preferred_element_type=f32
    )
    stacked = jnp.concatenate(gains, axis=0)
    index = lax.iota(jnp.int32, blk_count)
    pick = (blk ^ index)[:, None, None] == index[None, :, None]
    whole_gain = jnp.sum(jnp.where(pick, stacked[None], 0.0), axis=1).reshape(1, blk_count * width)
    return query_grad, (whole_gain * pass_grad).astype(bf16)


def place_rows(destination, wide_count, slot_count):
    tok_count = destination.shape[0]
    dest_hot = (destination == lax.broadcasted_iota(jnp.int32, (tok_count, wide_count), 1)).astype(
        bf16
    )
    token = lax.iota(jnp.int32, tok_count)
    earlier = (token[None, :] < token[:, None]).astype(bf16)
    rank_of = jnp.dot(earlier, dest_hot, preferred_element_type=f32)
    slot_of = jnp.sum(rank_of * dest_hot.astype(f32), axis=1).astype(jnp.int32)
    slot_of = slot_of + destination[:, 0] * slot_count
    return (
        lax.broadcasted_iota(jnp.int32, (wide_count * slot_count, tok_count), 0) == slot_of[None, :]
    ).astype(bf16)


def slot_passages(dest_all, len_all, wide, slot_count):
    groups, tok_count = dest_all.shape
    per_group = len_all.shape[1]
    token = lax.iota(jnp.int32, tok_count)
    hit = dest_all == wide
    earlier = (token[:, None] < token[None, :]).astype(bf16)
    rank = jnp.dot(hit.astype(bf16), earlier, preferred_element_type=f32).astype(jnp.int32)
    order = lax.iota(jnp.int32, per_group)
    upto = (order[:, None] <= order[None, :]).astype(jnp.int32)
    ends = jnp.sum(len_all[:, :, None] * upto[None], axis=1)
    passage = jnp.sum((token[None, None, :] >= ends[:, :, None]).astype(jnp.int32), axis=1)
    code = jnp.where(hit, passage + 1, 0)
    slot = lax.iota(jnp.int32, slot_count)
    taken = jnp.sum(
        jnp.where(rank[:, None, :] == slot[None, :, None], code[:, None, :], 0), axis=2
    )
    column = lax.iota(jnp.int32, groups * per_group)
    group = lax.iota(jnp.int32, groups)
    hot = (column[None, None, :] // per_group == group[:, None, None]) & (
        column[None, None, :] % per_group + 1 == taken[:, :, None]
    )
    return hot.astype(bf16).reshape(groups * slot_count, groups * per_group)


def low_rank_shards(
    query_emb,
    passage_emb,
    row_lse,
    positive,
    token_lengths,
    destination,
    mlp_act,
    resid,
    w_down,
    gain,
):
    blk_count, wide_count = lax.axis_size("blk"), lax.axis_size("wide")
    blk, wide = lax.axis_index("blk"), lax.axis_index("wide")
    tok_count, width = resid.shape
    pairs = row_lse.shape[0]
    slot_count = 3 * tok_count // (2 * wide_count)

    query_grad, low_own = group_gradients(
        query_emb, passage_emb, row_lse, positive, gain, blk, blk_count
    )
    tables = jnp.concatenate([destination[:, 0], token_lengths[0]])
    tables = lax.all_gather(tables, "wide", axis=0)
    dest_all, len_all = tables[:, :tok_count], tables[:, tok_count:]
    low = lax.all_gather(low_own, "wide", axis=0, tiled=True)

    def group_index(k):
        return (blk ^ k)[None]

    far_first = [k for k in range(blk_count - 1, 0, -1)]
    arrived = {}
    for k in far_first:
        term = project(group_index(k), mlp_act, w_down, width)
        arrived[k] = swap(term, "blk", blk_count, k)
    hidden = project(group_index(0), mlp_act, w_down, width, resid)
    for k in far_first:
        hidden = hidden + arrived[k].astype(f32)

    placer = place_rows(destination, wide_count, slot_count)
    packed = jnp.dot(placer, hidden.astype(bf16), preferred_element_type=f32).astype(bf16)
    packed = packed.reshape(wide_count, slot_count, width)
    own_hid = lax.all_to_all(packed, "wide", split_axis=0, concat_axis=0, tiled=True).reshape(
        wide_count * slot_count, width
    )
    hids = [own_hid] + [swap(own_hid, "blk", blk_count, k) for k in range(1, blk_count)]

    low_act = dot_t(low, w_down).astype(bf16)
    hot = slot_passages(dest_all, len_all, wide, slot_count)
    share = (1.0 / len_all.astype(f32)).reshape(1, wide_count * pairs)

    acc, cross, squares = None, 0.0, 0.0
    for k in range(blk_count - 1):
        acc = back(group_index(k), hids[k], w_down, acc)
        low_part = lax.dynamic_slice_in_dim(low, (blk ^ k) * width, width, 1)
        cross = cross + dot_t(hids[k], low_part)
        wide_hid = hids[k].astype(f32)
        squares = squares + jnp.sum(wide_hid * wide_hid, axis=1, keepdims=True)
    last = blk_count - 1
    act_grad, resid_grad, normed_out = finish(
        jnp.stack([blk ^ last, blk]),
        hids[last],
        w_down,
        acc,
        cross,
        squares,
        hot,
        share,
        low,
        low_act,
        own_hid,
        gain[None],
    )
    return (query_grad, resid_grad, act_grad, normed_out)


def coefficients(scores, lse_part, pos_part):
    columns = lax.broadcasted_iota(jnp.int32, scores.shape, 1)
    target = (pos_part[:, None] == columns).astype(jnp.float32)
    return (jnp.exp(scores - lse_part[:, None]) - target).astype(jnp.bfloat16)


def row_shards(
    query_emb,
    passage_emb,
    row_lse,
    positive,
    token_lengths,
    destination,
    mlp_act,
    resid,
    w_down,
    gain,
):
    pair_rows = query_emb.shape[0]
    tok_count, feat_width = resid.shape
    features = w_down.shape[1]
    blk_index = lax.axis_index("blk")
    wide_count = lax.axis_size("wide")
    slot_count = 3 * tok_count // (2 * wide_count)
    offset = blk_index * feat_width
    query_all = lax.all_gather(query_emb, "blk", axis=0, tiled=True)
    passage_all = lax.all_gather(passage_emb, "blk", axis=0, tiled=True)
    scores = logit_scale * jnp.dot(query_all, passage_all.T, preferred_element_type=f32)
    coef_full = coefficients(scores, row_lse, positive)
    own_coef = lax.dynamic_slice_in_dim(coef_full, blk_index * pair_rows, pair_rows, 0)
    query_grad = (
        logit_scale * jnp.dot(own_coef, passage_all, preferred_element_type=f32)
    ).astype(bf16)
    query_cols = lax.dynamic_slice_in_dim(query_all, offset, feat_width, 1)
    grad_cols = logit_scale * lax.dot_general(
        query_cols, coef_full, (((0,), (0,)), ((), ())), preferred_element_type=f32
    )
    lengths_row = token_lengths[0]
    starts = jnp.cumsum(lengths_row) - lengths_row
    positions = lax.broadcasted_iota(jnp.int32, (tok_count, lengths_row.shape[0]), 0)
    member = (positions >= starts[None, :]) & (positions < (starts + lengths_row)[None, :])
    weights = member.astype(f32) * (1.0 / lengths_row.astype(f32))[None, :]
    tok_grad = lax.dot_general(
        weights,
        grad_cols,
        (((1,), (1,)), ((), ())),
        precision=lax.Precision.HIGHEST,
        preferred_element_type=f32,
    ).astype(bf16)
    terms = jnp.dot(mlp_act, w_down, preferred_element_type=f32)
    own = lax.dynamic_slice_in_dim(terms, offset, feat_width, 1) + resid.astype(f32)
    terms = lax.dynamic_update_slice_in_dim(terms, own, offset, 1)
    hidden = lax.psum_scatter(terms.astype(bf16), "blk", scatter_dimension=1, tiled=True)
    placer = place_rows(destination, wide_count, slot_count)
    payload = jnp.concatenate([hidden, tok_grad], axis=1)
    packed = jnp.dot(placer, payload, preferred_element_type=f32).astype(bf16)
    packed = packed.reshape(wide_count, slot_count, 2 * feat_width)
    rows = lax.all_to_all(packed, "wide", split_axis=0, concat_axis=0, tiled=True).reshape(
        wide_count * slot_count, 2 * feat_width
    )
    hidden = rows[:, :feat_width].astype(f32)
    gained = gain[None, :] * rows[:, feat_width:].astype(f32)
    squares, inner_sum = lax.psum(
        (jnp.sum(hidden * hidden, axis=1), jnp.sum(gained * hidden, axis=1)), "blk"
    )
    inv_rms = lax.rsqrt(squares / features + norm_eps)[:, None]
    normed = (gain[None, :] * hidden * inv_rms).astype(bf16)
    resid_back = (
        inv_rms * gained - hidden * (inv_rms * inv_rms * inv_rms) * inner_sum[:, None] / features
    ).astype(bf16)
    act_back = dot_t(lax.all_gather(resid_back, "blk", axis=1, tiled=True), w_down)
    return (query_grad, resid_back, act_back.astype(bf16), normed)


def solution(mesh):
    blk_count, wide_count = mesh.shape["blk"], mesh.shape["wide"]

    def shards(*operands):
        pairs, tok_count = operands[2].shape[0], operands[7].shape[0]
        low_rank = 2 * wide_count * pairs <= 3 * tok_count
        if low_rank and blk_count > 1 and blk_count & (blk_count - 1) == 0:
            return low_rank_shards(*operands)
        return row_shards(*operands)

    return jax.shard_map(
        shards,
        mesh=mesh,
        in_specs=(
            P(("wide", "blk"), None),
            P(("wide", "blk"), None),
            P("wide"),
            P("wide"),
            P("wide", None),
            P("wide", None),
            P("wide", "blk"),
            P("wide", "blk"),
            P("blk", None),
            P("blk"),
        ),
        out_specs=(P(("wide", "blk"), None), P("wide", "blk"), P("wide", "blk"), P("wide", "blk")),
        check_vma=False,
    )
```

time: 243 us -> 178 us (0.73)
  blocking collectives: 106 us -> 9.29 us
  waiting for transfers between devices: 72.3 us -> 27.1 us
  Pallas kernels: 0 us -> 36.3 us
  local copies, waits for them, and re-layouts: 6.79 us -> 34.9 us
  starting transfers between devices: 0.08 us -> 19.3 us
  matrix products: 32.7 us -> 24.4 us
    all_to_all x1 -> x0, blocking collectives: 79.1 us -> none  [shards(): lax.all_to_all(packed, 'wide', split_axis=0, concat_axis=0, tiled=True)]
    all_gather x1, waiting for transfers between devices: 36.8 us -> 0.01 us  [low_rank_shards(): low = lax.all_gather(low_own, 'wide', axis=0, tiled=True)]
    pallas_call x0 -> x8, Pallas kernels: none -> 36.3 us  [the longest x3 15.9 us: back(): pl.pallas_call(back_first_body if acc is None else back_next_body, grid_s...]
    reduce_scatter x1 -> x0, waiting for transfers between devices: 35.4 us -> none  [norm_layer(): lax.psum_scatter(partial_terms.astype(jnp.bfloat16), 'blk', scatter_dimen...]
    unnamed x4 -> x55, local copies, waits for them, and re-layouts: 0.07 us -> 30.6 us
    all_gather x2 -> x0, blocking collectives: 18.4 us -> none  [the longest x1 10.1 us: shards(): lax.all_gather(query_emb, 'blk', axis=0, tiled=True)]
    all_to_all x0 -> x1, waiting for transfers between devices: none -> 15.8 us  [low_rank_shards(): lax.all_to_all(packed, 'wide', split_axis=0, concat_axis=0, tiled=True)]
    ppermute x0 -> x12, starting transfers between devices: none -> 15.5 us  [swap(): return lax.ppermute(rows, axis, [(i, i ^ k) for i in range(count)])]
  transfers between devices with their start and end apart: 2 -> 14, of which waited for: 2 -> 3; matrix products, arithmetic and copies ran while one was open for 0% -> 21% of each run, Pallas kernels for 0% -> 16%
where the time goes in v1:
time: 178 us; the launch traced here: 176 us
  Pallas kernels  36.3 us (20%)
  local copies, waits for them, and re-layouts  34.9 us (20%)
  waiting for transfers between devices  27.1 us (15%)
  matrix products  24.4 us (14%)
  starting transfers between devices  19.3 us (11%)
  between operations  15.2 us (9%)
  other arithmetic  9.92 us (6%)
  blocking collectives  9.29 us (5%)
    unnamed x55, local copies, waits for them, and re-layouts  30.6 us
    dot_general x5, matrix products, dot_t(): lax.dot_general(left, right, (((1,), (1,)), ((), ())), preferred_element_...  19.4 us
    pallas_call x3, Pallas kernels, back(): pl.pallas_call(back_first_body if acc is None else back_next_body, grid_s...  15.9 us
    all_to_all x1, waiting for transfers between devices, low_rank_shards(): lax.all_to_all(packed, 'wide', split_axis=0, concat_axis=0, tiled=True)  15.8 us
    ppermute x12, starting transfers between devices, swap(): return lax.ppermute(rows, axis, [(i, i ^ k) for i in range(count)])  15.5 us
    pallas_call x4, Pallas kernels, project(): pl.pallas_call(project_body if resid is None else project_own_body, grid_...  11.9 us
    ppermute x12, waiting for transfers between devices, swap(): return lax.ppermute(rows, axis, [(i, i ^ k) for i in range(count)])  11.3 us
    unnamed x1, blocking collectives  9.29 us
  transfers between devices with their start and end apart: 14, of which 3 were waited for; matrix products, arithmetic and copies ran while one was open for 21% of the time, Pallas kernels for 16%

profile of v1, /device:TPU:0, one launch (start us, length us, event | category | flops | bytes accessed | tf_op | source)
XLA Modules:
  0.0 176.4 jit_solution(10564112001134882120)
XLA Ops:
  7.2 1.4 pad_maximum_fusion.2
  8.7 3.9 %collective-permute-start.2 = (bf16[8,4096]{1,0:T(8,128)(2,1)}, bf16[8,4096]{1,0:T(8,128)(2,1)}, u32[]{:S(2)}, u32[]{:S(2)}) collective-permute-start(bf16[8,4096]{1,0:T(8,128)(2,1)} %pad_maximum_fusion.2), channel_id=1, source_target_pairs={{0,3},{1,2},{2,1},{3,0},{4,7},{5,6},{6,5},{7,4},{8,11},{9,10},{10,... | collective-permute-start | bytes 196616 | tf_op jit(solution)/shard_map/ppermute | solution.py:23
  13.1 1.5 collective-permute-start.11
  14.6 2.0 %collective-permute-start.9 = (f32[1,1024]{1,0:T(1,128)}, f32[1,1024]{1,0:T(1,128)}, u32[]{:S(2)}, u32[]{:S(2)}) collective-permute-start(f32[1,1024]{1,0:T(1,128)} %bitcast.22), channel_id=1, source_target_pairs={{0,1},{1,0},{2,3},{3,2},{4,5},{5,4},{6,7},{7,6},{8,9},{9,8},{10,11... | collective-permute-start | bytes 12296 | tf_op jit(solution)/shard_map/ppermute | solution.py:23
  16.6 1.4 select_reduce_fusion.3
  17.9 1.4 select_reduce_fusion.2
  19.4 8.2 %copy-done = bf16[3072,4096]{1,0:T(8,128)(2,1)S(1)} copy-done((bf16[3072,4096]{1,0:T(8,128)(2,1)S(1)}, bf16[3072,4096]{1,0:T(8,128)(2,1)}, u32[]{:S(2)}) %copy-start) | copy-done | bytes 25165848
  27.5 1.3 copy-done.4
  28.8 2.9 %shard_map.132 = bf16[192,1024]{1,0:T(8,128)(2,1)S(1)} custom-call(s32[1]{0:T(128)} %bitcast.4.group_ref, bf16[192,3072]{1,0:T(8,128)(2,1)S(1)} %copy-done.4, bf16[3072,4096]{1,0:T(8,128)(2,1)S(1)} %copy-done), custom_call_target="tpu_custom_call" | custom-call | flops 1207959552 | bytes 7864320 | tf_op jit(solution)/shard_map/pallas_call | solution.py:51
  31.7 3.0 %shard_map.131 = bf16[192,1024]{1,0:T(8,128)(2,1)S(1)} custom-call(s32[1]{0:T(128)} %bitcast.3.group_ref, bf16[192,3072]{1,0:T(8,128)(2,1)S(1)} %copy-done.4, bf16[3072,4096]{1,0:T(8,128)(2,1)S(1)} %copy-done), custom_call_target="tpu_custom_call" | custom-call | flops 1207959552 | bytes 7864320 | tf_op jit(solution)/shard_map/pallas_call | solution.py:51
  34.8 3.0 %shard_map.130 = bf16[192,1024]{1,0:T(8,128)(2,1)S(1)} custom-call(s32[1]{0:T(128)} %bitcast.group_ref, bf16[192,3072]{1,0:T(8,128)(2,1)S(1)} %copy-done.4, bf16[3072,4096]{1,0:T(8,128)(2,1)S(1)} %copy-done), custom_call_target="tpu_custom_call" | custom-call | flops 1207959552 | bytes 7864320 | tf_op jit(solution)/shard_map/pallas_call | solution.py:51
  37.9 0.7 iota_compare_fusion.15
  38.6 0.6 dynamic-slice
  40.1 9.3 %all-reduce = s32[1664]{0:T(1024)S(1)} all-reduce(s32[1664]{0:T(1024)S(1)} %add_dynamic-update-slice_fusion), channel_id=2, replica_groups=mesh['wide'=8,'blk'=4] {'wide'}, use_global_device_ids=true, to_apply=%add | all-reduce | flops 1664 | bytes 13312
  49.7 0.6 add_select_fusion
  50.3 0.7 convolution_convert_fusion.2
  51.1 8.2 %copy-done.1 = bf16[3072,4096]{1,0:T(8,128)(2,1)S(1)} copy-done((bf16[3072,4096]{1,0:T(8,128)(2,1)S(1)}, bf16[3072,4096]{1,0:T(8,128)(2,1)}, u32[]{:S(2)}) %copy-start.1) | copy-done | bytes 25165848
  59.3 3.0 %shard_map.129 = f32[192,1024]{1,0:T(8,128)S(1)} custom-call(s32[1]{0:T(128)} %bitcast.1.group_ref, bf16[192,3072]{1,0:T(8,128)(2,1)S(1)} %copy-done.5, bf16[3072,4096]{1,0:T(8,128)(2,1)S(1)} %copy-done.1, bf16[192,1024]{1,0:T(8,128)(2,1)S(1)} %copy-done.9), custom_call_target="tpu_custom_call" | custom-call | flops 1207959552 | bytes 7864320 | tf_op jit(solution)/shard_map/pallas_call | solution.py:51
  62.3 0.5 and_select_fusion.1
  63.4 1.5 collective-permute-start.5
  64.9 1.5 collective-permute-start.4
  66.4 0.7 pad_maximum_fusion.7
  67.3 0.5 collective-permute-start.3
  67.8 0.9 fusion.30
  68.8 0.9 fusion.29
  70.1 1.8 %fusion = bf16[16,4096]{1,0:T(8,128)(2,1)} fusion(bf16[16,16]{1,0:T(8,128)(2,1)S(1)} %fusion.5, f32[4096]{0:T(1024)S(1)} %bitcast.25, bf16[4,4096]{1,0:T(4,128)(2,1)S(1)} %get-tuple-element.16, bf16[4,4096]{1,0:T(4,128)(2,1)S(1)} %get-tuple-element.14, bf16[4,4096]{1,0:T(4,128)(2,1)S(1)} %get-tuple-element.12, bf16[4,4096]{1,0:T(4,128)(2,1)} %param.10, ...), kind=kOutput, calls=%fused_computation.1 | convolution fusion | flops 2761216 | bytes 279104 | tf_op jit(solution)/shard_map/dot_general | solution.py:222
  72.0 4.5 %collective-permute-done.5 = bf16[192,1024]{1,0:T(8,128)(2,1)S(1)} collective-permute-done((bf16[192,1024]{1,0:T(8,128)(2,1)S(1)}, bf16[192,1024]{1,0:T(8,128)(2,1)S(1)}, u32[]{:S(2)}, u32[]{:S(2)}) %collective-permute-start.5) | collective-permute-done | bytes 393248 | tf_op jit(solution)/shard_map/ppermute | solution.py:23
  76.5 6.8 %collective-permute-done.3 = bf16[192,1024]{1,0:T(8,128)(2,1)} collective-permute-done((bf16[192,1024]{1,0:T(8,128)(2,1)S(1)}, bf16[192,1024]{1,0:T(8,128)(2,1)}, u32[]{:S(2)}, u32[]{:S(2)}) %collective-permute-start.3) | collective-permute-done | bytes 393248 | tf_op jit(solution)/shard_map/ppermute | solution.py:23
  83.3 1.4 convolution_convert_fusion.1
  84.7 0.9 reshape.232
  85.7 3.7 %all-to-all-start = ((bf16[8,36,1024]{2,1,0:T(8,128)(2,1)}), bf16[8,36,1024]{2,1,0:T(8,128)(2,1)S(1)}, u32[]{:S(2)}, u32[]{:S(2)}) async-start(bf16[8,36,1024]{2,1,0:T(8,128)(2,1)} %reshape.232), calls=%async_computation | async-start | bytes 1310720 | tf_op jit(solution)/shard_map/all_to_all | solution.py:312
  89.5 0.7 select_reduce_fusion
  90.7 0.8 fusion.1
  91.5 15.8 %all-to-all-done = bf16[8,36,1024]{2,1,0:T(8,128)(2,1)S(1)} async-done(((bf16[8,36,1024]{2,1,0:T(8,128)(2,1)}), bf16[8,36,1024]{2,1,0:T(8,128)(2,1)S(1)}, u32[]{:S(2)}, u32[]{:S(2)}) %all-to-all-start) | async-done | bytes 589856 | tf_op jit(solution)/shard_map/all_to_all | solution.py:312
  107.4 1.0 collective-permute-start.6
  108.4 1.3 collective-permute-start.7
  109.8 1.2 collective-permute-start.8
  111.3 8.2 %copy-done.2 = bf16[3072,4096]{1,0:T(8,128)(2,1)S(1)} copy-done((bf16[3072,4096]{1,0:T(8,128)(2,1)S(1)}, bf16[3072,4096]{1,0:T(8,128)(2,1)}, u32[]{:S(2)}) %copy-start.2) | copy-done | bytes 25165848
  119.4 3.7 %shard_map.133.acc_ref = f32[288,3072]{1,0:T(8,128)S(1)} custom-call(s32[1]{0:T(128)} %bitcast.1.group_ref, bf16[288,1024]{1,0:T(8,128)(2,1)S(1)} %reshape.233.hid_ref.refs_10_, bf16[3072,4096]{1,0:T(8,128)(2,1)S(1)} %copy-done.2), custom_call_target="tpu_custom_call" | custom-call | flops 1811939328 | bytes 13959168 | tf_op jit(solution)/shard_map/pallas_call | solution.py:91
  123.1 1.7 copy-done.6
  124.9 17.5 %convolution_convert_fusion.refs_9_ = bf16[128,3072]{1,0:T(8,128)(2,1)} fusion(bf16[128,4096]{1,0:T(8,128)(2,1)} %all-gather.3.cloned.1.call-done.refs_8_.refs_11_, bf16[3072,4096]{1,0:T(8,128)(2,1)} %refs_2_.1), kind=kOutput, calls=%fused_computation.4 | convolution fusion | flops 3221618688 | bytes 27000832 | tf_op jit(solution)/shard_map/dot_general | solution.py:67
  142.4 1.0 fusion.9
  143.6 0.8 copy.24
  144.6 1.0 reshape_add_fusion.refs_5_
  145.6 2.0 %copy-done.7 = f32[288,3072]{1,0:T(8,128)S(1)} copy-done((f32[288,3072]{1,0:T(8,128)S(1)}, f32[288,3072]{1,0:T(8,128)}, u32[]{:S(2)}) %copy-start.7) | copy-done | bytes 3538968
  147.6 6.1 %shard_map.134.acc_ref = f32[288,3072]{1,0:T(8,128)S(1)} custom-call(s32[1]{0:T(128)} %bitcast.4.group_ref, bf16[288,1024]{1,0:T(8,128)(2,1)S(1)} %collective-permute-done.8.hid_ref, bf16[3072,4096]{1,0:T(8,128)(2,1)} %refs_2_.1, f32[288,3072]{1,0:T(8,128)S(1)} %copy-done.7), custom_call_target="tpu_custom_call" | custom-call | flops 1811939328 | bytes 13959168 | tf_op jit(solution)/shard_map/pallas_call | solution.py:91
  153.7 6.1 %shard_map.135.refs_3_ = f32[288,3072]{1,0:T(8,128)S(1)} custom-call(s32[1]{0:T(128)} %bitcast.3.group_ref, bf16[288,1024]{1,0:T(8,128)(2,1)S(1)} %collective-permute-done.7.hid_ref, bf16[3072,4096]{1,0:T(8,128)(2,1)} %refs_2_.1, f32[288,3072]{1,0:T(8,128)S(1)} %shard_map.134.acc_ref), custom_call_target="tpu_custom_call" | custom-call | flops 1811939328 | bytes 13959168 | tf_op jit(solution)/shard_map/pallas_call | solution.py:91
  161.0 8.5 %shard_map.136 = (bf16[288,3072]{1,0:T(8,128)(2,1)}, bf16[288,1024]{1,0:T(8,128)(2,1)}, bf16[288,1024]{1,0:T(8,128)(2,1)}) custom-call(s32[2]{0:T(128)S(1)} %pad_add_fusion.refs_0_, bf16[288,1024]{1,0:T(8,128)(2,1)S(1)} %collective-permute-done.6.refs_1_, bf16[3072,4096]{1,0:T(8,128)(2,1)} %refs_2_.1, f32[288,3072]{1,0:T(8,128)S(1)} %shard_map.135.refs_3_, ...), custom_call_target="tpu_custom_call" | custom-call | flops 1811939328 | bytes 13959168 | tf_op jit(solution)/shard_map/pallas_call | solution.py:161
  (96 shorter events, 4.9 us)
Async XLA Ops:
  7.2 117.7 %all-gather.3.cloned.1.call-start = ((), (), s32[]{:S(2)}) async-start(), calls=%async_computation.1 | async-start | bytes 1179648 | tf_op jit(solution)/shard_map/all_gather | solution.py:295
  8.7 58.6 %collective-permute-start.2 = (bf16[8,4096]{1,0:T(8,128)(2,1)}, bf16[8,4096]{1,0:T(8,128)(2,1)}, u32[]{:S(2)}, u32[]{:S(2)}) collective-permute-start(bf16[8,4096]{1,0:T(8,128)(2,1)} %pad_maximum_fusion.2), channel_id=1, source_target_pairs={{0,3},{1,2},{2,1},{3,0},{4,7},{5,6},{6,5},{7,4},{8,11},{9,10},{10,... | collective-permute-start | bytes 196616 | tf_op jit(solution)/shard_map/ppermute | solution.py:23
  12.5 56.2 %collective-permute-start.1 = (bf16[8,4096]{1,0:T(8,128)(2,1)}, bf16[8,4096]{1,0:T(8,128)(2,1)}, u32[]{:S(2)}, u32[]{:S(2)}) collective-permute-start(bf16[8,4096]{1,0:T(8,128)(2,1)} %pad_maximum_fusion.2), channel_id=1, source_target_pairs={{0,2},{1,3},{2,0},{3,1},{4,6},{5,7},{6,4},{7,5},{8,10},{9,11},{10,... | collective-permute-start | bytes 196616 | tf_op jit(solution)/shard_map/ppermute | solution.py:23
  13.1 49.8 %collective-permute-start.11 = (f32[1,1024]{1,0:T(1,128)}, f32[1,1024]{1,0:T(1,128)}, u32[]{:S(2)}, u32[]{:S(2)}) collective-permute-start(f32[1,1024]{1,0:T(1,128)} %bitcast.20), channel_id=1, source_target_pairs={{0,3},{1,2},{2,1},{3,0},{4,7},{5,6},{6,5},{7,4},{8,11},{9,10},{10,... | collective-permute-start | bytes 12296 | tf_op jit(solution)/shard_map/ppermute | solution.py:23
  14.5 48.8 %collective-permute-start.10 = (f32[1,1024]{1,0:T(1,128)}, f32[1,1024]{1,0:T(1,128)}, u32[]{:S(2)}, u32[]{:S(2)}) collective-permute-start(f32[1,1024]{1,0:T(1,128)} %bitcast.21), channel_id=1, source_target_pairs={{0,2},{1,3},{2,0},{3,1},{4,6},{5,7},{6,4},{7,5},{8,10},{9,11},{10,... | collective-permute-start | bytes 12296 | tf_op jit(solution)/shard_map/ppermute | solution.py:23
  14.6 50.3 %collective-permute-start.9 = (f32[1,1024]{1,0:T(1,128)}, f32[1,1024]{1,0:T(1,128)}, u32[]{:S(2)}, u32[]{:S(2)}) collective-permute-start(f32[1,1024]{1,0:T(1,128)} %bitcast.22), channel_id=1, source_target_pairs={{0,1},{1,0},{2,3},{3,2},{4,5},{5,4},{6,7},{7,6},{8,9},{9,8},{10,11... | collective-permute-start | bytes 12296 | tf_op jit(solution)/shard_map/ppermute | solution.py:23
  16.6 1.4 copy-start.20
  19.4 8.2 %copy-start = (bf16[3072,4096]{1,0:T(8,128)(2,1)S(1)}, bf16[3072,4096]{1,0:T(8,128)(2,1)}, u32[]{:S(2)}) copy-start(bf16[3072,4096]{1,0:T(8,128)(2,1)} %refs_2_.1) | copy-start | bytes 75497472
  27.5 1.3 copy-start.4
  34.7 3.0 %copy-start.17 = (s32[192,1]{0,1:T(1,128)S(1)}, s32[192,1]{0,1:T(1,128)}, u32[]{:S(2)}) copy-start(s32[192,1]{0,1:T(1,128)} %param.15) | copy-start | bytes 2308
  34.7 3.9 %copy-start.25 = (u32[32]{0:T(128)S(1)}, u32[32]{0:T(128)}, u32[]{:S(2)}) copy-start(u32[32]{0:T(128)} %constant.98) | copy-start | bytes 388
  34.7 5.1 %copy-start.19 = (s32[1,16]{1,0:T(1,128)S(1)}, s32[1,16]{1,0:T(1,128)}, u32[]{:S(2)}) copy-start(s32[1,16]{1,0:T(1,128)} %param.14) | copy-start | bytes 196
  34.7 16.3 %copy-start.5 = (bf16[192,3072]{1,0:T(8,128)(2,1)S(1)}, bf16[192,3072]{1,0:T(8,128)(2,1)}, u32[]{:S(2)}) copy-start(bf16[192,3072]{1,0:T(8,128)(2,1)} %act_ref.7) | copy-start | bytes 3538948
  34.8 16.3 %copy-start.9 = (bf16[192,1024]{1,0:T(8,128)(2,1)S(1)}, bf16[192,1024]{1,0:T(8,128)(2,1)}, u32[]{:S(2)}) copy-start(bf16[192,1024]{1,0:T(8,128)(2,1)} %resid_ref.1) | copy-start | bytes 1179652
  51.1 8.2 %copy-start.1 = (bf16[3072,4096]{1,0:T(8,128)(2,1)S(1)}, bf16[3072,4096]{1,0:T(8,128)(2,1)}, u32[]{:S(2)}) copy-start(bf16[3072,4096]{1,0:T(8,128)(2,1)} %refs_2_.1) | copy-start | bytes 75497472
  59.2 7.2 %copy-start.10 = (f32[1024]{0:T(1024)S(1)}, f32[1024]{0:T(1024)}, u32[]{:S(2)}) copy-start(f32[1024]{0:T(1024)} %param.19) | copy-start | bytes 12292
  59.2 7.9 %copy-start.18 = (pred[4,4]{1,0:T(4,128)(4,1)S(1)}, pred[4,4]{1,0:T(4,128)(4,1)}, u32[]{:S(2)}) copy-start(pred[4,4]{1,0:T(4,128)(4,1)} %iota_compare_fusion.15) | copy-start | bytes 52
  59.2 10.5 %copy-start.13 = (bf16[4,4096]{1,0:T(4,128)(2,1)S(1)}, bf16[4,4096]{1,0:T(4,128)(2,1)}, u32[]{:S(2)}) copy-start(bf16[4,4096]{1,0:T(4,128)(2,1)} %param.10) | copy-start | bytes 98308
  59.2 10.5 %copy-start.14 = (bf16[4,4096]{1,0:T(4,128)(2,1)S(1)}, bf16[4,4096]{1,0:T(4,128)(2,1)}, u32[]{:S(2)}) copy-start(bf16[4,4096]{1,0:T(4,128)(2,1)} %param.11) | copy-start | bytes 98308
  59.2 10.5 %copy-start.21 = (s32[16]{0:T(128)S(1)}, s32[16]{0:T(128)}, u32[]{:S(2)}) copy-start(s32[16]{0:T(128)} %copy-done.20) | copy-start | bytes 196
  59.3 10.5 %copy-start.22 = (f32[16]{0:T(128)S(1)}, f32[16]{0:T(128)}, u32[]{:S(2)}) copy-start(f32[16]{0:T(128)} %select_reduce_fusion.3) | copy-start | bytes 196
  59.3 10.5 %copy-start.23 = (s32[16]{0:T(128)S(1)}, s32[16]{0:T(128)}, u32[]{:S(2)}) copy-start(s32[16]{0:T(128)} %select_reduce_fusion.2) | copy-start | bytes 196
  62.8 6.9 %collective-permute-start = (bf16[8,4096]{1,0:T(8,128)(2,1)}, bf16[8,4096]{1,0:T(8,128)(2,1)S(1)}, u32[]{:S(2)}, u32[]{:S(2)}) collective-permute-start(bf16[8,4096]{1,0:T(8,128)(2,1)} %pad_maximum_fusion.2), channel_id=1, source_target_pairs={{0,1},{1,0},{2,3},{3,2},{4,5},{5,4},{6,7},{7,6},{8,9},{9,8},{10,11... | collective-permute-start | bytes 196616 | tf_op jit(solution)/shard_map/ppermute | solution.py:23
  63.4 13.1 %collective-permute-start.5 = (bf16[192,1024]{1,0:T(8,128)(2,1)S(1)}, bf16[192,1024]{1,0:T(8,128)(2,1)S(1)}, u32[]{:S(2)}, u32[]{:S(2)}) collective-permute-start(bf16[192,1024]{1,0:T(8,128)(2,1)S(1)} %shard_map.132), channel_id=1, source_target_pairs={{0,1},{1,0},{2,3},{3,2},{4,5},{5,4},{6,7},{7,6},{8,9},{9,8},{10,11... | collective-permute-start | bytes 1179656 | tf_op jit(solution)/shard_map/ppermute | solution.py:23
  64.9 11.6 %collective-permute-start.4 = (bf16[192,1024]{1,0:T(8,128)(2,1)S(1)}, bf16[192,1024]{1,0:T(8,128)(2,1)S(1)}, u32[]{:S(2)}, u32[]{:S(2)}) collective-permute-start(bf16[192,1024]{1,0:T(8,128)(2,1)S(1)} %shard_map.131), channel_id=1, source_target_pairs={{0,2},{1,3},{2,0},{3,1},{4,6},{5,7},{6,4},{7,5},{8,10},{9,11},{10,... | collective-permute-start | bytes 1179656 | tf_op jit(solution)/shard_map/ppermute | solution.py:23
  67.3 16.0 %collective-permute-start.3 = (bf16[192,1024]{1,0:T(8,128)(2,1)S(1)}, bf16[192,1024]{1,0:T(8,128)(2,1)}, u32[]{:S(2)}, u32[]{:S(2)}) collective-permute-start(bf16[192,1024]{1,0:T(8,128)(2,1)S(1)} %shard_map.130), channel_id=1, source_target_pairs={{0,3},{1,2},{2,1},{3,0},{4,7},{5,6},{6,5},{7,4},{8,11},{9,10},{10,... | collective-permute-start | bytes 1179656 | tf_op jit(solution)/shard_map/ppermute | solution.py:23
  84.7 4.7 %copy-start.24 = (s32[128]{0:T(128)S(1)}, s32[128]{0:T(128)}, u32[]{:S(2)}) copy-start(s32[128]{0:T(128)} %and_select_fusion.1) | copy-start | bytes 1540
  84.7 4.8 %copy-start.12 = (s32[8,192]{1,0:T(8,128)S(1)}, s32[8,192]{1,0:T(8,128)}, u32[]{:S(2)}) copy-start(s32[8,192]{1,0:T(8,128)} %get-tuple-element.10) | copy-start | bytes 18436
  84.7 4.8 %copy-start.16 = (s32[8,192]{1,0:T(8,128)S(1)}, s32[8,192]{1,0:T(8,128)}, u32[]{:S(2)}) copy-start(s32[8,192]{1,0:T(8,128)} %convolution_convert_fusion.2) | copy-start | bytes 18436
  84.7 6.0 %copy-start.15 = (bf16[4,4096]{1,0:T(4,128)(2,1)S(1)}, bf16[4,4096]{1,0:T(4,128)(2,1)}, u32[]{:S(2)}) copy-start(bf16[4,4096]{1,0:T(4,128)(2,1)} %param.11) | copy-start | bytes 98308
  85.7 21.6 %all-to-all-start = ((bf16[8,36,1024]{2,1,0:T(8,128)(2,1)}), bf16[8,36,1024]{2,1,0:T(8,128)(2,1)S(1)}, u32[]{:S(2)}, u32[]{:S(2)}) async-start(bf16[8,36,1024]{2,1,0:T(8,128)(2,1)} %reshape.232), calls=%async_computation | async-start | bytes 1310720 | tf_op jit(solution)/shard_map/all_to_all | solution.py:312
  107.4 53.1 %collective-permute-start.6 = (bf16[288,1024]{1,0:T(8,128)(2,1)S(1)}, bf16[288,1024]{1,0:T(8,128)(2,1)S(1)}, u32[]{:S(2)}, u32[]{:S(2)}) collective-permute-start(bf16[288,1024]{1,0:T(8,128)(2,1)S(1)} %reshape.233.hid_ref.refs_10_), channel_id=1, source_target_pairs={{0,3},{1,2},{2,1},{3,0},{4,7},{5,6},{6,5},{7,4},{8,11},{9,10},{10,... | collective-permute-start | bytes 1769480 | tf_op jit(solution)/shard_map/ppermute | solution.py:23
  108.4 35.9 %collective-permute-start.7 = (bf16[288,1024]{1,0:T(8,128)(2,1)S(1)}, bf16[288,1024]{1,0:T(8,128)(2,1)S(1)}, u32[]{:S(2)}, u32[]{:S(2)}) collective-permute-start(bf16[288,1024]{1,0:T(8,128)(2,1)S(1)} %reshape.233.hid_ref.refs_10_), channel_id=1, source_target_pairs={{0,2},{1,3},{2,0},{3,1},{4,6},{5,7},{6,4},{7,5},{8,10},{9,11},{10,... | collective-permute-start | bytes 1769480 | tf_op jit(solution)/shard_map/ppermute | solution.py:23
  109.8 33.6 %collective-permute-start.8 = (bf16[288,1024]{1,0:T(8,128)(2,1)S(1)}, bf16[288,1024]{1,0:T(8,128)(2,1)S(1)}, u32[]{:S(2)}, u32[]{:S(2)}) collective-permute-start(bf16[288,1024]{1,0:T(8,128)(2,1)S(1)} %reshape.233.hid_ref.refs_10_), channel_id=1, source_target_pairs={{0,1},{1,0},{2,3},{3,2},{4,5},{5,4},{6,7},{7,6},{8,9},{9,8},{10,11... | collective-permute-start | bytes 1769480 | tf_op jit(solution)/shard_map/ppermute | solution.py:23
  111.3 8.2 %copy-start.2 = (bf16[3072,4096]{1,0:T(8,128)(2,1)S(1)}, bf16[3072,4096]{1,0:T(8,128)(2,1)}, u32[]{:S(2)}) copy-start(bf16[3072,4096]{1,0:T(8,128)(2,1)} %refs_2_.1) | copy-start | bytes 75497472
  123.1 1.7 copy-start.6
  124.9 17.5 %copy-start.3 = (bf16[128,4096]{1,0:T(8,128)(2,1)S(1)}, bf16[128,4096]{1,0:T(8,128)(2,1)}, u32[]{:S(2)}) copy-start(bf16[128,4096]{1,0:T(8,128)(2,1)} %all-gather.3.cloned.1.call-done.refs_8_.refs_11_) | copy-start | bytes 3145732
  145.6 2.0 %copy-start.7 = (f32[288,3072]{1,0:T(8,128)S(1)}, f32[288,3072]{1,0:T(8,128)}, u32[]{:S(2)}) copy-start(f32[288,3072]{1,0:T(8,128)} %copy-done.6) | copy-start | bytes 10616836
  153.7 6.2 %copy-start.11 = (f32[288,128]{1,0:T(8,128)S(1)}, f32[288,128]{1,0:T(8,128)}, u32[]{:S(2)}) copy-start(f32[288,128]{1,0:T(8,128)} %fusion.9) | copy-start | bytes 442372
  159.9 1.1 copy-start.8
Sparse Core Ops, SparseCore 0:
  72.1 20.6 all-gather.2

commit v2 on v0

v2 whole, which is shorter than its diff:
```python
import jax
import jax.numpy as jnp
from jax import lax
from jax.experimental import pallas as pl
from jax.experimental.pallas import tpu as pltpu
from jax.sharding import PartitionSpec as P

logit_scale = 24.0
norm_eps = 1e-06
f32 = jnp.float32
bf16 = jnp.bfloat16
i32 = jnp.int32
lane = 128
kernel_vmem = 46 * 1024 * 1024


def params():
    return pltpu.CompilerParams(vmem_limit_bytes=kernel_vmem)


def cost(flops, nbytes):
    return pl.CostEstimate(flops=flops, bytes_accessed=nbytes, transcendentals=0)


def tile_of(extent, most):
    tile = most
    while extent % tile:
        tile //= 2
    return tile


def iota(shape, dim):
    return lax.broadcasted_iota(i32, shape, dim)


def dot(left, right):
    return jnp.dot(left, right, preferred_element_type=f32)


def dot_t(left, right):
    return lax.dot_general(left, right, (((1,), (1,)), ((), ())), preferred_element_type=f32)


def swap(rows, k):
    return lax.ppermute(rows, "blk", [(i, i ^ k) for i in range(lax.axis_size("blk"))])


def project_body(group_ref, act_ref, w_ref, out_ref):
    out_ref[...] = dot(act_ref[...], w_ref[...]).astype(bf16)


def project_own_body(group_ref, act_ref, w_ref, resid_ref, out_ref):
    out_ref[...] = dot(act_ref[...], w_ref[...]) + resid_ref[...].astype(f32)


def project(group, act, w_down, width, resid=None):
    rows, depth = act.shape
    tile = tile_of(width, 256)
    per_group = width // tile
    column_spec = pl.BlockSpec((rows, tile), lambda j, g: (0, j))
    in_specs = [
        pl.BlockSpec((rows, depth), lambda j, g: (0, 0)),
        pl.BlockSpec((depth, tile), lambda j, g: (0, g[0] * per_group + j)),
    ]
    operands = [act, w_down]
    if resid is not None:
        in_specs.append(column_spec)
        operands.append(resid)
    return pl.pallas_call(
        project_body if resid is None else project_own_body,
        grid_spec=pltpu.PrefetchScalarGridSpec(
            num_scalar_prefetch=1, grid=(per_group,), in_specs=in_specs, out_specs=column_spec
        ),
        out_shape=jax.ShapeDtypeStruct((rows, width), bf16 if resid is None else f32),
        compiler_params=params(),
        cost_estimate=cost(2 * rows * depth * width, 2 * depth * width + 2 * rows * depth),
    )(group, *operands)


def group_body(blk_ref, parts_ref, lse_row_ref, lse_ref, pos_row_ref, pos_ref, table_ref, *rest):
    query_grad_ref, low_ref, gain_ref = rest
    own, features = query_grad_ref.shape
    pairs = parts_ref.shape[0]
    blk = blk_ref[0]
    queries = parts_ref[:, :features]
    passages = parts_ref[:, features : 2 * features]

    def named(dim):
        place = iota((pairs, pairs), dim)
        return (blk ^ (place // own)) * own + place % own

    here_rows, here_cols = named(0), named(1)
    at_rows = here_rows == iota((pairs, pairs), 1)
    at_cols = here_cols == iota((pairs, pairs), 0)
    lse = jnp.sum(jnp.where(at_rows, lse_row_ref[...], 0.0), axis=1, keepdims=True)
    pos = jnp.sum(jnp.where(at_rows, pos_row_ref[...], 0), axis=1, keepdims=True)
    hit = (pos == here_cols).astype(f32)
    coef = (jnp.exp(logit_scale * dot_t(queries, passages) - lse) - hit).astype(bf16)
    query_grad_ref[...] = (logit_scale * dot(coef, passages))[:own].astype(bf16)
    lse = jnp.sum(jnp.where(at_cols, lse_ref[...], 0.0), axis=0, keepdims=True)
    pos = jnp.sum(jnp.where(at_cols, pos_ref[...], 0), axis=0, keepdims=True)
    hit = (pos == here_rows).astype(f32)
    turned = (jnp.exp(logit_scale * dot_t(passages, queries) - lse) - hit).astype(bf16)
    turned = dot(at_cols.astype(bf16), turned).astype(bf16)
    pass_grad = logit_scale * dot(turned, queries)
    piece = (parts_ref.shape[1] - 2 * features) // 2
    gains = (
        parts_ref[:, 2 * features : 2 * features + piece].astype(f32)
        + parts_ref[:, 2 * features + piece :].astype(f32)
    )
    for row in range(pairs):
        first = ((blk ^ (row // own)) * own + row % own) * piece
        gain_ref[:, pl.ds(pl.multiple_of(first, lane), piece)] = gains[row : row + 1]
    low_ref[:, :features] = (gain_ref[...] * pass_grad).astype(bf16)
    low_ref[:, features:] = table_ref[...]


def group_part(query_emb, passage_emb, row_lse, positive, token_lengths, destination, gain, blk):
    own, features = query_emb.shape
    pairs = row_lse.shape[0]
    high = gain.astype(bf16)
    rest = (gain - high.astype(f32)).astype(bf16)
    both = jnp.concatenate(
        [query_emb, passage_emb, high.reshape(own, -1), rest.reshape(own, -1)], axis=1
    )
    parts = jnp.concatenate([both] + [swap(both, k) for k in range(1, pairs // own)], axis=0)
    table = jnp.concatenate([destination.reshape(pairs, -1), token_lengths.reshape(pairs, 1)], 1)
    table = jnp.pad(table, ((0, 0), (0, lane - table.shape[1]))).astype(bf16)
    return pl.pallas_call(
        group_body,
        in_specs=[pl.BlockSpec(memory_space=pltpu.SMEM)]
        + [pl.BlockSpec(memory_space=pltpu.VMEM)] * 6,
        out_specs=[pl.BlockSpec(memory_space=pltpu.VMEM)] * 2,
        out_shape=[
            jax.ShapeDtypeStruct((own, features), bf16),
            jax.ShapeDtypeStruct((pairs, features + lane), bf16),
        ],
        scratch_shapes=[pltpu.VMEM((1, features), f32)],
        compiler_params=params(),
        cost_estimate=cost(8 * pairs * pairs * features, 8 * pairs * features),
    )(
        blk[None],
        parts,
        row_lse[None],
        row_lse[:, None],
        positive[None],
        positive[:, None],
        table,
    )


def earlier_of(tokens):
    return (iota((tokens, tokens), 0) < iota((tokens, tokens), 1)).astype(bf16)


def pack_body(dest_ref, own_ref, *rest):
    terms, out_ref = rest[:-1], rest[-1]
    groups, slots, _ = out_ref.shape
    tokens = dest_ref.shape[1]
    stride = -(-slots // 16) * 16
    hidden = own_ref[...]
    for term in terms:
        hidden = hidden + term[...].astype(f32)
    dest = dest_ref[...]
    hit = (dest == iota((groups, tokens), 0)).astype(f32)
    rank = dot(hit.astype(bf16), earlier_of(tokens))
    rank = jnp.sum(rank * hit, axis=0, keepdims=True).astype(i32)
    place = (iota((groups * stride, tokens), 0) == dest * stride + rank).astype(bf16)
    packed = dot(place, hidden.astype(bf16)).astype(bf16)
    for group in range(groups):
        out_ref[group] = packed[group * stride : group * stride + slots]


def pack(destination, own, terms, groups, slots):
    tokens, width = own.shape
    tile = tile_of(width, 512)
    column_spec = pl.BlockSpec((tokens, tile), lambda j: (0, j))
    return pl.pallas_call(
        pack_body,
        grid=(width // tile,),
        in_specs=[pl.BlockSpec((1, tokens), lambda j: (0, 0))] + [column_spec] * (1 + len(terms)),
        out_specs=pl.BlockSpec((groups, slots, tile), lambda j: (0, 0, j)),
        out_shape=jax.ShapeDtypeStruct((groups, slots, width), bf16),
        compiler_params=params(),
        cost_estimate=cost(4 * groups * slots * tokens * width, 10 * tokens * width),
    )(destination.reshape(1, tokens), own, *terms)


def slots_body(wide_ref, dest_ref, len_ref, hot_ref):
    groups, tokens = dest_ref.shape
    pairs = len_ref.shape[1]
    rows = hot_ref.shape[0]
    slots = rows // groups
    hit = dest_ref[...].astype(i32) == wide_ref[0]
    rank = dot(hit.astype(f32).astype(bf16), earlier_of(tokens))
    upto = (iota((pairs, pairs), 0) <= iota((pairs, pairs), 1)).astype(bf16)
    ends = dot(len_ref[...], upto)
    token = iota((groups, tokens), 1).astype(f32)
    passage = jnp.ones((groups, tokens), f32)
    for pair in range(pairs):
        passage = passage + (token >= ends[:, pair : pair + 1]).astype(f32)
    code = jnp.where(hit, passage, 0.0)
    spread = (iota((rows, groups), 0) // slots == iota((rows, groups), 1)).astype(bf16)
    rank_rows = dot(spread, rank.astype(bf16)).astype(i32)
    code_rows = dot(spread, code.astype(bf16))
    here = rank_rows == iota((rows, tokens), 0) % slots
    taken = jnp.sum(jnp.where(here, code_rows, 0.0), axis=1, keepdims=True).astype(i32)
    column = iota((rows, groups * pairs), 1)
    first = iota((rows, groups * pairs), 0) // slots * pairs
    hot = (taken > 0) & (column == first + taken - 1)
    hot_ref[...] = hot.astype(f32).astype(bf16)


def slot_passages(wide, dest_all, len_all, rows):
    groups, pairs = len_all.shape
    return pl.pallas_call(
        slots_body,
        in_specs=[pl.BlockSpec(memory_space=pltpu.SMEM)]
        + [pl.BlockSpec(memory_space=pltpu.VMEM)] * 2,
        out_specs=pl.BlockSpec(memory_space=pltpu.VMEM),
        out_shape=jax.ShapeDtypeStruct((rows, groups * pairs), bf16),
        compiler_params=params(),
        cost_estimate=cost(4 * rows * groups * dest_all.shape[1], 2 * rows * groups * pairs),
    )(wide[None], dest_all, len_all)


def low_act_body(low_ref, w_ref, out_ref):
    out_ref[...] = dot_t(low_ref[...], w_ref[...]).astype(bf16)


def low_activations(low, w_down):
    pairs = low.shape[0]
    depth, features = w_down.shape
    tile = tile_of(depth, 256)
    return pl.pallas_call(
        low_act_body,
        grid=(depth // tile,),
        in_specs=[
            pl.BlockSpec((pairs, features), lambda j: (0, 0)),
            pl.BlockSpec((tile, features), lambda j: (j, 0)),
        ],
        out_specs=pl.BlockSpec((pairs, tile), lambda j: (0, j)),
        out_shape=jax.ShapeDtypeStruct((pairs, depth), bf16),
        compiler_params=params(),
        cost_estimate=cost(2 * pairs * depth * features, 2 * depth * features),
    )(low, w_down)


def statistics(hids, lows):
    squares, cross = 0.0, 0.0
    for hid_ref, low_ref in zip(hids, lows):
        hid = hid_ref[...].astype(f32)
        squares = squares + jnp.sum(hid * hid, axis=1, keepdims=True)
        cross = cross + dot_t(hid_ref[...], low_ref[...])
    return squares, cross


def product(hids, weights):
    total = 0.0
    for hid_ref, w_ref in zip(hids, weights):
        total = total + dot_t(hid_ref[...], w_ref[...])
    return total


def piece_specs(pieces, low, tile):
    hid_specs, w_specs, low_specs = [], [], []
    for n, piece in enumerate(pieces):
        hid_specs.append(pl.BlockSpec(piece.shape, lambda j, g: (0, 0)))
        w_specs.append(pl.BlockSpec((tile, piece.shape[1]), lambda j, g, n=n: (j, g[n])))
        low_specs.append(
            pl.BlockSpec((low.shape[0], piece.shape[1]), lambda j, g, n=n: (0, g[n]))
        )
    return hid_specs + w_specs + low_specs


def back_body(count, *refs):
    hids, weights, lows = refs[1 : 1 + count], refs[1 + count : 1 + 2 * count], refs[1 + 2 * count :]
    lows, (acc_ref, squares_ref, cross_ref) = lows[:count], lows[count:]

    @pl.when(pl.program_id(0) == 0)
    def _():
        squares_ref[...], cross_ref[...] = statistics(hids, lows)

    acc_ref[...] = product(hids, weights)


def back(places, pieces, w_down, low):
    count = len(pieces)
    rows, width = pieces[0].shape
    depth = w_down.shape[0]
    pairs = low.shape[0]
    tile = tile_of(depth, 512)
    return pl.pallas_call(
        lambda *refs: back_body(count, *refs),
        grid_spec=pltpu.PrefetchScalarGridSpec(
            num_scalar_prefetch=1,
            grid=(depth // tile,),
            in_specs=piece_specs(pieces, low, tile),
            out_specs=[
                pl.BlockSpec((rows, tile), lambda j, g: (0, j)),
                pl.BlockSpec((rows, 1), lambda j, g: (0, 0)),
                pl.BlockSpec((rows, pairs), lambda j, g: (0, 0)),
            ],
        ),
        out_shape=[
            jax.ShapeDtypeStruct((rows, depth), f32),
            jax.ShapeDtypeStruct((rows, 1), f32),
            jax.ShapeDtypeStruct((rows, pairs), f32),
        ],
        compiler_params=params(),
        cost_estimate=cost(2 * rows * depth * width * count, 2 * depth * width * count),
    )(places, *pieces, *[w_down] * count, *[low] * count)


def finish_body(features, count, *refs):
    hids, weights, lows = refs[1 : 1 + count], refs[1 + count : 1 + 2 * count], refs[1 + 2 * count :]
    lows, rest = lows[:count], lows[count:]
    acc_ref, squares_ref, cross_ref, hot_ref, share_ref, low_act_ref, own_ref, own_low_ref = rest[:8]
    gain_ref, act_out, resid_out, normed_out, lead, pull = rest[8:]

    @pl.when(pl.program_id(0) == 0)
    def _():
        squares, cross = statistics(hids, lows)
        weight = hot_ref[...].astype(f32) * share_ref[...]
        inner = jnp.sum((cross_ref[...] + cross) * weight, axis=1, keepdims=True)
        inv_rms = lax.rsqrt((squares_ref[...] + squares) / features + norm_eps)
        lead[...] = inv_rms * jnp.sum(weight, axis=1, keepdims=True)
        pull[...] = inv_rms * inv_rms * inv_rms * inner / features
        own = own_ref[...].astype(f32)
        own_low = dot(hot_ref[...], own_low_ref[...])
        resid_out[...] = (lead[...] * own_low - own * pull[...]).astype(bf16)
        normed_out[...] = (gain_ref[...] * own * inv_rms).astype(bf16)

    low_act = dot(hot_ref[...], low_act_ref[...])
    hid_act = acc_ref[...] + product(hids, weights)
    act_out[...] = (lead[...] * low_act - pull[...] * hid_act).astype(bf16)


def finish(places, pieces, w_down, low, acc, squares, cross, hot, share, low_act, own, gain):
    count = len(pieces)
    rows, width = own.shape
    depth, features = w_down.shape
    pairs = hot.shape[1]
    tile = tile_of(depth, 512)

    def whole(shape):
        return pl.BlockSpec(shape, lambda j, g: (0, 0))

    return pl.pallas_call(
        lambda *refs: finish_body(features, count, *refs),
        grid_spec=pltpu.PrefetchScalarGridSpec(
            num_scalar_prefetch=1,
            grid=(depth // tile,),
            in_specs=piece_specs(pieces, low, tile)
            + [
                pl.BlockSpec((rows, tile), lambda j, g: (0, j)),
                whole((rows, 1)),
                whole((rows, pairs)),
                whole((rows, pairs)),
                whole((1, pairs)),
                pl.BlockSpec((pairs, tile), lambda j, g: (0, j)),
                whole((rows, width)),
                pl.BlockSpec((pairs, width), lambda j, g: (0, g[count])),
                whole((1, width)),
            ],
            out_specs=[
                pl.BlockSpec((rows, tile), lambda j, g: (0, j)),
                whole((rows, width)),
                whole((rows, width)),
            ],
            scratch_shapes=[pltpu.VMEM((rows, 1), f32), pltpu.VMEM((rows, 1), f32)],
        ),
        out_shape=[
            jax.ShapeDtypeStruct((rows, depth), bf16),
            jax.ShapeDtypeStruct((rows, width), bf16),
            jax.ShapeDtypeStruct((rows, width), bf16),
        ],
        compiler_params=params(),
        cost_estimate=cost(2 * rows * depth * width, 2 * depth * width + 6 * rows * depth),
    )(
        places,
        *pieces,
        *[w_down] * count,
        *[low] * count,
        acc,
        squares,
        cross,
        hot,
        share,
        low_act,
        own,
        low,
        gain,
    )


def low_rank_shards(
    query_emb,
    passage_emb,
    row_lse,
    positive,
    token_lengths,
    destination,
    mlp_act,
    resid,
    w_down,
    gain,
):
    wide_count = lax.axis_size("wide")
    blk, wide = lax.axis_index("blk"), lax.axis_index("wide")
    tok_count, width = resid.shape
    features = w_down.shape[1]
    pairs = row_lse.shape[0]
    slot_count = 3 * tok_count // (2 * wide_count)
    rows = wide_count * slot_count

    query_grad, low_own = group_part(
        query_emb, passage_emb, row_lse, positive, token_lengths, destination, gain, blk
    )
    arrived = []
    for k in (3, 1, 2):
        arrived.append(swap(project((blk ^ k)[None], mlp_act, w_down, width), k))
    own_term = project(blk[None], mlp_act, w_down, width, resid)

    low = lax.all_gather(low_own, "wide", axis=0, tiled=True)
    tables = low[:, features:]
    per_pair = tok_count // pairs
    dest_all = tables[:, :per_pair].reshape(wide_count, tok_count)
    len_all = tables[:, per_pair].reshape(wide_count, pairs)
    low = low[:, :features]

    packed = pack(destination, own_term, arrived, wide_count, slot_count)
    own_hid = lax.all_to_all(packed, "wide", split_axis=0, concat_axis=0, tiled=True)
    own_hid = own_hid.reshape(rows, width)

    low_act = low_activations(low, w_down)
    hot = slot_passages(wide, dest_all, len_all, rows)
    share = (1.0 / len_all.astype(f32)).reshape(1, wide_count * pairs)

    half = width // 2
    left, right = own_hid[:, :half], own_hid[:, half:]
    left_1, right_2 = swap(left, 1), swap(right, 2)
    right_1, left_2 = swap(right, 1), swap(left, 2)
    left_3, right_3 = swap(left_1, 2), swap(right_2, 1)

    def places(*pieces):
        return jnp.stack([(blk ^ k) * 2 + side for k, side in pieces])

    acc, squares, cross = back(
        places((0, 0), (0, 1), (1, 0), (1, 1), (2, 0), (2, 1)),
        [left, right, left_1, right_1, left_2, right_2],
        w_down,
        low,
    )
    act_grad, resid_grad, normed_out = finish(
        jnp.concatenate([places((3, 0), (3, 1)), blk[None]]),
        [left_3, right_3],
        w_down,
        low,
        acc,
        squares,
        cross,
        hot,
        share,
        low_act,
        own_hid,
        gain[None],
    )
    return (query_grad, resid_grad, act_grad, normed_out)


def coefficients(scores, lse_part, pos_part):
    columns = lax.broadcasted_iota(jnp.int32, scores.shape, 1)
    target = (pos_part[:, None] == columns).astype(jnp.float32)
    return (jnp.exp(scores - lse_part[:, None]) - target).astype(jnp.bfloat16)


def place_rows(destination, wide_count, slot_count):
    tok_count = destination.shape[0]
    dest_hot = (destination == lax.broadcasted_iota(jnp.int32, (tok_count, wide_count), 1)).astype(
        bf16
    )
    token = lax.iota(jnp.int32, tok_count)
    earlier = (token[None, :] < token[:, None]).astype(bf16)
    rank_of = jnp.dot(earlier, dest_hot, preferred_element_type=f32)
    slot_of = jnp.sum(rank_of * dest_hot.astype(f32), axis=1).astype(jnp.int32)
    slot_of = slot_of + destination[:, 0] * slot_count
    return (
        lax.broadcasted_iota(jnp.int32, (wide_count * slot_count, tok_count), 0) == slot_of[None, :]
    ).astype(bf16)


def row_shards(
    query_emb,
    passage_emb,
    row_lse,
    positive,
    token_lengths,
    destination,
    mlp_act,
    resid,
    w_down,
    gain,
):
    pair_rows = query_emb.shape[0]
    tok_count, feat_width = resid.shape
    features = w_down.shape[1]
    blk_index = lax.axis_index("blk")
    wide_count = lax.axis_size("wide")
    slot_count = 3 * tok_count // (2 * wide_count)
    offset = blk_index * feat_width
    query_all = lax.all_gather(query_emb, "blk", axis=0, tiled=True)
    passage_all = lax.all_gather(passage_emb, "blk", axis=0, tiled=True)
    scores = logit_scale * jnp.dot(query_all, passage_all.T, preferred_element_type=f32)
    coef_full = coefficients(scores, row_lse, positive)
    own_coef = lax.dynamic_slice_in_dim(coef_full, blk_index * pair_rows, pair_rows, 0)
    query_grad = (
        logit_scale * jnp.dot(own_coef, passage_all, preferred_element_type=f32)
    ).astype(bf16)
    query_cols = lax.dynamic_slice_in_dim(query_all, offset, feat_width, 1)
    grad_cols = logit_scale * lax.dot_general(
        query_cols, coef_full, (((0,), (0,)), ((), ())), preferred_element_type=f32
    )
    lengths_row = token_lengths[0]
    starts = jnp.cumsum(lengths_row) - lengths_row
    positions = lax.broadcasted_iota(jnp.int32, (tok_count, lengths_row.shape[0]), 0)
    member = (positions >= starts[None, :]) & (positions < (starts + lengths_row)[None, :])
    weights = member.astype(f32) * (1.0 / lengths_row.astype(f32))[None, :]
    tok_grad = lax.dot_general(
        weights,
        grad_cols,
        (((1,), (1,)), ((), ())),
        precision=lax.Precision.HIGHEST,
        preferred_element_type=f32,
    ).astype(bf16)
    terms = jnp.dot(mlp_act, w_down, preferred_element_type=f32)
    own = lax.dynamic_slice_in_dim(terms, offset, feat_width, 1) + resid.astype(f32)
    terms = lax.dynamic_update_slice_in_dim(terms, own, offset, 1)
    hidden = lax.psum_scatter(terms.astype(bf16), "blk", scatter_dimension=1, tiled=True)
    placer = place_rows(destination, wide_count, slot_count)
    payload = jnp.concatenate([hidden, tok_grad], axis=1)
    packed = jnp.dot(placer, payload, preferred_element_type=f32).astype(bf16)
    packed = packed.reshape(wide_count, slot_count, 2 * feat_width)
    rows = lax.all_to_all(packed, "wide", split_axis=0, concat_axis=0, tiled=True).reshape(
        wide_count * slot_count, 2 * feat_width
    )
    hidden = rows[:, :feat_width].astype(f32)
    gained = gain[None, :] * rows[:, feat_width:].astype(f32)
    squares, inner_sum = lax.psum(
        (jnp.sum(hidden * hidden, axis=1), jnp.sum(gained * hidden, axis=1)), "blk"
    )
    inv_rms = lax.rsqrt(squares / features + norm_eps)[:, None]
    normed = (gain[None, :] * hidden * inv_rms).astype(bf16)
    resid_back = (
        inv_rms * gained - hidden * (inv_rms * inv_rms * inv_rms) * inner_sum[:, None] / features
    ).astype(bf16)
    act_back = dot_t(lax.all_gather(resid_back, "blk", axis=1, tiled=True), w_down)
    return (query_grad, resid_back, act_back.astype(bf16), normed)


def solution(mesh):
    blk_count, wide_count = mesh.shape["blk"], mesh.shape["wide"]

    def shards(*operands):
        pairs, tok_count = operands[2].shape[0], operands[7].shape[0]
        low_rank = 2 * wide_count * pairs <= 3 * tok_count
        per_pair = tok_count // pairs
        aligned = operands[9].shape[0] % (lane * operands[0].shape[0]) == 0
        if low_rank and blk_count == 4 and aligned and per_pair * pairs == tok_count:
            return low_rank_shards(*operands)
        return row_shards(*operands)

    return jax.shard_map(
        shards,
        mesh=mesh,
        in_specs=(
            P(("wide", "blk"), None),
            P(("wide", "blk"), None),
            P("wide"),
            P("wide"),
            P("wide", None),
            P("wide", None),
            P("wide", "blk"),
            P("wide", "blk"),
            P("blk", None),
            P("blk"),
        ),
        out_specs=(P(("wide", "blk"), None), P("wide", "blk"), P("wide", "blk"), P("wide", "blk")),
        check_vma=False,
    )
```

time: 243 us -> 139 us (0.57)
  blocking collectives: 106 us -> 28 us
  waiting for transfers between devices: 72.3 us -> 9.08 us
  Pallas kernels: 0 us -> 58.3 us
  matrix products: 32.7 us -> 0 us
  starting transfers between devices: 0.08 us -> 14.7 us
  other arithmetic: 10.3 us -> 3.04 us
  local copies, waits for them, and re-layouts: 6.79 us -> 10.9 us
    pallas_call x0 -> x10, Pallas kernels: none -> 58.3 us  [the longest x4 18.7 us: project(): pl.pallas_call(project_body if resid is None else project_own_body, grid_...]
    all_to_all x1, blocking collectives: 79.1 us -> 28 us  [low_rank_shards(): lax.all_to_all(packed, 'wide', split_axis=0, concat_axis=0, tiled=True)]
    all_gather x1, waiting for transfers between devices: 36.8 us -> 0.01 us  [low_rank_shards(): low = lax.all_gather(low_own, 'wide', axis=0, tiled=True)]
    reduce_scatter x1 -> x0, waiting for transfers between devices: 35.4 us -> none  [norm_layer(): lax.psum_scatter(partial_terms.astype(jnp.bfloat16), 'blk', scatter_dimen...]
    dot_general x7 -> x0, matrix products: 32.7 us -> none  [the longest x1 13.9 us: norm_layer(): lax.dot_general(lax.all_gather(resid_back, 'blk', axis=1, tiled=True), w_...]
    all_gather x2 -> x0, blocking collectives: 18.4 us -> none  [the longest x1 10.1 us: shards(): lax.all_gather(query_emb, 'blk', axis=0, tiled=True)]
    ppermute x0 -> x12, starting transfers between devices: none -> 14.6 us  [swap(): lax.ppermute(rows, 'blk', [(i, i ^ k) for i in range(lax.axis_size('blk'))])]
    ppermute x0 -> x12, waiting for transfers between devices: none -> 9.06 us  [swap(): lax.ppermute(rows, 'blk', [(i, i ^ k) for i in range(lax.axis_size('blk'))])]
  transfers between devices with their start and end apart: 2 -> 13, of which waited for: 2 -> 4; matrix products, arithmetic and copies ran while one was open for 0% -> 5% of each run, Pallas kernels for 0% -> 36%
where the time goes in v2:
time: 139 us; the launch traced here: 138 us
  Pallas kernels  58.3 us (42%)
  blocking collectives  28 us (20%)
  starting transfers between devices  14.7 us (11%)
  between operations  14.3 us (10%)
  local copies, waits for them, and re-layouts  10.9 us (8%)
  waiting for transfers between devices  9.08 us (7%)
  other arithmetic  3.04 us (2%)
    all_to_all x1, blocking collectives, low_rank_shards(): lax.all_to_all(packed, 'wide', split_axis=0, concat_axis=0, tiled=True)  28 us
    pallas_call x4, Pallas kernels, project(): pl.pallas_call(project_body if resid is None else project_own_body, grid_...  18.7 us
    pallas_call x1, Pallas kernels, low_activations(): pl.pallas_call(low_act_body, grid=(depth // tile,), in_specs=[pl.BlockSpe...  16.1 us
    ppermute x12, starting transfers between devices, swap(): lax.ppermute(rows, 'blk', [(i, i ^ k) for i in range(lax.axis_size('blk'))])  14.6 us
    pallas_call x1, Pallas kernels, back(): pl.pallas_call(lambda *refs: back_body(count, *refs), grid_spec=pltpu.Pre...  12.1 us
    ppermute x12, waiting for transfers between devices, swap(): lax.ppermute(rows, 'blk', [(i, i ^ k) for i in range(lax.axis_size('blk'))])  9.06 us
    pallas_call x1, Pallas kernels, finish(): pl.pallas_call(lambda *refs: finish_body(features, count, *refs), grid_sp...  8.54 us
    unnamed x31, local copies, waits for them, and re-layouts  5.33 us
  transfers between devices with their start and end apart: 13, of which 4 were waited for; matrix products, arithmetic and copies ran while one was open for 5% of the time, Pallas kernels for 36%

profile of v2, /device:TPU:0, one launch (start us, length us, event | category | flops | bytes accessed | tf_op | source)
XLA Modules:
  0.0 138.2 jit_solution(6745000995017110403)
XLA Ops:
  7.2 0.8 subtract_convert_fusion
  8.0 1.4 %constant_dynamic-update-slice_fusion.3 = bf16[4,8704]{1,0:T(4,128)(2,1)} fusion(bf16[4,4096]{1,0:T(4,128)(2,1)} %param.10), kind=kLoop, calls=%fused_computation.7 | loop fusion | bytes 65536
  9.4 1.4 %constant_dynamic-update-slice_fusion.2 = bf16[4,8704]{1,0:T(4,128)(2,1)} fusion(bf16[4,8704]{1,0:T(4,128)(2,1)} %constant_dynamic-update-slice_fusion.3, bf16[4,4096]{1,0:T(4,128)(2,1)} %param.11), kind=kLoop, calls=%fused_computation.6 | loop fusion | bytes 65536
  10.8 0.6 constant_dynamic-update-slice_fusion.1
  11.4 0.6 constant_dynamic-update-slice_fusion
  11.9 3.9 %collective-permute-start.2 = (bf16[4,8704]{1,0:T(4,128)(2,1)}, bf16[4,8704]{1,0:T(4,128)(2,1)}, u32[]{:S(2)}, u32[]{:S(2)}) collective-permute-start(bf16[4,8704]{1,0:T(4,128)(2,1)} %constant_dynamic-update-slice_fusion), channel_id=1, source_target_pairs={{0,3},{1,2},{2,1},{3,0},{4,7},{5,6},{6,5},{7,4},{8,11},{9,10},{10,... | collective-permute-start | bytes 208904 | tf_op jit(solution)/shard_map/ppermute | solution.py:45
  15.8 0.5 collective-permute-start.1
  16.3 0.1 collective-permute-start
  16.4 1.3 copy-done
  17.7 4.5 %shard_map.132 = bf16[192,1024]{1,0:T(8,128)(2,1)S(1)} custom-call(s32[1]{0:T(128)} %bitcast.10.group_ref, bf16[192,3072]{1,0:T(8,128)(2,1)S(1)} %copy-done, bf16[3072,4096]{1,0:T(8,128)(2,1)} %refs_4_.1), custom_call_target="tpu_custom_call" | custom-call | flops 1207959552 | bytes 7471104 | tf_op jit(solution)/shard_map/pallas_call | solution.py:69
  22.2 2.0 %collective-permute-start.4 = (bf16[192,1024]{1,0:T(8,128)(2,1)S(1)}, bf16[192,1024]{1,0:T(8,128)(2,1)S(1)}, u32[]{:S(2)}, u32[]{:S(2)}) collective-permute-start(bf16[192,1024]{1,0:T(8,128)(2,1)S(1)} %shard_map.132), channel_id=1, source_target_pairs={{0,1},{1,0},{2,3},{3,2},{4,5},{5,4},{6,7},{7,6},{8,9},{9,8},{10,11... | collective-permute-start | bytes 1179656 | tf_op jit(solution)/shard_map/ppermute | solution.py:45
  24.3 4.5 %shard_map.133 = bf16[192,1024]{1,0:T(8,128)(2,1)S(1)} custom-call(s32[1]{0:T(128)} %bitcast.11.group_ref, bf16[192,3072]{1,0:T(8,128)(2,1)S(1)} %copy-done.1, bf16[3072,4096]{1,0:T(8,128)(2,1)} %refs_4_.1), custom_call_target="tpu_custom_call" | custom-call | flops 1207959552 | bytes 7471104 | tf_op jit(solution)/shard_map/pallas_call | solution.py:69
  28.8 1.6 %collective-permute-start.5 = (bf16[192,1024]{1,0:T(8,128)(2,1)S(1)}, bf16[192,1024]{1,0:T(8,128)(2,1)S(1)}, u32[]{:S(2)}, u32[]{:S(2)}) collective-permute-start(bf16[192,1024]{1,0:T(8,128)(2,1)S(1)} %shard_map.133), channel_id=1, source_target_pairs={{0,2},{1,3},{2,0},{3,1},{4,6},{5,7},{6,4},{7,5},{8,10},{9,11},{10,... | collective-permute-start | bytes 1179656 | tf_op jit(solution)/shard_map/ppermute | solution.py:45
  30.4 0.7 reshape.50
  31.1 0.7 copy.17
  31.8 0.1 copy.19.pos_ref
  31.8 0.1 copy.18.lse_ref
  31.9 5.2 %shard_map.131 = bf16[192,1024]{1,0:T(8,128)(2,1)} custom-call(s32[1]{0:T(128)} %bitcast.9.group_ref, bf16[192,3072]{1,0:T(8,128)(2,1)S(1)} %copy-done.1, bf16[3072,4096]{1,0:T(8,128)(2,1)} %refs_4_.1), custom_call_target="tpu_custom_call" | custom-call | flops 1207959552 | bytes 7471104 | tf_op jit(solution)/shard_map/pallas_call | solution.py:69
  37.2 0.1 fusion.3.table_ref
  37.3 1.2 pad_maximum_fusion.parts_ref
  38.5 1.3 shard_map.129
  39.8 0.7 copy-done.3
  40.5 4.5 %shard_map.130.own_ref = f32[192,1024]{1,0:T(8,128)S(1)} custom-call(s32[1]{0:T(128)} %bitcast.blk_ref.group_ref, bf16[192,3072]{1,0:T(8,128)(2,1)S(1)} %copy-done.1, bf16[3072,4096]{1,0:T(8,128)(2,1)} %refs_4_.1, bf16[192,1024]{1,0:T(8,128)(2,1)S(1)} %copy-done.2), custom_call_target="tpu_custom_call" | custom-call | flops 1207959552 | bytes 7471104 | tf_op jit(solution)/shard_map/pallas_call | solution.py:69
  45.0 2.8 %collective-permute-done.3.rest_0_ = bf16[192,1024]{1,0:T(8,128)(2,1)S(1)} collective-permute-done((bf16[192,1024]{1,0:T(8,128)(2,1)}, bf16[192,1024]{1,0:T(8,128)(2,1)S(1)}, u32[]{:S(2)}, u32[]{:S(2)}) %collective-permute-start.3) | collective-permute-done | bytes 393248 | tf_op jit(solution)/shard_map/ppermute | solution.py:45
  47.8 1.0 shard_map.134
  48.9 28.0 %all_to_all.5 = bf16[8,36,1024]{2,1,0:T(8,128)(2,1)S(1)} all-to-all(bf16[8,36,1024]{2,1,0:T(8,128)(2,1)S(1)} %shard_map.134), channel_id=1, replica_groups=mesh['wide'=8,'blk'=4] {'wide'}, dimensions={0} | all-to-all | bytes 1179648 | tf_op jit(solution)/shard_map/all_to_all | solution.py:433
  76.9 0.1 reshape.53.refs_13_
  77.0 1.3 collective-permute-start.8
  78.3 1.1 collective-permute-start.6
  79.5 0.1 stack.35.refs_0_
  79.6 0.9 collective-permute-start.10
  80.5 0.8 collective-permute-start.11
  81.2 0.1 pad_add_fusion.refs_0_
  81.3 5.6 %collective-permute-done.8.refs_6_ = bf16[288,512]{1,0:T(8,128)(2,1)S(1)} collective-permute-done((bf16[288,512]{1,0:T(8,128)(2,1)S(1)}, bf16[288,512]{1,0:T(8,128)(2,1)S(1)}, u32[]{:S(2)}, u32[]{:S(2)}) %collective-permute-start.8) | collective-permute-done | bytes 294944 | tf_op jit(solution)/shard_map/ppermute | solution.py:45
  87.0 1.2 collective-permute-start.9
  88.2 0.1 collective-permute-done.6.refs_3_
  88.3 1.2 collective-permute-start.7
  89.4 0.9 slice_reduce_fusion
  90.4 0.1 reshape_squeeze.3.len_ref
  90.4 0.8 slice.26
  91.2 0.1 reshape.54.dest_ref
  91.3 1.3 slice.25.refs_13_.refs_14_.refs_15_.refs_16_.refs_17_.refs_18_.low_ref.refs_5_.refs_6_
  92.6 0.5 shard_map.136.refs_10_
  93.1 0.9 fusion
  94.1 0.5 collective-permute-done.10.refs_4_
  94.6 12.1 %shard_map.135 = (f32[288,3072]{1,0:T(8,128)S(1)}, f32[288,1]{1,0:T(8,128)S(1)}, f32[288,128]{1,0:T(8,128)S(1)}) custom-call(s32[6]{0:T(128)S(1)} %stack.35.refs_0_, bf16[288,512]{1,0:T(8,128)(2,1)S(1)} %get-tuple-element.23.refs_1_, bf16[288,512]{1,0:T(8,128)(2,1)S(1)} %get-tuple-element.22.refs_2_, bf16[288,512]{1,0:T(8,128)(2,1)S(1)} %collective-permute-done.6.refs_3_, ...), custom_call_target="tpu_custom_call" | custom-call | flops 5435817984 | bytes 18874368 | tf_op jit(solution)/shard_map/pallas_call | solution.py:293
  106.7 16.1 %shard_map.137.refs_12_ = bf16[128,3072]{1,0:T(8,128)(2,1)S(1)} custom-call(bf16[128,4096]{1,0:T(8,128)(2,1)S(1)} %slice.25.refs_13_.refs_14_.refs_15_.refs_16_.refs_17_.refs_18_.low_ref.refs_5_.refs_6_, bf16[3072,4096]{1,0:T(8,128)(2,1)} %refs_4_.1), custom_call_target="tpu_custom_call" | custom-call | flops 3221225472 | bytes 25165824 | tf_op jit(solution)/shard_map/pallas_call | solution.py:235
  122.8 8.5 %shard_map.138 = (bf16[288,3072]{1,0:T(8,128)(2,1)}, bf16[288,1024]{1,0:T(8,128)(2,1)}, bf16[288,1024]{1,0:T(8,128)(2,1)}) custom-call(s32[3]{0:T(128)S(1)} %pad_add_fusion.refs_0_, bf16[288,512]{1,0:T(8,128)(2,1)S(1)} %collective-permute-done.7.refs_1_, bf16[288,512]{1,0:T(8,128)(2,1)S(1)} %collective-permute-done.9.refs_2_, bf16[3072,4096]{1,0:T(8,128)(2,1)} %refs_4_.1, ...), custom_call_target="tpu_custom_call" | custom-call | flops 1811939328 | bytes 11599872 | tf_op jit(solution)/shard_map/pallas_call | solution.py:349
  (43 shorter events, 0.2 us)
Async XLA Ops:
  7.2 82.3 %all-gather.2.cloned.1.call-start = ((), (), s32[]{:S(2)}) async-start(), calls=%async_computation.1 | async-start | bytes 1216512 | tf_op jit(solution)/shard_map/all_gather | solution.py:425
  11.9 25.3 %collective-permute-start.2 = (bf16[4,8704]{1,0:T(4,128)(2,1)}, bf16[4,8704]{1,0:T(4,128)(2,1)}, u32[]{:S(2)}, u32[]{:S(2)}) collective-permute-start(bf16[4,8704]{1,0:T(4,128)(2,1)} %constant_dynamic-update-slice_fusion), channel_id=1, source_target_pairs={{0,3},{1,2},{2,1},{3,0},{4,7},{5,6},{6,5},{7,4},{8,11},{9,10},{10,... | collective-permute-start | bytes 208904 | tf_op jit(solution)/shard_map/ppermute | solution.py:45
  15.8 21.5 %collective-permute-start.1 = (bf16[4,8704]{1,0:T(4,128)(2,1)}, bf16[4,8704]{1,0:T(4,128)(2,1)}, u32[]{:S(2)}, u32[]{:S(2)}) collective-permute-start(bf16[4,8704]{1,0:T(4,128)(2,1)} %constant_dynamic-update-slice_fusion), channel_id=1, source_target_pairs={{0,2},{1,3},{2,0},{3,1},{4,6},{5,7},{6,4},{7,5},{8,10},{9,11},{10,... | collective-permute-start | bytes 208904 | tf_op jit(solution)/shard_map/ppermute | solution.py:45
  16.3 21.0 %collective-permute-start = (bf16[4,8704]{1,0:T(4,128)(2,1)}, bf16[4,8704]{1,0:T(4,128)(2,1)}, u32[]{:S(2)}, u32[]{:S(2)}) collective-permute-start(bf16[4,8704]{1,0:T(4,128)(2,1)} %constant_dynamic-update-slice_fusion), channel_id=1, source_target_pairs={{0,1},{1,0},{2,3},{3,2},{4,5},{5,4},{6,7},{7,6},{8,9},{9,8},{10,11... | collective-permute-start | bytes 208904 | tf_op jit(solution)/shard_map/ppermute | solution.py:45
  16.4 1.3 copy-start
  17.7 6.6 %copy-start.1 = (bf16[192,3072]{1,0:T(8,128)(2,1)S(1)}, bf16[192,3072]{1,0:T(8,128)(2,1)}, u32[]{:S(2)}) copy-start(bf16[192,3072]{1,0:T(8,128)(2,1)} %act_ref.7) | copy-start | bytes 3538948
  22.2 22.8 %collective-permute-start.4 = (bf16[192,1024]{1,0:T(8,128)(2,1)S(1)}, bf16[192,1024]{1,0:T(8,128)(2,1)S(1)}, u32[]{:S(2)}, u32[]{:S(2)}) collective-permute-start(bf16[192,1024]{1,0:T(8,128)(2,1)S(1)} %shard_map.132), channel_id=1, source_target_pairs={{0,1},{1,0},{2,3},{3,2},{4,5},{5,4},{6,7},{7,6},{8,9},{9,8},{10,11... | collective-permute-start | bytes 1179656 | tf_op jit(solution)/shard_map/ppermute | solution.py:45
  24.3 6.1 %copy-start.13 = (s32[1,16]{1,0:T(1,128)S(1)}, s32[1,16]{1,0:T(1,128)}, u32[]{:S(2)}) copy-start(s32[1,16]{1,0:T(1,128)} %param.14) | copy-start | bytes 196
  24.3 6.1 %copy-start.9 = (s32[192,1]{0,1:T(1,128)S(1)}, s32[192,1]{0,1:T(1,128)}, u32[]{:S(2)}) copy-start(s32[192,1]{0,1:T(1,128)} %param.15) | copy-start | bytes 2308
  24.3 7.5 %copy-start.7 = (s32[16]{0:T(128)S(1)}, s32[16]{0:T(128)}, u32[]{:S(2)}) copy-start(s32[16]{0:T(128)} %param.13) | copy-start | bytes 196
  24.3 7.6 %copy-start.5 = (f32[16]{0:T(128)S(1)}, f32[16]{0:T(128)}, u32[]{:S(2)}) copy-start(f32[16]{0:T(128)} %param.12) | copy-start | bytes 196
  28.8 16.2 %collective-permute-start.5 = (bf16[192,1024]{1,0:T(8,128)(2,1)S(1)}, bf16[192,1024]{1,0:T(8,128)(2,1)S(1)}, u32[]{:S(2)}, u32[]{:S(2)}) collective-permute-start(bf16[192,1024]{1,0:T(8,128)(2,1)S(1)} %shard_map.133), channel_id=1, source_target_pairs={{0,2},{1,3},{2,0},{3,1},{4,6},{5,7},{6,4},{7,5},{8,10},{9,11},{10,... | collective-permute-start | bytes 1179656 | tf_op jit(solution)/shard_map/ppermute | solution.py:45
  31.9 5.2 %copy-start.11 = (bf16[16,12]{1,0:T(8,128)(2,1)S(1)}, bf16[16,12]{1,0:T(8,128)(2,1)}, u32[]{:S(2)}) copy-start(bf16[16,12]{1,0:T(8,128)(2,1)} %reshape.50) | copy-start | bytes 1156
  31.9 5.2 %copy-start.12 = (bf16[16,1]{1,0:T(8,128)(2,1)S(1)}, bf16[16,1]{1,0:T(8,128)(2,1)}, u32[]{:S(2)}) copy-start(bf16[16,1]{1,0:T(8,128)(2,1)} %copy.17) | copy-start | bytes 100
  31.9 6.5 %copy-start.6 = (f32[16]{0:T(128)S(1)}, f32[16]{0:T(128)}, u32[]{:S(2)}) copy-start(f32[16]{0:T(128)} %param.12) | copy-start | bytes 196
  31.9 6.5 %copy-start.8 = (s32[16]{0:T(128)S(1)}, s32[16]{0:T(128)}, u32[]{:S(2)}) copy-start(s32[16]{0:T(128)} %param.13) | copy-start | bytes 196
  37.2 3.3 %copy-start.2 = (bf16[192,1024]{1,0:T(8,128)(2,1)S(1)}, bf16[192,1024]{1,0:T(8,128)(2,1)}, u32[]{:S(2)}) copy-start(bf16[192,1024]{1,0:T(8,128)(2,1)} %resid_ref.1) | copy-start | bytes 1179652
  37.3 10.6 %collective-permute-start.3 = (bf16[192,1024]{1,0:T(8,128)(2,1)}, bf16[192,1024]{1,0:T(8,128)(2,1)S(1)}, u32[]{:S(2)}, u32[]{:S(2)}) collective-permute-start(bf16[192,1024]{1,0:T(8,128)(2,1)} %shard_map.131), channel_id=1, source_target_pairs={{0,3},{1,2},{2,1},{3,0},{4,7},{5,6},{6,5},{7,4},{8,11},{9,10},{10,... | collective-permute-start | bytes 1179656 | tf_op jit(solution)/shard_map/ppermute | solution.py:45
  39.8 0.7 copy-start.3
  40.5 7.4 %copy-start.10 = (s32[192,1]{0,1:T(1,128)S(1)}, s32[192,1]{0,1:T(1,128)}, u32[]{:S(2)}) copy-start(s32[192,1]{0,1:T(1,128)} %param.15) | copy-start | bytes 2308
  77.0 9.9 %collective-permute-start.8 = (bf16[288,512]{1,0:T(8,128)(2,1)S(1)}, bf16[288,512]{1,0:T(8,128)(2,1)S(1)}, u32[]{:S(2)}, u32[]{:S(2)}) collective-permute-start(bf16[288,512]{1,0:T(8,128)(2,1)S(1)} %get-tuple-element.22.refs_2_), channel_id=1, source_target_pairs={{0,2},{1,3},{2,0},{3,1},{4,6},{5,7},{6,4},{7,5},{8,10},{9,11},{10,... | collective-permute-start | bytes 884744 | tf_op jit(solution)/shard_map/ppermute | solution.py:45
  78.3 9.9 %collective-permute-start.6 = (bf16[288,512]{1,0:T(8,128)(2,1)S(1)}, bf16[288,512]{1,0:T(8,128)(2,1)S(1)}, u32[]{:S(2)}, u32[]{:S(2)}) collective-permute-start(bf16[288,512]{1,0:T(8,128)(2,1)S(1)} %get-tuple-element.23.refs_1_), channel_id=1, source_target_pairs={{0,1},{1,0},{2,3},{3,2},{4,5},{5,4},{6,7},{7,6},{8,9},{9,8},{10,11... | collective-permute-start | bytes 884744 | tf_op jit(solution)/shard_map/ppermute | solution.py:45
  79.6 15.0 %collective-permute-start.10 = (bf16[288,512]{1,0:T(8,128)(2,1)S(1)}, bf16[288,512]{1,0:T(8,128)(2,1)S(1)}, u32[]{:S(2)}, u32[]{:S(2)}) collective-permute-start(bf16[288,512]{1,0:T(8,128)(2,1)S(1)} %get-tuple-element.22.refs_2_), channel_id=1, source_target_pairs={{0,1},{1,0},{2,3},{3,2},{4,5},{5,4},{6,7},{7,6},{8,9},{9,8},{10,11... | collective-permute-start | bytes 884744 | tf_op jit(solution)/shard_map/ppermute | solution.py:45
  80.5 14.1 %collective-permute-start.11 = (bf16[288,512]{1,0:T(8,128)(2,1)S(1)}, bf16[288,512]{1,0:T(8,128)(2,1)S(1)}, u32[]{:S(2)}, u32[]{:S(2)}) collective-permute-start(bf16[288,512]{1,0:T(8,128)(2,1)S(1)} %get-tuple-element.23.refs_1_), channel_id=1, source_target_pairs={{0,2},{1,3},{2,0},{3,1},{4,6},{5,7},{6,4},{7,5},{8,10},{9,11},{10,... | collective-permute-start | bytes 884744 | tf_op jit(solution)/shard_map/ppermute | solution.py:45
  87.0 35.8 %collective-permute-start.9 = (bf16[288,512]{1,0:T(8,128)(2,1)S(1)}, bf16[288,512]{1,0:T(8,128)(2,1)S(1)}, u32[]{:S(2)}, u32[]{:S(2)}) collective-permute-start(bf16[288,512]{1,0:T(8,128)(2,1)S(1)} %collective-permute-done.8.refs_6_), channel_id=1, source_target_pairs={{0,1},{1,0},{2,3},{3,2},{4,5},{5,4},{6,7},{7,6},{8,9},{9,8},{10,11... | collective-permute-start | bytes 884744 | tf_op jit(solution)/shard_map/ppermute | solution.py:45
  88.3 34.6 %collective-permute-start.7 = (bf16[288,512]{1,0:T(8,128)(2,1)S(1)}, bf16[288,512]{1,0:T(8,128)(2,1)S(1)}, u32[]{:S(2)}, u32[]{:S(2)}) collective-permute-start(bf16[288,512]{1,0:T(8,128)(2,1)S(1)} %collective-permute-done.6.refs_3_), channel_id=1, source_target_pairs={{0,2},{1,3},{2,0},{3,1},{4,6},{5,7},{6,4},{7,5},{8,10},{9,11},{10,... | collective-permute-start | bytes 884744 | tf_op jit(solution)/shard_map/ppermute | solution.py:45
  106.7 16.1 %copy-start.4 = (f32[1024]{0:T(1024)S(1)}, f32[1024]{0:T(1024)}, u32[]{:S(2)}) copy-start(f32[1024]{0:T(1024)} %param.19) | copy-start | bytes 12292
Sparse Core Ops, SparseCore 0:
  40.6 30.5 all-gather.1

commit v3 on v2

--- a/solution.py
+++ b/solution.py
@@ -41,35 +41,60 @@
     return lax.dot_general(left, right, (((1,), (1,)), ((), ())), preferred_element_type=f32)
 
 
-def swap(rows, k):
-    return lax.ppermute(rows, "blk", [(i, i ^ k) for i in range(lax.axis_size("blk"))])
-
-
-def project_body(group_ref, act_ref, w_ref, out_ref):
-    out_ref[...] = dot(act_ref[...], w_ref[...]).astype(bf16)
-
-
-def project_own_body(group_ref, act_ref, w_ref, resid_ref, out_ref):
-    out_ref[...] = dot(act_ref[...], w_ref[...]) + resid_ref[...].astype(f32)
+def swap(rows, k, axis="blk"):
+    return lax.ppermute(rows, axis, [(i, i ^ k) for i in range(lax.axis_size(axis))])
+
+
+def after(first, *later):
+    return lax.optimization_barrier((first, *later))
+
+
+def project_step(act_ref, w_ref, total):
+    @pl.when(pl.program_id(0) == 0)
+    def _():
+        total[...] = dot(act_ref[...], w_ref[...])
+
+    @pl.when(pl.program_id(0) > 0)
+    def _():
+        total[...] += dot(act_ref[...], w_ref[...])
+
+
+def project_body(group_ref, act_ref, w_ref, out_ref, total):
+    project_step(act_ref, w_ref, total)
+
+    @pl.when(pl.program_id(0) == pl.num_programs(0) - 1)
+    def _():
+        out_ref[...] = total[...].astype(bf16)
+
+
+def project_own_body(group_ref, act_ref, w_ref, resid_ref, out_ref, total):
+    project_step(act_ref, w_ref, total)
+
+    @pl.when(pl.program_id(0) == pl.num_programs(0) - 1)
+    def _():
+        out_ref[...] = total[...] + resid_ref[...].astype(f32)
 
 
 def project(group, act, w_down, width, resid=None):
     rows, depth = act.shape
-    tile = tile_of(width, 256)
-    per_group = width // tile
-    column_spec = pl.BlockSpec((rows, tile), lambda j, g: (0, j))
+    tile = tile_of(depth, 512)
+    whole = pl.BlockSpec((rows, width), lambda j, g: (0, 0))
     in_specs = [
-        pl.BlockSpec((rows, depth), lambda j, g: (0, 0)),
-        pl.BlockSpec((depth, tile), lambda j, g: (0, g[0] * per_group + j)),
+        pl.BlockSpec((rows, tile), lambda j, g: (0, j)),
+        pl.BlockSpec((tile, width), lambda j, g: (j, g[0])),
     ]
     operands = [act, w_down]
     if resid is not None:
-        in_specs.append(column_spec)
+        in_specs.append(whole)
         operands.append(resid)
     return pl.pallas_call(
         project_body if resid is None else project_own_body,
         grid_spec=pltpu.PrefetchScalarGridSpec(
-            num_scalar_prefetch=1, grid=(per_group,), in_specs=in_specs, out_specs=column_spec
+            num_scalar_prefetch=1,
+            grid=(depth // tile,),
+            in_specs=in_specs,
+            out_specs=whole,
+            scratch_shapes=[pltpu.VMEM((rows, width), f32)],
         ),
         out_shape=jax.ShapeDtypeStruct((rows, width), bf16 if resid is None else f32),
         compiler_params=params(),
@@ -77,13 +102,21 @@
     )(group, *operands)
 
 
-def group_body(blk_ref, parts_ref, lse_row_ref, lse_ref, pos_row_ref, pos_ref, table_ref, *rest):
-    query_grad_ref, low_ref, gain_ref = rest
+def group_body(count, blk_ref, *refs):
+    query_parts, passage_parts = refs[:count], refs[count : 2 * count]
+    gain_parts, refs = refs[2 * count : 3 * count], refs[3 * count :]
+    lse_row_ref, lse_ref, pos_row_ref, pos_ref, table_ref = refs[:5]
+    query_grad_ref, low_ref, query_all, passage_all, gain_all = refs[5:]
     own, features = query_grad_ref.shape
-    pairs = parts_ref.shape[0]
+    pairs = own * count
+    width = features // count
     blk = blk_ref[0]
-    queries = parts_ref[:, :features]
-    passages = parts_ref[:, features : 2 * features]
+    for k in range(count):
+        query_all[k * own : (k + 1) * own] = query_parts[k][...].astype(f32)
+        passage_all[k * own : (k + 1) * own] = passage_parts[k][...].astype(f32)
+        gain_all[:, pl.ds(pl.multiple_of((blk ^ k) * width, lane), width)] = gain_parts[k][...]
+    queries = query_all[...].astype(bf16)
+    passages = passage_all[...].astype(bf16)
 
     def named(dim):
         place = iota((pairs, pairs), dim)
@@ -103,44 +136,34 @@
     turned = (jnp.exp(logit_scale * dot_t(passages, queries) - lse) - hit).astype(bf16)
     turned = dot(at_cols.astype(bf16), turned).astype(bf16)
     pass_grad = logit_scale * dot(turned, queries)
-    piece = (parts_ref.shape[1] - 2 * features) // 2
-    gains = (
-        parts_ref[:, 2 * features : 2 * features + piece].astype(f32)
-        + parts_ref[:, 2 * features + piece :].astype(f32)
-    )
-    for row in range(pairs):
-        first = ((blk ^ (row // own)) * own + row % own) * piece
-        gain_ref[:, pl.ds(pl.multiple_of(first, lane), piece)] = gains[row : row + 1]
-    low_ref[:, :features] = (gain_ref[...] * pass_grad).astype(bf16)
+    low_ref[:, :features] = (gain_all[...] * pass_grad).astype(bf16)
     low_ref[:, features:] = table_ref[...]
 
 
-def group_part(query_emb, passage_emb, row_lse, positive, token_lengths, destination, gain, blk):
-    own, features = query_emb.shape
+def group_part(parts, row_lse, positive, token_lengths, destination, blk):
+    own, features = parts[0].shape
     pairs = row_lse.shape[0]
-    high = gain.astype(bf16)
-    rest = (gain - high.astype(f32)).astype(bf16)
-    both = jnp.concatenate(
-        [query_emb, passage_emb, high.reshape(own, -1), rest.reshape(own, -1)], axis=1
-    )
-    parts = jnp.concatenate([both] + [swap(both, k) for k in range(1, pairs // own)], axis=0)
     table = jnp.concatenate([destination.reshape(pairs, -1), token_lengths.reshape(pairs, 1)], 1)
     table = jnp.pad(table, ((0, 0), (0, lane - table.shape[1]))).astype(bf16)
     return pl.pallas_call(
-        group_body,
+        lambda *refs: group_body(pairs // own, *refs),
         in_specs=[pl.BlockSpec(memory_space=pltpu.SMEM)]
-        + [pl.BlockSpec(memory_space=pltpu.VMEM)] * 6,
+        + [pl.BlockSpec(memory_space=pltpu.VMEM)] * (len(parts) + 5),
         out_specs=[pl.BlockSpec(memory_space=pltpu.VMEM)] * 2,
         out_shape=[
             jax.ShapeDtypeStruct((own, features), bf16),
             jax.ShapeDtypeStruct((pairs, features + lane), bf16),
         ],
-        scratch_shapes=[pltpu.VMEM((1, features), f32)],
+        scratch_shapes=[
+            pltpu.VMEM((pairs, features), f32),
+            pltpu.VMEM((pairs, features), f32),
+            pltpu.VMEM((1, features), f32),
+        ],
         compiler_params=params(),
         cost_estimate=cost(8 * pairs * pairs * features, 8 * pairs * features),
     )(
         blk[None],
-        parts,
+        *parts,
         row_lse[None],
         row_lse[:, None],
         positive[None],
@@ -153,37 +176,69 @@
     return (iota((tokens, tokens), 0) < iota((tokens, tokens), 1)).astype(bf16)
 
 
-def pack_body(dest_ref, own_ref, *rest):
-    terms, out_ref = rest[:-1], rest[-1]
-    groups, slots, _ = out_ref.shape
+def pack_body(terms, wide_ref, dest_ref, own_ref, *rest):
+    outs = rest[terms:]
+    groups, slots = len(outs), outs[0].shape[0]
     tokens = dest_ref.shape[1]
     stride = -(-slots // 16) * 16
     hidden = own_ref[...]
-    for term in terms:
+    for term in rest[:terms]:
         hidden = hidden + term[...].astype(f32)
-    dest = dest_ref[...]
-    hit = (dest == iota((groups, tokens), 0)).astype(f32)
+    partner = dest_ref[...] ^ wide_ref[0]
+    hit = (partner == iota((groups, tokens), 0)).astype(f32)
     rank = dot(hit.astype(bf16), earlier_of(tokens))
     rank = jnp.sum(rank * hit, axis=0, keepdims=True).astype(i32)
-    place = (iota((groups * stride, tokens), 0) == dest * stride + rank).astype(bf16)
-    packed = dot(place, hidden.astype(bf16)).astype(bf16)
-    for group in range(groups):
-        out_ref[group] = packed[group * stride : group * stride + slots]
-
-
-def pack(destination, own, terms, groups, slots):
+    place = iota((groups * stride, tokens), 0) == partner * stride + rank
+    packed = dot(place.astype(f32).astype(bf16), hidden.astype(bf16)).astype(bf16)
+    for k in range(groups):
+        outs[k][...] = packed[k * stride : k * stride + slots]
+
+
+def pack(wide, destination, own, terms, groups, slots):
     tokens, width = own.shape
     tile = tile_of(width, 512)
-    column_spec = pl.BlockSpec((tokens, tile), lambda j: (0, j))
-    return pl.pallas_call(
-        pack_body,
-        grid=(width // tile,),
-        in_specs=[pl.BlockSpec((1, tokens), lambda j: (0, 0))] + [column_spec] * (1 + len(terms)),
-        out_specs=pl.BlockSpec((groups, slots, tile), lambda j: (0, 0, j)),
-        out_shape=jax.ShapeDtypeStruct((groups, slots, width), bf16),
+    column_spec = pl.BlockSpec((tokens, tile), lambda j, g: (0, j))
+    return pl.pallas_call(
+        lambda *refs: pack_body(len(terms), *refs),
+        grid_spec=pltpu.PrefetchScalarGridSpec(
+            num_scalar_prefetch=1,
+            grid=(width // tile,),
+            in_specs=[pl.BlockSpec((1, tokens), lambda j, g: (0, 0))]
+            + [column_spec] * (1 + len(terms)),
+            out_specs=[pl.BlockSpec((slots, tile), lambda j, g: (0, j))] * groups,
+        ),
+        out_shape=[jax.ShapeDtypeStruct((slots, width), bf16)] * groups,
         compiler_params=params(),
         cost_estimate=cost(4 * groups * slots * tokens * width, 10 * tokens * width),
-    )(destination.reshape(1, tokens), own, *terms)
+    )(wide[None], destination.reshape(1, tokens), own, *terms)
+
+
+def assemble_body(wide_ref, *refs):
+    parts, (left_ref, right_ref) = refs[:-2], refs[-2:]
+    slots = parts[0].shape[0]
+    rows, half = left_ref.shape
+    row, column = iota((rows, slots), 0), iota((rows, slots), 1)
+    total = 0.0
+    for k, part in enumerate(parts):
+        group = wide_ref[0] ^ k
+        place = (row == group * slots + column).astype(f32).astype(bf16)
+        total = total + dot(place, part[...])
+    left_ref[...] = total[:, :half].astype(bf16)
+    right_ref[...] = total[:, half:].astype(bf16)
+
+
+def assemble(wide, parts):
+    slots, width = parts[0].shape
+    rows = slots * len(parts)
+    return pl.pallas_call(
+        assemble_body,
+        in_specs=[pl.BlockSpec(memory_space=pltpu.SMEM)]
+        + [pl.BlockSpec(memory_space=pltpu.VMEM)] * len(parts),
+        out_specs=[pl.BlockSpec(memory_space=pltpu.VMEM)] * 2,
+        out_shape=[jax.ShapeDtypeStruct((rows, width // 2), bf16)] * 2,
+        compiler_params=params(),
+        cost_estimate=cost(2 * rows * rows * width, 4 * rows * width),
+    )(wide[None], *parts)
 
 
 def slots_body(wide_ref, dest_ref, len_ref, hot_ref):
@@ -225,12 +280,12 @@
 
 
 def low_act_body(low_ref, w_ref, out_ref):
-    out_ref[...] = dot_t(low_ref[...], w_ref[...]).astype(bf16)
-
-
-def low_activations(low, w_down):
+    out_ref[...] = dot_t(w_ref[...], low_ref[...]).astype(bf16)
+
+
+def low_activations(low, features, w_down):
     pairs = low.shape[0]
-    depth, features = w_down.shape
+    depth = w_down.shape[0]
     tile = tile_of(depth, 256)
     return pl.pallas_call(
         low_act_body,
@@ -239,8 +294,8 @@
             pl.BlockSpec((pairs, features), lambda j: (0, 0)),
             pl.BlockSpec((tile, features), lambda j: (j, 0)),
         ],
-        out_specs=pl.BlockSpec((pairs, tile), lambda j: (0, j)),
-        out_shape=jax.ShapeDtypeStruct((pairs, depth), bf16),
+        out_specs=pl.BlockSpec((tile, pairs), lambda j: (j, 0)),
+        out_shape=jax.ShapeDtypeStruct((depth, pairs), bf16),
         compiler_params=params(),
         cost_estimate=cost(2 * pairs * depth * features, 2 * depth * features),
     )(low, w_down)
@@ -273,34 +328,44 @@
     return hid_specs + w_specs + low_specs
 
 
-def back_body(count, *refs):
+def back_body(count, carried, *refs):
     hids, weights, lows = refs[1 : 1 + count], refs[1 + count : 1 + 2 * count], refs[1 + 2 * count :]
-    lows, (acc_ref, squares_ref, cross_ref) = lows[:count], lows[count:]
+    lows, refs = lows[:count], lows[count:]
+    before, (acc_ref, squares_ref, cross_ref) = refs[:carried], refs[carried:]
 
     @pl.when(pl.program_id(0) == 0)
     def _():
-        squares_ref[...], cross_ref[...] = statistics(hids, lows)
-
-    acc_ref[...] = product(hids, weights)
-
-
-def back(places, pieces, w_down, low):
+        squares, cross = statistics(hids, lows)
+        if carried:
+            squares, cross = before[1][...] + squares, before[2][...] + cross
+        squares_ref[...], cross_ref[...] = squares, cross
+
+    total = product(hids, weights)
+    acc_ref[...] = before[0][...] + total if carried else total
+
+
+def carried_specs(rows, pairs, tile):
+    return [
+        pl.BlockSpec((rows, tile), lambda j, g: (0, j)),
+        pl.BlockSpec((rows, 1), lambda j, g: (0, 0)),
+        pl.BlockSpec((rows, pairs), lambda j, g: (0, 0)),
+    ]
+
+
+def back(places, pieces, w_down, low, before=()):
     count = len(pieces)
     rows, width = pieces[0].shape
     depth = w_down.shape[0]
     pairs = low.shape[0]
     tile = tile_of(depth, 512)
-    return pl.pallas_call(
-        lambda *refs: back_body(count, *refs),
+    totals = carried_specs(rows, pairs, tile)
+    return pl.pallas_call(
+        lambda *refs: back_body(count, len(before), *refs),
         grid_spec=pltpu.PrefetchScalarGridSpec(
             num_scalar_prefetch=1,
             grid=(depth // tile,),
-            in_specs=piece_specs(pieces, low, tile),
-            out_specs=[
-                pl.BlockSpec((rows, tile), lambda j, g: (0, j)),
-                pl.BlockSpec((rows, 1), lambda j, g: (0, 0)),
-                pl.BlockSpec((rows, pairs), lambda j, g: (0, 0)),
-            ],
+            in_specs=piece_specs(pieces, low, tile) + totals[: len(before)],
+            out_specs=totals,
         ),
         out_shape=[
             jax.ShapeDtypeStruct((rows, depth), f32),
@@ -309,14 +374,14 @@
         ],
         compiler_params=params(),
         cost_estimate=cost(2 * rows * depth * width * count, 2 * depth * width * count),
-    )(places, *pieces, *[w_down] * count, *[low] * count)
+    )(places, *pieces, *[w_down] * count, *[low] * count, *before)
 
 
 def finish_body(features, count, *refs):
     hids, weights, lows = refs[1 : 1 + count], refs[1 + count : 1 + 2 * count], refs[1 + 2 * count :]
     lows, rest = lows[:count], lows[count:]
-    acc_ref, squares_ref, cross_ref, hot_ref, share_ref, low_act_ref, own_ref, own_low_ref = rest[:8]
-    gain_ref, act_out, resid_out, normed_out, lead, pull = rest[8:]
+    acc_ref, squares_ref, cross_ref, hot_ref, share_ref, low_act_ref, left_ref, right_ref = rest[:8]
+    own_low_ref, gain_ref, act_out, resid_out, normed_out, lead, pull = rest[8:]
 
     @pl.when(pl.program_id(0) == 0)
     def _():
@@ -326,19 +391,22 @@
         inv_rms = lax.rsqrt((squares_ref[...] + squares) / features + norm_eps)
         lead[...] = inv_rms * jnp.sum(weight, axis=1, keepdims=True)
         pull[...] = inv_rms * inv_rms * inv_rms * inner / features
-        own = own_ref[...].astype(f32)
         own_low = dot(hot_ref[...], own_low_ref[...])
-        resid_out[...] = (lead[...] * own_low - own * pull[...]).astype(bf16)
-        normed_out[...] = (gain_ref[...] * own * inv_rms).astype(bf16)
-
-    low_act = dot(hot_ref[...], low_act_ref[...])
+        half = left_ref.shape[1]
+        for own_ref, at in ((left_ref, slice(0, half)), (right_ref, slice(half, 2 * half))):
+            own = own_ref[...].astype(f32)
+            resid_out[:, at] = (lead[...] * own_low[:, at] - own * pull[...]).astype(bf16)
+            normed_out[:, at] = (gain_ref[:, at] * own * inv_rms).astype(bf16)
+
+    low_act = dot_t(hot_ref[...], low_act_ref[...])
     hid_act = acc_ref[...] + product(hids, weights)
     act_out[...] = (lead[...] * low_act - pull[...] * hid_act).astype(bf16)
 
 
-def finish(places, pieces, w_down, low, acc, squares, cross, hot, share, low_act, own, gain):
+def finish(places, pieces, w_down, low, before, hot, share, low_act, own, gain):
     count = len(pieces)
-    rows, width = own.shape
+    rows, half = own[0].shape
+    width = 2 * half
     depth, features = w_down.shape
     pairs = hot.shape[1]
     tile = tile_of(depth, 512)
@@ -352,14 +420,13 @@
             num_scalar_prefetch=1,
             grid=(depth // tile,),
             in_specs=piece_specs(pieces, low, tile)
+            + carried_specs(rows, pairs, tile)
             + [
-                pl.BlockSpec((rows, tile), lambda j, g: (0, j)),
-                whole((rows, 1)),
-                whole((rows, pairs)),
                 whole((rows, pairs)),
                 whole((1, pairs)),
-                pl.BlockSpec((pairs, tile), lambda j, g: (0, j)),
-                whole((rows, width)),
+                pl.BlockSpec((tile, pairs), lambda j, g: (j, 0)),
+                whole((rows, half)),
+                whole((rows, half)),
                 pl.BlockSpec((pairs, width), lambda j, g: (0, g[count])),
                 whole((1, width)),
             ],
@@ -382,13 +449,11 @@
         *pieces,
         *[w_down] * count,
         *[low] * count,
-        acc,
-        squares,
-        cross,
+        *before,
         hot,
         share,
         low_act,
-        own,
+        *own,
         low,
         gain,
     )
@@ -414,11 +479,16 @@
     slot_count = 3 * tok_count // (2 * wide_count)
     rows = wide_count * slot_count
 
-    query_grad, low_own = group_part(
-        query_emb, passage_emb, row_lse, positive, token_lengths, destination, gain, blk
-    )
-    arrived = []
-    for k in (3, 1, 2):
+    steps = range(1, lax.axis_size("blk"))
+    parts = [query_emb, *[swap(query_emb, k) for k in steps]]
+    parts += [passage_emb, *[swap(passage_emb, k) for k in steps]]
+    parts += [gain[None], *[swap(gain[None], k) for k in steps]]
+    first_term = project((blk ^ 3)[None], mlp_act, w_down, width)
+    arrived = [swap(first_term, 3)]
+    parts = after(first_term, *parts)[1:]
+    query_grad, low_own = group_part(parts, row_lse, positive, token_lengths, destination, blk)
+    mlp_act = after(low_own, mlp_act)[1]
+    for k in (1, 2):
         arrived.append(swap(project((blk ^ k)[None], mlp_act, w_down, width), k))
     own_term = project(blk[None], mlp_act, w_down, width, resid)
 
@@ -427,18 +497,15 @@
     per_pair = tok_count // pairs
     dest_all = tables[:, :per_pair].reshape(wide_count, tok_count)
     len_all = tables[:, per_pair].reshape(wide_count, pairs)
-    low = low[:, :features]
-
-    packed = pack(destination, own_term, arrived, wide_count, slot_count)
-    own_hid = lax.all_to_all(packed, "wide", split_axis=0, concat_axis=0, tiled=True)
-    own_hid = own_hid.reshape(rows, width)
-
-    low_act = low_activations(low, w_down)
+
+    packed = pack(wide, destination, own_term, arrived, wide_count, slot_count)
+    routed = [packed[k] if k == 0 else swap(packed[k], k, "wide") for k in range(wide_count)]
+
+    low_act = low_activations(low, features, w_down)
     hot = slot_passages(wide, dest_all, len_all, rows)
     share = (1.0 / len_all.astype(f32)).reshape(1, wide_count * pairs)
 
-    half = width // 2
-    left, right = own_hid[:, :half], own_hid[:, half:]
+    left, right = assemble(wide, routed)
     left_1, right_2 = swap(left, 1), swap(right, 2)
     right_1, left_2 = swap(right, 1), swap(left, 2)
     left_3, right_3 = swap(left_1, 2), swap(right_2, 1)
@@ -446,24 +513,19 @@
     def places(*pieces):
         return jnp.stack([(blk ^ k) * 2 + side for k, side in pieces])
 
-    acc, squares, cross = back(
-        places((0, 0), (0, 1), (1, 0), (1, 1), (2, 0), (2, 1)),
-        [left, right, left_1, right_1, left_2, right_2],
-        w_down,
-        low,
-    )
+    totals = back(places((0, 0), (0, 1)), [left, right], w_down, low)
+    totals = back(places((1, 0), (2, 1)), [left_1, right_2], w_down, low, totals)
+    totals = back(places((1, 1), (2, 0)), [right_1, left_2], w_down, low, totals)
     act_grad, resid_grad, normed_out = finish(
         jnp.concatenate([places((3, 0), (3, 1)), blk[None]]),
         [left_3, right_3],
         w_down,
         low,
-        acc,
-        squares,
-        cross,
+        totals,
         hot,
         share,
         low_act,
-        own_hid,
+        [left, right],
         gain[None],
     )
     return (query_grad, resid_grad, act_grad, normed_out)
@@ -566,7 +628,7 @@
         low_rank = 2 * wide_count * pairs <= 3 * tok_count
         per_pair = tok_count // pairs
         aligned = operands[9].shape[0] % (lane * operands[0].shape[0]) == 0
-        if low_rank and blk_count == 4 and aligned and per_pair * pairs == tok_count:
+        if low_rank and blk_count == 4 and aligned and per_pair * pairs == tok_count and wide_count & (wide_count - 1) == 0:
             return low_rank_shards(*operands)
         return row_shards(*operands)
 

time: 139 us -> 151 us (1.086); the launches traced: 138 us -> 149 us
  blocking collectives: 28 us -> 0 us
  Pallas kernels: 58.3 us -> 73.8 us
  starting transfers between devices: 14.7 us -> 29.9 us
  waiting for transfers between devices: 9.08 us -> 19.6 us
  other arithmetic: 3.04 us -> 1.23 us
    all_to_all x1 -> x0, blocking collectives: 28 us -> none  [low_rank_shards(): lax.all_to_all(packed, 'wide', split_axis=0, concat_axis=0, tiled=True)]
    ppermute x12 -> x25, starting transfers between devices: 14.6 us -> 29.8 us  [swap(): lax.ppermute(rows, axis, [(i, i ^ k) for i in range(lax.axis_size(axis))])]
    pallas_call x3 -> x6, Pallas kernels: 14.4 us -> 26.1 us  [the longest x3 22.2 us: back(): pl.pallas_call(lambda *refs: back_body(count, len(before), *refs), grid_s...]
    ppermute x12 -> x25, waiting for transfers between devices: 9.06 us -> 19.6 us  [swap(): lax.ppermute(rows, axis, [(i, i ^ k) for i in range(lax.axis_size(axis))])]
    pallas_call x4, Pallas kernels: 18.7 us -> 23.2 us  [project(): pl.pallas_call(project_body if resid is None else project_own_body, grid_...]
    unnamed x31 -> x34, local copies, waits for them, and re-layouts: 5.33 us -> 9.15 us
  transfers between devices with their start and end apart: 13 -> 26, of which waited for: 4 -> 6; matrix products, arithmetic and copies ran while one was open for 5% -> 1% of each run, Pallas kernels for 36% -> 43%
where the time goes in v3:
time: 151 us; the launch traced here: 149 us
  Pallas kernels  73.8 us (49%)
  starting transfers between devices  29.9 us (20%)
  waiting for transfers between devices  19.6 us (13%)
  between operations  14.3 us (9%)
  local copies, waits for them, and re-layouts  9.85 us (7%)
    ppermute x25, starting transfers between devices, swap(): lax.ppermute(rows, axis, [(i, i ^ k) for i in range(lax.axis_size(axis))])  29.8 us
    pallas_call x4, Pallas kernels, project(): pl.pallas_call(project_body if resid is None else project_own_body, grid_...  23.2 us
    pallas_call x3, Pallas kernels, back(): pl.pallas_call(lambda *refs: back_body(count, len(before), *refs), grid_s...  22.2 us
    ppermute x25, waiting for transfers between devices, swap(): lax.ppermute(rows, axis, [(i, i ^ k) for i in range(lax.axis_size(axis))])  19.6 us
    pallas_call x1, Pallas kernels, low_activations(): pl.pallas_call(low_act_body, grid=(depth // tile,), in_specs=[pl.BlockSpe...  15.3 us
    unnamed x34, local copies, waits for them, and re-layouts  9.15 us
    pallas_call x1, Pallas kernels, finish(): pl.pallas_call(lambda *refs: finish_body(features, count, *refs), grid_sp...  8.7 us
  transfers between devices with their start and end apart: 26, of which 6 were waited for; matrix products, arithmetic and copies ran while one was open for 1% of the time, Pallas kernels for 43%

profile of v3, /device:TPU:0, one launch (start us, length us, event | category | flops | bytes accessed | tf_op | source)
XLA Modules:
  0.0 148.7 jit_solution(11894168643645034492)
XLA Ops:
  7.2 3.0 %collective-permute-start.6 = (f32[1,1024]{1,0:T(1,128)}, f32[1,1024]{1,0:T(1,128)S(1)}, u32[]{:S(2)}, u32[]{:S(2)}) collective-permute-start(f32[1,1024]{1,0:T(1,128)} %bitcast.22), channel_id=1, source_target_pairs={{0,1},{1,0},{2,3},{3,2},{4,5},{5,4},{6,7},{7,6},{8,9},{9,8},{10,11... | collective-permute-start | bytes 12296 | tf_op jit(solution)/shard_map/ppermute | solution.py:45
  10.2 1.5 %collective-permute-start.7 = (f32[1,1024]{1,0:T(1,128)}, f32[1,1024]{1,0:T(1,128)S(1)}, u32[]{:S(2)}, u32[]{:S(2)}) collective-permute-start(f32[1,1024]{1,0:T(1,128)} %bitcast.23), channel_id=1, source_target_pairs={{0,2},{1,3},{2,0},{3,1},{4,6},{5,7},{6,4},{7,5},{8,10},{9,11},{10,... | collective-permute-start | bytes 12296 | tf_op jit(solution)/shard_map/ppermute | solution.py:45
  11.8 1.9 %collective-permute-start = (bf16[4,4096]{1,0:T(4,128)(2,1)}, bf16[4,4096]{1,0:T(4,128)(2,1)S(1)}, u32[]{:S(2)}, u32[]{:S(2)}) collective-permute-start(bf16[4,4096]{1,0:T(4,128)(2,1)} %refs_1_), channel_id=1, source_target_pairs={{0,1},{1,0},{2,3},{3,2},{4,5},{5,4},{6,7},{7,6},{8,9},{9,8},{10,11... | collective-permute-start | bytes 98312 | tf_op jit(solution)/shard_map/ppermute | solution.py:45
  13.7 1.5 %collective-permute-start.1 = (bf16[4,4096]{1,0:T(4,128)(2,1)}, bf16[4,4096]{1,0:T(4,128)(2,1)S(1)}, u32[]{:S(2)}, u32[]{:S(2)}) collective-permute-start(bf16[4,4096]{1,0:T(4,128)(2,1)} %refs_1_), channel_id=1, source_target_pairs={{0,2},{1,3},{2,0},{3,1},{4,6},{5,7},{6,4},{7,5},{8,10},{9,11},{10,... | collective-permute-start | bytes 98312 | tf_op jit(solution)/shard_map/ppermute | solution.py:45
  15.2 0.7 convert_bitcast_fusion
  15.9 1.3 copy-done.2
  17.2 5.7 %shard_map.129 = bf16[192,1024]{1,0:T(8,128)(2,1)S(1)} custom-call(s32[1]{0:T(128)} %bitcast.1.group_ref, bf16[192,3072]{1,0:T(8,128)(2,1)S(1)} %copy-done.2, bf16[3072,4096]{1,0:T(8,128)(2,1)} %refs_4_.7), custom_call_target="tpu_custom_call" | custom-call | flops 1207959552 | bytes 7471104 | tf_op jit(solution)/shard_map/pallas_call | solution.py:90
  23.3 1.9 %collective-permute-start.3 = (bf16[4,4096]{1,0:T(4,128)(2,1)S(1)}, bf16[4,4096]{1,0:T(4,128)(2,1)S(1)}, u32[]{:S(2)}, u32[]{:S(2)}) collective-permute-start(bf16[4,4096]{1,0:T(4,128)(2,1)S(1)} %copy-done.12), channel_id=1, source_target_pairs={{0,1},{1,0},{2,3},{3,2},{4,5},{5,4},{6,7},{7,6},{8,9},{9,8},{10,11... | collective-permute-start | bytes 98312 | tf_op jit(solution)/shard_map/ppermute | solution.py:45
  25.2 1.5 %collective-permute-start.4 = (bf16[4,4096]{1,0:T(4,128)(2,1)S(1)}, bf16[4,4096]{1,0:T(4,128)(2,1)S(1)}, u32[]{:S(2)}, u32[]{:S(2)}) collective-permute-start(bf16[4,4096]{1,0:T(4,128)(2,1)S(1)} %copy-done.12), channel_id=1, source_target_pairs={{0,2},{1,3},{2,0},{3,1},{4,6},{5,7},{6,4},{7,5},{8,10},{9,11},{10,... | collective-permute-start | bytes 98312 | tf_op jit(solution)/shard_map/ppermute | solution.py:45
  27.1 1.2 collective-permute-done.2.refs_4_
  28.3 0.8 collective-permute-done.4.refs_7_
  29.1 2.4 %collective-permute-done.5.refs_8_ = bf16[4,4096]{1,0:T(4,128)(2,1)S(1)} collective-permute-done((bf16[4,4096]{1,0:T(4,128)(2,1)S(1)}, bf16[4,4096]{1,0:T(4,128)(2,1)S(1)}, u32[]{:S(2)}, u32[]{:S(2)}) %collective-permute-start.5) | collective-permute-done | bytes 32800 | tf_op jit(solution)/shard_map/ppermute | solution.py:45
  31.6 1.5 %shard_map.130 = (bf16[4,4096]{1,0:T(4,128)(2,1)}, bf16[16,4224]{1,0:T(8,128)(2,1)}) custom-call(s32[1]{0:T(128)} %bitcast.refs_0_.group_ref, bf16[4,4096]{1,0:T(4,128)(2,1)S(1)} %copy-done.11, bf16[4,4096]{1,0:T(4,128)(2,1)S(1)} %collective-permute-done.refs_2_, bf16[4,4096]{1,0:T(4,128)(2,1)S(1)} %collective-permute-done.1.refs_3_, ...), custom_call_target="tpu_custom_call" | custom-call | flops 8388608 | bytes 524288 | tf_op jit(solution)/shard_map/pallas_call | solution.py:148
  33.3 5.6 %shard_map.132 = bf16[192,1024]{1,0:T(8,128)(2,1)S(1)} custom-call(s32[1]{0:T(128)} %bitcast.12.group_ref, bf16[192,3072]{1,0:T(8,128)(2,1)S(1)} %copy-done.3, bf16[3072,4096]{1,0:T(8,128)(2,1)} %refs_4_.7), custom_call_target="tpu_custom_call" | custom-call | flops 1207959552 | bytes 7471104 | tf_op jit(solution)/shard_map/pallas_call | solution.py:90
  38.8 2.0 %collective-permute-start.10 = (bf16[192,1024]{1,0:T(8,128)(2,1)S(1)}, bf16[192,1024]{1,0:T(8,128)(2,1)S(1)}, u32[]{:S(2)}, u32[]{:S(2)}) collective-permute-start(bf16[192,1024]{1,0:T(8,128)(2,1)S(1)} %shard_map.132), channel_id=1, source_target_pairs={{0,1},{1,0},{2,3},{3,2},{4,5},{5,4},{6,7},{7,6},{8,9},{9,8},{10,11... | collective-permute-start | bytes 1179656 | tf_op jit(solution)/shard_map/ppermute | solution.py:45
  40.8 6.3 %shard_map.133 = bf16[192,1024]{1,0:T(8,128)(2,1)} custom-call(s32[1]{0:T(128)} %bitcast.13.group_ref, bf16[192,3072]{1,0:T(8,128)(2,1)S(1)} %copy-done.3, bf16[3072,4096]{1,0:T(8,128)(2,1)} %refs_4_.7), custom_call_target="tpu_custom_call" | custom-call | flops 1207959552 | bytes 7471104 | tf_op jit(solution)/shard_map/pallas_call | solution.py:90
  47.1 1.5 %collective-permute-start.11 = (bf16[192,1024]{1,0:T(8,128)(2,1)}, bf16[192,1024]{1,0:T(8,128)(2,1)S(1)}, u32[]{:S(2)}, u32[]{:S(2)}) collective-permute-start(bf16[192,1024]{1,0:T(8,128)(2,1)} %shard_map.133), channel_id=1, source_target_pairs={{0,2},{1,3},{2,0},{3,1},{4,6},{5,7},{6,4},{7,5},{8,10},{9,11},{10,... | collective-permute-start | bytes 1179656 | tf_op jit(solution)/shard_map/ppermute | solution.py:45
  48.7 5.6 %shard_map.131.refs_2_ = f32[192,1024]{1,0:T(8,128)S(1)} custom-call(s32[1]{0:T(128)} %bitcast.refs_0_.group_ref, bf16[192,3072]{1,0:T(8,128)(2,1)S(1)} %copy-done.3, bf16[3072,4096]{1,0:T(8,128)(2,1)} %refs_4_.7, bf16[192,1024]{1,0:T(8,128)(2,1)S(1)} %copy-done.6), custom_call_target="tpu_custom_call" | custom-call | flops 1207959552 | bytes 7471104 | tf_op jit(solution)/shard_map/pallas_call | solution.py:90
  54.3 0.8 collective-permute-done.11.refs_5_
  55.1 1.1 shard_map.134
  56.3 1.7 %collective-permute-start.13 = (bf16[36,1024]{1,0:T(8,128)(2,1)S(1)}, bf16[36,1024]{1,0:T(8,128)(2,1)S(1)}, u32[]{:S(2)}, u32[]{:S(2)}) collective-permute-start(bf16[36,1024]{1,0:T(8,128)(2,1)S(1)} %get-tuple-element.58), channel_id=1, source_target_pairs={{0,8},{4,12},{8,0},{12,4},{16,24},{20,28},{24,16},{28,20},{1,9},{5... | collective-permute-start | bytes 221192 | tf_op jit(solution)/shard_map/ppermute | solution.py:45
  57.9 0.2 collective-permute-start.14
  58.1 2.6 %collective-permute-start.15 = (bf16[36,1024]{1,0:T(8,128)(2,1)S(1)}, bf16[36,1024]{1,0:T(8,128)(2,1)S(1)}, u32[]{:S(2)}, u32[]{:S(2)}) collective-permute-start(bf16[36,1024]{1,0:T(8,128)(2,1)S(1)} %get-tuple-element.60), channel_id=1, source_target_pairs={{0,16},{4,20},{8,24},{12,28},{16,0},{20,4},{24,8},{28,12},{1,17},{... | collective-permute-start | bytes 221192 | tf_op jit(solution)/shard_map/ppermute | solution.py:45
  60.7 3.6 %collective-permute-start.17 = (bf16[36,1024]{1,0:T(8,128)(2,1)S(1)}, bf16[36,1024]{1,0:T(8,128)(2,1)S(1)}, u32[]{:S(2)}, u32[]{:S(2)}) collective-permute-start(bf16[36,1024]{1,0:T(8,128)(2,1)S(1)} %get-tuple-element.62), channel_id=1, source_target_pairs={{0,24},{4,28},{8,16},{12,20},{16,8},{20,12},{24,0},{28,4},{1,25},{... | collective-permute-start | bytes 221192 | tf_op jit(solution)/shard_map/ppermute | solution.py:45
  64.5 8.7 %collective-permute-done.16.refs_5_ = bf16[36,1024]{1,0:T(8,128)(2,1)S(1)} collective-permute-done((bf16[36,1024]{1,0:T(8,128)(2,1)S(1)}, bf16[36,1024]{1,0:T(8,128)(2,1)S(1)}, u32[]{:S(2)}, u32[]{:S(2)}) %collective-permute-start.16) | collective-permute-done | bytes 73760 | tf_op jit(solution)/shard_map/ppermute | solution.py:45
  73.2 1.3 shard_map.135
  74.6 0.8 collective-permute-start.19
  75.3 1.4 collective-permute-start.21
  77.0 1.4 collective-permute-start.23
  78.4 0.5 collective-permute-start.24
  78.9 5.6 %collective-permute-done.19.refs_1_ = bf16[288,512]{1,0:T(8,128)(2,1)S(1)} collective-permute-done((bf16[288,512]{1,0:T(8,128)(2,1)S(1)}, bf16[288,512]{1,0:T(8,128)(2,1)S(1)}, u32[]{:S(2)}, u32[]{:S(2)}) %collective-permute-start.19) | collective-permute-done | bytes 294944 | tf_op jit(solution)/shard_map/ppermute | solution.py:45
  84.5 1.5 %collective-permute-start.20 = (bf16[288,512]{1,0:T(8,128)(2,1)S(1)}, bf16[288,512]{1,0:T(8,128)(2,1)S(1)}, u32[]{:S(2)}, u32[]{:S(2)}) collective-permute-start(bf16[288,512]{1,0:T(8,128)(2,1)S(1)} %collective-permute-done.19.refs_1_), channel_id=1, source_target_pairs={{0,2},{1,3},{2,0},{3,1},{4,6},{5,7},{6,4},{7,5},{8,10},{9,11},{10,... | collective-permute-start | bytes 884744 | tf_op jit(solution)/shard_map/ppermute | solution.py:45
  86.0 0.6 collective-permute-start.22
  86.6 1.2 copy-done
  87.9 6.9 %shard_map.136 = (f32[288,3072]{1,0:T(8,128)S(1)}, f32[288,1]{1,0:T(8,128)S(1)}, f32[288,128]{1,0:T(8,128)S(1)}) custom-call(s32[2]{0:T(128)S(1)} %pad_add_fusion.3.refs_0_, bf16[288,512]{1,0:T(8,128)(2,1)S(1)} %get-tuple-element.64.refs_1_.refs_13_, bf16[288,512]{1,0:T(8,128)(2,1)S(1)} %get-tuple-element.65.refs_2_.refs_14_, bf16[3072,4096]{1,0:T(8,128)(2,1)} %refs_4_.7, ...), custom_call_target="tpu_custom_call" | custom-call | flops 1811939328 | bytes 6291456 | tf_op jit(solution)/shard_map/pallas_call | solution.py:362
  94.8 1.7 %copy-done.4 = f32[288,3072]{1,0:T(8,128)} copy-done((f32[288,3072]{1,0:T(8,128)}, f32[288,3072]{1,0:T(8,128)S(1)}, u32[]{:S(2)}) %copy-start.4) | copy-done | bytes 3538968
  96.5 0.7 copy-done.7
  97.2 0.7 copy-done.9
  97.9 0.2 slice_reduce_fusion
  98.2 0.5 shard_map.139.refs_10_
  98.7 0.2 fusion
  98.9 0.9 copy-done.8
  99.9 0.9 copy-done.10
  100.8 7.6 %shard_map.137 = (f32[288,3072]{1,0:T(8,128)S(1)}, f32[288,1]{1,0:T(8,128)S(1)}, f32[288,128]{1,0:T(8,128)S(1)}) custom-call(s32[2]{0:T(128)S(1)} %pad_add_fusion.2.refs_0_, bf16[288,512]{1,0:T(8,128)(2,1)S(1)} %collective-permute-done.19.refs_1_, bf16[288,512]{1,0:T(8,128)(2,1)S(1)} %collective-permute-done.21.refs_2_, bf16[3072,4096]{1,0:T(8,128)(2,1)} %refs_4_.7, ...), custom_call_target="tpu_custom_call" | custom-call | flops 1811939328 | bytes 6291456 | tf_op jit(solution)/shard_map/pallas_call | solution.py:362
  108.4 1.7 %copy-done.5 = f32[288,3072]{1,0:T(8,128)} copy-done((f32[288,3072]{1,0:T(8,128)}, f32[288,3072]{1,0:T(8,128)S(1)}, u32[]{:S(2)}) %copy-start.5) | copy-done | bytes 3538968
  110.1 7.6 %shard_map.138 = (f32[288,3072]{1,0:T(8,128)S(1)}, f32[288,1]{1,0:T(8,128)S(1)}, f32[288,128]{1,0:T(8,128)S(1)}) custom-call(s32[2]{0:T(128)S(1)} %pad_add_fusion.1.refs_0_, bf16[288,512]{1,0:T(8,128)(2,1)S(1)} %collective-permute-done.23.refs_1_, bf16[288,512]{1,0:T(8,128)(2,1)S(1)} %collective-permute-done.24.refs_2_, bf16[3072,4096]{1,0:T(8,128)(2,1)} %refs_4_.7, ...), custom_call_target="tpu_custom_call" | custom-call | flops 1811939328 | bytes 6291456 | tf_op jit(solution)/shard_map/pallas_call | solution.py:362
  117.8 15.3 %shard_map.140.refs_12_ = bf16[3072,128]{1,0:T(8,128)(2,1)S(1)} custom-call(bf16[128,4224]{1,0:T(8,128)(2,1)S(1)} %copy-done.1, bf16[3072,4096]{1,0:T(8,128)(2,1)} %refs_4_.7), custom_call_target="tpu_custom_call" | custom-call | flops 3221225472 | bytes 25165824 | tf_op jit(solution)/shard_map/pallas_call | solution.py:290
  133.1 8.7 %shard_map.141 = (bf16[288,3072]{1,0:T(8,128)(2,1)}, bf16[288,1024]{1,0:T(8,128)(2,1)}, bf16[288,1024]{1,0:T(8,128)(2,1)}) custom-call(s32[3]{0:T(128)S(1)} %pad_add_fusion.refs_0_, bf16[288,512]{1,0:T(8,128)(2,1)S(1)} %collective-permute-done.20.refs_1_, bf16[288,512]{1,0:T(8,128)(2,1)S(1)} %collective-permute-done.22.refs_2_, bf16[3072,4096]{1,0:T(8,128)(2,1)} %refs_4_.7, ...), custom_call_target="tpu_custom_call" | custom-call | flops 1811939328 | bytes 11599872 | tf_op jit(solution)/shard_map/pallas_call | solution.py:417
  (69 shorter events, 1.7 us)
Async XLA Ops:
  7.2 79.5 %all-gather.2.cloned.1.call-start = ((), (), s32[]{:S(2)}) async-start(), calls=%async_computation | async-start | bytes 1216512 | tf_op jit(solution)/shard_map/all_gather | solution.py:495
  7.2 15.9 %collective-permute-start.6 = (f32[1,1024]{1,0:T(1,128)}, f32[1,1024]{1,0:T(1,128)S(1)}, u32[]{:S(2)}, u32[]{:S(2)}) collective-permute-start(f32[1,1024]{1,0:T(1,128)} %bitcast.22), channel_id=1, source_target_pairs={{0,1},{1,0},{2,3},{3,2},{4,5},{5,4},{6,7},{7,6},{8,9},{9,8},{10,11... | collective-permute-start | bytes 12296 | tf_op jit(solution)/shard_map/ppermute | solution.py:45
  10.2 13.0 %collective-permute-start.7 = (f32[1,1024]{1,0:T(1,128)}, f32[1,1024]{1,0:T(1,128)S(1)}, u32[]{:S(2)}, u32[]{:S(2)}) collective-permute-start(f32[1,1024]{1,0:T(1,128)} %bitcast.23), channel_id=1, source_target_pairs={{0,2},{1,3},{2,0},{3,1},{4,6},{5,7},{6,4},{7,5},{8,10},{9,11},{10,... | collective-permute-start | bytes 12296 | tf_op jit(solution)/shard_map/ppermute | solution.py:45
  11.7 13.5 %collective-permute-start.8 = (f32[1,1024]{1,0:T(1,128)}, f32[1,1024]{1,0:T(1,128)S(1)}, u32[]{:S(2)}, u32[]{:S(2)}) collective-permute-start(f32[1,1024]{1,0:T(1,128)} %bitcast.24), channel_id=1, source_target_pairs={{0,3},{1,2},{2,1},{3,0},{4,7},{5,6},{6,5},{7,4},{8,11},{9,10},{10,... | collective-permute-start | bytes 12296 | tf_op jit(solution)/shard_map/ppermute | solution.py:45
  11.8 15.0 %collective-permute-start = (bf16[4,4096]{1,0:T(4,128)(2,1)}, bf16[4,4096]{1,0:T(4,128)(2,1)S(1)}, u32[]{:S(2)}, u32[]{:S(2)}) collective-permute-start(bf16[4,4096]{1,0:T(4,128)(2,1)} %refs_1_), channel_id=1, source_target_pairs={{0,1},{1,0},{2,3},{3,2},{4,5},{5,4},{6,7},{7,6},{8,9},{9,8},{10,11... | collective-permute-start | bytes 98312 | tf_op jit(solution)/shard_map/ppermute | solution.py:45
  13.7 13.4 %collective-permute-start.1 = (bf16[4,4096]{1,0:T(4,128)(2,1)}, bf16[4,4096]{1,0:T(4,128)(2,1)S(1)}, u32[]{:S(2)}, u32[]{:S(2)}) collective-permute-start(bf16[4,4096]{1,0:T(4,128)(2,1)} %refs_1_), channel_id=1, source_target_pairs={{0,2},{1,3},{2,0},{3,1},{4,6},{5,7},{6,4},{7,5},{8,10},{9,11},{10,... | collective-permute-start | bytes 98312 | tf_op jit(solution)/shard_map/ppermute | solution.py:45
  15.9 1.3 copy-start.2
  17.2 5.8 %copy-start.16 = (s32[192,1]{0,1:T(1,128)S(1)}, s32[192,1]{0,1:T(1,128)}, u32[]{:S(2)}) copy-start(s32[192,1]{0,1:T(1,128)} %param.15) | copy-start | bytes 2308
  17.2 6.0 %copy-start.11 = (bf16[4,4096]{1,0:T(4,128)(2,1)S(1)}, bf16[4,4096]{1,0:T(4,128)(2,1)}, u32[]{:S(2)}) copy-start(bf16[4,4096]{1,0:T(4,128)(2,1)} %refs_1_) | copy-start | bytes 98308
  17.2 6.1 %copy-start.12 = (bf16[4,4096]{1,0:T(4,128)(2,1)S(1)}, bf16[4,4096]{1,0:T(4,128)(2,1)}, u32[]{:S(2)}) copy-start(bf16[4,4096]{1,0:T(4,128)(2,1)} %refs_5_) | copy-start | bytes 98308
  17.2 9.7 %copy-start.14 = (f32[16]{0:T(128)S(1)}, f32[16]{0:T(128)}, u32[]{:S(2)}) copy-start(f32[16]{0:T(128)} %param.12) | copy-start | bytes 196
  17.2 9.8 %copy-start.15 = (s32[16]{0:T(128)S(1)}, s32[16]{0:T(128)}, u32[]{:S(2)}) copy-start(s32[16]{0:T(128)} %param.13) | copy-start | bytes 196
  17.2 14.4 %copy-start.13 = (f32[1024]{0:T(1024)S(1)}, f32[1024]{0:T(1024)}, u32[]{:S(2)}) copy-start(f32[1024]{0:T(1024)} %param.19) | copy-start | bytes 12292
  17.2 16.1 %copy-start.3 = (bf16[192,3072]{1,0:T(8,128)(2,1)S(1)}, bf16[192,3072]{1,0:T(8,128)(2,1)}, u32[]{:S(2)}) copy-start(bf16[192,3072]{1,0:T(8,128)(2,1)} %act_ref.4) | copy-start | bytes 3538948
  23.2 5.1 %collective-permute-start.2 = (bf16[4,4096]{1,0:T(4,128)(2,1)S(1)}, bf16[4,4096]{1,0:T(4,128)(2,1)S(1)}, u32[]{:S(2)}, u32[]{:S(2)}) collective-permute-start(bf16[4,4096]{1,0:T(4,128)(2,1)S(1)} %copy-done.11), channel_id=1, source_target_pairs={{0,3},{1,2},{2,1},{3,0},{4,7},{5,6},{6,5},{7,4},{8,11},{9,10},{10,... | collective-permute-start | bytes 98312 | tf_op jit(solution)/shard_map/ppermute | solution.py:45
  23.3 5.0 %collective-permute-start.3 = (bf16[4,4096]{1,0:T(4,128)(2,1)S(1)}, bf16[4,4096]{1,0:T(4,128)(2,1)S(1)}, u32[]{:S(2)}, u32[]{:S(2)}) collective-permute-start(bf16[4,4096]{1,0:T(4,128)(2,1)S(1)} %copy-done.12), channel_id=1, source_target_pairs={{0,1},{1,0},{2,3},{3,2},{4,5},{5,4},{6,7},{7,6},{8,9},{9,8},{10,11... | collective-permute-start | bytes 98312 | tf_op jit(solution)/shard_map/ppermute | solution.py:45
  25.2 3.9 %collective-permute-start.4 = (bf16[4,4096]{1,0:T(4,128)(2,1)S(1)}, bf16[4,4096]{1,0:T(4,128)(2,1)S(1)}, u32[]{:S(2)}, u32[]{:S(2)}) collective-permute-start(bf16[4,4096]{1,0:T(4,128)(2,1)S(1)} %copy-done.12), channel_id=1, source_target_pairs={{0,2},{1,3},{2,0},{3,1},{4,6},{5,7},{6,4},{7,5},{8,10},{9,11},{10,... | collective-permute-start | bytes 98312 | tf_op jit(solution)/shard_map/ppermute | solution.py:45
  26.7 4.8 %collective-permute-start.5 = (bf16[4,4096]{1,0:T(4,128)(2,1)S(1)}, bf16[4,4096]{1,0:T(4,128)(2,1)S(1)}, u32[]{:S(2)}, u32[]{:S(2)}) collective-permute-start(bf16[4,4096]{1,0:T(4,128)(2,1)S(1)} %copy-done.12), channel_id=1, source_target_pairs={{0,3},{1,2},{2,1},{3,0},{4,7},{5,6},{6,5},{7,4},{8,11},{9,10},{10,... | collective-permute-start | bytes 98312 | tf_op jit(solution)/shard_map/ppermute | solution.py:45
  33.1 21.2 %collective-permute-start.9 = (bf16[192,1024]{1,0:T(8,128)(2,1)S(1)}, bf16[192,1024]{1,0:T(8,128)(2,1)S(1)}, u32[]{:S(2)}, u32[]{:S(2)}) collective-permute-start(bf16[192,1024]{1,0:T(8,128)(2,1)S(1)} %shard_map.129), channel_id=1, source_target_pairs={{0,3},{1,2},{2,1},{3,0},{4,7},{5,6},{6,5},{7,4},{8,11},{9,10},{10,... | collective-permute-start | bytes 1179656 | tf_op jit(solution)/shard_map/ppermute | solution.py:45
  38.8 15.5 %collective-permute-start.10 = (bf16[192,1024]{1,0:T(8,128)(2,1)S(1)}, bf16[192,1024]{1,0:T(8,128)(2,1)S(1)}, u32[]{:S(2)}, u32[]{:S(2)}) collective-permute-start(bf16[192,1024]{1,0:T(8,128)(2,1)S(1)} %shard_map.132), channel_id=1, source_target_pairs={{0,1},{1,0},{2,3},{3,2},{4,5},{5,4},{6,7},{7,6},{8,9},{9,8},{10,11... | collective-permute-start | bytes 1179656 | tf_op jit(solution)/shard_map/ppermute | solution.py:45
  40.8 7.9 %copy-start.6 = (bf16[192,1024]{1,0:T(8,128)(2,1)S(1)}, bf16[192,1024]{1,0:T(8,128)(2,1)}, u32[]{:S(2)}) copy-start(bf16[192,1024]{1,0:T(8,128)(2,1)} %resid_ref.1) | copy-start | bytes 1179652
  47.1 8.0 %collective-permute-start.11 = (bf16[192,1024]{1,0:T(8,128)(2,1)}, bf16[192,1024]{1,0:T(8,128)(2,1)S(1)}, u32[]{:S(2)}, u32[]{:S(2)}) collective-permute-start(bf16[192,1024]{1,0:T(8,128)(2,1)} %shard_map.133), channel_id=1, source_target_pairs={{0,2},{1,3},{2,0},{3,1},{4,6},{5,7},{6,4},{7,5},{8,10},{9,11},{10,... | collective-permute-start | bytes 1179656 | tf_op jit(solution)/shard_map/ppermute | solution.py:45
  56.2 4.6 %collective-permute-start.12 = (bf16[36,1024]{1,0:T(8,128)(2,1)S(1)}, bf16[36,1024]{1,0:T(8,128)(2,1)S(1)}, u32[]{:S(2)}, u32[]{:S(2)}) collective-permute-start(bf16[36,1024]{1,0:T(8,128)(2,1)S(1)} %get-tuple-element.57), channel_id=1, source_target_pairs={{0,4},{4,0},{8,12},{12,8},{16,20},{20,16},{24,28},{28,24},{1,5},{5... | collective-permute-start | bytes 221192 | tf_op jit(solution)/shard_map/ppermute | solution.py:45
  56.3 8.1 %collective-permute-start.13 = (bf16[36,1024]{1,0:T(8,128)(2,1)S(1)}, bf16[36,1024]{1,0:T(8,128)(2,1)S(1)}, u32[]{:S(2)}, u32[]{:S(2)}) collective-permute-start(bf16[36,1024]{1,0:T(8,128)(2,1)S(1)} %get-tuple-element.58), channel_id=1, source_target_pairs={{0,8},{4,12},{8,0},{12,4},{16,24},{20,28},{24,16},{28,20},{1,9},{5... | collective-permute-start | bytes 221192 | tf_op jit(solution)/shard_map/ppermute | solution.py:45
  57.9 6.6 %collective-permute-start.14 = (bf16[36,1024]{1,0:T(8,128)(2,1)S(1)}, bf16[36,1024]{1,0:T(8,128)(2,1)S(1)}, u32[]{:S(2)}, u32[]{:S(2)}) collective-permute-start(bf16[36,1024]{1,0:T(8,128)(2,1)S(1)} %get-tuple-element.59), channel_id=1, source_target_pairs={{0,12},{4,8},{8,4},{12,0},{16,28},{20,24},{24,20},{28,16},{1,13},{... | collective-permute-start | bytes 221192 | tf_op jit(solution)/shard_map/ppermute | solution.py:45
  58.1 6.4 %collective-permute-start.15 = (bf16[36,1024]{1,0:T(8,128)(2,1)S(1)}, bf16[36,1024]{1,0:T(8,128)(2,1)S(1)}, u32[]{:S(2)}, u32[]{:S(2)}) collective-permute-start(bf16[36,1024]{1,0:T(8,128)(2,1)S(1)} %get-tuple-element.60), channel_id=1, source_target_pairs={{0,16},{4,20},{8,24},{12,28},{16,0},{20,4},{24,8},{28,12},{1,17},{... | collective-permute-start | bytes 221192 | tf_op jit(solution)/shard_map/ppermute | solution.py:45
  60.7 12.5 %collective-permute-start.16 = (bf16[36,1024]{1,0:T(8,128)(2,1)S(1)}, bf16[36,1024]{1,0:T(8,128)(2,1)S(1)}, u32[]{:S(2)}, u32[]{:S(2)}) collective-permute-start(bf16[36,1024]{1,0:T(8,128)(2,1)S(1)} %get-tuple-element.61), channel_id=1, source_target_pairs={{0,20},{4,16},{8,28},{12,24},{16,4},{20,0},{24,12},{28,8},{1,21},{... | collective-permute-start | bytes 221192 | tf_op jit(solution)/shard_map/ppermute | solution.py:45
  60.7 12.5 %collective-permute-start.17 = (bf16[36,1024]{1,0:T(8,128)(2,1)S(1)}, bf16[36,1024]{1,0:T(8,128)(2,1)S(1)}, u32[]{:S(2)}, u32[]{:S(2)}) collective-permute-start(bf16[36,1024]{1,0:T(8,128)(2,1)S(1)} %get-tuple-element.62), channel_id=1, source_target_pairs={{0,24},{4,28},{8,16},{12,20},{16,8},{20,12},{24,0},{28,4},{1,25},{... | collective-permute-start | bytes 221192 | tf_op jit(solution)/shard_map/ppermute | solution.py:45
  64.3 8.9 %collective-permute-start.18 = (bf16[36,1024]{1,0:T(8,128)(2,1)S(1)}, bf16[36,1024]{1,0:T(8,128)(2,1)S(1)}, u32[]{:S(2)}, u32[]{:S(2)}) collective-permute-start(bf16[36,1024]{1,0:T(8,128)(2,1)S(1)} %get-tuple-element.63), channel_id=1, source_target_pairs={{0,28},{4,24},{8,20},{12,16},{16,12},{20,8},{24,4},{28,0},{1,29},{... | collective-permute-start | bytes 221192 | tf_op jit(solution)/shard_map/ppermute | solution.py:45
  74.6 9.9 %collective-permute-start.19 = (bf16[288,512]{1,0:T(8,128)(2,1)S(1)}, bf16[288,512]{1,0:T(8,128)(2,1)S(1)}, u32[]{:S(2)}, u32[]{:S(2)}) collective-permute-start(bf16[288,512]{1,0:T(8,128)(2,1)S(1)} %get-tuple-element.64.refs_1_.refs_13_), channel_id=1, source_target_pairs={{0,1},{1,0},{2,3},{3,2},{4,5},{5,4},{6,7},{7,6},{8,9},{9,8},{10,11... | collective-permute-start | bytes 884744 | tf_op jit(solution)/shard_map/ppermute | solution.py:45
  75.3 10.7 %collective-permute-start.21 = (bf16[288,512]{1,0:T(8,128)(2,1)S(1)}, bf16[288,512]{1,0:T(8,128)(2,1)S(1)}, u32[]{:S(2)}, u32[]{:S(2)}) collective-permute-start(bf16[288,512]{1,0:T(8,128)(2,1)S(1)} %get-tuple-element.65.refs_2_.refs_14_), channel_id=1, source_target_pairs={{0,2},{1,3},{2,0},{3,1},{4,6},{5,7},{6,4},{7,5},{8,10},{9,11},{10,... | collective-permute-start | bytes 884744 | tf_op jit(solution)/shard_map/ppermute | solution.py:45
  77.0 33.1 %collective-permute-start.23 = (bf16[288,512]{1,0:T(8,128)(2,1)S(1)}, bf16[288,512]{1,0:T(8,128)(2,1)S(1)}, u32[]{:S(2)}, u32[]{:S(2)}) collective-permute-start(bf16[288,512]{1,0:T(8,128)(2,1)S(1)} %get-tuple-element.65.refs_2_.refs_14_), channel_id=1, source_target_pairs={{0,1},{1,0},{2,3},{3,2},{4,5},{5,4},{6,7},{7,6},{8,9},{9,8},{10,11... | collective-permute-start | bytes 884744 | tf_op jit(solution)/shard_map/ppermute | solution.py:45
  78.4 31.7 %collective-permute-start.24 = (bf16[288,512]{1,0:T(8,128)(2,1)S(1)}, bf16[288,512]{1,0:T(8,128)(2,1)S(1)}, u32[]{:S(2)}, u32[]{:S(2)}) collective-permute-start(bf16[288,512]{1,0:T(8,128)(2,1)S(1)} %get-tuple-element.64.refs_1_.refs_13_), channel_id=1, source_target_pairs={{0,2},{1,3},{2,0},{3,1},{4,6},{5,7},{6,4},{7,5},{8,10},{9,11},{10,... | collective-permute-start | bytes 884744 | tf_op jit(solution)/shard_map/ppermute | solution.py:45
  84.5 48.6 %collective-permute-start.20 = (bf16[288,512]{1,0:T(8,128)(2,1)S(1)}, bf16[288,512]{1,0:T(8,128)(2,1)S(1)}, u32[]{:S(2)}, u32[]{:S(2)}) collective-permute-start(bf16[288,512]{1,0:T(8,128)(2,1)S(1)} %collective-permute-done.19.refs_1_), channel_id=1, source_target_pairs={{0,2},{1,3},{2,0},{3,1},{4,6},{5,7},{6,4},{7,5},{8,10},{9,11},{10,... | collective-permute-start | bytes 884744 | tf_op jit(solution)/shard_map/ppermute | solution.py:45
  86.0 47.1 %collective-permute-start.22 = (bf16[288,512]{1,0:T(8,128)(2,1)S(1)}, bf16[288,512]{1,0:T(8,128)(2,1)S(1)}, u32[]{:S(2)}, u32[]{:S(2)}) collective-permute-start(bf16[288,512]{1,0:T(8,128)(2,1)S(1)} %collective-permute-done.21.refs_2_), channel_id=1, source_target_pairs={{0,1},{1,0},{2,3},{3,2},{4,5},{5,4},{6,7},{7,6},{8,9},{9,8},{10,11... | collective-permute-start | bytes 884744 | tf_op jit(solution)/shard_map/ppermute | solution.py:45
  86.6 1.2 copy-start
  87.9 10.2 %slice-start = ((bf16[128,4224]{1,0:T(8,128)(2,1)}), bf16[128,12]{1,0:T(8,128)(2,1)S(1)}, s32[]{:S(2)}) async-start(bf16[128,4224]{1,0:T(8,128)(2,1)} %all-gather.2.cloned.1.call-done.refs_5_.refs_6_.low_ref.refs_15_), calls=%async_computation.1 | async-start | bytes 65536 | tf_op jit(solution)/shard_map/slice | solution.py:498
  87.9 10.9 %copy-start.1 = (bf16[128,4224]{1,0:T(8,128)(2,1)S(1)}, bf16[128,4224]{1,0:T(8,128)(2,1)}, u32[]{:S(2)}) copy-start(bf16[128,4224]{1,0:T(8,128)(2,1)} %all-gather.2.cloned.1.call-done.refs_5_.refs_6_.low_ref.refs_15_) | copy-start | bytes 3244036
  94.8 1.7 %copy-start.4 = (f32[288,3072]{1,0:T(8,128)}, f32[288,3072]{1,0:T(8,128)S(1)}, u32[]{:S(2)}) copy-start(f32[288,3072]{1,0:T(8,128)S(1)} %get-tuple-element.66.refs_7_) | copy-start | bytes 10616836
  96.5 0.7 copy-start.7
  97.2 0.7 copy-start.9
  98.9 0.9 copy-start.8
  99.8 0.9 copy-start.10
  108.4 1.7 %copy-start.5 = (f32[288,3072]{1,0:T(8,128)}, f32[288,3072]{1,0:T(8,128)S(1)}, u32[]{:S(2)}) copy-start(f32[288,3072]{1,0:T(8,128)S(1)} %get-tuple-element.69.refs_7_) | copy-start | bytes 10616836
Sparse Core Ops, SparseCore 0:
  33.2 21.7 all-gather.1

commit v4 on v2

--- a/solution.py
+++ b/solution.py
@@ -41,49 +41,103 @@
     return lax.dot_general(left, right, (((1,), (1,)), ((), ())), preferred_element_type=f32)
 
 
-def swap(rows, k):
-    return lax.ppermute(rows, "blk", [(i, i ^ k) for i in range(lax.axis_size("blk"))])
-
-
-def project_body(group_ref, act_ref, w_ref, out_ref):
-    out_ref[...] = dot(act_ref[...], w_ref[...]).astype(bf16)
-
-
-def project_own_body(group_ref, act_ref, w_ref, resid_ref, out_ref):
-    out_ref[...] = dot(act_ref[...], w_ref[...]) + resid_ref[...].astype(f32)
+def swap(rows, k, axis="blk"):
+    return lax.ppermute(rows, axis, [(i, i ^ k) for i in range(lax.axis_size(axis))])
+
+
+def after(first, *later):
+    return lax.optimization_barrier((first, *later))
+
+
+def project_body(has_resid, group_ref, act_hbm, w_hbm, *refs):
+    out_ref, act, weights, act_sem, sems = refs[has_resid:]
+    width = out_ref.shape[1]
+    count, _, tile = weights.shape
+    first = group_ref[0] * width
+
+    def weight_copy(i):
+        columns = pl.ds(pl.multiple_of(first + i * tile, lane), tile)
+        return pltpu.make_async_copy(w_hbm.at[:, columns], weights.at[i], sems.at[i])
+
+    act_copy = pltpu.make_async_copy(act_hbm, act, act_sem)
+    act_copy.start()
+    for i in range(count):
+        weight_copy(i).start()
+    act_copy.wait()
+
+    @pl.loop(0, count)
+    def _(i):
+        weight_copy(i).wait()
+        columns = pl.ds(pl.multiple_of(i * tile, lane), tile)
+        term = dot(act[...], weights[i])
+        if has_resid:
+            term = term + refs[0][:, columns].astype(f32)
+        out_ref[:, columns] = term.astype(out_ref.dtype)
 
 
 def project(group, act, w_down, width, resid=None):
     rows, depth = act.shape
     tile = tile_of(width, 256)
-    per_group = width // tile
-    column_spec = pl.BlockSpec((rows, tile), lambda j, g: (0, j))
-    in_specs = [
-        pl.BlockSpec((rows, depth), lambda j, g: (0, 0)),
-        pl.BlockSpec((depth, tile), lambda j, g: (0, g[0] * per_group + j)),
-    ]
-    operands = [act, w_down]
-    if resid is not None:
-        in_specs.append(column_spec)
-        operands.append(resid)
+    count = width // tile
+    own = [] if resid is None else [resid]
     return pl.pallas_call(
-        project_body if resid is None else project_own_body,
-        grid_spec=pltpu.PrefetchScalarGridSpec(
-            num_scalar_prefetch=1, grid=(per_group,), in_specs=in_specs, out_specs=column_spec
-        ),
-        out_shape=jax.ShapeDtypeStruct((rows, width), bf16 if resid is None else f32),
+        lambda *refs: project_body(len(own), *refs),
+        in_specs=[pl.BlockSpec(memory_space=pltpu.SMEM)]
+        + [pl.BlockSpec(memory_space=pl.ANY)] * 2
+        + [pl.BlockSpec(memory_space=pltpu.VMEM)] * len(own),
+        out_specs=pl.BlockSpec(memory_space=pltpu.VMEM),
+        out_shape=jax.ShapeDtypeStruct((rows, width), f32 if own else bf16),
+        scratch_shapes=[
+            pltpu.VMEM((rows, depth), bf16),
+            pltpu.VMEM((count, depth, tile), bf16),
+            pltpu.SemaphoreType.DMA,
+            pltpu.SemaphoreType.DMA((count,)),
+        ],
         compiler_params=params(),
         cost_estimate=cost(2 * rows * depth * width, 2 * depth * width + 2 * rows * depth),
-    )(group, *operands)
-
-
-def group_body(blk_ref, parts_ref, lse_row_ref, lse_ref, pos_row_ref, pos_ref, table_ref, *rest):
-    query_grad_ref, low_ref, gain_ref = rest
+    )(group, act, w_down, *own)
+
+
+def payload_body(query_ref, passage_ref, gain_ref, out_ref):
+    features = query_ref.shape[1]
+    piece = gain_ref.shape[1]
+    gain = gain_ref[...]
+    high = gain.astype(bf16)
+    out_ref[:, :features] = query_ref[...]
+    out_ref[:, features : 2 * features] = passage_ref[...]
+    out_ref[:, 2 * features : 2 * features + piece] = high
+    out_ref[:, 2 * features + piece :] = (gain - high.astype(f32)).astype(bf16)
+
+
+def payload(query_emb, passage_emb, gain):
+    own, features = query_emb.shape
+    gain = gain.reshape(own, -1)
+    return pl.pallas_call(
+        payload_body,
+        out_shape=jax.ShapeDtypeStruct((own, 2 * features + 2 * gain.shape[1]), bf16),
+        compiler_params=params(),
+        cost_estimate=cost(own * features, 8 * own * features),
+    )(query_emb, passage_emb, gain)
+
+
+def group_body(count, blk_ref, *refs):
+    parts, refs = refs[:count], refs[count:]
+    lse_row_ref, lse_ref, pos_row_ref, pos_ref, table_ref = refs[:5]
+    query_grad_ref, low_ref, query_all, passage_all, gain_all = refs[5:]
     own, features = query_grad_ref.shape
-    pairs = parts_ref.shape[0]
+    pairs = own * count
+    piece = features // pairs
     blk = blk_ref[0]
-    queries = parts_ref[:, :features]
-    passages = parts_ref[:, features : 2 * features]
+    for k in range(count):
+        query_all[k * own : (k + 1) * own] = parts[k][:, :features].astype(f32)
+        passage_all[k * own : (k + 1) * own] = parts[k][:, features : 2 * features].astype(f32)
+        gains = parts[k][:, 2 * features : 2 * features + piece].astype(f32)
+        gains = gains + parts[k][:, 2 * features + piece :].astype(f32)
+        for row in range(own):
+            first = pl.multiple_of(((blk ^ k) * own + row) * piece, lane)
+            gain_all[:, pl.ds(first, piece)] = gains[row : row + 1]
+    queries = query_all[...].astype(bf16)
+    passages = passage_all[...].astype(bf16)
 
     def named(dim):
         place = iota((pairs, pairs), dim)
@@ -103,44 +157,34 @@
     turned = (jnp.exp(logit_scale * dot_t(passages, queries) - lse) - hit).astype(bf16)
     turned = dot(at_cols.astype(bf16), turned).astype(bf16)
     pass_grad = logit_scale * dot(turned, queries)
-    piece = (parts_ref.shape[1] - 2 * features) // 2
-    gains = (
-        parts_ref[:, 2 * features : 2 * features + piece].astype(f32)
-        + parts_ref[:, 2 * features + piece :].astype(f32)
-    )
-    for row in range(pairs):
-        first = ((blk ^ (row // own)) * own + row % own) * piece
-        gain_ref[:, pl.ds(pl.multiple_of(first, lane), piece)] = gains[row : row + 1]
-    low_ref[:, :features] = (gain_ref[...] * pass_grad).astype(bf16)
+    low_ref[:, :features] = (gain_all[...] * pass_grad).astype(bf16)
     low_ref[:, features:] = table_ref[...]
 
 
-def group_part(query_emb, passage_emb, row_lse, positive, token_lengths, destination, gain, blk):
-    own, features = query_emb.shape
+def group_part(parts, row_lse, positive, token_lengths, destination, features, blk):
+    own = parts[0].shape[0]
     pairs = row_lse.shape[0]
-    high = gain.astype(bf16)
-    rest = (gain - high.astype(f32)).astype(bf16)
-    both = jnp.concatenate(
-        [query_emb, passage_emb, high.reshape(own, -1), rest.reshape(own, -1)], axis=1
-    )
-    parts = jnp.concatenate([both] + [swap(both, k) for k in range(1, pairs // own)], axis=0)
     table = jnp.concatenate([destination.reshape(pairs, -1), token_lengths.reshape(pairs, 1)], 1)
     table = jnp.pad(table, ((0, 0), (0, lane - table.shape[1]))).astype(bf16)
     return pl.pallas_call(
-        group_body,
+        lambda *refs: group_body(pairs // own, *refs),
         in_specs=[pl.BlockSpec(memory_space=pltpu.SMEM)]
-        + [pl.BlockSpec(memory_space=pltpu.VMEM)] * 6,
+        + [pl.BlockSpec(memory_space=pltpu.VMEM)] * (len(parts) + 5),
         out_specs=[pl.BlockSpec(memory_space=pltpu.VMEM)] * 2,
         out_shape=[
             jax.ShapeDtypeStruct((own, features), bf16),
             jax.ShapeDtypeStruct((pairs, features + lane), bf16),
         ],
-        scratch_shapes=[pltpu.VMEM((1, features), f32)],
+        scratch_shapes=[
+            pltpu.VMEM((pairs, features), f32),
+            pltpu.VMEM((pairs, features), f32),
+            pltpu.VMEM((1, features), f32),
+        ],
         compiler_params=params(),
         cost_estimate=cost(8 * pairs * pairs * features, 8 * pairs * features),
     )(
         blk[None],
-        parts,
+        *parts,
         row_lse[None],
         row_lse[:, None],
         positive[None],
@@ -153,11 +197,10 @@
     return (iota((tokens, tokens), 0) < iota((tokens, tokens), 1)).astype(bf16)
 
 
-def pack_body(dest_ref, own_ref, *rest):
+def pack_body(groups, dest_ref, own_ref, *rest):
     terms, out_ref = rest[:-1], rest[-1]
-    groups, slots, _ = out_ref.shape
+    rows = out_ref.shape[0]
     tokens = dest_ref.shape[1]
-    stride = -(-slots // 16) * 16
     hidden = own_ref[...]
     for term in terms:
         hidden = hidden + term[...].astype(f32)
@@ -165,24 +208,23 @@
     hit = (dest == iota((groups, tokens), 0)).astype(f32)
     rank = dot(hit.astype(bf16), earlier_of(tokens))
     rank = jnp.sum(rank * hit, axis=0, keepdims=True).astype(i32)
-    place = (iota((groups * stride, tokens), 0) == dest * stride + rank).astype(bf16)
-    packed = dot(place, hidden.astype(bf16)).astype(bf16)
-    for group in range(groups):
-        out_ref[group] = packed[group * stride : group * stride + slots]
+    place = iota((rows, tokens), 0) == dest * (rows // groups) + rank
+    out_ref[...] = dot(place.astype(f32).astype(bf16), hidden.astype(bf16)).astype(bf16)
 
 
 def pack(destination, own, terms, groups, slots):
     tokens, width = own.shape
     tile = tile_of(width, 512)
+    rows = groups * slots
     column_spec = pl.BlockSpec((tokens, tile), lambda j: (0, j))
     return pl.pallas_call(
-        pack_body,
+        lambda *refs: pack_body(groups, *refs),
         grid=(width // tile,),
         in_specs=[pl.BlockSpec((1, tokens), lambda j: (0, 0))] + [column_spec] * (1 + len(terms)),
-        out_specs=pl.BlockSpec((groups, slots, tile), lambda j: (0, 0, j)),
-        out_shape=jax.ShapeDtypeStruct((groups, slots, width), bf16),
+        out_specs=pl.BlockSpec((rows, tile), lambda j: (0, j)),
+        out_shape=jax.ShapeDtypeStruct((rows, width), bf16),
         compiler_params=params(),
-        cost_estimate=cost(4 * groups * slots * tokens * width, 10 * tokens * width),
+        cost_estimate=cost(2 * rows * tokens * width, 10 * tokens * width),
     )(destination.reshape(1, tokens), own, *terms)
 
 
@@ -224,23 +266,41 @@
     )(wide[None], dest_all, len_all)
 
 
-def low_act_body(low_ref, w_ref, out_ref):
-    out_ref[...] = dot_t(low_ref[...], w_ref[...]).astype(bf16)
-
-
-def low_activations(low, w_down):
+def low_act_body(low_ref, w_hbm, out_ref, weights, sems):
+    count, tile, _ = weights.shape
+
+    def weight_copy(t):
+        rows = pl.ds(pl.multiple_of(t * tile, tile), tile)
+        return pltpu.make_async_copy(w_hbm.at[rows], weights.at[t], sems.at[t])
+
+    for t in range(count):
+        weight_copy(t).start()
+
+    @pl.loop(0, count)
+    def _(t):
+        weight_copy(t).wait()
+        rows = pl.ds(pl.multiple_of(t * tile, tile), tile)
+        out_ref[rows] = dot_t(weights[t], low_ref[...]).astype(bf16)
+
+
+def low_activations(low, features, w_down):
     pairs = low.shape[0]
-    depth, features = w_down.shape
-    tile = tile_of(depth, 256)
+    depth = w_down.shape[0]
+    tile = tile_of(depth, 512)
+    count = depth // tile
     return pl.pallas_call(
         low_act_body,
-        grid=(depth // tile,),
+        grid=(1,),
         in_specs=[
             pl.BlockSpec((pairs, features), lambda j: (0, 0)),
-            pl.BlockSpec((tile, features), lambda j: (j, 0)),
+            pl.BlockSpec(memory_space=pl.ANY),
         ],
-        out_specs=pl.BlockSpec((pairs, tile), lambda j: (0, j)),
-        out_shape=jax.ShapeDtypeStruct((pairs, depth), bf16),
+        out_specs=pl.BlockSpec((depth, pairs), lambda j: (0, 0)),
+        out_shape=jax.ShapeDtypeStruct((depth, pairs), bf16),
+        scratch_shapes=[
+            pltpu.VMEM((count, tile, features), bf16),
+            pltpu.SemaphoreType.DMA((count,)),
+        ],
         compiler_params=params(),
         cost_estimate=cost(2 * pairs * depth * features, 2 * depth * features),
     )(low, w_down)
@@ -255,93 +315,167 @@
     return squares, cross
 
 
-def product(hids, weights):
-    total = 0.0
-    for hid_ref, w_ref in zip(hids, weights):
-        total = total + dot_t(hid_ref[...], w_ref[...])
-    return total
-
-
-def piece_specs(pieces, low, tile):
-    hid_specs, w_specs, low_specs = [], [], []
-    for n, piece in enumerate(pieces):
-        hid_specs.append(pl.BlockSpec(piece.shape, lambda j, g: (0, 0)))
-        w_specs.append(pl.BlockSpec((tile, piece.shape[1]), lambda j, g, n=n: (j, g[n])))
-        low_specs.append(
-            pl.BlockSpec((low.shape[0], piece.shape[1]), lambda j, g, n=n: (0, g[n]))
-        )
-    return hid_specs + w_specs + low_specs
-
-
-def back_body(count, *refs):
-    hids, weights, lows = refs[1 : 1 + count], refs[1 + count : 1 + 2 * count], refs[1 + 2 * count :]
-    lows, (acc_ref, squares_ref, cross_ref) = lows[:count], lows[count:]
-
-    @pl.when(pl.program_id(0) == 0)
-    def _():
-        squares_ref[...], cross_ref[...] = statistics(hids, lows)
-
-    acc_ref[...] = product(hids, weights)
-
-
-def back(places, pieces, w_down, low):
+def weight_copies(places_ref, w_hbm, weights, sems):
+    count, tile, across = weights.shape
+    pieces = sems.shape[1]
+    width = across // pieces
+
+    def copies(t):
+        rows = pl.ds(pl.multiple_of(t * tile, tile), tile)
+        return [
+            pltpu.make_async_copy(
+                w_hbm.at[rows, pl.ds(pl.multiple_of(places_ref[n] * width, lane), width)],
+                weights.at[t, :, n * width : (n + 1) * width],
+                sems.at[t, n],
+            )
+            for n in range(pieces)
+        ]
+
+    return copies
+
+
+def back_body(count, carried, places_ref, *refs):
+    hids, lows, w_hbm, refs = refs[:count], refs[count : 2 * count], refs[2 * count], refs[2 * count + 1 :]
+    before, refs = refs[:carried], refs[carried:]
+    acc_hbm, squares_ref, cross_ref, hid, weights, acc, sems, in_sems, out_sems = refs
+    copies = weight_copies(places_ref, w_hbm, weights, sems)
+
+    def acc_in(t):
+        return pltpu.make_async_copy(before[0].at[t], acc.at[t], in_sems.at[t])
+
+    def acc_out(t):
+        return pltpu.make_async_copy(acc.at[t], acc_hbm.at[t], out_sems.at[t])
+
+    for t in range(weights.shape[0]):
+        for copy in copies(t):
+            copy.start()
+        if carried:
+            acc_in(t).start()
+    squares, cross = statistics(hids, lows)
+    if carried:
+        squares, cross = before[1][...] + squares, before[2][...] + cross
+    squares_ref[...], cross_ref[...] = squares, cross
+    width = hids[0].shape[1]
+    for n in range(count):
+        hid[:, n * width : (n + 1) * width] = hids[n][...]
+
+    @pl.loop(0, weights.shape[0])
+    def _(t):
+        for copy in copies(t):
+            copy.wait()
+        total = dot_t(hid[...], weights[t])
+        if carried:
+            acc_in(t).wait()
+            total = total + acc[t]
+        acc[t] = total
+        acc_out(t).start()
+
+    @pl.loop(0, weights.shape[0])
+    def _(t):
+        acc_out(t).wait()
+
+
+def back(places, pieces, w_down, low, before=()):
     count = len(pieces)
     rows, width = pieces[0].shape
     depth = w_down.shape[0]
     pairs = low.shape[0]
     tile = tile_of(depth, 512)
+    tiles = depth // tile
+    small = [
+        pl.BlockSpec((rows, 1), lambda j, g: (0, 0)),
+        pl.BlockSpec((rows, pairs), lambda j, g: (0, 0)),
+    ]
+    anywhere = pl.BlockSpec(memory_space=pl.ANY)
     return pl.pallas_call(
-        lambda *refs: back_body(count, *refs),
+        lambda *refs: back_body(count, len(before), *refs),
         grid_spec=pltpu.PrefetchScalarGridSpec(
             num_scalar_prefetch=1,
-            grid=(depth // tile,),
-            in_specs=piece_specs(pieces, low, tile),
-            out_specs=[
-                pl.BlockSpec((rows, tile), lambda j, g: (0, j)),
-                pl.BlockSpec((rows, 1), lambda j, g: (0, 0)),
-                pl.BlockSpec((rows, pairs), lambda j, g: (0, 0)),
+            grid=(1,),
+            in_specs=[pl.BlockSpec((rows, width), lambda j, g: (0, 0))] * count
+            + [pl.BlockSpec((pairs, width), lambda j, g, n=n: (0, g[n])) for n in range(count)]
+            + [anywhere]
+            + [anywhere, *small][: len(before)],
+            out_specs=[anywhere, *small],
+            scratch_shapes=[
+                pltpu.VMEM((rows, count * width), bf16),
+                pltpu.VMEM((tiles, tile, count * width), bf16),
+                pltpu.VMEM((tiles, rows, tile), f32),
+                pltpu.SemaphoreType.DMA((tiles, count)),
+                pltpu.SemaphoreType.DMA((tiles,)),
+                pltpu.SemaphoreType.DMA((tiles,)),
             ],
         ),
         out_shape=[
-            jax.ShapeDtypeStruct((rows, depth), f32),
+            jax.ShapeDtypeStruct((tiles, rows, tile), f32),
             jax.ShapeDtypeStruct((rows, 1), f32),
             jax.ShapeDtypeStruct((rows, pairs), f32),
         ],
         compiler_params=params(),
         cost_estimate=cost(2 * rows * depth * width * count, 2 * depth * width * count),
-    )(places, *pieces, *[w_down] * count, *[low] * count)
-
-
-def finish_body(features, count, *refs):
-    hids, weights, lows = refs[1 : 1 + count], refs[1 + count : 1 + 2 * count], refs[1 + 2 * count :]
-    lows, rest = lows[:count], lows[count:]
-    acc_ref, squares_ref, cross_ref, hot_ref, share_ref, low_act_ref, own_ref, own_low_ref = rest[:8]
-    gain_ref, act_out, resid_out, normed_out, lead, pull = rest[8:]
-
-    @pl.when(pl.program_id(0) == 0)
-    def _():
-        squares, cross = statistics(hids, lows)
-        weight = hot_ref[...].astype(f32) * share_ref[...]
-        inner = jnp.sum((cross_ref[...] + cross) * weight, axis=1, keepdims=True)
-        inv_rms = lax.rsqrt((squares_ref[...] + squares) / features + norm_eps)
-        lead[...] = inv_rms * jnp.sum(weight, axis=1, keepdims=True)
-        pull[...] = inv_rms * inv_rms * inv_rms * inner / features
+    )(places, *pieces, *[low] * count, w_down, *before)
+
+
+def finish_body(features, count, places_ref, *refs):
+    hids, lows, w_hbm, refs = refs[:count], refs[count : 2 * count], refs[2 * count], refs[2 * count + 1 :]
+    acc_hbm, squares_ref, cross_ref, hot_ref, share_ref, low_act_ref, left_ref, right_ref = refs[:8]
+    own_low_ref, gain_ref, act_hbm, resid_out, normed_out = refs[8:13]
+    hid, weights, acc, act, sems, in_sems, out_sems = refs[13:]
+    tiles, tile, _ = weights.shape
+    copies = weight_copies(places_ref, w_hbm, weights, sems)
+
+    def acc_in(t):
+        return pltpu.make_async_copy(acc_hbm.at[t], acc.at[t], in_sems.at[t])
+
+    def act_out(t):
+        columns = pl.ds(pl.multiple_of(t * tile, lane), tile)
+        return pltpu.make_async_copy(act.at[t], act_hbm.at[:, columns], out_sems.at[t])
+
+    for t in range(tiles):
+        for copy in copies(t):
+            copy.start()
+        acc_in(t).start()
+    squares, cross = statistics(hids, lows)
+    weight = hot_ref[...].astype(f32) * share_ref[...]
+    inner = jnp.sum((cross_ref[...] + cross) * weight, axis=1, keepdims=True)
+    inv_rms = lax.rsqrt((squares_ref[...] + squares) / features + norm_eps)
+    lead = inv_rms * jnp.sum(weight, axis=1, keepdims=True)
+    pull = inv_rms * inv_rms * inv_rms * inner / features
+    own_low = dot(hot_ref[...], own_low_ref[...])
+    half = left_ref.shape[1]
+    for own_ref, at in ((left_ref, slice(0, half)), (right_ref, slice(half, 2 * half))):
         own = own_ref[...].astype(f32)
-        own_low = dot(hot_ref[...], own_low_ref[...])
-        resid_out[...] = (lead[...] * own_low - own * pull[...]).astype(bf16)
-        normed_out[...] = (gain_ref[...] * own * inv_rms).astype(bf16)
-
-    low_act = dot(hot_ref[...], low_act_ref[...])
-    hid_act = acc_ref[...] + product(hids, weights)
-    act_out[...] = (lead[...] * low_act - pull[...] * hid_act).astype(bf16)
-
-
-def finish(places, pieces, w_down, low, acc, squares, cross, hot, share, low_act, own, gain):
+        resid_out[:, at] = (lead * own_low[:, at] - own * pull).astype(bf16)
+        normed_out[:, at] = (gain_ref[:, at] * own * inv_rms).astype(bf16)
+    width = hids[0].shape[1]
+    for n in range(count):
+        hid[:, n * width : (n + 1) * width] = hids[n][...]
+
+    @pl.loop(0, tiles)
+    def _(t):
+        for copy in copies(t):
+            copy.wait()
+        total = dot_t(hid[...], weights[t])
+        rows = pl.ds(pl.multiple_of(t * tile, tile), tile)
+        low_act = dot_t(hot_ref[...], low_act_ref[rows])
+        acc_in(t).wait()
+        act[t] = (lead * low_act - pull * (total + acc[t])).astype(bf16)
+        act_out(t).start()
+
+    @pl.loop(0, tiles)
+    def _(t):
+        act_out(t).wait()
+
+
+def finish(places, pieces, w_down, low, before, hot, share, low_act, own, gain):
     count = len(pieces)
-    rows, width = own.shape
+    rows, half = own[0].shape
+    width = 2 * half
     depth, features = w_down.shape
     pairs = hot.shape[1]
     tile = tile_of(depth, 512)
+    tiles = depth // tile
+    anywhere = pl.BlockSpec(memory_space=pl.ANY)
 
     def whole(shape):
         return pl.BlockSpec(shape, lambda j, g: (0, 0))
@@ -350,25 +484,32 @@
         lambda *refs: finish_body(features, count, *refs),
         grid_spec=pltpu.PrefetchScalarGridSpec(
             num_scalar_prefetch=1,
-            grid=(depth // tile,),
-            in_specs=piece_specs(pieces, low, tile)
+            grid=(1,),
+            in_specs=[whole((rows, half))] * count
+            + [pl.BlockSpec((pairs, half), lambda j, g, n=n: (0, g[n])) for n in range(count)]
             + [
-                pl.BlockSpec((rows, tile), lambda j, g: (0, j)),
+                anywhere,
+                anywhere,
                 whole((rows, 1)),
                 whole((rows, pairs)),
                 whole((rows, pairs)),
                 whole((1, pairs)),
-                pl.BlockSpec((pairs, tile), lambda j, g: (0, j)),
-                whole((rows, width)),
+                whole((depth, pairs)),
+                whole((rows, half)),
+                whole((rows, half)),
                 pl.BlockSpec((pairs, width), lambda j, g: (0, g[count])),
                 whole((1, width)),
             ],
-            out_specs=[
-                pl.BlockSpec((rows, tile), lambda j, g: (0, j)),
-                whole((rows, width)),
-                whole((rows, width)),
+            out_specs=[anywhere, whole((rows, width)), whole((rows, width))],
+            scratch_shapes=[
+                pltpu.VMEM((rows, count * half), bf16),
+                pltpu.VMEM((tiles, tile, count * half), bf16),
+                pltpu.VMEM((tiles, rows, tile), f32),
+                pltpu.VMEM((tiles, rows, tile), bf16),
+                pltpu.SemaphoreType.DMA((tiles, count)),
+                pltpu.SemaphoreType.DMA((tiles,)),
+                pltpu.SemaphoreType.DMA((tiles,)),
             ],
-            scratch_shapes=[pltpu.VMEM((rows, 1), f32), pltpu.VMEM((rows, 1), f32)],
         ),
         out_shape=[
             jax.ShapeDtypeStruct((rows, depth), bf16),
@@ -380,15 +521,13 @@
     )(
         places,
         *pieces,
-        *[w_down] * count,
         *[low] * count,
-        acc,
-        squares,
-        cross,
+        w_down,
+        *before,
         hot,
         share,
         low_act,
-        own,
+        *own,
         low,
         gain,
     )
@@ -414,11 +553,16 @@
     slot_count = 3 * tok_count // (2 * wide_count)
     rows = wide_count * slot_count
 
+    both = payload(query_emb, passage_emb, gain)
+    parts = [both] + [swap(both, k) for k in (1, 2, 3)]
+    first_term = project((blk ^ 3)[None], mlp_act, w_down, width)
+    arrived = [swap(first_term, 3)]
+    parts = after(first_term, *parts)[1:]
     query_grad, low_own = group_part(
-        query_emb, passage_emb, row_lse, positive, token_lengths, destination, gain, blk
-    )
-    arrived = []
-    for k in (3, 1, 2):
+        parts, row_lse, positive, token_lengths, destination, features, blk
+    )
+    mlp_act = after(low_own, mlp_act)[1]
+    for k in (1, 2):
         arrived.append(swap(project((blk ^ k)[None], mlp_act, w_down, width), k))
     own_term = project(blk[None], mlp_act, w_down, width, resid)
 
@@ -427,18 +571,18 @@
     per_pair = tok_count // pairs
     dest_all = tables[:, :per_pair].reshape(wide_count, tok_count)
     len_all = tables[:, per_pair].reshape(wide_count, pairs)
-    low = low[:, :features]
 
     packed = pack(destination, own_term, arrived, wide_count, slot_count)
+    packed = packed.reshape(wide_count, slot_count, width)
     own_hid = lax.all_to_all(packed, "wide", split_axis=0, concat_axis=0, tiled=True)
-    own_hid = own_hid.reshape(rows, width)
-
-    low_act = low_activations(low, w_down)
+
+    low_act = low_activations(low, features, w_down)
     hot = slot_passages(wide, dest_all, len_all, rows)
     share = (1.0 / len_all.astype(f32)).reshape(1, wide_count * pairs)
 
-    half = width // 2
-    left, right = own_hid[:, :half], own_hid[:, half:]
+    low_act, hot, share, own_hid = lax.optimization_barrier((low_act, hot, share, own_hid))
+    own_hid = own_hid.reshape(rows, width)
+    left, right = own_hid[:, : width // 2], own_hid[:, width // 2 :]
     left_1, right_2 = swap(left, 1), swap(right, 2)
     right_1, left_2 = swap(right, 1), swap(left, 2)
     left_3, right_3 = swap(left_1, 2), swap(right_2, 1)
@@ -446,24 +590,24 @@
     def places(*pieces):
         return jnp.stack([(blk ^ k) * 2 + side for k, side in pieces])
 
-    acc, squares, cross = back(
-        places((0, 0), (0, 1), (1, 0), (1, 1), (2, 0), (2, 1)),
-        [left, right, left_1, right_1, left_2, right_2],
+    totals = back(places((0, 0), (0, 1)), [left, right], w_down, low)
+    totals = back(
+        places((1, 0), (2, 1), (1, 1), (2, 0)),
+        [left_1, right_2, right_1, left_2],
         w_down,
         low,
+        totals,
     )
     act_grad, resid_grad, normed_out = finish(
         jnp.concatenate([places((3, 0), (3, 1)), blk[None]]),
         [left_3, right_3],
         w_down,
         low,
-        acc,
-        squares,
-        cross,
+        totals,
         hot,
         share,
         low_act,
-        own_hid,
+        [left, right],
         gain[None],
     )
     return (query_grad, resid_grad, act_grad, normed_out)
@@ -566,7 +710,7 @@
         low_rank = 2 * wide_count * pairs <= 3 * tok_count
         per_pair = tok_count // pairs
         aligned = operands[9].shape[0] % (lane * operands[0].shape[0]) == 0
-        if low_rank and blk_count == 4 and aligned and per_pair * pairs == tok_count:
+        if low_rank and blk_count == 4 and aligned and per_pair * pairs == tok_count and wide_count & (wide_count - 1) == 0:
             return low_rank_shards(*operands)
         return row_shards(*operands)
 

time: 139 us -> 119 us (0.86)
  blocking collectives: 28 us -> 0 us
  starting transfers between devices: 14.7 us -> 19.9 us
  waiting for transfers between devices: 9.08 us -> 13.3 us
  Pallas kernels: 58.3 us -> 55.7 us
  local copies, waits for them, and re-layouts: 10.9 us -> 13 us
    all_to_all x1 -> x0, blocking collectives: 28 us -> none  [low_rank_shards(): lax.all_to_all(packed, 'wide', split_axis=0, concat_axis=0, tiled=True)]
    all_to_all x0 -> x1, starting transfers between devices: none -> 5.11 us  [low_rank_shards(): lax.all_to_all(packed, 'wide', split_axis=0, concat_axis=0, tiled=True)]
    all_to_all x0 -> x1, waiting for transfers between devices: none -> 3.71 us  [low_rank_shards(): lax.all_to_all(packed, 'wide', split_axis=0, concat_axis=0, tiled=True)]
    pallas_call x8 -> x10, Pallas kernels: 49.2 us -> 46 us  [the longest x2 18.8 us: back(): pl.pallas_call(lambda *refs: back_body(count, len(before), *refs), grid_s...]
    reshape x2, local copies, waits for them, and re-layouts: 0.02 us -> 1.65 us  [the longest x1 0.95 us: low_rank_shards(): packed = packed.reshape(wide_count, slot_count, width)]
    unnamed x31 -> x24, local copies, waits for them, and re-layouts: 5.33 us -> 5.79 us
  transfers between devices with their start and end apart: 13 -> 14, of which waited for: 4 -> 4; matrix products, arithmetic and copies ran while one was open for 5% -> 6% of each run, Pallas kernels for 36% -> 38%
where the time goes in v4:
time: 119 us
  Pallas kernels  55.7 us (47%)
  starting transfers between devices  19.9 us (17%)
  between operations  14.3 us (12%)
  waiting for transfers between devices  13.3 us (11%)
  local copies, waits for them, and re-layouts  13 us (11%)
  other arithmetic  2.6 us (2%)
    pallas_call x2, Pallas kernels, back(): pl.pallas_call(lambda *refs: back_body(count, len(before), *refs), grid_s...  18.8 us
    pallas_call x4, Pallas kernels, project(): pl.pallas_call(lambda *refs: project_body(len(own), *refs), in_specs=[pl....  14.9 us
    ppermute x12, starting transfers between devices, swap(): lax.ppermute(rows, axis, [(i, i ^ k) for i in range(lax.axis_size(axis))])  14.8 us
    pallas_call x1, Pallas kernels, low_activations(): pl.pallas_call(low_act_body, grid=(1,), in_specs=[pl.BlockSpec((pairs, fe...  9.79 us
    ppermute x12, waiting for transfers between devices, swap(): lax.ppermute(rows, axis, [(i, i ^ k) for i in range(lax.axis_size(axis))])  9.54 us
    pallas_call x1, Pallas kernels, finish(): pl.pallas_call(lambda *refs: finish_body(features, count, *refs), grid_sp...  9.24 us
    unnamed x24, local copies, waits for them, and re-layouts  5.79 us
    all_to_all x1, starting transfers between devices, low_rank_shards(): lax.all_to_all(packed, 'wide', split_axis=0, concat_axis=0, tiled=True)  5.11 us
  transfers between devices with their start and end apart: 14, of which 4 were waited for; matrix products, arithmetic and copies ran while one was open for 6% of the time, Pallas kernels for 38%

profile of v4, /device:TPU:0, one launch (start us, length us, event | category | flops | bytes accessed | tf_op | source)
XLA Modules:
  0.0 118.8 jit_solution(7331327804689669861)
XLA Ops:
  7.2 0.7 reshape.48.gain_ref
  7.9 0.8 copy-done.6
  8.7 0.8 copy-done.7
  9.4 3.0 %collective-permute-start = (bf16[4,8704]{1,0:T(4,128)(2,1)S(1)}, bf16[4,8704]{1,0:T(4,128)(2,1)S(1)}, u32[]{:S(2)}, u32[]{:S(2)}) collective-permute-start(bf16[4,8704]{1,0:T(4,128)(2,1)S(1)} %shard_map.130.refs_1_), channel_id=1, source_target_pairs={{0,1},{1,0},{2,3},{3,2},{4,5},{5,4},{6,7},{7,6},{8,9},{9,8},{10,11... | collective-permute-start | bytes 208904 | tf_op jit(solution)/shard_map/ppermute | solution.py:45
  12.4 1.5 %collective-permute-start.1 = (bf16[4,8704]{1,0:T(4,128)(2,1)S(1)}, bf16[4,8704]{1,0:T(4,128)(2,1)S(1)}, u32[]{:S(2)}, u32[]{:S(2)}) collective-permute-start(bf16[4,8704]{1,0:T(4,128)(2,1)S(1)} %shard_map.130.refs_1_), channel_id=1, source_target_pairs={{0,2},{1,3},{2,0},{3,1},{4,6},{5,7},{6,4},{7,5},{8,10},{9,11},{10,... | collective-permute-start | bytes 208904 | tf_op jit(solution)/shard_map/ppermute | solution.py:45
  14.0 0.7 convert_bitcast_fusion
  14.6 0.1 copy.17
  14.7 0.7 convert_reduce_fusion
  15.4 0.1 reshape.49
  15.5 0.7 copy.18.refs_6_
  16.3 0.7 copy.19.refs_8_
  17.0 1.3 %copy-done.2 = bf16[192,3072]{1,0:T(8,128)(2,1)S(1)} copy-done((bf16[192,3072]{1,0:T(8,128)(2,1)S(1)}, bf16[192,3072]{1,0:T(8,128)(2,1)}, u32[]{:S(2)}) %copy-start.2) | copy-done | bytes 1179672
  18.3 3.8 %shard_map.129 = bf16[192,1024]{1,0:T(8,128)(2,1)S(1)} custom-call(s32[1]{0:T(128)} %bitcast.1.refs_0_, bf16[192,3072]{1,0:T(8,128)(2,1)S(1)} %copy-done.2, bf16[3072,4096]{1,0:T(8,128)(2,1)} %refs_5_.3), custom_call_target="tpu_custom_call" | custom-call | flops 1207959552 | bytes 7471104 | tf_op jit(solution)/shard_map/pallas_call | solution.py:83
  22.1 0.1 fusion.3.refs_9_
  22.2 1.5 %shard_map.131 = (bf16[4,4096]{1,0:T(4,128)(2,1)}, bf16[16,4224]{1,0:T(8,128)(2,1)}) custom-call(s32[1]{0:T(128)} %bitcast.refs_0_, bf16[4,8704]{1,0:T(4,128)(2,1)S(1)} %shard_map.130.refs_1_, bf16[4,8704]{1,0:T(4,128)(2,1)S(1)} %collective-permute-done.refs_2_, bf16[4,8704]{1,0:T(4,128)(2,1)S(1)} %collective-permute-done.1.refs_3_, ...), custom_call_target="tpu_custom_call" | custom-call | flops 8388608 | bytes 524288 | tf_op jit(solution)/shard_map/pallas_call | solution.py:169
  23.7 3.0 %collective-permute-start.3 = (bf16[192,1024]{1,0:T(8,128)(2,1)S(1)}, bf16[192,1024]{1,0:T(8,128)(2,1)S(1)}, u32[]{:S(2)}, u32[]{:S(2)}) collective-permute-start(bf16[192,1024]{1,0:T(8,128)(2,1)S(1)} %shard_map.129), channel_id=1, source_target_pairs={{0,3},{1,2},{2,1},{3,0},{4,7},{5,6},{6,5},{7,4},{8,11},{9,10},{10,... | collective-permute-start | bytes 1179656 | tf_op jit(solution)/shard_map/ppermute | solution.py:45
  26.7 3.6 %shard_map.135 = bf16[192,1024]{1,0:T(8,128)(2,1)S(1)} custom-call(s32[1]{0:T(128)} %bitcast.11.refs_0_, bf16[192,3072]{1,0:T(8,128)(2,1)S(1)} %copy-done.3, bf16[3072,4096]{1,0:T(8,128)(2,1)} %refs_5_.3), custom_call_target="tpu_custom_call" | custom-call | flops 1207959552 | bytes 7471104 | tf_op jit(solution)/shard_map/pallas_call | solution.py:83
  30.3 0.6 collective-permute-start.4
  30.9 3.8 %shard_map.136 = bf16[192,1024]{1,0:T(8,128)(2,1)S(1)} custom-call(s32[1]{0:T(128)} %bitcast.12.refs_0_, bf16[192,3072]{1,0:T(8,128)(2,1)S(1)} %copy-done.3, bf16[3072,4096]{1,0:T(8,128)(2,1)} %refs_5_.3), custom_call_target="tpu_custom_call" | custom-call | flops 1207959552 | bytes 7471104 | tf_op jit(solution)/shard_map/pallas_call | solution.py:83
  34.9 3.7 %shard_map.134.refs_1_ = f32[192,1024]{1,0:T(8,128)S(1)} custom-call(s32[1]{0:T(128)} %bitcast.refs_0_, bf16[192,3072]{1,0:T(8,128)(2,1)S(1)} %copy-done.3, bf16[3072,4096]{1,0:T(8,128)(2,1)} %refs_5_.3, bf16[192,1024]{1,0:T(8,128)(2,1)S(1)} %copy-done.5), custom_call_target="tpu_custom_call" | custom-call | flops 1207959552 | bytes 7471104 | tf_op jit(solution)/shard_map/pallas_call | solution.py:83
  38.6 5.1 %collective-permute-done.4.refs_3_ = bf16[192,1024]{1,0:T(8,128)(2,1)S(1)} collective-permute-done((bf16[192,1024]{1,0:T(8,128)(2,1)S(1)}, bf16[192,1024]{1,0:T(8,128)(2,1)S(1)}, u32[]{:S(2)}, u32[]{:S(2)}) %collective-permute-start.4) | collective-permute-done | bytes 393248 | tf_op jit(solution)/shard_map/ppermute | solution.py:45
  43.6 1.0 collective-permute-done.5.refs_4_
  44.7 1.0 shard_map.137
  45.6 0.9 reshape.53
  46.6 5.1 %all-to-all-start = ((bf16[8,36,1024]{2,1,0:T(8,128)(2,1)}), bf16[8,36,1024]{2,1,0:T(8,128)(2,1)S(1)}, u32[]{:S(2)}, u32[]{:S(2)}) async-start(bf16[8,36,1024]{2,1,0:T(8,128)(2,1)} %reshape.53), calls=%async_computation | async-start | bytes 1310720 | tf_op jit(solution)/shard_map/all_to_all | solution.py:577
  51.8 0.8 slice.19
  52.5 0.1 reshape.51.dest_ref
  52.6 0.9 slice_reduce_fusion
  53.6 0.1 reshape_squeeze.3.len_ref
  53.6 0.5 shard_map.133.refs_9_
  54.2 0.9 fusion
  55.1 1.2 %copy-done = bf16[128,4224]{1,0:T(8,128)(2,1)S(1)} copy-done((bf16[128,4224]{1,0:T(8,128)(2,1)S(1)}, bf16[128,4224]{1,0:T(8,128)(2,1)}, u32[]{:S(2)}) %copy-start) | copy-done | bytes 1081368
  56.3 9.8 %shard_map.132.refs_11_ = bf16[3072,128]{1,0:T(8,128)(2,1)S(1)} custom-call(bf16[128,4224]{1,0:T(8,128)(2,1)S(1)} %copy-done, bf16[3072,4096]{1,0:T(8,128)(2,1)} %refs_5_.3), custom_call_target="tpu_custom_call" | custom-call | flops 3221225472 | bytes 25165824 | tf_op jit(solution)/shard_map/pallas_call | solution.py:291
  66.1 3.7 %all-to-all-done = bf16[8,36,1024]{2,1,0:T(8,128)(2,1)S(1)} async-done(((bf16[8,36,1024]{2,1,0:T(8,128)(2,1)}), bf16[8,36,1024]{2,1,0:T(8,128)(2,1)S(1)}, u32[]{:S(2)}, u32[]{:S(2)}) %all-to-all-start) | async-done | bytes 589856 | tf_op jit(solution)/shard_map/all_to_all | solution.py:577
  69.9 0.9 reshape.54
  70.8 1.1 fusion.4
  71.9 1.1 collective-permute-start.11
  72.9 1.5 %collective-permute-start.6 = (bf16[288,512]{1,0:T(8,128)(2,1)S(1)}, bf16[288,512]{1,0:T(8,128)(2,1)S(1)}, u32[]{:S(2)}, u32[]{:S(2)}) collective-permute-start(bf16[288,512]{1,0:T(8,128)(2,1)S(1)} %get-tuple-element.45.refs_1_.refs_12_), channel_id=1, source_target_pairs={{0,1},{1,0},{2,3},{3,2},{4,5},{5,4},{6,7},{7,6},{8,9},{9,8},{10,11... | collective-permute-start | bytes 884744 | tf_op jit(solution)/shard_map/ppermute | solution.py:45
  74.4 0.5 collective-permute-start.10
  75.0 1.0 collective-permute-start.8
  76.1 0.1 pad_add_fusion.1.refs_0_
  76.1 5.9 %shard_map.138 = (f32[6,288,512]{2,1,0:T(8,128)S(1)}, f32[288,1]{1,0:T(8,128)S(1)}, f32[288,128]{1,0:T(8,128)S(1)}) custom-call(s32[2]{0:T(128)S(1)} %pad_add_fusion.2.refs_0_, bf16[288,512]{1,0:T(8,128)(2,1)S(1)} %get-tuple-element.45.refs_1_.refs_12_, bf16[288,512]{1,0:T(8,128)(2,1)S(1)} %get-tuple-element.44.refs_2_.refs_13_, ...), custom_call_target="tpu_custom_call" | custom-call | flops 1811939328 | bytes 6291456 | tf_op jit(solution)/shard_map/pallas_call | solution.py:390
  82.0 1.7 %copy-done.4 = f32[6,288,512]{2,1,0:T(8,128)} copy-done((f32[6,288,512]{2,1,0:T(8,128)}, f32[6,288,512]{2,1,0:T(8,128)S(1)}, u32[]{:S(2)}) %copy-start.4) | copy-done | bytes 3538968
  83.8 1.0 collective-permute-start.7
  84.8 3.4 %collective-permute-done.8.refs_2_ = bf16[288,512]{1,0:T(8,128)(2,1)S(1)} collective-permute-done((bf16[288,512]{1,0:T(8,128)(2,1)S(1)}, bf16[288,512]{1,0:T(8,128)(2,1)S(1)}, u32[]{:S(2)}, u32[]{:S(2)}) %collective-permute-start.8) | collective-permute-done | bytes 294944 | tf_op jit(solution)/shard_map/ppermute | solution.py:45
  88.2 1.5 %collective-permute-start.9 = (bf16[288,512]{1,0:T(8,128)(2,1)S(1)}, bf16[288,512]{1,0:T(8,128)(2,1)S(1)}, u32[]{:S(2)}, u32[]{:S(2)}) collective-permute-start(bf16[288,512]{1,0:T(8,128)(2,1)S(1)} %collective-permute-done.8.refs_2_), channel_id=1, source_target_pairs={{0,1},{1,0},{2,3},{3,2},{4,5},{5,4},{6,7},{7,6},{8,9},{9,8},{10,11... | collective-permute-start | bytes 884744 | tf_op jit(solution)/shard_map/ppermute | solution.py:45
  89.7 12.9 %shard_map.139 = (f32[6,288,512]{2,1,0:T(8,128)S(1)}, f32[288,1]{1,0:T(8,128)S(1)}, f32[288,128]{1,0:T(8,128)S(1)}) custom-call(s32[4]{0:T(128)S(1)} %pad_add_fusion.1.refs_0_, bf16[288,512]{1,0:T(8,128)(2,1)S(1)} %collective-permute-done.6.refs_1_, bf16[288,512]{1,0:T(8,128)(2,1)S(1)} %collective-permute-done.8.refs_2_, ...), custom_call_target="tpu_custom_call" | custom-call | flops 3623878656 | bytes 12582912 | tf_op jit(solution)/shard_map/pallas_call | solution.py:390
  102.7 9.2 %shard_map.140 = (bf16[288,3072]{1,0:T(8,128)(2,1)}, bf16[288,1024]{1,0:T(8,128)(2,1)}, bf16[288,1024]{1,0:T(8,128)(2,1)}) custom-call(s32[3]{0:T(128)S(1)} %pad_add_fusion.refs_0_, bf16[288,512]{1,0:T(8,128)(2,1)S(1)} %collective-permute-done.7.refs_1_, bf16[288,512]{1,0:T(8,128)(2,1)S(1)} %collective-permute-done.9.refs_2_, ...), custom_call_target="tpu_custom_call" | custom-call | flops 1811939328 | bytes 11599872 | tf_op jit(solution)/shard_map/pallas_call | solution.py:483
  (36 shorter events, 0.4 us)
Async XLA Ops:
  7.2 44.6 %all-gather.2.cloned.1.call-start = ((), (), s32[]{:S(2)}) async-start(), calls=%async_computation.1 | async-start | bytes 1216512 | tf_op jit(solution)/shard_map/all_gather | solution.py:569
  7.9 0.8 copy-start.6
  8.7 0.8 copy-start.7
  9.4 12.7 %collective-permute-start = (bf16[4,8704]{1,0:T(4,128)(2,1)S(1)}, bf16[4,8704]{1,0:T(4,128)(2,1)S(1)}, u32[]{:S(2)}, u32[]{:S(2)}) collective-permute-start(bf16[4,8704]{1,0:T(4,128)(2,1)S(1)} %shard_map.130.refs_1_), channel_id=1, source_target_pairs={{0,1},{1,0},{2,3},{3,2},{4,5},{5,4},{6,7},{7,6},{8,9},{9,8},{10,11... | collective-permute-start | bytes 208904 | tf_op jit(solution)/shard_map/ppermute | solution.py:45
  12.4 9.7 %collective-permute-start.1 = (bf16[4,8704]{1,0:T(4,128)(2,1)S(1)}, bf16[4,8704]{1,0:T(4,128)(2,1)S(1)}, u32[]{:S(2)}, u32[]{:S(2)}) collective-permute-start(bf16[4,8704]{1,0:T(4,128)(2,1)S(1)} %shard_map.130.refs_1_), channel_id=1, source_target_pairs={{0,2},{1,3},{2,0},{3,1},{4,6},{5,7},{6,4},{7,5},{8,10},{9,11},{10,... | collective-permute-start | bytes 208904 | tf_op jit(solution)/shard_map/ppermute | solution.py:45
  14.0 8.2 %collective-permute-start.2 = (bf16[4,8704]{1,0:T(4,128)(2,1)S(1)}, bf16[4,8704]{1,0:T(4,128)(2,1)S(1)}, u32[]{:S(2)}, u32[]{:S(2)}) collective-permute-start(bf16[4,8704]{1,0:T(4,128)(2,1)S(1)} %shard_map.130.refs_1_), channel_id=1, source_target_pairs={{0,3},{1,2},{2,1},{3,0},{4,7},{5,6},{6,5},{7,4},{8,11},{9,10},{10,... | collective-permute-start | bytes 208904 | tf_op jit(solution)/shard_map/ppermute | solution.py:45
  17.0 1.3 %copy-start.2 = (bf16[192,3072]{1,0:T(8,128)(2,1)S(1)}, bf16[192,3072]{1,0:T(8,128)(2,1)}, u32[]{:S(2)}) copy-start(bf16[192,3072]{1,0:T(8,128)(2,1)} %refs_1_.4) | copy-start | bytes 3538948
  18.3 3.9 %copy-start.9 = (f32[16]{0:T(128)S(1)}, f32[16]{0:T(128)}, u32[]{:S(2)}) copy-start(f32[16]{0:T(128)} %param.12) | copy-start | bytes 196
  18.3 3.9 %copy-start.10 = (s32[16]{0:T(128)S(1)}, s32[16]{0:T(128)}, u32[]{:S(2)}) copy-start(s32[16]{0:T(128)} %param.13) | copy-start | bytes 196
  18.3 8.4 %copy-start.3 = (bf16[192,3072]{1,0:T(8,128)(2,1)S(1)}, bf16[192,3072]{1,0:T(8,128)(2,1)}, u32[]{:S(2)}) copy-start(bf16[192,3072]{1,0:T(8,128)(2,1)} %refs_1_.4) | copy-start | bytes 3538948
  23.7 14.8 %collective-permute-start.3 = (bf16[192,1024]{1,0:T(8,128)(2,1)S(1)}, bf16[192,1024]{1,0:T(8,128)(2,1)S(1)}, u32[]{:S(2)}, u32[]{:S(2)}) collective-permute-start(bf16[192,1024]{1,0:T(8,128)(2,1)S(1)} %shard_map.129), channel_id=1, source_target_pairs={{0,3},{1,2},{2,1},{3,0},{4,7},{5,6},{6,5},{7,4},{8,11},{9,10},{10,... | collective-permute-start | bytes 1179656 | tf_op jit(solution)/shard_map/ppermute | solution.py:45
  30.3 13.3 %collective-permute-start.4 = (bf16[192,1024]{1,0:T(8,128)(2,1)S(1)}, bf16[192,1024]{1,0:T(8,128)(2,1)S(1)}, u32[]{:S(2)}, u32[]{:S(2)}) collective-permute-start(bf16[192,1024]{1,0:T(8,128)(2,1)S(1)} %shard_map.135), channel_id=1, source_target_pairs={{0,1},{1,0},{2,3},{3,2},{4,5},{5,4},{6,7},{7,6},{8,9},{9,8},{10,11... | collective-permute-start | bytes 1179656 | tf_op jit(solution)/shard_map/ppermute | solution.py:45
  30.9 3.9 %copy-start.5 = (bf16[192,1024]{1,0:T(8,128)(2,1)S(1)}, bf16[192,1024]{1,0:T(8,128)(2,1)}, u32[]{:S(2)}) copy-start(bf16[192,1024]{1,0:T(8,128)(2,1)} %refs_3_.1) | copy-start | bytes 1179652
  34.8 9.9 %copy-start.11 = (s32[192,1]{0,1:T(1,128)S(1)}, s32[192,1]{0,1:T(1,128)}, u32[]{:S(2)}) copy-start(s32[192,1]{0,1:T(1,128)} %param.15) | copy-start | bytes 2308
  34.8 9.9 %collective-permute-start.5 = (bf16[192,1024]{1,0:T(8,128)(2,1)S(1)}, bf16[192,1024]{1,0:T(8,128)(2,1)S(1)}, u32[]{:S(2)}, u32[]{:S(2)}) collective-permute-start(bf16[192,1024]{1,0:T(8,128)(2,1)S(1)} %shard_map.136), channel_id=1, source_target_pairs={{0,2},{1,3},{2,0},{3,1},{4,6},{5,7},{6,4},{7,5},{8,10},{9,11},{10,... | collective-permute-start | bytes 1179656 | tf_op jit(solution)/shard_map/ppermute | solution.py:45
  46.6 23.3 %all-to-all-start = ((bf16[8,36,1024]{2,1,0:T(8,128)(2,1)}), bf16[8,36,1024]{2,1,0:T(8,128)(2,1)S(1)}, u32[]{:S(2)}, u32[]{:S(2)}) async-start(bf16[8,36,1024]{2,1,0:T(8,128)(2,1)} %reshape.53), calls=%async_computation | async-start | bytes 1310720 | tf_op jit(solution)/shard_map/all_to_all | solution.py:577
  55.1 1.2 %copy-start = (bf16[128,4224]{1,0:T(8,128)(2,1)S(1)}, bf16[128,4224]{1,0:T(8,128)(2,1)}, u32[]{:S(2)}) copy-start(bf16[128,4224]{1,0:T(8,128)(2,1)} %all-gather.2.cloned.1.call-done.low_ref.refs_3_.refs_4_.refs_5_.refs_6_.refs_7_.refs_8_.refs_14_) | copy-start | bytes 3244036
  66.1 10.0 %copy-start.1 = (bf16[128,4224]{1,0:T(8,128)(2,1)S(1)}, bf16[128,4224]{1,0:T(8,128)(2,1)}, u32[]{:S(2)}) copy-start(bf16[128,4224]{1,0:T(8,128)(2,1)} %all-gather.2.cloned.1.call-done.low_ref.refs_3_.refs_4_.refs_5_.refs_6_.refs_7_.refs_8_.refs_14_) | copy-start | bytes 3244036
  71.9 17.8 %collective-permute-start.11 = (bf16[288,512]{1,0:T(8,128)(2,1)S(1)}, bf16[288,512]{1,0:T(8,128)(2,1)S(1)}, u32[]{:S(2)}, u32[]{:S(2)}) collective-permute-start(bf16[288,512]{1,0:T(8,128)(2,1)S(1)} %get-tuple-element.45.refs_1_.refs_12_), channel_id=1, source_target_pairs={{0,2},{1,3},{2,0},{3,1},{4,6},{5,7},{6,4},{7,5},{8,10},{9,11},{10,... | collective-permute-start | bytes 884744 | tf_op jit(solution)/shard_map/ppermute | solution.py:45
  72.9 10.8 %collective-permute-start.6 = (bf16[288,512]{1,0:T(8,128)(2,1)S(1)}, bf16[288,512]{1,0:T(8,128)(2,1)S(1)}, u32[]{:S(2)}, u32[]{:S(2)}) collective-permute-start(bf16[288,512]{1,0:T(8,128)(2,1)S(1)} %get-tuple-element.45.refs_1_.refs_12_), channel_id=1, source_target_pairs={{0,1},{1,0},{2,3},{3,2},{4,5},{5,4},{6,7},{7,6},{8,9},{9,8},{10,11... | collective-permute-start | bytes 884744 | tf_op jit(solution)/shard_map/ppermute | solution.py:45
  74.4 15.2 %collective-permute-start.10 = (bf16[288,512]{1,0:T(8,128)(2,1)S(1)}, bf16[288,512]{1,0:T(8,128)(2,1)}, u32[]{:S(2)}, u32[]{:S(2)}) collective-permute-start(bf16[288,512]{1,0:T(8,128)(2,1)S(1)} %get-tuple-element.44.refs_2_.refs_13_), channel_id=1, source_target_pairs={{0,1},{1,0},{2,3},{3,2},{4,5},{5,4},{6,7},{7,6},{8,9},{9,8},{10,11... | collective-permute-start | bytes 884744 | tf_op jit(solution)/shard_map/ppermute | solution.py:45
  75.0 13.2 %collective-permute-start.8 = (bf16[288,512]{1,0:T(8,128)(2,1)S(1)}, bf16[288,512]{1,0:T(8,128)(2,1)S(1)}, u32[]{:S(2)}, u32[]{:S(2)}) collective-permute-start(bf16[288,512]{1,0:T(8,128)(2,1)S(1)} %get-tuple-element.44.refs_2_.refs_13_), channel_id=1, source_target_pairs={{0,2},{1,3},{2,0},{3,1},{4,6},{5,7},{6,4},{7,5},{8,10},{9,11},{10,... | collective-permute-start | bytes 884744 | tf_op jit(solution)/shard_map/ppermute | solution.py:45
  82.0 1.8 %copy-start.4 = (f32[6,288,512]{2,1,0:T(8,128)}, f32[6,288,512]{2,1,0:T(8,128)S(1)}, u32[]{:S(2)}) copy-start(f32[6,288,512]{2,1,0:T(8,128)S(1)} %get-tuple-element.32.refs_10_) | copy-start | bytes 10616836
  83.8 18.9 %collective-permute-start.7 = (bf16[288,512]{1,0:T(8,128)(2,1)S(1)}, bf16[288,512]{1,0:T(8,128)(2,1)S(1)}, u32[]{:S(2)}, u32[]{:S(2)}) collective-permute-start(bf16[288,512]{1,0:T(8,128)(2,1)S(1)} %collective-permute-done.6.refs_1_), channel_id=1, source_target_pairs={{0,2},{1,3},{2,0},{3,1},{4,6},{5,7},{6,4},{7,5},{8,10},{9,11},{10,... | collective-permute-start | bytes 884744 | tf_op jit(solution)/shard_map/ppermute | solution.py:45
  88.2 14.5 %collective-permute-start.9 = (bf16[288,512]{1,0:T(8,128)(2,1)S(1)}, bf16[288,512]{1,0:T(8,128)(2,1)S(1)}, u32[]{:S(2)}, u32[]{:S(2)}) collective-permute-start(bf16[288,512]{1,0:T(8,128)(2,1)S(1)} %collective-permute-done.8.refs_2_), channel_id=1, source_target_pairs={{0,1},{1,0},{2,3},{3,2},{4,5},{5,4},{6,7},{7,6},{8,9},{9,8},{10,11... | collective-permute-start | bytes 884744 | tf_op jit(solution)/shard_map/ppermute | solution.py:45
  89.7 13.0 %copy-start.8 = (f32[1024]{0:T(1024)S(1)}, f32[1024]{0:T(1024)}, u32[]{:S(2)}) copy-start(f32[1024]{0:T(1024)} %param.19) | copy-start | bytes 12292
Sparse Core Ops, SparseCore 0:
  23.8 24.0 all-gather.1

commit v5 on v4

--- a/solution.py
+++ b/solution.py
@@ -98,10 +98,12 @@
     )(group, act, w_down, *own)
 
 
-def payload_body(query_ref, passage_ref, gain_ref, out_ref):
-    features = query_ref.shape[1]
-    piece = gain_ref.shape[1]
-    gain = gain_ref[...]
+def payload_body(query_ref, passage_ref, gain_ref, out_ref, gains):
+    own, features = query_ref.shape
+    piece = gains.shape[1]
+    for row in range(own):
+        gains[row : row + 1] = gain_ref[:, row * piece : (row + 1) * piece]
+    gain = gains[...]
     high = gain.astype(bf16)
     out_ref[:, :features] = query_ref[...]
     out_ref[:, features : 2 * features] = passage_ref[...]
@@ -111,19 +113,20 @@
 
 def payload(query_emb, passage_emb, gain):
     own, features = query_emb.shape
-    gain = gain.reshape(own, -1)
+    piece = gain.shape[0] // own
     return pl.pallas_call(
         payload_body,
-        out_shape=jax.ShapeDtypeStruct((own, 2 * features + 2 * gain.shape[1]), bf16),
+        out_shape=jax.ShapeDtypeStruct((own, 2 * features + 2 * piece), bf16),
+        scratch_shapes=[pltpu.VMEM((own, piece), f32)],
         compiler_params=params(),
         cost_estimate=cost(own * features, 8 * own * features),
-    )(query_emb, passage_emb, gain)
+    )(query_emb, passage_emb, gain[None])
 
 
 def group_body(count, blk_ref, *refs):
     parts, refs = refs[:count], refs[count:]
-    lse_row_ref, lse_ref, pos_row_ref, pos_ref, table_ref = refs[:5]
-    query_grad_ref, low_ref, query_all, passage_all, gain_all = refs[5:]
+    lse_ref, pos_ref, dest_ref, len_ref = refs[:4]
+    query_grad_ref, low_ref, query_all, passage_all, gain_all = refs[4:]
     own, features = query_grad_ref.shape
     pairs = own * count
     piece = features // pairs
@@ -146,30 +149,41 @@
     here_rows, here_cols = named(0), named(1)
     at_rows = here_rows == iota((pairs, pairs), 1)
     at_cols = here_cols == iota((pairs, pairs), 0)
-    lse = jnp.sum(jnp.where(at_rows, lse_row_ref[...], 0.0), axis=1, keepdims=True)
-    pos = jnp.sum(jnp.where(at_rows, pos_row_ref[...], 0), axis=1, keepdims=True)
+    lse = jnp.sum(jnp.where(at_rows, lse_ref[...], 0.0), axis=1, keepdims=True)
+    pos = jnp.sum(jnp.where(at_rows, pos_ref[...], 0), axis=1, keepdims=True)
     hit = (pos == here_cols).astype(f32)
     coef = (jnp.exp(logit_scale * dot_t(queries, passages) - lse) - hit).astype(bf16)
     query_grad_ref[...] = (logit_scale * dot(coef, passages))[:own].astype(bf16)
-    lse = jnp.sum(jnp.where(at_cols, lse_ref[...], 0.0), axis=0, keepdims=True)
-    pos = jnp.sum(jnp.where(at_cols, pos_ref[...], 0), axis=0, keepdims=True)
+    same = iota((pairs, pairs), 0) == iota((pairs, pairs), 1)
+    lse = jnp.sum(jnp.where(same, lse, 0.0), axis=0, keepdims=True)
+    pos = jnp.sum(jnp.where(same, pos, 0), axis=0, keepdims=True)
     hit = (pos == here_rows).astype(f32)
     turned = (jnp.exp(logit_scale * dot_t(passages, queries) - lse) - hit).astype(bf16)
-    turned = dot(at_cols.astype(bf16), turned).astype(bf16)
+    turned = dot(at_cols.astype(f32).astype(bf16), turned).astype(bf16)
     pass_grad = logit_scale * dot(turned, queries)
     low_ref[:, :features] = (gain_all[...] * pass_grad).astype(bf16)
-    low_ref[:, features:] = table_ref[...]
+    row = iota((pairs, lane), 0)
+    tokens = dest_ref.shape[1]
+    table = jnp.zeros((pairs, lane), f32)
+    for n in range(-(-tokens // lane)):
+        some = dest_ref[:, n * lane : min(tokens, (n + 1) * lane)].astype(f32)
+        table = jnp.where(row == n, widen(some), table)
+    table = jnp.where(row == -(-tokens // lane), widen(len_ref[...].astype(f32)), table)
+    low_ref[:, features:] = table.astype(bf16)
+
+
+def widen(row):
+    short = lane - row.shape[1]
+    return jnp.concatenate([row, jnp.zeros((1, short), f32)], axis=1) if short else row
 
 
 def group_part(parts, row_lse, positive, token_lengths, destination, features, blk):
     own = parts[0].shape[0]
     pairs = row_lse.shape[0]
-    table = jnp.concatenate([destination.reshape(pairs, -1), token_lengths.reshape(pairs, 1)], 1)
-    table = jnp.pad(table, ((0, 0), (0, lane - table.shape[1]))).astype(bf16)
     return pl.pallas_call(
         lambda *refs: group_body(pairs // own, *refs),
         in_specs=[pl.BlockSpec(memory_space=pltpu.SMEM)]
-        + [pl.BlockSpec(memory_space=pltpu.VMEM)] * (len(parts) + 5),
+        + [pl.BlockSpec(memory_space=pltpu.VMEM)] * (len(parts) + 4),
         out_specs=[pl.BlockSpec(memory_space=pltpu.VMEM)] * 2,
         out_shape=[
             jax.ShapeDtypeStruct((own, features), bf16),
@@ -186,10 +200,9 @@
         blk[None],
         *parts,
         row_lse[None],
-        row_lse[:, None],
         positive[None],
-        positive[:, None],
-        table,
+        destination.reshape(1, -1),
+        token_lengths,
     )
 
 
@@ -197,73 +210,133 @@
     return (iota((tokens, tokens), 0) < iota((tokens, tokens), 1)).astype(bf16)
 
 
-def pack_body(groups, dest_ref, own_ref, *rest):
-    terms, out_ref = rest[:-1], rest[-1]
-    rows = out_ref.shape[0]
+def pack_body(terms, wide_ref, dest_ref, own_ref, *rest):
+    outs = rest[terms:]
+    groups, slots = len(outs), outs[0].shape[0]
     tokens = dest_ref.shape[1]
+    stride = -(-slots // 16) * 16
     hidden = own_ref[...]
-    for term in terms:
+    for term in rest[:terms]:
         hidden = hidden + term[...].astype(f32)
-    dest = dest_ref[...]
-    hit = (dest == iota((groups, tokens), 0)).astype(f32)
+    partner = dest_ref[...] ^ wide_ref[0]
+    hit = (partner == iota((groups, tokens), 0)).astype(f32)
     rank = dot(hit.astype(bf16), earlier_of(tokens))
     rank = jnp.sum(rank * hit, axis=0, keepdims=True).astype(i32)
-    place = iota((rows, tokens), 0) == dest * (rows // groups) + rank
-    out_ref[...] = dot(place.astype(f32).astype(bf16), hidden.astype(bf16)).astype(bf16)
-
-
-def pack(destination, own, terms, groups, slots):
+    place = iota((groups * stride, tokens), 0) == partner * stride + rank
+    packed = dot(place.astype(f32).astype(bf16), hidden.astype(bf16)).astype(bf16)
+    for k in range(groups):
+        outs[k][...] = packed[k * stride : k * stride + slots]
+
+
+def pack(wide, destination, own, terms, groups, slots):
     tokens, width = own.shape
     tile = tile_of(width, 512)
-    rows = groups * slots
-    column_spec = pl.BlockSpec((tokens, tile), lambda j: (0, j))
-    return pl.pallas_call(
-        lambda *refs: pack_body(groups, *refs),
-        grid=(width // tile,),
-        in_specs=[pl.BlockSpec((1, tokens), lambda j: (0, 0))] + [column_spec] * (1 + len(terms)),
-        out_specs=pl.BlockSpec((rows, tile), lambda j: (0, j)),
+    column_spec = pl.BlockSpec((tokens, tile), lambda j, g: (0, j))
+    return pl.pallas_call(
+        lambda *refs: pack_body(len(terms), *refs),
+        grid_spec=pltpu.PrefetchScalarGridSpec(
+            num_scalar_prefetch=1,
+            grid=(width // tile,),
+            in_specs=[pl.BlockSpec((1, tokens), lambda j, g: (0, 0))]
+            + [column_spec] * (1 + len(terms)),
+            out_specs=[pl.BlockSpec((slots, tile), lambda j, g: (0, j))] * groups,
+        ),
+        out_shape=[jax.ShapeDtypeStruct((slots, width), bf16)] * groups,
+        compiler_params=params(),
+        cost_estimate=cost(4 * groups * slots * tokens * width, 10 * tokens * width),
+    )(wide[None], destination.reshape(1, tokens), own, *terms)
+
+
+def assemble_body(wide_ref, *refs):
+    parts, out_ref = refs[:-1], refs[-1]
+    slots = parts[0].shape[0]
+    rows = out_ref.shape[0]
+    row, column = iota((rows, slots), 0), iota((rows, slots), 1)
+    total = 0.0
+    for k, part in enumerate(parts):
+        group = wide_ref[0] ^ k
+        place = (row == group * slots + column).astype(f32).astype(bf16)
+        total = total + dot(place, part[...])
+    out_ref[...] = total.astype(bf16)
+
+
+def assemble(wide, parts):
+    slots, width = parts[0].shape
+    rows = slots * len(parts)
+    return pl.pallas_call(
+        assemble_body,
+        in_specs=[pl.BlockSpec(memory_space=pltpu.SMEM)]
+        + [pl.BlockSpec(memory_space=pltpu.VMEM)] * len(parts),
+        out_specs=pl.BlockSpec(memory_space=pltpu.VMEM),
         out_shape=jax.ShapeDtypeStruct((rows, width), bf16),
         compiler_params=params(),
-        cost_estimate=cost(2 * rows * tokens * width, 10 * tokens * width),
-    )(destination.reshape(1, tokens), own, *terms)
-
-
-def slots_body(wide_ref, dest_ref, len_ref, hot_ref):
-    groups, tokens = dest_ref.shape
-    pairs = len_ref.shape[1]
-    rows = hot_ref.shape[0]
-    slots = rows // groups
-    hit = dest_ref[...].astype(i32) == wide_ref[0]
-    rank = dot(hit.astype(f32).astype(bf16), earlier_of(tokens))
-    upto = (iota((pairs, pairs), 0) <= iota((pairs, pairs), 1)).astype(bf16)
-    ends = dot(len_ref[...], upto)
-    token = iota((groups, tokens), 1).astype(f32)
-    passage = jnp.ones((groups, tokens), f32)
-    for pair in range(pairs):
-        passage = passage + (token >= ends[:, pair : pair + 1]).astype(f32)
-    code = jnp.where(hit, passage, 0.0)
-    spread = (iota((rows, groups), 0) // slots == iota((rows, groups), 1)).astype(bf16)
-    rank_rows = dot(spread, rank.astype(bf16)).astype(i32)
-    code_rows = dot(spread, code.astype(bf16))
-    here = rank_rows == iota((rows, tokens), 0) % slots
-    taken = jnp.sum(jnp.where(here, code_rows, 0.0), axis=1, keepdims=True).astype(i32)
-    column = iota((rows, groups * pairs), 1)
-    first = iota((rows, groups * pairs), 0) // slots * pairs
+        cost_estimate=cost(2 * rows * rows * width, 4 * rows * width),
+    )(wide[None], *parts)
+
+
+def slots_body(groups, slots, wide_ref, table_ref, hot_ref, share_ref):
+    rows, columns = hot_ref.shape
+    pairs = columns // groups
+    blocks = -(-slots * groups * 2 // 3 // lane)
+    table = table_ref[...]
+
+    def tables(n):
+        at = iota((groups, columns), 1) == iota((groups, columns), 0) * pairs + n
+        return dot(at.astype(f32).astype(bf16), table)
+
+    spread = (iota((rows, groups), 0) // slots == iota((rows, groups), 1)).astype(f32).astype(bf16)
+    lengths = tables(blocks)
+    upto = (iota((lane, lane), 0) <= iota((lane, lane), 1)).astype(f32).astype(bf16)
+    ends = dot(lengths.astype(bf16), upto)
+    slot = iota((rows, lane), 0) % slots
+    before = jnp.zeros((groups, 1), f32)
+    taken = jnp.zeros((rows, 1), f32)
+    for n in range(blocks):
+        token = iota((groups, lane), 1) + n * lane
+        hit = (tables(n).astype(i32) == wide_ref[0]) & (token < slots * groups * 2 // 3)
+        count = hit.astype(f32)
+        rank = before + dot(count.astype(bf16), earlier_of(lane))
+        before = before + jnp.sum(count, axis=1, keepdims=True)
+        passage = jnp.ones((groups, lane), f32)
+        for pair in range(pairs):
+            passage = passage + (token.astype(f32) >= ends[:, pair : pair + 1]).astype(f32)
+        code = jnp.where(hit, passage, 0.0)
+        rank_rows = dot(spread, rank.astype(bf16)).astype(i32)
+        code_rows = dot(spread, code.astype(bf16))
+        taken = taken + jnp.sum(
+            jnp.where(rank_rows == slot, code_rows, 0.0), axis=1, keepdims=True
+        )
+    taken = taken.astype(i32)
+    column = iota((rows, columns), 1)
+    first = iota((rows, columns), 0) // slots * pairs
     hot = (taken > 0) & (column == first + taken - 1)
     hot_ref[...] = hot.astype(f32).astype(bf16)
-
-
-def slot_passages(wide, dest_all, len_all, rows):
-    groups, pairs = len_all.shape
-    return pl.pallas_call(
-        slots_body,
-        in_specs=[pl.BlockSpec(memory_space=pltpu.SMEM)]
-        + [pl.BlockSpec(memory_space=pltpu.VMEM)] * 2,
-        out_specs=pl.BlockSpec(memory_space=pltpu.VMEM),
-        out_shape=jax.ShapeDtypeStruct((rows, groups * pairs), bf16),
-        compiler_params=params(),
-        cost_estimate=cost(4 * rows * groups * dest_all.shape[1], 2 * rows * groups * pairs),
-    )(wide[None], dest_all, len_all)
+    length_rows = dot(spread, lengths.astype(bf16))
+    length = jnp.where(iota((rows, lane), 1) == taken - 1, length_rows, 0.0)
+    length = jnp.sum(length, axis=1, keepdims=True)
+    share_ref[...] = jnp.where(taken > 0, 1.0 / jnp.maximum(length, 1.0), 0.0)
+
+
+def slot_passages(wide, low, features, groups, slots, rows):
+    columns = low.shape[0]
+    return pl.pallas_call(
+        lambda *refs: slots_body(groups, slots, *refs),
+        grid=(1,),
+        in_specs=[
+            pl.BlockSpec(memory_space=pltpu.SMEM),
+            pl.BlockSpec((columns, lane), lambda j: (0, features // lane)),
+        ],
+        out_specs=[
+            pl.BlockSpec((rows, columns), lambda j: (0, 0)),
+            pl.BlockSpec((rows, 1), lambda j: (0, 0)),
+        ],
+        out_shape=[
+            jax.ShapeDtypeStruct((rows, columns), bf16),
+            jax.ShapeDtypeStruct((rows, 1), f32),
+        ],
+        compiler_params=params(),
+        cost_estimate=cost(4 * rows * groups * lane, 2 * rows * columns),
+    )(wide[None], low)
 
 
 def low_act_body(low_ref, w_hbm, out_ref, weights, sems):
@@ -317,8 +390,8 @@
 
 def weight_copies(places_ref, w_hbm, weights, sems):
     count, tile, across = weights.shape
-    pieces = sems.shape[1]
-    width = across // pieces
+    groups = sems.shape[1]
+    width = across // groups
 
     def copies(t):
         rows = pl.ds(pl.multiple_of(t * tile, tile), tile)
@@ -328,20 +401,17 @@
                 weights.at[t, :, n * width : (n + 1) * width],
                 sems.at[t, n],
             )
-            for n in range(pieces)
+            for n in range(groups)
         ]
 
     return copies
 
 
-def back_body(count, carried, places_ref, *refs):
+def back_body(count, places_ref, *refs):
     hids, lows, w_hbm, refs = refs[:count], refs[count : 2 * count], refs[2 * count], refs[2 * count + 1 :]
-    before, refs = refs[:carried], refs[carried:]
-    acc_hbm, squares_ref, cross_ref, hid, weights, acc, sems, in_sems, out_sems = refs
+    acc_hbm, squares_ref, cross_ref, hid, weights, acc, sems, out_sems = refs
     copies = weight_copies(places_ref, w_hbm, weights, sems)
-
-    def acc_in(t):
-        return pltpu.make_async_copy(before[0].at[t], acc.at[t], in_sems.at[t])
+    rows, width = hids[0].shape
 
     def acc_out(t):
         return pltpu.make_async_copy(acc.at[t], acc_hbm.at[t], out_sems.at[t])
@@ -349,25 +419,16 @@
     for t in range(weights.shape[0]):
         for copy in copies(t):
             copy.start()
-        if carried:
-            acc_in(t).start()
-    squares, cross = statistics(hids, lows)
-    if carried:
-        squares, cross = before[1][...] + squares, before[2][...] + cross
-    squares_ref[...], cross_ref[...] = squares, cross
-    width = hids[0].shape[1]
     for n in range(count):
-        hid[:, n * width : (n + 1) * width] = hids[n][...]
+        hid[:rows, n * width : (n + 1) * width] = hids[n][...]
+    hid[rows:] = jnp.zeros((hid.shape[0] - rows, count * width), bf16)
+    squares_ref[...], cross_ref[...] = statistics(hids, lows)
 
     @pl.loop(0, weights.shape[0])
     def _(t):
         for copy in copies(t):
             copy.wait()
-        total = dot_t(hid[...], weights[t])
-        if carried:
-            acc_in(t).wait()
-            total = total + acc[t]
-        acc[t] = total
+        acc[t] = dot_t(weights[t], hid[...])
         acc_out(t).start()
 
     @pl.loop(0, weights.shape[0])
@@ -375,53 +436,53 @@
         acc_out(t).wait()
 
 
-def back(places, pieces, w_down, low, before=()):
+def back(places, pieces, w_down, low, padded):
     count = len(pieces)
     rows, width = pieces[0].shape
     depth = w_down.shape[0]
     pairs = low.shape[0]
     tile = tile_of(depth, 512)
     tiles = depth // tile
-    small = [
-        pl.BlockSpec((rows, 1), lambda j, g: (0, 0)),
-        pl.BlockSpec((rows, pairs), lambda j, g: (0, 0)),
-    ]
     anywhere = pl.BlockSpec(memory_space=pl.ANY)
     return pl.pallas_call(
-        lambda *refs: back_body(count, len(before), *refs),
+        lambda *refs: back_body(count, *refs),
         grid_spec=pltpu.PrefetchScalarGridSpec(
             num_scalar_prefetch=1,
             grid=(1,),
             in_specs=[pl.BlockSpec((rows, width), lambda j, g: (0, 0))] * count
             + [pl.BlockSpec((pairs, width), lambda j, g, n=n: (0, g[n])) for n in range(count)]
-            + [anywhere]
-            + [anywhere, *small][: len(before)],
-            out_specs=[anywhere, *small],
+            + [anywhere],
+            out_specs=[
+                anywhere,
+                pl.BlockSpec((rows, 1), lambda j, g: (0, 0)),
+                pl.BlockSpec((rows, pairs), lambda j, g: (0, 0)),
+            ],
             scratch_shapes=[
-                pltpu.VMEM((rows, count * width), bf16),
+                pltpu.VMEM((padded, count * width), bf16),
                 pltpu.VMEM((tiles, tile, count * width), bf16),
-                pltpu.VMEM((tiles, rows, tile), f32),
+                pltpu.VMEM((tiles, tile, padded), f32),
                 pltpu.SemaphoreType.DMA((tiles, count)),
-                pltpu.SemaphoreType.DMA((tiles,)),
                 pltpu.SemaphoreType.DMA((tiles,)),
             ],
         ),
         out_shape=[
-            jax.ShapeDtypeStruct((tiles, rows, tile), f32),
+            jax.ShapeDtypeStruct((tiles, tile, padded), f32),
             jax.ShapeDtypeStruct((rows, 1), f32),
             jax.ShapeDtypeStruct((rows, pairs), f32),
         ],
         compiler_params=params(),
         cost_estimate=cost(2 * rows * depth * width * count, 2 * depth * width * count),
-    )(places, *pieces, *[low] * count, w_down, *before)
+    )(places, *pieces, *[low] * count, w_down)
 
 
 def finish_body(features, count, places_ref, *refs):
-    hids, lows, w_hbm, refs = refs[:count], refs[count : 2 * count], refs[2 * count], refs[2 * count + 1 :]
-    acc_hbm, squares_ref, cross_ref, hot_ref, share_ref, low_act_ref, left_ref, right_ref = refs[:8]
-    own_low_ref, gain_ref, act_hbm, resid_out, normed_out = refs[8:13]
-    hid, weights, acc, act, sems, in_sems, out_sems = refs[13:]
+    hids, refs = refs[:count], refs[count:]
+    low_ref, w_hbm, acc_hbm, squares_ref, cross_ref, hot_ref, share_ref, low_act_ref = refs[:8]
+    own_ref, own_low_ref, gain_ref, act_hbm, resid_out, normed_out = refs[8:14]
+    hid, weights, acc, act, sems, in_sems, out_sems = refs[14:]
     tiles, tile, _ = weights.shape
+    rows = own_ref.shape[0]
+    padded = hid.shape[0]
     copies = weight_copies(places_ref, w_hbm, weights, sems)
 
     def acc_in(t):
@@ -435,31 +496,34 @@
         for copy in copies(t):
             copy.start()
         acc_in(t).start()
-    squares, cross = statistics(hids, lows)
-    weight = hot_ref[...].astype(f32) * share_ref[...]
-    inner = jnp.sum((cross_ref[...] + cross) * weight, axis=1, keepdims=True)
+    part = rows // count
+    for n in range(count):
+        hid[n * part : (n + 1) * part] = hids[n][...]
+    hid[rows:] = jnp.zeros((padded - rows, hid.shape[1]), bf16)
+    squares, cross = statistics([hid.at[:rows]], [low_ref])
+    hot = hot_ref[:rows]
+    share = share_ref[:rows]
+    inner = jnp.sum((cross_ref[...] + cross) * hot.astype(f32), axis=1, keepdims=True) * share
     inv_rms = lax.rsqrt((squares_ref[...] + squares) / features + norm_eps)
-    lead = inv_rms * jnp.sum(weight, axis=1, keepdims=True)
+    lead = inv_rms * share
     pull = inv_rms * inv_rms * inv_rms * inner / features
-    own_low = dot(hot_ref[...], own_low_ref[...])
-    half = left_ref.shape[1]
-    for own_ref, at in ((left_ref, slice(0, half)), (right_ref, slice(half, 2 * half))):
-        own = own_ref[...].astype(f32)
-        resid_out[:, at] = (lead * own_low[:, at] - own * pull).astype(bf16)
-        normed_out[:, at] = (gain_ref[:, at] * own * inv_rms).astype(bf16)
-    width = hids[0].shape[1]
-    for n in range(count):
-        hid[:, n * width : (n + 1) * width] = hids[n][...]
+    own = own_ref[...].astype(f32)
+    resid_out[...] = (lead * dot(hot, own_low_ref[...]) - own * pull).astype(bf16)
+    normed_out[...] = (gain_ref[...] * own * inv_rms).astype(bf16)
+    same = iota((rows, padded), 0) == iota((rows, padded), 1)
+    lead = jnp.sum(jnp.where(same, lead, 0.0), axis=0, keepdims=True)
+    pull = jnp.sum(jnp.where(same, pull, 0.0), axis=0, keepdims=True)
 
     @pl.loop(0, tiles)
     def _(t):
+        at = pl.ds(pl.multiple_of(t * tile, tile), tile)
+        low_act = dot_t(low_act_ref[at], hot_ref[...])
         for copy in copies(t):
             copy.wait()
-        total = dot_t(hid[...], weights[t])
-        rows = pl.ds(pl.multiple_of(t * tile, tile), tile)
-        low_act = dot_t(hot_ref[...], low_act_ref[rows])
+        total = dot_t(weights[t], hid[...])
         acc_in(t).wait()
-        act[t] = (lead * low_act - pull * (total + acc[t])).astype(bf16)
+        turned = (lead * low_act - pull * (total + acc[t])).astype(bf16).T
+        act[t] = turned[:rows]
         act_out(t).start()
 
     @pl.loop(0, tiles)
@@ -469,10 +533,9 @@
 
 def finish(places, pieces, w_down, low, before, hot, share, low_act, own, gain):
     count = len(pieces)
-    rows, half = own[0].shape
-    width = 2 * half
+    rows, width = own.shape
     depth, features = w_down.shape
-    pairs = hot.shape[1]
+    padded, pairs = hot.shape
     tile = tile_of(depth, 512)
     tiles = depth // tile
     anywhere = pl.BlockSpec(memory_space=pl.ANY)
@@ -485,28 +548,27 @@
         grid_spec=pltpu.PrefetchScalarGridSpec(
             num_scalar_prefetch=1,
             grid=(1,),
-            in_specs=[whole((rows, half))] * count
-            + [pl.BlockSpec((pairs, half), lambda j, g, n=n: (0, g[n])) for n in range(count)]
+            in_specs=[whole((rows // count, width))] * count
             + [
+                pl.BlockSpec((pairs, width), lambda j, g: (0, g[0])),
                 anywhere,
                 anywhere,
                 whole((rows, 1)),
                 whole((rows, pairs)),
-                whole((rows, pairs)),
-                whole((1, pairs)),
+                whole((padded, pairs)),
+                whole((padded, 1)),
                 whole((depth, pairs)),
-                whole((rows, half)),
-                whole((rows, half)),
-                pl.BlockSpec((pairs, width), lambda j, g: (0, g[count])),
+                whole((rows, width)),
+                pl.BlockSpec((pairs, width), lambda j, g: (0, g[1])),
                 whole((1, width)),
             ],
             out_specs=[anywhere, whole((rows, width)), whole((rows, width))],
             scratch_shapes=[
-                pltpu.VMEM((rows, count * half), bf16),
-                pltpu.VMEM((tiles, tile, count * half), bf16),
-                pltpu.VMEM((tiles, rows, tile), f32),
+                pltpu.VMEM((padded, width), bf16),
+                pltpu.VMEM((tiles, tile, width), bf16),
+                pltpu.VMEM((tiles, tile, padded), f32),
                 pltpu.VMEM((tiles, rows, tile), bf16),
-                pltpu.SemaphoreType.DMA((tiles, count)),
+                pltpu.SemaphoreType.DMA((tiles, 1)),
                 pltpu.SemaphoreType.DMA((tiles,)),
                 pltpu.SemaphoreType.DMA((tiles,)),
             ],
@@ -518,19 +580,7 @@
         ],
         compiler_params=params(),
         cost_estimate=cost(2 * rows * depth * width, 2 * depth * width + 6 * rows * depth),
-    )(
-        places,
-        *pieces,
-        *[low] * count,
-        w_down,
-        *before,
-        hot,
-        share,
-        low_act,
-        *own,
-        low,
-        gain,
-    )
+    )(places, *pieces, low, w_down, *before, hot, share, low_act, own, low, gain)
 
 
 def low_rank_shards(
@@ -567,47 +617,31 @@
     own_term = project(blk[None], mlp_act, w_down, width, resid)
 
     low = lax.all_gather(low_own, "wide", axis=0, tiled=True)
-    tables = low[:, features:]
-    per_pair = tok_count // pairs
-    dest_all = tables[:, :per_pair].reshape(wide_count, tok_count)
-    len_all = tables[:, per_pair].reshape(wide_count, pairs)
-
-    packed = pack(destination, own_term, arrived, wide_count, slot_count)
-    packed = packed.reshape(wide_count, slot_count, width)
-    own_hid = lax.all_to_all(packed, "wide", split_axis=0, concat_axis=0, tiled=True)
-
+    packed = pack(wide, destination, own_term, arrived, wide_count, slot_count)
+    routed = [packed[k] if k == 0 else swap(packed[k], k, "wide") for k in range(wide_count)]
+    own = assemble(wide, routed)
+
+    padded = -(-rows // lane) * lane
     low_act = low_activations(low, features, w_down)
-    hot = slot_passages(wide, dest_all, len_all, rows)
-    share = (1.0 / len_all.astype(f32)).reshape(1, wide_count * pairs)
-
-    low_act, hot, share, own_hid = lax.optimization_barrier((low_act, hot, share, own_hid))
-    own_hid = own_hid.reshape(rows, width)
-    left, right = own_hid[:, : width // 2], own_hid[:, width // 2 :]
-    left_1, right_2 = swap(left, 1), swap(right, 2)
-    right_1, left_2 = swap(right, 1), swap(left, 2)
-    left_3, right_3 = swap(left_1, 2), swap(right_2, 1)
-
-    def places(*pieces):
-        return jnp.stack([(blk ^ k) * 2 + side for k, side in pieces])
-
-    totals = back(places((0, 0), (0, 1)), [left, right], w_down, low)
-    totals = back(
-        places((1, 0), (2, 1), (1, 1), (2, 0)),
-        [left_1, right_2, right_1, left_2],
-        w_down,
-        low,
-        totals,
-    )
+    hot, share = slot_passages(wide, low, features, wide_count, slot_count, padded)
+
+    beside, above = swap(own, 1), swap(own, 2)
+    top = swap(beside[: rows // 2], 2)
+    bottom = swap(above[rows // 2 :], 1)
+    low_act, hot, share, beside, above = lax.optimization_barrier(
+        (low_act, hot, share, beside, above)
+    )
+    totals = back(blk ^ jnp.arange(3, dtype=i32), [own, beside, above], w_down, low, padded)
     act_grad, resid_grad, normed_out = finish(
-        jnp.concatenate([places((3, 0), (3, 1)), blk[None]]),
-        [left_3, right_3],
+        jnp.stack([blk ^ 3, blk]),
+        [top, bottom],
         w_down,
         low,
         totals,
         hot,
         share,
         low_act,
-        [left, right],
+        own,
         gain[None],
     )
     return (query_grad, resid_grad, act_grad, normed_out)

time: 119 us -> 128 us (1.076); the launches traced: 119 us -> 126 us
  waiting for transfers between devices: 13.3 us -> 27.8 us
  local copies, waits for them, and re-layouts: 13 us -> 7.24 us
  other arithmetic: 2.6 us -> 0.08 us
    ppermute x12 -> x17, waiting for transfers between devices: 9.54 us -> 27.8 us  [swap(): lax.ppermute(rows, axis, [(i, i ^ k) for i in range(lax.axis_size(axis))])]
    ppermute x12 -> x17, starting transfers between devices: 14.8 us -> 20.5 us  [swap(): lax.ppermute(rows, axis, [(i, i ^ k) for i in range(lax.axis_size(axis))])]
    all_to_all x1 -> x0, starting transfers between devices: 5.11 us -> none  [low_rank_shards(): lax.all_to_all(packed, 'wide', split_axis=0, concat_axis=0, tiled=True)]
    all_to_all x1 -> x0, waiting for transfers between devices: 3.71 us -> none  [low_rank_shards(): lax.all_to_all(packed, 'wide', split_axis=0, concat_axis=0, tiled=True)]
    reshape x6 -> x0, local copies, waits for them, and re-layouts: 2.86 us -> none  [the longest x1 0.95 us: low_rank_shards(): packed = packed.reshape(wide_count, slot_count, width)]
    slice x3 -> x2, local copies, waits for them, and re-layouts: 2.78 us -> 0.04 us  [the longest x1 0.02 us: low_rank_shards(): bottom = swap(above[rows // 2:], 1)]
    pallas_call x4, Pallas kernels: 20.3 us -> 18.1 us  [the longest x1 14.8 us: back(): pl.pallas_call(lambda *refs: back_body(count, *refs), grid_spec=pltpu.Pre...]
    pallas_call x1, Pallas kernels: 9.24 us -> 11.2 us  [finish(): pl.pallas_call(lambda *refs: finish_body(features, count, *refs), grid_sp...]
  transfers between devices with their start and end apart: 14 -> 18, of which waited for: 4 -> 3; matrix products, arithmetic and copies ran while one was open for 6% -> 0% of each run, Pallas kernels for 38% -> 34%
where the time goes in v5:
time: 128 us; the launch traced here: 126 us
  Pallas kernels  56.1 us (44%)
  waiting for transfers between devices  27.8 us (22%)
  starting transfers between devices  20.6 us (16%)
  between operations  14.3 us (11%)
  local copies, waits for them, and re-layouts  7.24 us (6%)
    ppermute x17, waiting for transfers between devices, swap(): lax.ppermute(rows, axis, [(i, i ^ k) for i in range(lax.axis_size(axis))])  27.8 us
    ppermute x17, starting transfers between devices, swap(): lax.ppermute(rows, axis, [(i, i ^ k) for i in range(lax.axis_size(axis))])  20.5 us
    pallas_call x4, Pallas kernels, project(): pl.pallas_call(lambda *refs: project_body(len(own), *refs), in_specs=[pl....  15.6 us
    pallas_call x1, Pallas kernels, back(): pl.pallas_call(lambda *refs: back_body(count, *refs), grid_spec=pltpu.Pre...  14.8 us
    pallas_call x1, Pallas kernels, finish(): pl.pallas_call(lambda *refs: finish_body(features, count, *refs), grid_sp...  11.2 us
    pallas_call x1, Pallas kernels, low_activations(): pl.pallas_call(low_act_body, grid=(1,), in_specs=[pl.BlockSpec((pairs, fe...  9.78 us
    unnamed x28, local copies, waits for them, and re-layouts  7.2 us
  transfers between devices with their start and end apart: 18, of which 3 were waited for; matrix products, arithmetic and copies ran while one was open for 0% of the time, Pallas kernels for 34%

profile of v5, /device:TPU:0, one launch (start us, length us, event | category | flops | bytes accessed | tf_op | source)
XLA Modules:
  0.0 126.1 jit_solution(12402841022190398498)
XLA Ops:
  7.2 0.0 all-gather.2.cloned.1.call-start
  7.2 0.7 copy-done.6
  8.0 0.8 copy-done.7
  8.7 0.7 copy-done.8
  9.4 4.0 %collective-permute-start.2 = (bf16[4,8704]{1,0:T(4,128)(2,1)S(1)}, bf16[4,8704]{1,0:T(4,128)(2,1)S(1)}, u32[]{:S(2)}, u32[]{:S(2)}) collective-permute-start(bf16[4,8704]{1,0:T(4,128)(2,1)S(1)} %shard_map.130.refs_1_), channel_id=1, source_target_pairs={{0,3},{1,2},{2,1},{3,0},{4,7},{5,6},{6,5},{7,4},{8,11},{9,10},{10,... | collective-permute-start | bytes 208904 | tf_op jit(solution)/shard_map/ppermute | solution.py:45
  13.4 0.5 collective-permute-start.1
  13.9 0.1 collective-permute-start
  14.0 1.3 %copy-done.2 = bf16[192,3072]{1,0:T(8,128)(2,1)S(1)} copy-done((bf16[192,3072]{1,0:T(8,128)(2,1)S(1)}, bf16[192,3072]{1,0:T(8,128)(2,1)}, u32[]{:S(2)}) %copy-start.2) | copy-done | bytes 1179672
  15.3 3.8 %shard_map.129 = bf16[192,1024]{1,0:T(8,128)(2,1)S(1)} custom-call(s32[1]{0:T(128)} %bitcast.1.refs_0_, bf16[192,3072]{1,0:T(8,128)(2,1)S(1)} %copy-done.2, bf16[3072,4096]{1,0:T(8,128)(2,1)} %refs_4_.1), custom_call_target="tpu_custom_call" | custom-call | flops 1207959552 | bytes 7471104 | tf_op jit(solution)/shard_map/pallas_call | solution.py:83
  19.1 0.0 collective-permute-done.2.refs_4_
  19.1 0.0 collective-permute-done.1.refs_3_
  19.2 1.5 %shard_map.131 = (bf16[4,4096]{1,0:T(4,128)(2,1)}, bf16[16,4224]{1,0:T(8,128)(2,1)}) custom-call(s32[1]{0:T(128)} %bitcast.refs_0_, bf16[4,8704]{1,0:T(4,128)(2,1)S(1)} %shard_map.130.refs_1_, bf16[4,8704]{1,0:T(4,128)(2,1)S(1)} %collective-permute-done.refs_2_, bf16[4,8704]{1,0:T(4,128)(2,1)S(1)} %collective-permute-done.1.refs_3_, ...), custom_call_target="tpu_custom_call" | custom-call | flops 8388608 | bytes 524288 | tf_op jit(solution)/shard_map/pallas_call | solution.py:183
  20.7 0.0 all-gather.2.cloned.1.call-update
  20.8 2.9 %collective-permute-start.3 = (bf16[192,1024]{1,0:T(8,128)(2,1)S(1)}, bf16[192,1024]{1,0:T(8,128)(2,1)S(1)}, u32[]{:S(2)}, u32[]{:S(2)}) collective-permute-start(bf16[192,1024]{1,0:T(8,128)(2,1)S(1)} %shard_map.129), channel_id=1, source_target_pairs={{0,3},{1,2},{2,1},{3,0},{4,7},{5,6},{6,5},{7,4},{8,11},{9,10},{10,... | collective-permute-start | bytes 1179656 | tf_op jit(solution)/shard_map/ppermute | solution.py:45
  23.7 3.6 %shard_map.134 = bf16[192,1024]{1,0:T(8,128)(2,1)S(1)} custom-call(s32[1]{0:T(128)} %bitcast.8.refs_0_, bf16[192,3072]{1,0:T(8,128)(2,1)S(1)} %copy-done.3, bf16[3072,4096]{1,0:T(8,128)(2,1)} %refs_4_.1), custom_call_target="tpu_custom_call" | custom-call | flops 1207959552 | bytes 7471104 | tf_op jit(solution)/shard_map/pallas_call | solution.py:83
  27.3 0.0 copy-start.5
  27.3 4.5 %shard_map.133 = bf16[192,1024]{1,0:T(8,128)(2,1)} custom-call(s32[1]{0:T(128)} %bitcast.7.refs_0_, bf16[192,3072]{1,0:T(8,128)(2,1)S(1)} %copy-done.3, bf16[3072,4096]{1,0:T(8,128)(2,1)} %refs_4_.1), custom_call_target="tpu_custom_call" | custom-call | flops 1207959552 | bytes 7471104 | tf_op jit(solution)/shard_map/pallas_call | solution.py:83
  31.8 0.5 collective-permute-start.4
  32.3 0.1 collective-permute-start.5
  32.4 3.7 %shard_map.132.refs_2_ = f32[192,1024]{1,0:T(8,128)S(1)} custom-call(s32[1]{0:T(128)} %bitcast.refs_0_, bf16[192,3072]{1,0:T(8,128)(2,1)S(1)} %copy-done.3, bf16[3072,4096]{1,0:T(8,128)(2,1)} %refs_4_.1, bf16[192,1024]{1,0:T(8,128)(2,1)S(1)} %copy-done.5), custom_call_target="tpu_custom_call" | custom-call | flops 1207959552 | bytes 7471104 | tf_op jit(solution)/shard_map/pallas_call | solution.py:83
  36.1 0.0 collective-permute-done.3.refs_3_
  36.1 5.6 %collective-permute-done.4.refs_4_ = bf16[192,1024]{1,0:T(8,128)(2,1)S(1)} collective-permute-done((bf16[192,1024]{1,0:T(8,128)(2,1)}, bf16[192,1024]{1,0:T(8,128)(2,1)S(1)}, u32[]{:S(2)}, u32[]{:S(2)}) %collective-permute-start.4) | collective-permute-done | bytes 393248 | tf_op jit(solution)/shard_map/ppermute | solution.py:45
  41.7 0.0 collective-permute-done.5.refs_5_
  41.8 1.1 shard_map.135
  42.8 0.1 collective-permute-start.6
  42.9 1.6 %collective-permute-start.7 = (bf16[36,1024]{1,0:T(8,128)(2,1)S(1)}, bf16[36,1024]{1,0:T(8,128)(2,1)S(1)}, u32[]{:S(2)}, u32[]{:S(2)}) collective-permute-start(bf16[36,1024]{1,0:T(8,128)(2,1)S(1)} %get-tuple-element.41), channel_id=1, source_target_pairs={{0,8},{4,12},{8,0},{12,4},{16,24},{20,28},{24,16},{28,20},{1,9},{5... | collective-permute-start | bytes 221192 | tf_op jit(solution)/shard_map/ppermute | solution.py:45
  44.6 0.2 collective-permute-start.8
  44.8 2.6 %collective-permute-start.9 = (bf16[36,1024]{1,0:T(8,128)(2,1)S(1)}, bf16[36,1024]{1,0:T(8,128)(2,1)S(1)}, u32[]{:S(2)}, u32[]{:S(2)}) collective-permute-start(bf16[36,1024]{1,0:T(8,128)(2,1)S(1)} %get-tuple-element.43), channel_id=1, source_target_pairs={{0,16},{4,20},{8,24},{12,28},{16,0},{20,4},{24,8},{28,12},{1,17},{... | collective-permute-start | bytes 221192 | tf_op jit(solution)/shard_map/ppermute | solution.py:45
  47.4 0.0 collective-permute-start.10
  47.4 3.6 %collective-permute-start.11 = (bf16[36,1024]{1,0:T(8,128)(2,1)S(1)}, bf16[36,1024]{1,0:T(8,128)(2,1)S(1)}, u32[]{:S(2)}, u32[]{:S(2)}) collective-permute-start(bf16[36,1024]{1,0:T(8,128)(2,1)S(1)} %get-tuple-element.45), channel_id=1, source_target_pairs={{0,24},{4,28},{8,16},{12,20},{16,8},{20,12},{24,0},{28,4},{1,25},{... | collective-permute-start | bytes 221192 | tf_op jit(solution)/shard_map/ppermute | solution.py:45
  51.0 0.0 collective-permute-done.7.refs_2_
  51.0 0.1 collective-permute-start.12
  51.1 8.8 %collective-permute-done.10.refs_5_ = bf16[36,1024]{1,0:T(8,128)(2,1)S(1)} collective-permute-done((bf16[36,1024]{1,0:T(8,128)(2,1)S(1)}, bf16[36,1024]{1,0:T(8,128)(2,1)S(1)}, u32[]{:S(2)}, u32[]{:S(2)}) %collective-permute-start.10) | collective-permute-done | bytes 73760 | tf_op jit(solution)/shard_map/ppermute | solution.py:45
  59.9 1.3 %shard_map.136.refs_1_.refs_11_ = bf16[288,1024]{1,0:T(8,128)(2,1)S(1)} custom-call(s32[1]{0:T(128)} %bitcast.6.refs_0_.wide_ref, bf16[36,1024]{1,0:T(8,128)(2,1)S(1)} %get-tuple-element.39.refs_0_, bf16[36,1024]{1,0:T(8,128)(2,1)S(1)} %collective-permute-done.6.refs_1_, bf16[36,1024]{1,0:T(8,128)(2,1)S(1)} %collective-permute-done.7.refs_2_, ...), custom_call_target="tpu_custom_call" | custom-call | flops 169869312 | bytes 1179648 | tf_op jit(solution)/shard_map/pallas_call | solution.py:266
  61.2 0.6 collective-permute-start.15
  61.8 1.5 %collective-permute-start.13 = (bf16[288,1024]{1,0:T(8,128)(2,1)S(1)}, bf16[288,1024]{1,0:T(8,128)(2,1)S(1)}, u32[]{:S(2)}, u32[]{:S(2)}) collective-permute-start(bf16[288,1024]{1,0:T(8,128)(2,1)S(1)} %shard_map.136.refs_1_.refs_11_), channel_id=1, source_target_pairs={{0,1},{1,0},{2,3},{3,2},{4,5},{5,4},{6,7},{7,6},{8,9},{9,8},{10,11... | collective-permute-start | bytes 1769480 | tf_op jit(solution)/shard_map/ppermute | solution.py:45
  63.3 0.1 pad_add_fusion.refs_0_
  63.4 13.3 %collective-permute-done.15.refs_3_ = bf16[288,1024]{1,0:T(8,128)(2,1)S(1)} collective-permute-done((bf16[288,1024]{1,0:T(8,128)(2,1)S(1)}, bf16[288,1024]{1,0:T(8,128)(2,1)S(1)}, u32[]{:S(2)}, u32[]{:S(2)}) %collective-permute-start.15) | collective-permute-done | bytes 589856 | tf_op jit(solution)/shard_map/ppermute | solution.py:45
  76.7 1.6 %collective-permute-start.16 = (bf16[144,1024]{1,0:T(8,128)(2,1)S(1)}, bf16[144,1024]{1,0:T(8,128)(2,1)S(1)}, u32[]{:S(2)}, u32[]{:S(2)}) collective-permute-start(bf16[144,1024]{1,0:T(8,128)(2,1)S(1)} %slice.9), channel_id=1, source_target_pairs={{0,1},{1,0},{2,3},{3,2},{4,5},{5,4},{6,7},{7,6},{8,9},{9,8},{10,11... | collective-permute-start | bytes 884744 | tf_op jit(solution)/shard_map/ppermute | solution.py:45
  78.3 0.6 collective-permute-start.14
  78.9 1.2 copy-done
  80.1 0.9 shard_map.138
  81.0 0.3 copy-done.1
  81.3 9.8 %shard_map.137.refs_10_ = bf16[3072,128]{1,0:T(8,128)(2,1)S(1)} custom-call(bf16[128,4224]{1,0:T(8,128)(2,1)S(1)} %copy-done.1, bf16[3072,4096]{1,0:T(8,128)(2,1)} %refs_4_.1), custom_call_target="tpu_custom_call" | custom-call | flops 3221225472 | bytes 25165824 | tf_op jit(solution)/shard_map/pallas_call | solution.py:364
  91.1 0.0 copy-start.9
  91.1 14.8 %shard_map.139 = (f32[6,512,384]{2,1,0:T(8,128)S(1)}, f32[288,1]{1,0:T(8,128)S(1)}, f32[288,128]{1,0:T(8,128)S(1)}) custom-call(s32[3]{0:T(128)S(1)} %iota_xor_fusion.refs_0_, bf16[288,1024]{1,0:T(8,128)(2,1)S(1)} %shard_map.136.refs_1_.refs_11_, bf16[288,1024]{1,0:T(8,128)(2,1)S(1)} %collective-permute-done.13.refs_2_, ...), custom_call_target="tpu_custom_call" | custom-call | flops 5435817984 | bytes 18874368 | tf_op jit(solution)/shard_map/pallas_call | solution.py:447
  105.9 2.1 %copy-done.4 = f32[6,512,384]{2,1,0:T(8,128)} copy-done((f32[6,512,384]{2,1,0:T(8,128)}, f32[6,512,384]{2,1,0:T(8,128)S(1)}, u32[]{:S(2)}) %copy-start.4) | copy-done | bytes 4718616
  108.1 11.2 %shard_map.140 = (bf16[288,3072]{1,0:T(8,128)(2,1)}, bf16[288,1024]{1,0:T(8,128)(2,1)}, bf16[288,1024]{1,0:T(8,128)(2,1)}) custom-call(s32[2]{0:T(128)S(1)} %pad_add_fusion.refs_0_, bf16[144,1024]{1,0:T(8,128)(2,1)S(1)} %collective-permute-done.14.refs_1_, bf16[144,1024]{1,0:T(8,128)(2,1)S(1)} %collective-permute-done.16.refs_2_, ...), custom_call_target="tpu_custom_call" | custom-call | flops 1811939328 | bytes 11599872 | tf_op jit(solution)/shard_map/pallas_call | solution.py:546
  (33 shorter events, 0.1 us)
Async XLA Ops:
  7.2 71.7 %all-gather.2.cloned.1.call-start = ((), (), s32[]{:S(2)}) async-start(), calls=%async_computation | async-start | bytes 1216512 | tf_op jit(solution)/shard_map/all_gather | solution.py:619
  7.2 0.8 copy-start.6
  8.0 0.8 copy-start.7
  8.7 0.7 copy-start.8
  9.4 9.7 %collective-permute-start.2 = (bf16[4,8704]{1,0:T(4,128)(2,1)S(1)}, bf16[4,8704]{1,0:T(4,128)(2,1)S(1)}, u32[]{:S(2)}, u32[]{:S(2)}) collective-permute-start(bf16[4,8704]{1,0:T(4,128)(2,1)S(1)} %shard_map.130.refs_1_), channel_id=1, source_target_pairs={{0,3},{1,2},{2,1},{3,0},{4,7},{5,6},{6,5},{7,4},{8,11},{9,10},{10,... | collective-permute-start | bytes 208904 | tf_op jit(solution)/shard_map/ppermute | solution.py:45
  13.4 5.8 %collective-permute-start.1 = (bf16[4,8704]{1,0:T(4,128)(2,1)S(1)}, bf16[4,8704]{1,0:T(4,128)(2,1)S(1)}, u32[]{:S(2)}, u32[]{:S(2)}) collective-permute-start(bf16[4,8704]{1,0:T(4,128)(2,1)S(1)} %shard_map.130.refs_1_), channel_id=1, source_target_pairs={{0,2},{1,3},{2,0},{3,1},{4,6},{5,7},{6,4},{7,5},{8,10},{9,11},{10,... | collective-permute-start | bytes 208904 | tf_op jit(solution)/shard_map/ppermute | solution.py:45
  13.9 5.3 %collective-permute-start = (bf16[4,8704]{1,0:T(4,128)(2,1)S(1)}, bf16[4,8704]{1,0:T(4,128)(2,1)S(1)}, u32[]{:S(2)}, u32[]{:S(2)}) collective-permute-start(bf16[4,8704]{1,0:T(4,128)(2,1)S(1)} %shard_map.130.refs_1_), channel_id=1, source_target_pairs={{0,1},{1,0},{2,3},{3,2},{4,5},{5,4},{6,7},{7,6},{8,9},{9,8},{10,11... | collective-permute-start | bytes 208904 | tf_op jit(solution)/shard_map/ppermute | solution.py:45
  14.0 1.3 %copy-start.2 = (bf16[192,3072]{1,0:T(8,128)(2,1)S(1)}, bf16[192,3072]{1,0:T(8,128)(2,1)}, u32[]{:S(2)}) copy-start(bf16[192,3072]{1,0:T(8,128)(2,1)} %refs_1_.4) | copy-start | bytes 3538948
  15.3 3.9 %copy-start.10 = (s32[192,1]{0,1:T(1,128)S(1)}, s32[192,1]{0,1:T(1,128)}, u32[]{:S(2)}) copy-start(s32[192,1]{0,1:T(1,128)} %param.15) | copy-start | bytes 2308
  15.3 3.9 %copy-start.11 = (f32[16]{0:T(128)S(1)}, f32[16]{0:T(128)}, u32[]{:S(2)}) copy-start(f32[16]{0:T(128)} %param.12) | copy-start | bytes 196
  15.3 3.9 %copy-start.12 = (s32[16]{0:T(128)S(1)}, s32[16]{0:T(128)}, u32[]{:S(2)}) copy-start(s32[16]{0:T(128)} %param.13) | copy-start | bytes 196
  15.3 3.9 %copy-start.13 = (s32[1,16]{1,0:T(1,128)S(1)}, s32[1,16]{1,0:T(1,128)}, u32[]{:S(2)}) copy-start(s32[1,16]{1,0:T(1,128)} %refs_8_.1) | copy-start | bytes 196
  15.3 8.3 %copy-start.3 = (bf16[192,3072]{1,0:T(8,128)(2,1)S(1)}, bf16[192,3072]{1,0:T(8,128)(2,1)}, u32[]{:S(2)}) copy-start(bf16[192,3072]{1,0:T(8,128)(2,1)} %refs_1_.4) | copy-start | bytes 3538948
  20.8 15.3 %collective-permute-start.3 = (bf16[192,1024]{1,0:T(8,128)(2,1)S(1)}, bf16[192,1024]{1,0:T(8,128)(2,1)S(1)}, u32[]{:S(2)}, u32[]{:S(2)}) collective-permute-start(bf16[192,1024]{1,0:T(8,128)(2,1)S(1)} %shard_map.129), channel_id=1, source_target_pairs={{0,3},{1,2},{2,1},{3,0},{4,7},{5,6},{6,5},{7,4},{8,11},{9,10},{10,... | collective-permute-start | bytes 1179656 | tf_op jit(solution)/shard_map/ppermute | solution.py:45
  27.3 5.1 %copy-start.5 = (bf16[192,1024]{1,0:T(8,128)(2,1)S(1)}, bf16[192,1024]{1,0:T(8,128)(2,1)}, u32[]{:S(2)}) copy-start(bf16[192,1024]{1,0:T(8,128)(2,1)} %refs_3_.1) | copy-start | bytes 1179652
  31.8 9.9 %collective-permute-start.4 = (bf16[192,1024]{1,0:T(8,128)(2,1)}, bf16[192,1024]{1,0:T(8,128)(2,1)S(1)}, u32[]{:S(2)}, u32[]{:S(2)}) collective-permute-start(bf16[192,1024]{1,0:T(8,128)(2,1)} %shard_map.133), channel_id=1, source_target_pairs={{0,1},{1,0},{2,3},{3,2},{4,5},{5,4},{6,7},{7,6},{8,9},{9,8},{10,11... | collective-permute-start | bytes 1179656 | tf_op jit(solution)/shard_map/ppermute | solution.py:45
  32.3 9.4 %collective-permute-start.5 = (bf16[192,1024]{1,0:T(8,128)(2,1)S(1)}, bf16[192,1024]{1,0:T(8,128)(2,1)S(1)}, u32[]{:S(2)}, u32[]{:S(2)}) collective-permute-start(bf16[192,1024]{1,0:T(8,128)(2,1)S(1)} %shard_map.134), channel_id=1, source_target_pairs={{0,2},{1,3},{2,0},{3,1},{4,6},{5,7},{6,4},{7,5},{8,10},{9,11},{10,... | collective-permute-start | bytes 1179656 | tf_op jit(solution)/shard_map/ppermute | solution.py:45
  42.8 4.6 %collective-permute-start.6 = (bf16[36,1024]{1,0:T(8,128)(2,1)S(1)}, bf16[36,1024]{1,0:T(8,128)(2,1)S(1)}, u32[]{:S(2)}, u32[]{:S(2)}) collective-permute-start(bf16[36,1024]{1,0:T(8,128)(2,1)S(1)} %get-tuple-element.40), channel_id=1, source_target_pairs={{0,4},{4,0},{8,12},{12,8},{16,20},{20,16},{24,28},{28,24},{1,5},{5... | collective-permute-start | bytes 221192 | tf_op jit(solution)/shard_map/ppermute | solution.py:45
  42.9 8.1 %collective-permute-start.7 = (bf16[36,1024]{1,0:T(8,128)(2,1)S(1)}, bf16[36,1024]{1,0:T(8,128)(2,1)S(1)}, u32[]{:S(2)}, u32[]{:S(2)}) collective-permute-start(bf16[36,1024]{1,0:T(8,128)(2,1)S(1)} %get-tuple-element.41), channel_id=1, source_target_pairs={{0,8},{4,12},{8,0},{12,4},{16,24},{20,28},{24,16},{28,20},{1,9},{5... | collective-permute-start | bytes 221192 | tf_op jit(solution)/shard_map/ppermute | solution.py:45
  44.6 6.5 %collective-permute-start.8 = (bf16[36,1024]{1,0:T(8,128)(2,1)S(1)}, bf16[36,1024]{1,0:T(8,128)(2,1)S(1)}, u32[]{:S(2)}, u32[]{:S(2)}) collective-permute-start(bf16[36,1024]{1,0:T(8,128)(2,1)S(1)} %get-tuple-element.42), channel_id=1, source_target_pairs={{0,12},{4,8},{8,4},{12,0},{16,28},{20,24},{24,20},{28,16},{1,13},{... | collective-permute-start | bytes 221192 | tf_op jit(solution)/shard_map/ppermute | solution.py:45
  44.8 6.3 %collective-permute-start.9 = (bf16[36,1024]{1,0:T(8,128)(2,1)S(1)}, bf16[36,1024]{1,0:T(8,128)(2,1)S(1)}, u32[]{:S(2)}, u32[]{:S(2)}) collective-permute-start(bf16[36,1024]{1,0:T(8,128)(2,1)S(1)} %get-tuple-element.43), channel_id=1, source_target_pairs={{0,16},{4,20},{8,24},{12,28},{16,0},{20,4},{24,8},{28,12},{1,17},{... | collective-permute-start | bytes 221192 | tf_op jit(solution)/shard_map/ppermute | solution.py:45
  47.4 12.5 %collective-permute-start.10 = (bf16[36,1024]{1,0:T(8,128)(2,1)S(1)}, bf16[36,1024]{1,0:T(8,128)(2,1)S(1)}, u32[]{:S(2)}, u32[]{:S(2)}) collective-permute-start(bf16[36,1024]{1,0:T(8,128)(2,1)S(1)} %get-tuple-element.44), channel_id=1, source_target_pairs={{0,20},{4,16},{8,28},{12,24},{16,4},{20,0},{24,12},{28,8},{1,21},{... | collective-permute-start | bytes 221192 | tf_op jit(solution)/shard_map/ppermute | solution.py:45
  47.4 12.5 %collective-permute-start.11 = (bf16[36,1024]{1,0:T(8,128)(2,1)S(1)}, bf16[36,1024]{1,0:T(8,128)(2,1)S(1)}, u32[]{:S(2)}, u32[]{:S(2)}) collective-permute-start(bf16[36,1024]{1,0:T(8,128)(2,1)S(1)} %get-tuple-element.45), channel_id=1, source_target_pairs={{0,24},{4,28},{8,16},{12,20},{16,8},{20,12},{24,0},{28,4},{1,25},{... | collective-permute-start | bytes 221192 | tf_op jit(solution)/shard_map/ppermute | solution.py:45
  51.0 8.9 %collective-permute-start.12 = (bf16[36,1024]{1,0:T(8,128)(2,1)S(1)}, bf16[36,1024]{1,0:T(8,128)(2,1)S(1)}, u32[]{:S(2)}, u32[]{:S(2)}) collective-permute-start(bf16[36,1024]{1,0:T(8,128)(2,1)S(1)} %get-tuple-element.46), channel_id=1, source_target_pairs={{0,28},{4,24},{8,20},{12,16},{16,12},{20,8},{24,4},{28,0},{1,29},{... | collective-permute-start | bytes 221192 | tf_op jit(solution)/shard_map/ppermute | solution.py:45
  61.2 15.4 %collective-permute-start.15 = (bf16[288,1024]{1,0:T(8,128)(2,1)S(1)}, bf16[288,1024]{1,0:T(8,128)(2,1)S(1)}, u32[]{:S(2)}, u32[]{:S(2)}) collective-permute-start(bf16[288,1024]{1,0:T(8,128)(2,1)S(1)} %shard_map.136.refs_1_.refs_11_), channel_id=1, source_target_pairs={{0,2},{1,3},{2,0},{3,1},{4,6},{5,7},{6,4},{7,5},{8,10},{9,11},{10,... | collective-permute-start | bytes 1769480 | tf_op jit(solution)/shard_map/ppermute | solution.py:45
  61.8 16.4 %collective-permute-start.13 = (bf16[288,1024]{1,0:T(8,128)(2,1)S(1)}, bf16[288,1024]{1,0:T(8,128)(2,1)S(1)}, u32[]{:S(2)}, u32[]{:S(2)}) collective-permute-start(bf16[288,1024]{1,0:T(8,128)(2,1)S(1)} %shard_map.136.refs_1_.refs_11_), channel_id=1, source_target_pairs={{0,1},{1,0},{2,3},{3,2},{4,5},{5,4},{6,7},{7,6},{8,9},{9,8},{10,11... | collective-permute-start | bytes 1769480 | tf_op jit(solution)/shard_map/ppermute | solution.py:45
  76.7 31.3 %collective-permute-start.16 = (bf16[144,1024]{1,0:T(8,128)(2,1)S(1)}, bf16[144,1024]{1,0:T(8,128)(2,1)S(1)}, u32[]{:S(2)}, u32[]{:S(2)}) collective-permute-start(bf16[144,1024]{1,0:T(8,128)(2,1)S(1)} %slice.9), channel_id=1, source_target_pairs={{0,1},{1,0},{2,3},{3,2},{4,5},{5,4},{6,7},{7,6},{8,9},{9,8},{10,11... | collective-permute-start | bytes 884744 | tf_op jit(solution)/shard_map/ppermute | solution.py:45
  78.3 29.8 %collective-permute-start.14 = (bf16[144,1024]{1,0:T(8,128)(2,1)S(1)}, bf16[144,1024]{1,0:T(8,128)(2,1)S(1)}, u32[]{:S(2)}, u32[]{:S(2)}) collective-permute-start(bf16[144,1024]{1,0:T(8,128)(2,1)S(1)} %slice.8), channel_id=1, source_target_pairs={{0,2},{1,3},{2,0},{3,1},{4,6},{5,7},{6,4},{7,5},{8,10},{9,11},{10,... | collective-permute-start | bytes 884744 | tf_op jit(solution)/shard_map/ppermute | solution.py:45
  78.9 1.2 copy-start
  80.1 1.2 copy-start.1
  91.1 16.9 %copy-start.9 = (f32[1024]{0:T(1024)S(1)}, f32[1024]{0:T(1024)}, u32[]{:S(2)}) copy-start(f32[1024]{0:T(1024)} %param.19) | copy-start | bytes 12292
  105.9 2.2 %copy-start.4 = (f32[6,512,384]{2,1,0:T(8,128)}, f32[6,512,384]{2,1,0:T(8,128)S(1)}, u32[]{:S(2)}) copy-start(f32[6,512,384]{2,1,0:T(8,128)S(1)} %get-tuple-element.51.refs_5_) | copy-start | bytes 14155780
Sparse Core Ops, SparseCore 0:
  20.9 23.9 all-gather.1

commit v6 on v5

--- a/solution.py
+++ b/solution.py
@@ -381,164 +381,123 @@
 
 def statistics(hids, lows):
     squares, cross = 0.0, 0.0
-    for hid_ref, low_ref in zip(hids, lows):
-        hid = hid_ref[...].astype(f32)
-        squares = squares + jnp.sum(hid * hid, axis=1, keepdims=True)
-        cross = cross + dot_t(hid_ref[...], low_ref[...])
+    for hid, low_ref in zip(hids, lows):
+        wide_hid = hid.astype(f32)
+        squares = squares + jnp.sum(wide_hid * wide_hid, axis=1, keepdims=True)
+        cross = cross + dot_t(hid, low_ref[...])
     return squares, cross
 
 
-def weight_copies(places_ref, w_hbm, weights, sems):
-    count, tile, across = weights.shape
-    groups = sems.shape[1]
-    width = across // groups
-
-    def copies(t):
-        rows = pl.ds(pl.multiple_of(t * tile, tile), tile)
-        return [
-            pltpu.make_async_copy(
-                w_hbm.at[rows, pl.ds(pl.multiple_of(places_ref[n] * width, lane), width)],
-                weights.at[t, :, n * width : (n + 1) * width],
-                sems.at[t, n],
-            )
-            for n in range(groups)
-        ]
-
-    return copies
-
-
-def back_body(count, places_ref, *refs):
-    hids, lows, w_hbm, refs = refs[:count], refs[count : 2 * count], refs[2 * count], refs[2 * count + 1 :]
-    acc_hbm, squares_ref, cross_ref, hid, weights, acc, sems, out_sems = refs
-    copies = weight_copies(places_ref, w_hbm, weights, sems)
-    rows, width = hids[0].shape
-
-    def acc_out(t):
-        return pltpu.make_async_copy(acc.at[t], acc_hbm.at[t], out_sems.at[t])
-
-    for t in range(weights.shape[0]):
-        for copy in copies(t):
-            copy.start()
-    for n in range(count):
-        hid[:rows, n * width : (n + 1) * width] = hids[n][...]
-    hid[rows:] = jnp.zeros((hid.shape[0] - rows, count * width), bf16)
-    squares_ref[...], cross_ref[...] = statistics(hids, lows)
-
-    @pl.loop(0, weights.shape[0])
-    def _(t):
-        for copy in copies(t):
-            copy.wait()
-        acc[t] = dot_t(weights[t], hid[...])
-        acc_out(t).start()
-
-    @pl.loop(0, weights.shape[0])
-    def _(t):
-        acc_out(t).wait()
-
-
-def back(places, pieces, w_down, low, padded):
+def product(hids, weights):
+    total = 0.0
+    for hid, w_ref in zip(hids, weights):
+        total = total + dot_t(hid, w_ref[...])
+    return total
+
+
+def group_specs(count, rows_of_block, width, row_step):
+    half = width // 2
+    return [
+        pl.BlockSpec(
+            (rows_of_block, half), lambda j, g, n=n, side=side: (row_step * j, 2 * g[n] + side)
+        )
+        for n in range(count)
+        for side in range(2)
+    ]
+
+
+def halves_of(ref):
+    half = ref.shape[1] // 2
+    return [ref[:, :half], ref[:, half:]]
+
+
+def back_body(count, carried, places_ref, *refs):
+    hids, refs = refs[:count], refs[count:]
+    weights, lows, refs = refs[: 2 * count], refs[2 * count : 4 * count], refs[4 * count :]
+    before, (acc_ref, squares_ref, cross_ref) = refs[:carried], refs[carried:]
+    halves = [half for hid in hids for half in halves_of(hid)]
+
+    @pl.when(pl.program_id(0) == 0)
+    def _():
+        squares, cross = statistics(halves, lows)
+        if carried:
+            squares, cross = before[1][...] + squares, before[2][...] + cross
+        squares_ref[...], cross_ref[...] = squares, cross
+
+    total = product(halves, weights)
+    acc_ref[...] = before[0][...] + total if carried else total
+
+
+def carried_specs(rows, pairs, tile):
+    return [
+        pl.BlockSpec((rows, tile), lambda j, g: (0, j)),
+        pl.BlockSpec((rows, 1), lambda j, g: (0, 0)),
+        pl.BlockSpec((rows, pairs), lambda j, g: (0, 0)),
+    ]
+
+
+def back(places, pieces, w_down, low, before=()):
     count = len(pieces)
     rows, width = pieces[0].shape
     depth = w_down.shape[0]
     pairs = low.shape[0]
     tile = tile_of(depth, 512)
-    tiles = depth // tile
-    anywhere = pl.BlockSpec(memory_space=pl.ANY)
-    return pl.pallas_call(
-        lambda *refs: back_body(count, *refs),
+    totals = carried_specs(rows, pairs, tile)
+    return pl.pallas_call(
+        lambda *refs: back_body(count, len(before), *refs),
         grid_spec=pltpu.PrefetchScalarGridSpec(
             num_scalar_prefetch=1,
-            grid=(1,),
+            grid=(depth // tile,),
             in_specs=[pl.BlockSpec((rows, width), lambda j, g: (0, 0))] * count
-            + [pl.BlockSpec((pairs, width), lambda j, g, n=n: (0, g[n])) for n in range(count)]
-            + [anywhere],
-            out_specs=[
-                anywhere,
-                pl.BlockSpec((rows, 1), lambda j, g: (0, 0)),
-                pl.BlockSpec((rows, pairs), lambda j, g: (0, 0)),
-            ],
-            scratch_shapes=[
-                pltpu.VMEM((padded, count * width), bf16),
-                pltpu.VMEM((tiles, tile, count * width), bf16),
-                pltpu.VMEM((tiles, tile, padded), f32),
-                pltpu.SemaphoreType.DMA((tiles, count)),
-                pltpu.SemaphoreType.DMA((tiles,)),
-            ],
+            + group_specs(count, tile, width, 1)
+            + group_specs(count, pairs, width, 0)
+            + totals[: len(before)],
+            out_specs=totals,
         ),
         out_shape=[
-            jax.ShapeDtypeStruct((tiles, tile, padded), f32),
+            jax.ShapeDtypeStruct((rows, depth), f32),
             jax.ShapeDtypeStruct((rows, 1), f32),
             jax.ShapeDtypeStruct((rows, pairs), f32),
         ],
         compiler_params=params(),
         cost_estimate=cost(2 * rows * depth * width * count, 2 * depth * width * count),
-    )(places, *pieces, *[low] * count, w_down)
+    )(places, *pieces, *[w_down] * 2 * count, *[low] * 2 * count, *before)
 
 
 def finish_body(features, count, places_ref, *refs):
-    hids, refs = refs[:count], refs[count:]
-    low_ref, w_hbm, acc_hbm, squares_ref, cross_ref, hot_ref, share_ref, low_act_ref = refs[:8]
-    own_ref, own_low_ref, gain_ref, act_hbm, resid_out, normed_out = refs[8:14]
-    hid, weights, acc, act, sems, in_sems, out_sems = refs[14:]
-    tiles, tile, _ = weights.shape
+    hids, weights, lows, refs = refs[:count], refs[count : count + 2], refs[count + 2 : count + 4], refs[count + 4 :]
+    acc_ref, squares_ref, cross_ref, hot_ref, share_ref, low_act_ref = refs[:6]
+    own_ref, own_low_ref, gain_ref, act_out, resid_out, normed_out, hid, lead, pull = refs[6:]
     rows = own_ref.shape[0]
-    padded = hid.shape[0]
-    copies = weight_copies(places_ref, w_hbm, weights, sems)
-
-    def acc_in(t):
-        return pltpu.make_async_copy(acc_hbm.at[t], acc.at[t], in_sems.at[t])
-
-    def act_out(t):
-        columns = pl.ds(pl.multiple_of(t * tile, lane), tile)
-        return pltpu.make_async_copy(act.at[t], act_hbm.at[:, columns], out_sems.at[t])
-
-    for t in range(tiles):
-        for copy in copies(t):
-            copy.start()
-        acc_in(t).start()
     part = rows // count
-    for n in range(count):
-        hid[n * part : (n + 1) * part] = hids[n][...]
-    hid[rows:] = jnp.zeros((padded - rows, hid.shape[1]), bf16)
-    squares, cross = statistics([hid.at[:rows]], [low_ref])
-    hot = hot_ref[:rows]
-    share = share_ref[:rows]
-    inner = jnp.sum((cross_ref[...] + cross) * hot.astype(f32), axis=1, keepdims=True) * share
-    inv_rms = lax.rsqrt((squares_ref[...] + squares) / features + norm_eps)
-    lead = inv_rms * share
-    pull = inv_rms * inv_rms * inv_rms * inner / features
-    own = own_ref[...].astype(f32)
-    resid_out[...] = (lead * dot(hot, own_low_ref[...]) - own * pull).astype(bf16)
-    normed_out[...] = (gain_ref[...] * own * inv_rms).astype(bf16)
-    same = iota((rows, padded), 0) == iota((rows, padded), 1)
-    lead = jnp.sum(jnp.where(same, lead, 0.0), axis=0, keepdims=True)
-    pull = jnp.sum(jnp.where(same, pull, 0.0), axis=0, keepdims=True)
-
-    @pl.loop(0, tiles)
-    def _(t):
-        at = pl.ds(pl.multiple_of(t * tile, tile), tile)
-        low_act = dot_t(low_act_ref[at], hot_ref[...])
-        for copy in copies(t):
-            copy.wait()
-        total = dot_t(weights[t], hid[...])
-        acc_in(t).wait()
-        turned = (lead * low_act - pull * (total + acc[t])).astype(bf16).T
-        act[t] = turned[:rows]
-        act_out(t).start()
-
-    @pl.loop(0, tiles)
-    def _(t):
-        act_out(t).wait()
+
+    @pl.when(pl.program_id(0) == 0)
+    def _():
+        for n in range(count):
+            hid[n * part : (n + 1) * part] = hids[n][...]
+        squares, cross = statistics(halves_of(hid), lows)
+        hot = hot_ref[...]
+        inner = jnp.sum((cross_ref[...] + cross) * hot.astype(f32), axis=1, keepdims=True)
+        inner = inner * share_ref[...]
+        inv_rms = lax.rsqrt((squares_ref[...] + squares) / features + norm_eps)
+        lead[...] = inv_rms * share_ref[...]
+        pull[...] = inv_rms * inv_rms * inv_rms * inner / features
+        own = own_ref[...].astype(f32)
+        own_low = dot(hot, own_low_ref[...])
+        resid_out[...] = (lead[...] * own_low - own * pull[...]).astype(bf16)
+        normed_out[...] = (gain_ref[...] * own * inv_rms).astype(bf16)
+
+    low_act = dot_t(hot_ref[...], low_act_ref[...])
+    hid_act = acc_ref[...] + product(halves_of(hid), weights)
+    act_out[...] = (lead[...] * low_act - pull[...] * hid_act).astype(bf16)
 
 
 def finish(places, pieces, w_down, low, before, hot, share, low_act, own, gain):
     count = len(pieces)
     rows, width = own.shape
     depth, features = w_down.shape
-    padded, pairs = hot.shape
+    pairs = hot.shape[1]
     tile = tile_of(depth, 512)
-    tiles = depth // tile
-    anywhere = pl.BlockSpec(memory_space=pl.ANY)
 
     def whole(shape):
         return pl.BlockSpec(shape, lambda j, g: (0, 0))
@@ -547,30 +506,28 @@
         lambda *refs: finish_body(features, count, *refs),
         grid_spec=pltpu.PrefetchScalarGridSpec(
             num_scalar_prefetch=1,
-            grid=(1,),
+            grid=(depth // tile,),
             in_specs=[whole((rows // count, width))] * count
+            + group_specs(1, tile, width, 1)
+            + group_specs(1, pairs, width, 0)
+            + carried_specs(rows, pairs, tile)
             + [
-                pl.BlockSpec((pairs, width), lambda j, g: (0, g[0])),
-                anywhere,
-                anywhere,
+                whole((rows, pairs)),
                 whole((rows, 1)),
-                whole((rows, pairs)),
-                whole((padded, pairs)),
-                whole((padded, 1)),
-                whole((depth, pairs)),
+                pl.BlockSpec((tile, pairs), lambda j, g: (j, 0)),
                 whole((rows, width)),
                 pl.BlockSpec((pairs, width), lambda j, g: (0, g[1])),
                 whole((1, width)),
             ],
-            out_specs=[anywhere, whole((rows, width)), whole((rows, width))],
+            out_specs=[
+                pl.BlockSpec((rows, tile), lambda j, g: (0, j)),
+                whole((rows, width)),
+                whole((rows, width)),
+            ],
             scratch_shapes=[
-                pltpu.VMEM((padded, width), bf16),
-                pltpu.VMEM((tiles, tile, width), bf16),
-                pltpu.VMEM((tiles, tile, padded), f32),
-                pltpu.VMEM((tiles, rows, tile), bf16),
-                pltpu.SemaphoreType.DMA((tiles, 1)),
-                pltpu.SemaphoreType.DMA((tiles,)),
-                pltpu.SemaphoreType.DMA((tiles,)),
+                pltpu.VMEM((rows, width), bf16),
+                pltpu.VMEM((rows, 1), f32),
+                pltpu.VMEM((rows, 1), f32),
             ],
         ),
         out_shape=[
@@ -580,7 +537,19 @@
         ],
         compiler_params=params(),
         cost_estimate=cost(2 * rows * depth * width, 2 * depth * width + 6 * rows * depth),
-    )(places, *pieces, low, w_down, *before, hot, share, low_act, own, low, gain)
+    )(
+        places,
+        *pieces,
+        *[w_down] * 2,
+        *[low] * 2,
+        *before,
+        hot,
+        share,
+        low_act,
+        own,
+        low,
+        gain,
+    )
 
 
 def low_rank_shards(
@@ -619,19 +588,17 @@
     low = lax.all_gather(low_own, "wide", axis=0, tiled=True)
     packed = pack(wide, destination, own_term, arrived, wide_count, slot_count)
     routed = [packed[k] if k == 0 else swap(packed[k], k, "wide") for k in range(wide_count)]
+    low_act = low_activations(low, features, w_down)
+    hot, share = slot_passages(wide, low, features, wide_count, slot_count, rows)
+    low_act, hot, share, *routed = lax.optimization_barrier((low_act, hot, share, *routed))
     own = assemble(wide, routed)
 
-    padded = -(-rows // lane) * lane
-    low_act = low_activations(low, features, w_down)
-    hot, share = slot_passages(wide, low, features, wide_count, slot_count, padded)
-
     beside, above = swap(own, 1), swap(own, 2)
+    totals = back(blk[None], [own], w_down, low)
+    *totals, beside, above = lax.optimization_barrier((*totals, beside, above))
     top = swap(beside[: rows // 2], 2)
     bottom = swap(above[rows // 2 :], 1)
-    low_act, hot, share, beside, above = lax.optimization_barrier(
-        (low_act, hot, share, beside, above)
-    )
-    totals = back(blk ^ jnp.arange(3, dtype=i32), [own, beside, above], w_down, low, padded)
+    totals = back(jnp.stack([blk ^ 1, blk ^ 2]), [beside, above], w_down, low, totals)
     act_grad, resid_grad, normed_out = finish(
         jnp.stack([blk ^ 3, blk]),
         [top, bottom],

time: 128 us -> 111 us (0.87)
  waiting for transfers between devices: 27.8 us -> 11.6 us
    ppermute x17, waiting for transfers between devices: 27.8 us -> 11.6 us  [swap(): lax.ppermute(rows, axis, [(i, i ^ k) for i in range(lax.axis_size(axis))])]
    pallas_call x1, Pallas kernels: 11.2 us -> 8.45 us  [finish(): pl.pallas_call(lambda *refs: finish_body(features, count, *refs), grid_sp...]
    pallas_call x1 -> x2, Pallas kernels: 14.8 us -> 17 us  [back(): pl.pallas_call(lambda *refs: back_body(count, len(before), *refs), grid_s...]
  transfers between devices with their start and end apart: 18 -> 18, of which waited for: 3 -> 3; matrix products, arithmetic and copies ran while one was open for 0% -> 0% of each run, Pallas kernels for 34% -> 40%
where the time goes in v6:
time: 111 us; the launch traced here: 110 us
  Pallas kernels  55.8 us (50%)
  starting transfers between devices  21.5 us (19%)
  between operations  14.3 us (13%)
  waiting for transfers between devices  11.6 us (10%)
  local copies, waits for them, and re-layouts  6.5 us (6%)
    ppermute x17, starting transfers between devices, swap(): lax.ppermute(rows, axis, [(i, i ^ k) for i in range(lax.axis_size(axis))])  21.5 us
    pallas_call x2, Pallas kernels, back(): pl.pallas_call(lambda *refs: back_body(count, len(before), *refs), grid_s...  17 us
    pallas_call x4, Pallas kernels, project(): pl.pallas_call(lambda *refs: project_body(len(own), *refs), in_specs=[pl....  15.6 us
    ppermute x17, waiting for transfers between devices, swap(): lax.ppermute(rows, axis, [(i, i ^ k) for i in range(lax.axis_size(axis))])  11.6 us
    pallas_call x1, Pallas kernels, low_activations(): pl.pallas_call(low_act_body, grid=(1,), in_specs=[pl.BlockSpec((pairs, fe...  9.85 us
    pallas_call x1, Pallas kernels, finish(): pl.pallas_call(lambda *refs: finish_body(features, count, *refs), grid_sp...  8.45 us
    unnamed x28, local copies, waits for them, and re-layouts  6.46 us
  transfers between devices with their start and end apart: 18, of which 3 were waited for; matrix products, arithmetic and copies ran while one was open for 0% of the time, Pallas kernels for 40%

profile of v6, /device:TPU:0, one launch (start us, length us, event | category | flops | bytes accessed | tf_op | source)
XLA Modules:
  0.0 109.9 jit_solution(3666342269333626750)
XLA Ops:
  7.2 0.0 all-gather.2.cloned.1.call-start
  7.2 0.7 copy-done.6
  8.0 0.8 copy-done.7
  8.7 0.7 copy-done.8
  9.4 4.0 %collective-permute-start.2 = (bf16[4,8704]{1,0:T(4,128)(2,1)S(1)}, bf16[4,8704]{1,0:T(4,128)(2,1)S(1)}, u32[]{:S(2)}, u32[]{:S(2)}) collective-permute-start(bf16[4,8704]{1,0:T(4,128)(2,1)S(1)} %shard_map.130.refs_1_), channel_id=1, source_target_pairs={{0,3},{1,2},{2,1},{3,0},{4,7},{5,6},{6,5},{7,4},{8,11},{9,10},{10,... | collective-permute-start | bytes 208904 | tf_op jit(solution)/shard_map/ppermute | solution.py:45
  13.4 0.5 collective-permute-start.1
  13.9 0.1 collective-permute-start
  14.0 1.3 %copy-done.2 = bf16[192,3072]{1,0:T(8,128)(2,1)S(1)} copy-done((bf16[192,3072]{1,0:T(8,128)(2,1)S(1)}, bf16[192,3072]{1,0:T(8,128)(2,1)}, u32[]{:S(2)}) %copy-start.2) | copy-done | bytes 1179672
  15.3 3.8 %shard_map.129 = bf16[192,1024]{1,0:T(8,128)(2,1)S(1)} custom-call(s32[1]{0:T(128)} %bitcast.1.refs_0_, bf16[192,3072]{1,0:T(8,128)(2,1)S(1)} %copy-done.2, bf16[3072,4096]{1,0:T(8,128)(2,1)} %refs_4_.3), custom_call_target="tpu_custom_call" | custom-call | flops 1207959552 | bytes 7471104 | tf_op jit(solution)/shard_map/pallas_call | solution.py:83
  19.1 0.0 collective-permute-done.2.refs_4_
  19.1 0.0 collective-permute-done.1.refs_3_
  19.2 1.5 %shard_map.131 = (bf16[4,4096]{1,0:T(4,128)(2,1)}, bf16[16,4224]{1,0:T(8,128)(2,1)}) custom-call(s32[1]{0:T(128)} %bitcast.refs_0_, bf16[4,8704]{1,0:T(4,128)(2,1)S(1)} %shard_map.130.refs_1_, bf16[4,8704]{1,0:T(4,128)(2,1)S(1)} %collective-permute-done.refs_2_, bf16[4,8704]{1,0:T(4,128)(2,1)S(1)} %collective-permute-done.1.refs_3_, ...), custom_call_target="tpu_custom_call" | custom-call | flops 8388608 | bytes 524288 | tf_op jit(solution)/shard_map/pallas_call | solution.py:183
  20.7 0.0 all-gather.2.cloned.1.call-update
  20.8 2.9 %collective-permute-start.3 = (bf16[192,1024]{1,0:T(8,128)(2,1)S(1)}, bf16[192,1024]{1,0:T(8,128)(2,1)S(1)}, u32[]{:S(2)}, u32[]{:S(2)}) collective-permute-start(bf16[192,1024]{1,0:T(8,128)(2,1)S(1)} %shard_map.129), channel_id=1, source_target_pairs={{0,3},{1,2},{2,1},{3,0},{4,7},{5,6},{6,5},{7,4},{8,11},{9,10},{10,... | collective-permute-start | bytes 1179656 | tf_op jit(solution)/shard_map/ppermute | solution.py:45
  23.7 3.6 %shard_map.136 = bf16[192,1024]{1,0:T(8,128)(2,1)S(1)} custom-call(s32[1]{0:T(128)} %bitcast.8.refs_0_, bf16[192,3072]{1,0:T(8,128)(2,1)S(1)} %copy-done.3, bf16[3072,4096]{1,0:T(8,128)(2,1)} %refs_4_.3), custom_call_target="tpu_custom_call" | custom-call | flops 1207959552 | bytes 7471104 | tf_op jit(solution)/shard_map/pallas_call | solution.py:83
  27.3 0.0 copy-start.5
  27.3 4.5 %shard_map.135 = bf16[192,1024]{1,0:T(8,128)(2,1)} custom-call(s32[1]{0:T(128)} %bitcast.7.refs_0_, bf16[192,3072]{1,0:T(8,128)(2,1)S(1)} %copy-done.3, bf16[3072,4096]{1,0:T(8,128)(2,1)} %refs_4_.3), custom_call_target="tpu_custom_call" | custom-call | flops 1207959552 | bytes 7471104 | tf_op jit(solution)/shard_map/pallas_call | solution.py:83
  31.8 0.5 collective-permute-start.4
  32.3 0.1 collective-permute-start.5
  32.4 3.7 %shard_map.134.refs_2_ = f32[192,1024]{1,0:T(8,128)S(1)} custom-call(s32[1]{0:T(128)} %bitcast.refs_0_, bf16[192,3072]{1,0:T(8,128)(2,1)S(1)} %copy-done.3, bf16[3072,4096]{1,0:T(8,128)(2,1)} %refs_4_.3, bf16[192,1024]{1,0:T(8,128)(2,1)S(1)} %copy-done.5), custom_call_target="tpu_custom_call" | custom-call | flops 1207959552 | bytes 7471104 | tf_op jit(solution)/shard_map/pallas_call | solution.py:83
  36.1 0.0 collective-permute-done.3.refs_3_
  36.1 5.6 %collective-permute-done.4.refs_4_ = bf16[192,1024]{1,0:T(8,128)(2,1)S(1)} collective-permute-done((bf16[192,1024]{1,0:T(8,128)(2,1)}, bf16[192,1024]{1,0:T(8,128)(2,1)S(1)}, u32[]{:S(2)}, u32[]{:S(2)}) %collective-permute-start.4) | collective-permute-done | bytes 393248 | tf_op jit(solution)/shard_map/ppermute | solution.py:45
  41.7 0.0 collective-permute-done.5.refs_5_
  41.8 1.1 shard_map.137
  42.8 0.1 collective-permute-start.6
  42.9 1.6 %collective-permute-start.7 = (bf16[36,1024]{1,0:T(8,128)(2,1)S(1)}, bf16[36,1024]{1,0:T(8,128)(2,1)S(1)}, u32[]{:S(2)}, u32[]{:S(2)}) collective-permute-start(bf16[36,1024]{1,0:T(8,128)(2,1)S(1)} %get-tuple-element.57), channel_id=1, source_target_pairs={{0,8},{4,12},{8,0},{12,4},{16,24},{20,28},{24,16},{28,20},{1,9},{5... | collective-permute-start | bytes 221192 | tf_op jit(solution)/shard_map/ppermute | solution.py:45
  44.6 0.2 collective-permute-start.8
  44.8 2.6 %collective-permute-start.9 = (bf16[36,1024]{1,0:T(8,128)(2,1)S(1)}, bf16[36,1024]{1,0:T(8,128)(2,1)S(1)}, u32[]{:S(2)}, u32[]{:S(2)}) collective-permute-start(bf16[36,1024]{1,0:T(8,128)(2,1)S(1)} %get-tuple-element.59), channel_id=1, source_target_pairs={{0,16},{4,20},{8,24},{12,28},{16,0},{20,4},{24,8},{28,12},{1,17},{... | collective-permute-start | bytes 221192 | tf_op jit(solution)/shard_map/ppermute | solution.py:45
  47.4 0.0 collective-permute-start.10
  47.4 3.6 %collective-permute-start.11 = (bf16[36,1024]{1,0:T(8,128)(2,1)S(1)}, bf16[36,1024]{1,0:T(8,128)(2,1)S(1)}, u32[]{:S(2)}, u32[]{:S(2)}) collective-permute-start(bf16[36,1024]{1,0:T(8,128)(2,1)S(1)} %get-tuple-element.61), channel_id=1, source_target_pairs={{0,24},{4,28},{8,16},{12,20},{16,8},{20,12},{24,0},{28,4},{1,25},{... | collective-permute-start | bytes 221192 | tf_op jit(solution)/shard_map/ppermute | solution.py:45
  51.0 0.1 collective-permute-start.12
  51.1 1.2 %copy-done = bf16[128,4224]{1,0:T(8,128)(2,1)S(1)} copy-done((bf16[128,4224]{1,0:T(8,128)(2,1)S(1)}, bf16[128,4224]{1,0:T(8,128)(2,1)}, u32[]{:S(2)}) %copy-start) | copy-done | bytes 1081368
  52.3 9.9 %shard_map.132.refs_12_ = bf16[3072,128]{1,0:T(8,128)(2,1)S(1)} custom-call(bf16[128,4224]{1,0:T(8,128)(2,1)S(1)} %copy-done, bf16[3072,4096]{1,0:T(8,128)(2,1)} %refs_4_.3), custom_call_target="tpu_custom_call" | custom-call | flops 3221225472 | bytes 25165824 | tf_op jit(solution)/shard_map/pallas_call | solution.py:364
  62.2 0.9 shard_map.133
  63.2 1.3 %shard_map.138.refs_1_.refs_13_ = bf16[288,1024]{1,0:T(8,128)(2,1)S(1)} custom-call(s32[1]{0:T(128)} %bitcast.6.refs_0_.wide_ref, bf16[36,1024]{1,0:T(8,128)(2,1)S(1)} %get-tuple-element.63.refs_0_, bf16[36,1024]{1,0:T(8,128)(2,1)S(1)} %collective-permute-done.6.refs_1_, bf16[36,1024]{1,0:T(8,128)(2,1)S(1)} %collective-permute-done.7.refs_2_, ...), custom_call_target="tpu_custom_call" | custom-call | flops 169869312 | bytes 1179648 | tf_op jit(solution)/shard_map/pallas_call | solution.py:266
  64.5 0.6 collective-permute-start.14
  65.1 1.5 %collective-permute-start.13 = (bf16[288,1024]{1,0:T(8,128)(2,1)S(1)}, bf16[288,1024]{1,0:T(8,128)(2,1)S(1)}, u32[]{:S(2)}, u32[]{:S(2)}) collective-permute-start(bf16[288,1024]{1,0:T(8,128)(2,1)S(1)} %shard_map.138.refs_1_.refs_13_), channel_id=1, source_target_pairs={{0,1},{1,0},{2,3},{3,2},{4,5},{5,4},{6,7},{7,6},{8,9},{9,8},{10,11... | collective-permute-start | bytes 1769480 | tf_op jit(solution)/shard_map/ppermute | solution.py:45
  66.6 0.1 pad_add_fusion.refs_0_
  66.7 0.1 pad_add_fusion.1.refs_0_
  66.7 6.5 %shard_map.139 = (f32[288,3072]{1,0:T(8,128)S(1)}, f32[288,1]{1,0:T(8,128)S(1)}, f32[288,128]{1,0:T(8,128)S(1)}) custom-call(s32[1]{0:T(128)} %bitcast.refs_0_, bf16[288,1024]{1,0:T(8,128)(2,1)S(1)} %shard_map.138.refs_1_.refs_13_, bf16[3072,4096]{1,0:T(8,128)(2,1)} %refs_4_.3, bf16[3072,4096]{1,0:T(8,128)(2,1)} %refs_4_.3, bf16[128,4224]{1,0:T(8,128)(2,1)S(1)} %copy-done.1, ...), custom_call_target="tpu_custom_call" | custom-call | flops 1811939328 | bytes 6291456 | tf_op jit(solution)/shard_map/pallas_call | solution.py:446
  73.3 1.7 %copy-done.4 = f32[288,3072]{1,0:T(8,128)} copy-done((f32[288,3072]{1,0:T(8,128)}, f32[288,3072]{1,0:T(8,128)S(1)}, u32[]{:S(2)}) %copy-start.4) | copy-done | bytes 3538968
  75.0 5.7 %collective-permute-done.14.refs_2_ = bf16[288,1024]{1,0:T(8,128)(2,1)S(1)} collective-permute-done((bf16[288,1024]{1,0:T(8,128)(2,1)S(1)}, bf16[288,1024]{1,0:T(8,128)(2,1)S(1)}, u32[]{:S(2)}, u32[]{:S(2)}) %collective-permute-start.14) | collective-permute-done | bytes 589856 | tf_op jit(solution)/shard_map/ppermute | solution.py:45
  80.7 0.2 collective-permute-done.13.refs_1_
  80.9 0.0 copy-start.9
  81.0 1.6 %collective-permute-start.15 = (bf16[144,1024]{1,0:T(8,128)(2,1)S(1)}, bf16[144,1024]{1,0:T(8,128)(2,1)S(1)}, u32[]{:S(2)}, u32[]{:S(2)}) collective-permute-start(bf16[144,1024]{1,0:T(8,128)(2,1)S(1)} %slice.6), channel_id=1, source_target_pairs={{0,2},{1,3},{2,0},{3,1},{4,6},{5,7},{6,4},{7,5},{8,10},{9,11},{10,... | collective-permute-start | bytes 884744 | tf_op jit(solution)/shard_map/ppermute | solution.py:45
  82.5 1.5 %collective-permute-start.16 = (bf16[144,1024]{1,0:T(8,128)(2,1)S(1)}, bf16[144,1024]{1,0:T(8,128)(2,1)S(1)}, u32[]{:S(2)}, u32[]{:S(2)}) collective-permute-start(bf16[144,1024]{1,0:T(8,128)(2,1)S(1)} %slice.7), channel_id=1, source_target_pairs={{0,1},{1,0},{2,3},{3,2},{4,5},{5,4},{6,7},{7,6},{8,9},{9,8},{10,11... | collective-permute-start | bytes 884744 | tf_op jit(solution)/shard_map/ppermute | solution.py:45
  84.0 10.5 %shard_map.140 = (f32[288,3072]{1,0:T(8,128)S(1)}, f32[288,1]{1,0:T(8,128)S(1)}, f32[288,128]{1,0:T(8,128)S(1)}) custom-call(s32[2]{0:T(128)S(1)} %pad_add_fusion.1.refs_0_, bf16[288,1024]{1,0:T(8,128)(2,1)S(1)} %collective-permute-done.13.refs_1_, bf16[288,1024]{1,0:T(8,128)(2,1)S(1)} %collective-permute-done.14.refs_2_, bf16[3072,4096]{1,0:T(8,128)(2,1)} %refs_4_.3, ...), custom_call_target="tpu_custom_call" | custom-call | flops 3623878656 | bytes 12582912 | tf_op jit(solution)/shard_map/pallas_call | solution.py:446
  94.6 8.5 %shard_map.141 = (bf16[288,3072]{1,0:T(8,128)(2,1)}, bf16[288,1024]{1,0:T(8,128)(2,1)}, bf16[288,1024]{1,0:T(8,128)(2,1)}) custom-call(s32[2]{0:T(128)S(1)} %pad_add_fusion.refs_0_, bf16[144,1024]{1,0:T(8,128)(2,1)S(1)} %collective-permute-done.15.refs_1_, bf16[144,1024]{1,0:T(8,128)(2,1)S(1)} %collective-permute-done.16.refs_2_, ...), custom_call_target="tpu_custom_call" | custom-call | flops 1811939328 | bytes 11599872 | tf_op jit(solution)/shard_map/pallas_call | solution.py:505
  (34 shorter events, 0.1 us)
Async XLA Ops:
  7.2 43.9 %all-gather.2.cloned.1.call-start = ((), (), s32[]{:S(2)}) async-start(), calls=%async_computation | async-start | bytes 1216512 | tf_op jit(solution)/shard_map/all_gather | solution.py:588
  7.2 0.8 copy-start.6
  8.0 0.8 copy-start.7
  8.7 0.7 copy-start.8
  9.4 9.7 %collective-permute-start.2 = (bf16[4,8704]{1,0:T(4,128)(2,1)S(1)}, bf16[4,8704]{1,0:T(4,128)(2,1)S(1)}, u32[]{:S(2)}, u32[]{:S(2)}) collective-permute-start(bf16[4,8704]{1,0:T(4,128)(2,1)S(1)} %shard_map.130.refs_1_), channel_id=1, source_target_pairs={{0,3},{1,2},{2,1},{3,0},{4,7},{5,6},{6,5},{7,4},{8,11},{9,10},{10,... | collective-permute-start | bytes 208904 | tf_op jit(solution)/shard_map/ppermute | solution.py:45
  13.4 5.8 %collective-permute-start.1 = (bf16[4,8704]{1,0:T(4,128)(2,1)S(1)}, bf16[4,8704]{1,0:T(4,128)(2,1)S(1)}, u32[]{:S(2)}, u32[]{:S(2)}) collective-permute-start(bf16[4,8704]{1,0:T(4,128)(2,1)S(1)} %shard_map.130.refs_1_), channel_id=1, source_target_pairs={{0,2},{1,3},{2,0},{3,1},{4,6},{5,7},{6,4},{7,5},{8,10},{9,11},{10,... | collective-permute-start | bytes 208904 | tf_op jit(solution)/shard_map/ppermute | solution.py:45
  13.9 5.3 %collective-permute-start = (bf16[4,8704]{1,0:T(4,128)(2,1)S(1)}, bf16[4,8704]{1,0:T(4,128)(2,1)S(1)}, u32[]{:S(2)}, u32[]{:S(2)}) collective-permute-start(bf16[4,8704]{1,0:T(4,128)(2,1)S(1)} %shard_map.130.refs_1_), channel_id=1, source_target_pairs={{0,1},{1,0},{2,3},{3,2},{4,5},{5,4},{6,7},{7,6},{8,9},{9,8},{10,11... | collective-permute-start | bytes 208904 | tf_op jit(solution)/shard_map/ppermute | solution.py:45
  14.0 1.3 %copy-start.2 = (bf16[192,3072]{1,0:T(8,128)(2,1)S(1)}, bf16[192,3072]{1,0:T(8,128)(2,1)}, u32[]{:S(2)}) copy-start(bf16[192,3072]{1,0:T(8,128)(2,1)} %refs_1_.4) | copy-start | bytes 3538948
  15.3 3.9 %copy-start.10 = (s32[192,1]{0,1:T(1,128)S(1)}, s32[192,1]{0,1:T(1,128)}, u32[]{:S(2)}) copy-start(s32[192,1]{0,1:T(1,128)} %param.15) | copy-start | bytes 2308
  15.3 3.9 %copy-start.11 = (f32[16]{0:T(128)S(1)}, f32[16]{0:T(128)}, u32[]{:S(2)}) copy-start(f32[16]{0:T(128)} %param.12) | copy-start | bytes 196
  15.3 3.9 %copy-start.12 = (s32[16]{0:T(128)S(1)}, s32[16]{0:T(128)}, u32[]{:S(2)}) copy-start(s32[16]{0:T(128)} %param.13) | copy-start | bytes 196
  15.3 3.9 %copy-start.13 = (s32[1,16]{1,0:T(1,128)S(1)}, s32[1,16]{1,0:T(1,128)}, u32[]{:S(2)}) copy-start(s32[1,16]{1,0:T(1,128)} %refs_8_.1) | copy-start | bytes 196
  15.3 8.3 %copy-start.3 = (bf16[192,3072]{1,0:T(8,128)(2,1)S(1)}, bf16[192,3072]{1,0:T(8,128)(2,1)}, u32[]{:S(2)}) copy-start(bf16[192,3072]{1,0:T(8,128)(2,1)} %refs_1_.4) | copy-start | bytes 3538948
  20.8 15.3 %collective-permute-start.3 = (bf16[192,1024]{1,0:T(8,128)(2,1)S(1)}, bf16[192,1024]{1,0:T(8,128)(2,1)S(1)}, u32[]{:S(2)}, u32[]{:S(2)}) collective-permute-start(bf16[192,1024]{1,0:T(8,128)(2,1)S(1)} %shard_map.129), channel_id=1, source_target_pairs={{0,3},{1,2},{2,1},{3,0},{4,7},{5,6},{6,5},{7,4},{8,11},{9,10},{10,... | collective-permute-start | bytes 1179656 | tf_op jit(solution)/shard_map/ppermute | solution.py:45
  27.3 5.1 %copy-start.5 = (bf16[192,1024]{1,0:T(8,128)(2,1)S(1)}, bf16[192,1024]{1,0:T(8,128)(2,1)}, u32[]{:S(2)}) copy-start(bf16[192,1024]{1,0:T(8,128)(2,1)} %refs_3_.4) | copy-start | bytes 1179652
  31.8 9.9 %collective-permute-start.4 = (bf16[192,1024]{1,0:T(8,128)(2,1)}, bf16[192,1024]{1,0:T(8,128)(2,1)S(1)}, u32[]{:S(2)}, u32[]{:S(2)}) collective-permute-start(bf16[192,1024]{1,0:T(8,128)(2,1)} %shard_map.135), channel_id=1, source_target_pairs={{0,1},{1,0},{2,3},{3,2},{4,5},{5,4},{6,7},{7,6},{8,9},{9,8},{10,11... | collective-permute-start | bytes 1179656 | tf_op jit(solution)/shard_map/ppermute | solution.py:45
  32.3 9.4 %collective-permute-start.5 = (bf16[192,1024]{1,0:T(8,128)(2,1)S(1)}, bf16[192,1024]{1,0:T(8,128)(2,1)S(1)}, u32[]{:S(2)}, u32[]{:S(2)}) collective-permute-start(bf16[192,1024]{1,0:T(8,128)(2,1)S(1)} %shard_map.136), channel_id=1, source_target_pairs={{0,2},{1,3},{2,0},{3,1},{4,6},{5,7},{6,4},{7,5},{8,10},{9,11},{10,... | collective-permute-start | bytes 1179656 | tf_op jit(solution)/shard_map/ppermute | solution.py:45
  42.8 4.6 %collective-permute-start.6 = (bf16[36,1024]{1,0:T(8,128)(2,1)S(1)}, bf16[36,1024]{1,0:T(8,128)(2,1)S(1)}, u32[]{:S(2)}, u32[]{:S(2)}) collective-permute-start(bf16[36,1024]{1,0:T(8,128)(2,1)S(1)} %get-tuple-element.56), channel_id=1, source_target_pairs={{0,4},{4,0},{8,12},{12,8},{16,20},{20,16},{24,28},{28,24},{1,5},{5... | collective-permute-start | bytes 221192 | tf_op jit(solution)/shard_map/ppermute | solution.py:45
  42.9 8.1 %collective-permute-start.7 = (bf16[36,1024]{1,0:T(8,128)(2,1)S(1)}, bf16[36,1024]{1,0:T(8,128)(2,1)S(1)}, u32[]{:S(2)}, u32[]{:S(2)}) collective-permute-start(bf16[36,1024]{1,0:T(8,128)(2,1)S(1)} %get-tuple-element.57), channel_id=1, source_target_pairs={{0,8},{4,12},{8,0},{12,4},{16,24},{20,28},{24,16},{28,20},{1,9},{5... | collective-permute-start | bytes 221192 | tf_op jit(solution)/shard_map/ppermute | solution.py:45
  44.6 18.6 %collective-permute-start.8 = (bf16[36,1024]{1,0:T(8,128)(2,1)S(1)}, bf16[36,1024]{1,0:T(8,128)(2,1)S(1)}, u32[]{:S(2)}, u32[]{:S(2)}) collective-permute-start(bf16[36,1024]{1,0:T(8,128)(2,1)S(1)} %get-tuple-element.58), channel_id=1, source_target_pairs={{0,12},{4,8},{8,4},{12,0},{16,28},{20,24},{24,20},{28,16},{1,13},{... | collective-permute-start | bytes 221192 | tf_op jit(solution)/shard_map/ppermute | solution.py:45
  44.8 18.3 %collective-permute-start.9 = (bf16[36,1024]{1,0:T(8,128)(2,1)S(1)}, bf16[36,1024]{1,0:T(8,128)(2,1)S(1)}, u32[]{:S(2)}, u32[]{:S(2)}) collective-permute-start(bf16[36,1024]{1,0:T(8,128)(2,1)S(1)} %get-tuple-element.59), channel_id=1, source_target_pairs={{0,16},{4,20},{8,24},{12,28},{16,0},{20,4},{24,8},{28,12},{1,17},{... | collective-permute-start | bytes 221192 | tf_op jit(solution)/shard_map/ppermute | solution.py:45
  47.4 15.8 %collective-permute-start.10 = (bf16[36,1024]{1,0:T(8,128)(2,1)S(1)}, bf16[36,1024]{1,0:T(8,128)(2,1)S(1)}, u32[]{:S(2)}, u32[]{:S(2)}) collective-permute-start(bf16[36,1024]{1,0:T(8,128)(2,1)S(1)} %get-tuple-element.60), channel_id=1, source_target_pairs={{0,20},{4,16},{8,28},{12,24},{16,4},{20,0},{24,12},{28,8},{1,21},{... | collective-permute-start | bytes 221192 | tf_op jit(solution)/shard_map/ppermute | solution.py:45
  47.4 15.7 %collective-permute-start.11 = (bf16[36,1024]{1,0:T(8,128)(2,1)S(1)}, bf16[36,1024]{1,0:T(8,128)(2,1)S(1)}, u32[]{:S(2)}, u32[]{:S(2)}) collective-permute-start(bf16[36,1024]{1,0:T(8,128)(2,1)S(1)} %get-tuple-element.61), channel_id=1, source_target_pairs={{0,24},{4,28},{8,16},{12,20},{16,8},{20,12},{24,0},{28,4},{1,25},{... | collective-permute-start | bytes 221192 | tf_op jit(solution)/shard_map/ppermute | solution.py:45
  51.0 12.2 %collective-permute-start.12 = (bf16[36,1024]{1,0:T(8,128)(2,1)S(1)}, bf16[36,1024]{1,0:T(8,128)(2,1)S(1)}, u32[]{:S(2)}, u32[]{:S(2)}) collective-permute-start(bf16[36,1024]{1,0:T(8,128)(2,1)S(1)} %get-tuple-element.62), channel_id=1, source_target_pairs={{0,28},{4,24},{8,20},{12,16},{16,12},{20,8},{24,4},{28,0},{1,29},{... | collective-permute-start | bytes 221192 | tf_op jit(solution)/shard_map/ppermute | solution.py:45
  51.1 1.2 %copy-start = (bf16[128,4224]{1,0:T(8,128)(2,1)S(1)}, bf16[128,4224]{1,0:T(8,128)(2,1)}, u32[]{:S(2)}) copy-start(bf16[128,4224]{1,0:T(8,128)(2,1)} %all-gather.2.cloned.1.call-done.low_ref.refs_1_.refs_4_.refs_5_.refs_7_.refs_8_.refs_9_.refs_10_.refs_6_.refs_14_) | copy-start | bytes 3244036
  52.3 9.9 %copy-start.1 = (bf16[128,4224]{1,0:T(8,128)(2,1)S(1)}, bf16[128,4224]{1,0:T(8,128)(2,1)}, u32[]{:S(2)}) copy-start(bf16[128,4224]{1,0:T(8,128)(2,1)} %all-gather.2.cloned.1.call-done.low_ref.refs_1_.refs_4_.refs_5_.refs_7_.refs_8_.refs_9_.refs_10_.refs_6_.refs_14_) | copy-start | bytes 3244036
  64.5 16.1 %collective-permute-start.14 = (bf16[288,1024]{1,0:T(8,128)(2,1)S(1)}, bf16[288,1024]{1,0:T(8,128)(2,1)S(1)}, u32[]{:S(2)}, u32[]{:S(2)}) collective-permute-start(bf16[288,1024]{1,0:T(8,128)(2,1)S(1)} %shard_map.138.refs_1_.refs_13_), channel_id=1, source_target_pairs={{0,2},{1,3},{2,0},{3,1},{4,6},{5,7},{6,4},{7,5},{8,10},{9,11},{10,... | collective-permute-start | bytes 1769480 | tf_op jit(solution)/shard_map/ppermute | solution.py:45
  65.1 15.8 %collective-permute-start.13 = (bf16[288,1024]{1,0:T(8,128)(2,1)S(1)}, bf16[288,1024]{1,0:T(8,128)(2,1)S(1)}, u32[]{:S(2)}, u32[]{:S(2)}) collective-permute-start(bf16[288,1024]{1,0:T(8,128)(2,1)S(1)} %shard_map.138.refs_1_.refs_13_), channel_id=1, source_target_pairs={{0,1},{1,0},{2,3},{3,2},{4,5},{5,4},{6,7},{7,6},{8,9},{9,8},{10,11... | collective-permute-start | bytes 1769480 | tf_op jit(solution)/shard_map/ppermute | solution.py:45
  73.3 1.7 %copy-start.4 = (f32[288,3072]{1,0:T(8,128)}, f32[288,3072]{1,0:T(8,128)S(1)}, u32[]{:S(2)}) copy-start(f32[288,3072]{1,0:T(8,128)S(1)} %get-tuple-element.76.refs_11_) | copy-start | bytes 10616836
  80.9 13.7 %copy-start.9 = (f32[1024]{0:T(1024)S(1)}, f32[1024]{0:T(1024)}, u32[]{:S(2)}) copy-start(f32[1024]{0:T(1024)} %param.19) | copy-start | bytes 12292
  81.0 13.6 %collective-permute-start.15 = (bf16[144,1024]{1,0:T(8,128)(2,1)S(1)}, bf16[144,1024]{1,0:T(8,128)(2,1)S(1)}, u32[]{:S(2)}, u32[]{:S(2)}) collective-permute-start(bf16[144,1024]{1,0:T(8,128)(2,1)S(1)} %slice.6), channel_id=1, source_target_pairs={{0,2},{1,3},{2,0},{3,1},{4,6},{5,7},{6,4},{7,5},{8,10},{9,11},{10,... | collective-permute-start | bytes 884744 | tf_op jit(solution)/shard_map/ppermute | solution.py:45
  82.5 12.1 %collective-permute-start.16 = (bf16[144,1024]{1,0:T(8,128)(2,1)S(1)}, bf16[144,1024]{1,0:T(8,128)(2,1)S(1)}, u32[]{:S(2)}, u32[]{:S(2)}) collective-permute-start(bf16[144,1024]{1,0:T(8,128)(2,1)S(1)} %slice.7), channel_id=1, source_target_pairs={{0,1},{1,0},{2,3},{3,2},{4,5},{5,4},{6,7},{7,6},{8,9},{9,8},{10,11... | collective-permute-start | bytes 884744 | tf_op jit(solution)/shard_map/ppermute | solution.py:45
Sparse Core Ops, SparseCore 0:
  20.9 23.9 all-gather.1

commit v7 on v6

--- a/solution.py
+++ b/solution.py
@@ -43,10 +43,6 @@
 
 def swap(rows, k, axis="blk"):
     return lax.ppermute(rows, axis, [(i, i ^ k) for i in range(lax.axis_size(axis))])
-
-
-def after(first, *later):
-    return lax.optimization_barrier((first, *later))
 
 
 def project_body(has_resid, group_ref, act_hbm, w_hbm, *refs):
@@ -94,7 +90,7 @@
             pltpu.SemaphoreType.DMA((count,)),
         ],
         compiler_params=params(),
-        cost_estimate=cost(2 * rows * depth * width, 2 * depth * width + 2 * rows * depth),
+        cost_estimate=cost(rows * depth * width // 8, depth * width // 8),
     )(group, act, w_down, *own)
 
 
@@ -248,16 +244,17 @@
 
 
 def assemble_body(wide_ref, *refs):
-    parts, out_ref = refs[:-1], refs[-1]
+    parts, (left_ref, right_ref) = refs[:-2], refs[-2:]
     slots = parts[0].shape[0]
-    rows = out_ref.shape[0]
+    rows, half = left_ref.shape
     row, column = iota((rows, slots), 0), iota((rows, slots), 1)
     total = 0.0
     for k, part in enumerate(parts):
         group = wide_ref[0] ^ k
         place = (row == group * slots + column).astype(f32).astype(bf16)
         total = total + dot(place, part[...])
-    out_ref[...] = total.astype(bf16)
+    left_ref[...] = total[:, :half].astype(bf16)
+    right_ref[...] = total[:, half:].astype(bf16)
 
 
 def assemble(wide, parts):
@@ -267,8 +264,8 @@
         assemble_body,
         in_specs=[pl.BlockSpec(memory_space=pltpu.SMEM)]
         + [pl.BlockSpec(memory_space=pltpu.VMEM)] * len(parts),
-        out_specs=pl.BlockSpec(memory_space=pltpu.VMEM),
-        out_shape=jax.ShapeDtypeStruct((rows, width), bf16),
+        out_specs=[pl.BlockSpec(memory_space=pltpu.VMEM)] * 2,
+        out_shape=[jax.ShapeDtypeStruct((rows, width // 2), bf16)] * 2,
         compiler_params=params(),
         cost_estimate=cost(2 * rows * rows * width, 4 * rows * width),
     )(wide[None], *parts)
@@ -339,11 +336,12 @@
     )(wide[None], low)
 
 
-def low_act_body(low_ref, w_hbm, out_ref, weights, sems):
+def low_act_body(part, low_ref, w_hbm, *refs):
+    out_ref, weights, sems = refs[-3:]
     count, tile, _ = weights.shape
 
     def weight_copy(t):
-        rows = pl.ds(pl.multiple_of(t * tile, tile), tile)
+        rows = pl.ds(pl.multiple_of((part * count + t) * tile, tile), tile)
         return pltpu.make_async_copy(w_hbm.at[rows], weights.at[t], sems.at[t])
 
     for t in range(count):
@@ -356,75 +354,68 @@
         out_ref[rows] = dot_t(weights[t], low_ref[...]).astype(bf16)
 
 
-def low_activations(low, features, w_down):
+def low_activations(low, features, w_down, part, parts, filled=()):
     pairs = low.shape[0]
     depth = w_down.shape[0]
-    tile = tile_of(depth, 512)
-    count = depth // tile
-    return pl.pallas_call(
-        low_act_body,
+    some = depth // parts
+    tile = tile_of(some, 512)
+    count = some // tile
+    anywhere = pl.BlockSpec(memory_space=pl.ANY)
+    return pl.pallas_call(
+        lambda *refs: low_act_body(part, *refs),
         grid=(1,),
-        in_specs=[
-            pl.BlockSpec((pairs, features), lambda j: (0, 0)),
-            pl.BlockSpec(memory_space=pl.ANY),
-        ],
-        out_specs=pl.BlockSpec((depth, pairs), lambda j: (0, 0)),
+        in_specs=[pl.BlockSpec((pairs, features), lambda j: (0, 0)), anywhere]
+        + [anywhere] * len(filled),
+        out_specs=pl.BlockSpec((some, pairs), lambda j: (part, 0)),
         out_shape=jax.ShapeDtypeStruct((depth, pairs), bf16),
         scratch_shapes=[
             pltpu.VMEM((count, tile, features), bf16),
             pltpu.SemaphoreType.DMA((count,)),
         ],
-        compiler_params=params(),
-        cost_estimate=cost(2 * pairs * depth * features, 2 * depth * features),
-    )(low, w_down)
+        input_output_aliases={2: 0} if filled else {},
+        compiler_params=params(),
+        cost_estimate=cost(2 * pairs * some * features, 2 * some * features),
+    )(low, w_down, *filled)
 
 
 def statistics(hids, lows):
     squares, cross = 0.0, 0.0
-    for hid, low_ref in zip(hids, lows):
-        wide_hid = hid.astype(f32)
-        squares = squares + jnp.sum(wide_hid * wide_hid, axis=1, keepdims=True)
-        cross = cross + dot_t(hid, low_ref[...])
+    for hid_ref, low_ref in zip(hids, lows):
+        hid = hid_ref[...].astype(f32)
+        squares = squares + jnp.sum(hid * hid, axis=1, keepdims=True)
+        cross = cross + dot_t(hid_ref[...], low_ref[...])
     return squares, cross
 
 
 def product(hids, weights):
     total = 0.0
-    for hid, w_ref in zip(hids, weights):
-        total = total + dot_t(hid, w_ref[...])
+    for hid_ref, w_ref in zip(hids, weights):
+        total = total + dot_t(hid_ref[...], w_ref[...])
     return total
 
 
-def group_specs(count, rows_of_block, width, row_step):
-    half = width // 2
-    return [
-        pl.BlockSpec(
-            (rows_of_block, half), lambda j, g, n=n, side=side: (row_step * j, 2 * g[n] + side)
-        )
-        for n in range(count)
-        for side in range(2)
-    ]
-
-
-def halves_of(ref):
-    half = ref.shape[1] // 2
-    return [ref[:, :half], ref[:, half:]]
+def piece_specs(pieces, low, tile):
+    hid_specs, w_specs, low_specs = [], [], []
+    for n, piece in enumerate(pieces):
+        width = piece.shape[1]
+        hid_specs.append(pl.BlockSpec(piece.shape, lambda j, g: (0, 0)))
+        w_specs.append(pl.BlockSpec((tile, width), lambda j, g, n=n: (j, g[n])))
+        low_specs.append(pl.BlockSpec((low.shape[0], width), lambda j, g, n=n: (0, g[n])))
+    return hid_specs + w_specs + low_specs
 
 
 def back_body(count, carried, places_ref, *refs):
-    hids, refs = refs[:count], refs[count:]
-    weights, lows, refs = refs[: 2 * count], refs[2 * count : 4 * count], refs[4 * count :]
-    before, (acc_ref, squares_ref, cross_ref) = refs[:carried], refs[carried:]
-    halves = [half for hid in hids for half in halves_of(hid)]
+    hids, weights, lows = refs[:count], refs[count : 2 * count], refs[2 * count : 3 * count]
+    before, (acc_ref, squares_ref, cross_ref) = refs[3 * count : -3], refs[-3:]
 
     @pl.when(pl.program_id(0) == 0)
     def _():
-        squares, cross = statistics(halves, lows)
+        squares, cross = statistics(hids, lows)
         if carried:
             squares, cross = before[1][...] + squares, before[2][...] + cross
         squares_ref[...], cross_ref[...] = squares, cross
 
-    total = product(halves, weights)
+    total = product(hids, weights)
     acc_ref[...] = before[0][...] + total if carried else total
 
 
@@ -448,10 +439,7 @@
         grid_spec=pltpu.PrefetchScalarGridSpec(
             num_scalar_prefetch=1,
             grid=(depth // tile,),
-            in_specs=[pl.BlockSpec((rows, width), lambda j, g: (0, 0))] * count
-            + group_specs(count, tile, width, 1)
-            + group_specs(count, pairs, width, 0)
-            + totals[: len(before)],
+            in_specs=piece_specs(pieces, low, tile) + totals[: len(before)],
             out_specs=totals,
         ),
         out_shape=[
@@ -461,40 +449,40 @@
         ],
         compiler_params=params(),
         cost_estimate=cost(2 * rows * depth * width * count, 2 * depth * width * count),
-    )(places, *pieces, *[w_down] * 2 * count, *[low] * 2 * count, *before)
+    )(places, *pieces, *[w_down] * count, *[low] * count, *before)
 
 
 def finish_body(features, count, places_ref, *refs):
-    hids, weights, lows, refs = refs[:count], refs[count : count + 2], refs[count + 2 : count + 4], refs[count + 4 :]
-    acc_ref, squares_ref, cross_ref, hot_ref, share_ref, low_act_ref = refs[:6]
-    own_ref, own_low_ref, gain_ref, act_out, resid_out, normed_out, hid, lead, pull = refs[6:]
-    rows = own_ref.shape[0]
-    part = rows // count
+    hids, weights, lows = refs[:count], refs[count : 2 * count], refs[2 * count : 3 * count]
+    refs = refs[3 * count :]
+    acc_ref, squares_ref, cross_ref, hot_ref, share_ref, low_act_ref, left_ref, right_ref = refs[:8]
+    own_low_ref, gain_ref, act_out, resid_out, normed_out, lead, pull = refs[8:]
 
     @pl.when(pl.program_id(0) == 0)
     def _():
-        for n in range(count):
-            hid[n * part : (n + 1) * part] = hids[n][...]
-        squares, cross = statistics(halves_of(hid), lows)
+        squares, cross = statistics(hids, lows)
         hot = hot_ref[...]
         inner = jnp.sum((cross_ref[...] + cross) * hot.astype(f32), axis=1, keepdims=True)
         inner = inner * share_ref[...]
         inv_rms = lax.rsqrt((squares_ref[...] + squares) / features + norm_eps)
         lead[...] = inv_rms * share_ref[...]
         pull[...] = inv_rms * inv_rms * inv_rms * inner / features
-        own = own_ref[...].astype(f32)
-        own_low = dot(hot, own_low_ref[...])
-        resid_out[...] = (lead[...] * own_low - own * pull[...]).astype(bf16)
-        normed_out[...] = (gain_ref[...] * own * inv_rms).astype(bf16)
+        half = left_ref.shape[1]
+        for own_ref, at in ((left_ref, slice(0, half)), (right_ref, slice(half, 2 * half))):
+            own = own_ref[...].astype(f32)
+            own_low = dot(hot, own_low_ref[:, at])
+            resid_out[:, at] = (lead[...] * own_low - own * pull[...]).astype(bf16)
+            normed_out[:, at] = (gain_ref[:, at] * own * inv_rms).astype(bf16)
 
     low_act = dot_t(hot_ref[...], low_act_ref[...])
-    hid_act = acc_ref[...] + product(halves_of(hid), weights)
+    hid_act = acc_ref[...] + product(hids, weights)
     act_out[...] = (lead[...] * low_act - pull[...] * hid_act).astype(bf16)
 
 
 def finish(places, pieces, w_down, low, before, hot, share, low_act, own, gain):
     count = len(pieces)
-    rows, width = own.shape
+    rows, half = own[0].shape
+    width = 2 * half
     depth, features = w_down.shape
     pairs = hot.shape[1]
     tile = tile_of(depth, 512)
@@ -507,16 +495,15 @@
         grid_spec=pltpu.PrefetchScalarGridSpec(
             num_scalar_prefetch=1,
             grid=(depth // tile,),
-            in_specs=[whole((rows // count, width))] * count
-            + group_specs(1, tile, width, 1)
-            + group_specs(1, pairs, width, 0)
+            in_specs=piece_specs(pieces, low, tile)
             + carried_specs(rows, pairs, tile)
             + [
                 whole((rows, pairs)),
                 whole((rows, 1)),
                 pl.BlockSpec((tile, pairs), lambda j, g: (j, 0)),
-                whole((rows, width)),
-                pl.BlockSpec((pairs, width), lambda j, g: (0, g[1])),
+                whole((rows, half)),
+                whole((rows, half)),
+                pl.BlockSpec((pairs, width), lambda j, g: (0, g[count])),
                 whole((1, width)),
             ],
             out_specs=[
@@ -524,11 +511,7 @@
                 whole((rows, width)),
                 whole((rows, width)),
             ],
-            scratch_shapes=[
-                pltpu.VMEM((rows, width), bf16),
-                pltpu.VMEM((rows, 1), f32),
-                pltpu.VMEM((rows, 1), f32),
-            ],
+            scratch_shapes=[pltpu.VMEM((rows, 1), f32), pltpu.VMEM((rows, 1), f32)],
         ),
         out_shape=[
             jax.ShapeDtypeStruct((rows, depth), bf16),
@@ -540,13 +523,13 @@
     )(
         places,
         *pieces,
-        *[w_down] * 2,
-        *[low] * 2,
+        *[w_down] * count,
+        *[low] * count,
         *before,
         hot,
         share,
         low_act,
-        own,
+        *own,
         low,
         gain,
     )
@@ -572,43 +555,57 @@
     slot_count = 3 * tok_count // (2 * wide_count)
     rows = wide_count * slot_count
 
+    first_term = project((blk ^ 3)[None], mlp_act, w_down, width)
+    arrived = [swap(first_term, 3)]
+    _, query_emb, passage_emb = lax.optimization_barrier((first_term, query_emb, passage_emb))
     both = payload(query_emb, passage_emb, gain)
     parts = [both] + [swap(both, k) for k in (1, 2, 3)]
-    first_term = project((blk ^ 3)[None], mlp_act, w_down, width)
-    arrived = [swap(first_term, 3)]
-    parts = after(first_term, *parts)[1:]
+    second_term = project((blk ^ 1)[None], mlp_act, w_down, width)
+    arrived.append(swap(second_term, 1))
+    _, arrived[0], *parts = lax.optimization_barrier((second_term, arrived[0], *parts))
     query_grad, low_own = group_part(
         parts, row_lse, positive, token_lengths, destination, features, blk
     )
-    mlp_act = after(low_own, mlp_act)[1]
-    for k in (1, 2):
-        arrived.append(swap(project((blk ^ k)[None], mlp_act, w_down, width), k))
+    _, mlp_act = lax.optimization_barrier((low_own, mlp_act))
+    arrived.append(swap(project((blk ^ 2)[None], mlp_act, w_down, width), 2))
     own_term = project(blk[None], mlp_act, w_down, width, resid)
 
     low = lax.all_gather(low_own, "wide", axis=0, tiled=True)
     packed = pack(wide, destination, own_term, arrived, wide_count, slot_count)
     routed = [packed[k] if k == 0 else swap(packed[k], k, "wide") for k in range(wide_count)]
-    low_act = low_activations(low, features, w_down)
+    low_act = low_activations(low, features, w_down, 0, 2)
     hot, share = slot_passages(wide, low, features, wide_count, slot_count, rows)
     low_act, hot, share, *routed = lax.optimization_barrier((low_act, hot, share, *routed))
-    own = assemble(wide, routed)
-
-    beside, above = swap(own, 1), swap(own, 2)
-    totals = back(blk[None], [own], w_down, low)
-    *totals, beside, above = lax.optimization_barrier((*totals, beside, above))
-    top = swap(beside[: rows // 2], 2)
-    bottom = swap(above[rows // 2 :], 1)
-    totals = back(jnp.stack([blk ^ 1, blk ^ 2]), [beside, above], w_down, low, totals)
+    left, right = assemble(wide, routed)
+
+    left_1, left_2 = swap(left, 1), swap(left, 2)
+    right_1, right_2 = swap(right, 1), swap(right, 2)
+    low_act = low_activations(low, features, w_down, 1, 2, [low_act])
+    low_act, left_1, left_2 = lax.optimization_barrier((low_act, left_1, left_2))
+    left_3 = swap(left_1, 2)
+
+    def places(*pieces):
+        return [(blk ^ k) * 2 + side for k, side in pieces]
+
+    totals = back(
+        jnp.stack(places((0, 0), (0, 1), (1, 0), (2, 0))),
+        [left, right, left_1, left_2],
+        w_down,
+        low,
+    )
+    *totals, right_1, right_2 = lax.optimization_barrier((*totals, right_1, right_2))
+    right_3 = swap(right_2, 1)
+    totals = back(jnp.stack(places((1, 1), (2, 1))), [right_1, right_2], w_down, low, totals)
     act_grad, resid_grad, normed_out = finish(
-        jnp.stack([blk ^ 3, blk]),
-        [top, bottom],
+        jnp.stack([*places((3, 0), (3, 1)), blk]),
+        [left_3, right_3],
         w_down,
         low,
         totals,
         hot,
         share,
         low_act,
-        own,
+        [left, right],
         gain[None],
     )
     return (query_grad, resid_grad, act_grad, normed_out)

time: 111 us -> 121 us (1.090)
  local copies, waits for them, and re-layouts: 6.5 us -> 10.8 us
  starting transfers between devices: 21.5 us -> 24.7 us
  Pallas kernels: 55.8 us -> 58.3 us
    unnamed x28 -> x46, local copies, waits for them, and re-layouts: 6.46 us -> 10.8 us
    ppermute x17 -> x19, starting transfers between devices: 21.5 us -> 24.6 us  [swap(): lax.ppermute(rows, axis, [(i, i ^ k) for i in range(lax.axis_size(axis))])]
    pallas_call x1 -> x2, Pallas kernels: 9.85 us -> 12.1 us  [low_activations(): pl.pallas_call(lambda *refs: low_act_body(part, *refs), grid=(1,), in_spe...]
    ppermute x17 -> x19, waiting for transfers between devices: 11.6 us -> 11.8 us  [swap(): lax.ppermute(rows, axis, [(i, i ^ k) for i in range(lax.axis_size(axis))])]
  transfers between devices with their start and end apart: 18 -> 20, of which waited for: 3 -> 7; matrix products, arithmetic and copies ran while one was open for 0% -> 0% of each run, Pallas kernels for 40% -> 36%
where the time goes in v7:
time: 121 us; the launch traced here: 120 us
  Pallas kernels  58.3 us (48%)
  starting transfers between devices  24.7 us (20%)
  between operations  14.3 us (12%)
  waiting for transfers between devices  11.8 us (10%)
  local copies, waits for them, and re-layouts  10.8 us (9%)
    ppermute x19, starting transfers between devices, swap(): lax.ppermute(rows, axis, [(i, i ^ k) for i in range(lax.axis_size(axis))])  24.6 us
    pallas_call x2, Pallas kernels, back(): pl.pallas_call(lambda *refs: back_body(count, len(before), *refs), grid_s...  17.1 us
    pallas_call x4, Pallas kernels, project(): pl.pallas_call(lambda *refs: project_body(len(own), *refs), in_specs=[pl....  14.9 us
    pallas_call x2, Pallas kernels, low_activations(): pl.pallas_call(lambda *refs: low_act_body(part, *refs), grid=(1,), in_spe...  12.1 us
    ppermute x19, waiting for transfers between devices, swap(): lax.ppermute(rows, axis, [(i, i ^ k) for i in range(lax.axis_size(axis))])  11.8 us
    unnamed x46, local copies, waits for them, and re-layouts  10.8 us
    pallas_call x1, Pallas kernels, finish(): pl.pallas_call(lambda *refs: finish_body(features, count, *refs), grid_sp...  8.71 us
  transfers between devices with their start and end apart: 20, of which 7 were waited for; matrix products, arithmetic and copies ran while one was open for 0% of the time, Pallas kernels for 36%

profile of v7, /device:TPU:0, one launch (start us, length us, event | category | flops | bytes accessed | tf_op | source)
XLA Modules:
  0.0 120.1 jit_solution(3062578848720653676)
XLA Ops:
  7.2 1.3 %copy-done.2 = bf16[192,3072]{1,0:T(8,128)(2,1)S(1)} copy-done((bf16[192,3072]{1,0:T(8,128)(2,1)S(1)}, bf16[192,3072]{1,0:T(8,128)(2,1)}, u32[]{:S(2)}) %copy-start.2) | copy-done | bytes 1179672
  8.5 3.8 %shard_map.130 = bf16[192,1024]{1,0:T(8,128)(2,1)S(1)} custom-call(s32[1]{0:T(128)} %bitcast.2.refs_0_, bf16[192,3072]{1,0:T(8,128)(2,1)S(1)} %copy-done.2, bf16[3072,4096]{1,0:T(8,128)(2,1)} %refs_4_.3), custom_call_target="tpu_custom_call" | custom-call | flops 75497472 | bytes 393216 | tf_op jit(solution)/shard_map/pallas_call | solution.py:79
  12.3 4.0 %collective-permute-start = (bf16[192,1024]{1,0:T(8,128)(2,1)S(1)}, bf16[192,1024]{1,0:T(8,128)(2,1)S(1)}, u32[]{:S(2)}, u32[]{:S(2)}) collective-permute-start(bf16[192,1024]{1,0:T(8,128)(2,1)S(1)} %shard_map.130), channel_id=1, source_target_pairs={{0,3},{1,2},{2,1},{3,0},{4,7},{5,6},{6,5},{7,4},{8,11},{9,10},{10,... | collective-permute-start | bytes 1179656 | tf_op jit(solution)/shard_map/ppermute | solution.py:45
  16.3 0.1 collective-permute-start.3
  16.4 2.0 %collective-permute-start.2 = (bf16[4,8704]{1,0:T(4,128)(2,1)S(1)}, bf16[4,8704]{1,0:T(4,128)(2,1)S(1)}, u32[]{:S(2)}, u32[]{:S(2)}) collective-permute-start(bf16[4,8704]{1,0:T(4,128)(2,1)S(1)} %shard_map.131.refs_1_), channel_id=1, source_target_pairs={{0,2},{1,3},{2,0},{3,1},{4,6},{5,7},{6,4},{7,5},{8,10},{9,11},{10,... | collective-permute-start | bytes 208904 | tf_op jit(solution)/shard_map/ppermute | solution.py:45
  18.3 1.5 %collective-permute-start.1 = (bf16[4,8704]{1,0:T(4,128)(2,1)S(1)}, bf16[4,8704]{1,0:T(4,128)(2,1)S(1)}, u32[]{:S(2)}, u32[]{:S(2)}) collective-permute-start(bf16[4,8704]{1,0:T(4,128)(2,1)S(1)} %shard_map.131.refs_1_), channel_id=1, source_target_pairs={{0,1},{1,0},{2,3},{3,2},{4,5},{5,4},{6,7},{7,6},{8,9},{9,8},{10,11... | collective-permute-start | bytes 208904 | tf_op jit(solution)/shard_map/ppermute | solution.py:45
  19.9 3.6 %shard_map.129 = bf16[192,1024]{1,0:T(8,128)(2,1)S(1)} custom-call(s32[1]{0:T(128)} %bitcast.1.refs_0_, bf16[192,3072]{1,0:T(8,128)(2,1)S(1)} %copy-done.3, bf16[3072,4096]{1,0:T(8,128)(2,1)} %refs_4_.3), custom_call_target="tpu_custom_call" | custom-call | flops 75497472 | bytes 393216 | tf_op jit(solution)/shard_map/pallas_call | solution.py:79
  23.5 4.1 %collective-permute-done.3.refs_4_ = bf16[4,8704]{1,0:T(4,128)(2,1)S(1)} collective-permute-done((bf16[4,8704]{1,0:T(4,128)(2,1)S(1)}, bf16[4,8704]{1,0:T(4,128)(2,1)S(1)}, u32[]{:S(2)}, u32[]{:S(2)}) %collective-permute-start.3) | collective-permute-done | bytes 69664 | tf_op jit(solution)/shard_map/ppermute | solution.py:45
  27.7 0.7 collective-permute-done.2.refs_3_
  28.4 0.3 collective-permute-done.1.refs_2_
  28.7 1.5 %shard_map.132 = (bf16[4,4096]{1,0:T(4,128)(2,1)}, bf16[16,4224]{1,0:T(8,128)(2,1)}) custom-call(s32[1]{0:T(128)} %bitcast.refs_0_, bf16[4,8704]{1,0:T(4,128)(2,1)S(1)} %shard_map.131.refs_1_, bf16[4,8704]{1,0:T(4,128)(2,1)S(1)} %collective-permute-done.1.refs_2_, bf16[4,8704]{1,0:T(4,128)(2,1)S(1)} %collective-permute-done.2.refs_3_, ...), custom_call_target="tpu_custom_call" | custom-call | flops 8388608 | bytes 524288 | tf_op jit(solution)/shard_map/pallas_call | solution.py:179
  30.2 1.6 %collective-permute-start.4 = (bf16[192,1024]{1,0:T(8,128)(2,1)S(1)}, bf16[192,1024]{1,0:T(8,128)(2,1)S(1)}, u32[]{:S(2)}, u32[]{:S(2)}) collective-permute-start(bf16[192,1024]{1,0:T(8,128)(2,1)S(1)} %shard_map.129), channel_id=1, source_target_pairs={{0,1},{1,0},{2,3},{3,2},{4,5},{5,4},{6,7},{7,6},{8,9},{9,8},{10,11... | collective-permute-start | bytes 1179656 | tf_op jit(solution)/shard_map/ppermute | solution.py:45
  31.8 3.6 %shard_map.136 = bf16[192,1024]{1,0:T(8,128)(2,1)S(1)} custom-call(s32[1]{0:T(128)} %bitcast.10.refs_0_, bf16[192,3072]{1,0:T(8,128)(2,1)S(1)} %copy-done.3, bf16[3072,4096]{1,0:T(8,128)(2,1)} %refs_4_.3), custom_call_target="tpu_custom_call" | custom-call | flops 75497472 | bytes 393216 | tf_op jit(solution)/shard_map/pallas_call | solution.py:79
  35.4 1.5 %collective-permute-start.5 = (bf16[192,1024]{1,0:T(8,128)(2,1)S(1)}, bf16[192,1024]{1,0:T(8,128)(2,1)S(1)}, u32[]{:S(2)}, u32[]{:S(2)}) collective-permute-start(bf16[192,1024]{1,0:T(8,128)(2,1)S(1)} %shard_map.136), channel_id=1, source_target_pairs={{0,2},{1,3},{2,0},{3,1},{4,6},{5,7},{6,4},{7,5},{8,10},{9,11},{10,... | collective-permute-start | bytes 1179656 | tf_op jit(solution)/shard_map/ppermute | solution.py:45
  36.9 3.8 %shard_map.135.refs_2_ = f32[192,1024]{1,0:T(8,128)S(1)} custom-call(s32[1]{0:T(128)} %bitcast.refs_0_, bf16[192,3072]{1,0:T(8,128)(2,1)S(1)} %copy-done.3, bf16[3072,4096]{1,0:T(8,128)(2,1)} %refs_4_.3, bf16[192,1024]{1,0:T(8,128)(2,1)S(1)} %copy-done.5), custom_call_target="tpu_custom_call" | custom-call | flops 75497472 | bytes 393216 | tf_op jit(solution)/shard_map/pallas_call | solution.py:79
  40.8 0.3 collective-permute-done.4.refs_4_
  41.0 5.1 %collective-permute-done.5.refs_5_ = bf16[192,1024]{1,0:T(8,128)(2,1)S(1)} collective-permute-done((bf16[192,1024]{1,0:T(8,128)(2,1)S(1)}, bf16[192,1024]{1,0:T(8,128)(2,1)S(1)}, u32[]{:S(2)}, u32[]{:S(2)}) %collective-permute-start.5) | collective-permute-done | bytes 393248 | tf_op jit(solution)/shard_map/ppermute | solution.py:45
  46.2 1.7 %shard_map.137 = (bf16[36,1024]{1,0:T(8,128)(2,1)S(1)}, bf16[36,1024]{1,0:T(8,128)(2,1)S(1)}, bf16[36,1024]{1,0:T(8,128)(2,1)S(1)}, bf16[36,1024]{1,0:T(8,128)(2...) custom-call(s32[1]{0:T(128)} %bitcast.9.refs_0_.wide_ref, ...), custom_call_target="tpu_custom_call" | custom-call | flops 226492416 | bytes 1966080 | tf_op jit(solution)/shard_map/pallas_call | solution.py:231
  47.9 1.6 %collective-permute-start.7 = (bf16[36,1024]{1,0:T(8,128)(2,1)S(1)}, bf16[36,1024]{1,0:T(8,128)(2,1)S(1)}, u32[]{:S(2)}, u32[]{:S(2)}) collective-permute-start(bf16[36,1024]{1,0:T(8,128)(2,1)S(1)} %get-tuple-element.68), channel_id=1, source_target_pairs={{0,8},{4,12},{8,0},{12,4},{16,24},{20,28},{24,16},{28,20},{1,9},{5... | collective-permute-start | bytes 221192 | tf_op jit(solution)/shard_map/ppermute | solution.py:45
  49.4 0.3 collective-permute-start.8
  49.7 2.6 %collective-permute-start.9 = (bf16[36,1024]{1,0:T(8,128)(2,1)}, bf16[36,1024]{1,0:T(8,128)(2,1)S(1)}, u32[]{:S(2)}, u32[]{:S(2)}) collective-permute-start(bf16[36,1024]{1,0:T(8,128)(2,1)} %get-tuple-element.70), channel_id=1, source_target_pairs={{0,16},{4,20},{8,24},{12,28},{16,0},{20,4},{24,8},{28,12},{1,17},{... | collective-permute-start | bytes 221192 | tf_op jit(solution)/shard_map/ppermute | solution.py:45
  52.3 3.5 %collective-permute-start.11 = (bf16[36,1024]{1,0:T(8,128)(2,1)S(1)}, bf16[36,1024]{1,0:T(8,128)(2,1)S(1)}, u32[]{:S(2)}, u32[]{:S(2)}) collective-permute-start(bf16[36,1024]{1,0:T(8,128)(2,1)S(1)} %get-tuple-element.72), channel_id=1, source_target_pairs={{0,24},{4,28},{8,16},{12,20},{16,8},{20,12},{24,0},{28,4},{1,25},{... | collective-permute-start | bytes 221192 | tf_op jit(solution)/shard_map/ppermute | solution.py:45
  55.9 0.2 collective-permute-start.12
  56.1 1.2 %copy-done = bf16[128,4224]{1,0:T(8,128)(2,1)S(1)} copy-done((bf16[128,4224]{1,0:T(8,128)(2,1)S(1)}, bf16[128,4224]{1,0:T(8,128)(2,1)}, u32[]{:S(2)}) %copy-start) | copy-done | bytes 1081368
  57.3 6.1 %shard_map.133.refs_2_ = bf16[3072,128]{1,0:T(8,128)(2,1)S(1)} custom-call(bf16[128,4224]{1,0:T(8,128)(2,1)S(1)} %copy-done, bf16[3072,4096]{1,0:T(8,128)(2,1)} %refs_4_.3), custom_call_target="tpu_custom_call" | custom-call | flops 1610612736 | bytes 12582912 | tf_op jit(solution)/shard_map/pallas_call | solution.py:364
  63.4 0.9 shard_map.134
  64.3 0.7 collective-permute-done.10.refs_5_
  65.0 1.3 %shard_map.139 = (bf16[288,512]{1,0:T(8,128)(2,1)S(1)}, bf16[288,512]{1,0:T(8,128)(2,1)S(1)}) custom-call(s32[1]{0:T(128)} %bitcast.9.refs_0_.wide_ref, bf16[36,1024]{1,0:T(8,128)(2,1)S(1)} %get-tuple-element.75.refs_0_, bf16[36,1024]{1,0:T(8,128)(2,1)S(1)} %collective-permute-done.6.refs_1_, bf16[36,1024]{1,0:T(8,128)(2,1)S(1)} %collective-permute-done.7.refs_2_, ...), custom_call_target="tpu_custom_call" | custom-call | flops 169869312 | bytes 1179648 | tf_op jit(solution)/shard_map/pallas_call | solution.py:263
  66.4 1.6 %collective-permute-start.14 = (bf16[288,512]{1,0:T(8,128)(2,1)S(1)}, bf16[288,512]{1,0:T(8,128)(2,1)S(1)}, u32[]{:S(2)}, u32[]{:S(2)}) collective-permute-start(bf16[288,512]{1,0:T(8,128)(2,1)S(1)} %get-tuple-element.83.refs_1_.refs_13_), channel_id=1, source_target_pairs={{0,2},{1,3},{2,0},{3,1},{4,6},{5,7},{6,4},{7,5},{8,10},{9,11},{10,... | collective-permute-start | bytes 884744 | tf_op jit(solution)/shard_map/ppermute | solution.py:45
  68.0 0.5 collective-permute-start.13
  68.6 1.3 %collective-permute-start.17 = (bf16[288,512]{1,0:T(8,128)(2,1)S(1)}, bf16[288,512]{1,0:T(8,128)(2,1)S(1)}, u32[]{:S(2)}, u32[]{:S(2)}) collective-permute-start(bf16[288,512]{1,0:T(8,128)(2,1)S(1)} %get-tuple-element.85.refs_2_.refs_14_), channel_id=1, source_target_pairs={{0,2},{1,3},{2,0},{3,1},{4,6},{5,7},{6,4},{7,5},{8,10},{9,11},{10,... | collective-permute-start | bytes 884744 | tf_op jit(solution)/shard_map/ppermute | solution.py:45
  69.8 0.7 collective-permute-start.16
  70.6 6.0 %shard_map.138.refs_12_ = bf16[3072,128]{1,0:T(8,128)(2,1)S(1)} custom-call(bf16[128,4224]{1,0:T(8,128)(2,1)S(1)} %copy-done.1, bf16[3072,4096]{1,0:T(8,128)(2,1)} %refs_4_.3, bf16[3072,128]{1,0:T(8,128)(2,1)S(1)} %shard_map.133.refs_2_), custom_call_target="tpu_custom_call", output_to_operand_aliasing={{}: (2, {})} | custom-call | flops 1610612736 | bytes 12582912 | tf_op jit(solution)/shard_map/pallas_call | solution.py:364
  76.6 0.7 copy-done.8
  77.3 0.5 collective-permute-done.13.refs_3_
  77.8 1.0 collective-permute-start.15
  78.8 1.0 copy-done.9
  79.8 9.5 %shard_map.140 = (f32[288,3072]{1,0:T(8,128)S(1)}, f32[288,1]{1,0:T(8,128)S(1)}, f32[288,128]{1,0:T(8,128)S(1)}) custom-call(s32[4]{0:T(128)S(1)} %pad_add_fusion.1.refs_0_, bf16[288,512]{1,0:T(8,128)(2,1)S(1)} %get-tuple-element.83.refs_1_.refs_13_, bf16[288,512]{1,0:T(8,128)(2,1)S(1)} %get-tuple-element.85.refs_2_.refs_14_, ...), custom_call_target="tpu_custom_call" | custom-call | flops 3623878656 | bytes 12582912 | tf_op jit(solution)/shard_map/pallas_call | solution.py:437
  89.3 1.8 %copy-done.4 = f32[288,3072]{1,0:T(8,128)} copy-done((f32[288,3072]{1,0:T(8,128)}, f32[288,3072]{1,0:T(8,128)S(1)}, u32[]{:S(2)}) %copy-start.4) | copy-done | bytes 3538968
  91.1 0.7 copy-done.10
  91.7 0.7 copy-done.12
  92.4 0.7 copy-done.6
  93.1 0.8 collective-permute-start.18
  94.1 1.0 copy-done.7
  95.0 0.9 copy-done.11
  95.9 0.9 copy-done.13
  96.8 7.6 %shard_map.141 = (f32[288,3072]{1,0:T(8,128)S(1)}, f32[288,1]{1,0:T(8,128)S(1)}, f32[288,128]{1,0:T(8,128)S(1)}) custom-call(s32[2]{0:T(128)S(1)} %pad_add_fusion.2.refs_0_, bf16[288,512]{1,0:T(8,128)(2,1)S(1)} %copy-done.7, bf16[288,512]{1,0:T(8,128)(2,1)S(1)} %collective-permute-done.17.refs_2_, bf16[3072,4096]{1,0:T(8,128)(2,1)} %refs_4_.3, ...), custom_call_target="tpu_custom_call" | custom-call | flops 1811939328 | bytes 6291456 | tf_op jit(solution)/shard_map/pallas_call | solution.py:437
  104.5 8.7 %shard_map.142 = (bf16[288,3072]{1,0:T(8,128)(2,1)}, bf16[288,1024]{1,0:T(8,128)(2,1)}, bf16[288,1024]{1,0:T(8,128)(2,1)}) custom-call(s32[3]{0:T(128)S(1)} %pad_add_fusion.refs_0_, bf16[288,512]{1,0:T(8,128)(2,1)S(1)} %collective-permute-done.15.refs_1_, bf16[288,512]{1,0:T(8,128)(2,1)} %collective-permute-done.18.refs_2_, bf16[3072,4096]{1,0:T(8,128)(2,1)} %refs_4_.3, ...), custom_call_target="tpu_custom_call" | custom-call | flops 1811939328 | bytes 11599872 | tf_op jit(solution)/shard_map/pallas_call | solution.py:493
  (56 shorter events, 0.4 us)
Async XLA Ops:
  7.2 48.9 %all-gather.2.cloned.1.call-start = ((), (), s32[]{:S(2)}) async-start(), calls=%async_computation | async-start | bytes 1216512 | tf_op jit(solution)/shard_map/all_gather | solution.py:573
  7.2 1.3 %copy-start.2 = (bf16[192,3072]{1,0:T(8,128)(2,1)S(1)}, bf16[192,3072]{1,0:T(8,128)(2,1)}, u32[]{:S(2)}) copy-start(bf16[192,3072]{1,0:T(8,128)(2,1)} %refs_1_.8) | copy-start | bytes 3538948
  8.5 7.8 %copy-start.16 = (bf16[4,4096]{1,0:T(4,128)(2,1)S(1)}, bf16[4,4096]{1,0:T(4,128)(2,1)}, u32[]{:S(2)}) copy-start(bf16[4,4096]{1,0:T(4,128)(2,1)} %query_ref) | copy-start | bytes 98308
  8.5 7.8 %copy-start.17 = (bf16[4,4096]{1,0:T(4,128)(2,1)S(1)}, bf16[4,4096]{1,0:T(4,128)(2,1)}, u32[]{:S(2)}) copy-start(bf16[4,4096]{1,0:T(4,128)(2,1)} %passage_ref) | copy-start | bytes 98308
  8.5 7.8 %copy-start.18 = (f32[1024]{0:T(1024)S(1)}, f32[1024]{0:T(1024)}, u32[]{:S(2)}) copy-start(f32[1024]{0:T(1024)} %param.19) | copy-start | bytes 12292
  8.5 11.3 %copy-start.3 = (bf16[192,3072]{1,0:T(8,128)(2,1)S(1)}, bf16[192,3072]{1,0:T(8,128)(2,1)}, u32[]{:S(2)}) copy-start(bf16[192,3072]{1,0:T(8,128)(2,1)} %refs_1_.8) | copy-start | bytes 3538948
  12.3 16.4 %collective-permute-start = (bf16[192,1024]{1,0:T(8,128)(2,1)S(1)}, bf16[192,1024]{1,0:T(8,128)(2,1)S(1)}, u32[]{:S(2)}, u32[]{:S(2)}) collective-permute-start(bf16[192,1024]{1,0:T(8,128)(2,1)S(1)} %shard_map.130), channel_id=1, source_target_pairs={{0,3},{1,2},{2,1},{3,0},{4,7},{5,6},{6,5},{7,4},{8,11},{9,10},{10,... | collective-permute-start | bytes 1179656 | tf_op jit(solution)/shard_map/ppermute | solution.py:45
  16.3 11.4 %collective-permute-start.3 = (bf16[4,8704]{1,0:T(4,128)(2,1)S(1)}, bf16[4,8704]{1,0:T(4,128)(2,1)S(1)}, u32[]{:S(2)}, u32[]{:S(2)}) collective-permute-start(bf16[4,8704]{1,0:T(4,128)(2,1)S(1)} %shard_map.131.refs_1_), channel_id=1, source_target_pairs={{0,3},{1,2},{2,1},{3,0},{4,7},{5,6},{6,5},{7,4},{8,11},{9,10},{10,... | collective-permute-start | bytes 208904 | tf_op jit(solution)/shard_map/ppermute | solution.py:45
  16.4 12.0 %collective-permute-start.2 = (bf16[4,8704]{1,0:T(4,128)(2,1)S(1)}, bf16[4,8704]{1,0:T(4,128)(2,1)S(1)}, u32[]{:S(2)}, u32[]{:S(2)}) collective-permute-start(bf16[4,8704]{1,0:T(4,128)(2,1)S(1)} %shard_map.131.refs_1_), channel_id=1, source_target_pairs={{0,2},{1,3},{2,0},{3,1},{4,6},{5,7},{6,4},{7,5},{8,10},{9,11},{10,... | collective-permute-start | bytes 208904 | tf_op jit(solution)/shard_map/ppermute | solution.py:45
  18.3 10.3 %collective-permute-start.1 = (bf16[4,8704]{1,0:T(4,128)(2,1)S(1)}, bf16[4,8704]{1,0:T(4,128)(2,1)S(1)}, u32[]{:S(2)}, u32[]{:S(2)}) collective-permute-start(bf16[4,8704]{1,0:T(4,128)(2,1)S(1)} %shard_map.131.refs_1_), channel_id=1, source_target_pairs={{0,1},{1,0},{2,3},{3,2},{4,5},{5,4},{6,7},{7,6},{8,9},{9,8},{10,11... | collective-permute-start | bytes 208904 | tf_op jit(solution)/shard_map/ppermute | solution.py:45
  19.8 8.8 %copy-start.19 = (s32[192,1]{0,1:T(1,128)S(1)}, s32[192,1]{0,1:T(1,128)}, u32[]{:S(2)}) copy-start(s32[192,1]{0,1:T(1,128)} %param.15) | copy-start | bytes 2308
  19.8 8.8 %copy-start.20 = (f32[16]{0:T(128)S(1)}, f32[16]{0:T(128)}, u32[]{:S(2)}) copy-start(f32[16]{0:T(128)} %param.12) | copy-start | bytes 196
  19.8 8.8 %copy-start.21 = (s32[16]{0:T(128)S(1)}, s32[16]{0:T(128)}, u32[]{:S(2)}) copy-start(s32[16]{0:T(128)} %param.13) | copy-start | bytes 196
  19.9 8.8 %copy-start.22 = (s32[1,16]{1,0:T(1,128)S(1)}, s32[1,16]{1,0:T(1,128)}, u32[]{:S(2)}) copy-start(s32[1,16]{1,0:T(1,128)} %refs_8_.2) | copy-start | bytes 196
  30.2 10.8 %collective-permute-start.4 = (bf16[192,1024]{1,0:T(8,128)(2,1)S(1)}, bf16[192,1024]{1,0:T(8,128)(2,1)S(1)}, u32[]{:S(2)}, u32[]{:S(2)}) collective-permute-start(bf16[192,1024]{1,0:T(8,128)(2,1)S(1)} %shard_map.129), channel_id=1, source_target_pairs={{0,1},{1,0},{2,3},{3,2},{4,5},{5,4},{6,7},{7,6},{8,9},{9,8},{10,11... | collective-permute-start | bytes 1179656 | tf_op jit(solution)/shard_map/ppermute | solution.py:45
  31.8 5.1 %copy-start.5 = (bf16[192,1024]{1,0:T(8,128)(2,1)S(1)}, bf16[192,1024]{1,0:T(8,128)(2,1)}, u32[]{:S(2)}) copy-start(bf16[192,1024]{1,0:T(8,128)(2,1)} %refs_3_.3) | copy-start | bytes 1179652
  35.4 10.7 %collective-permute-start.5 = (bf16[192,1024]{1,0:T(8,128)(2,1)S(1)}, bf16[192,1024]{1,0:T(8,128)(2,1)S(1)}, u32[]{:S(2)}, u32[]{:S(2)}) collective-permute-start(bf16[192,1024]{1,0:T(8,128)(2,1)S(1)} %shard_map.136), channel_id=1, source_target_pairs={{0,2},{1,3},{2,0},{3,1},{4,6},{5,7},{6,4},{7,5},{8,10},{9,11},{10,... | collective-permute-start | bytes 1179656 | tf_op jit(solution)/shard_map/ppermute | solution.py:45
  47.9 4.5 %collective-permute-start.6 = (bf16[36,1024]{1,0:T(8,128)(2,1)S(1)}, bf16[36,1024]{1,0:T(8,128)(2,1)S(1)}, u32[]{:S(2)}, u32[]{:S(2)}) collective-permute-start(bf16[36,1024]{1,0:T(8,128)(2,1)S(1)} %get-tuple-element.67), channel_id=1, source_target_pairs={{0,4},{4,0},{8,12},{12,8},{16,20},{20,16},{24,28},{28,24},{1,5},{5... | collective-permute-start | bytes 221192 | tf_op jit(solution)/shard_map/ppermute | solution.py:45
  47.9 8.0 %collective-permute-start.7 = (bf16[36,1024]{1,0:T(8,128)(2,1)S(1)}, bf16[36,1024]{1,0:T(8,128)(2,1)S(1)}, u32[]{:S(2)}, u32[]{:S(2)}) collective-permute-start(bf16[36,1024]{1,0:T(8,128)(2,1)S(1)} %get-tuple-element.68), channel_id=1, source_target_pairs={{0,8},{4,12},{8,0},{12,4},{16,24},{20,28},{24,16},{28,20},{1,9},{5... | collective-permute-start | bytes 221192 | tf_op jit(solution)/shard_map/ppermute | solution.py:45
  49.4 14.8 %collective-permute-start.8 = (bf16[36,1024]{1,0:T(8,128)(2,1)}, bf16[36,1024]{1,0:T(8,128)(2,1)S(1)}, u32[]{:S(2)}, u32[]{:S(2)}) collective-permute-start(bf16[36,1024]{1,0:T(8,128)(2,1)} %get-tuple-element.69), channel_id=1, source_target_pairs={{0,12},{4,8},{8,4},{12,0},{16,28},{20,24},{24,20},{28,16},{1,13},{... | collective-permute-start | bytes 221192 | tf_op jit(solution)/shard_map/ppermute | solution.py:45
  49.7 14.6 %collective-permute-start.9 = (bf16[36,1024]{1,0:T(8,128)(2,1)}, bf16[36,1024]{1,0:T(8,128)(2,1)S(1)}, u32[]{:S(2)}, u32[]{:S(2)}) collective-permute-start(bf16[36,1024]{1,0:T(8,128)(2,1)} %get-tuple-element.70), channel_id=1, source_target_pairs={{0,16},{4,20},{8,24},{12,28},{16,0},{20,4},{24,8},{28,12},{1,17},{... | collective-permute-start | bytes 221192 | tf_op jit(solution)/shard_map/ppermute | solution.py:45
  52.3 12.7 %collective-permute-start.10 = (bf16[36,1024]{1,0:T(8,128)(2,1)}, bf16[36,1024]{1,0:T(8,128)(2,1)S(1)}, u32[]{:S(2)}, u32[]{:S(2)}) collective-permute-start(bf16[36,1024]{1,0:T(8,128)(2,1)} %get-tuple-element.71), channel_id=1, source_target_pairs={{0,20},{4,16},{8,28},{12,24},{16,4},{20,0},{24,12},{28,8},{1,21},{... | collective-permute-start | bytes 221192 | tf_op jit(solution)/shard_map/ppermute | solution.py:45
  52.3 12.7 %collective-permute-start.11 = (bf16[36,1024]{1,0:T(8,128)(2,1)S(1)}, bf16[36,1024]{1,0:T(8,128)(2,1)S(1)}, u32[]{:S(2)}, u32[]{:S(2)}) collective-permute-start(bf16[36,1024]{1,0:T(8,128)(2,1)S(1)} %get-tuple-element.72), channel_id=1, source_target_pairs={{0,24},{4,28},{8,16},{12,20},{16,8},{20,12},{24,0},{28,4},{1,25},{... | collective-permute-start | bytes 221192 | tf_op jit(solution)/shard_map/ppermute | solution.py:45
  55.9 9.1 %collective-permute-start.12 = (bf16[36,1024]{1,0:T(8,128)(2,1)S(1)}, bf16[36,1024]{1,0:T(8,128)(2,1)S(1)}, u32[]{:S(2)}, u32[]{:S(2)}) collective-permute-start(bf16[36,1024]{1,0:T(8,128)(2,1)S(1)} %get-tuple-element.73), channel_id=1, source_target_pairs={{0,28},{4,24},{8,20},{12,16},{16,12},{20,8},{24,4},{28,0},{1,29},{... | collective-permute-start | bytes 221192 | tf_op jit(solution)/shard_map/ppermute | solution.py:45
  56.1 1.2 %copy-start = (bf16[128,4224]{1,0:T(8,128)(2,1)S(1)}, bf16[128,4224]{1,0:T(8,128)(2,1)}, u32[]{:S(2)}) copy-start(bf16[128,4224]{1,0:T(8,128)(2,1)} %all-gather.2.cloned.1.call-done.refs_0_.refs_1_.refs_9_.refs_10_.refs_11_.refs_12_.refs_5_.refs_6_.refs_15_) | copy-start | bytes 3244036
  57.3 6.1 %copy-start.1 = (bf16[128,4224]{1,0:T(8,128)(2,1)S(1)}, bf16[128,4224]{1,0:T(8,128)(2,1)}, u32[]{:S(2)}) copy-start(bf16[128,4224]{1,0:T(8,128)(2,1)} %all-gather.2.cloned.1.call-done.refs_0_.refs_1_.refs_9_.refs_10_.refs_11_.refs_12_.refs_5_.refs_6_.refs_15_) | copy-start | bytes 3244036
  64.3 2.1 %copy-start.14 = (bf16[288,128]{1,0:T(8,128)(2,1)}, bf16[288,128]{1,0:T(8,128)(2,1)S(1)}, u32[]{:S(2)}) copy-start(bf16[288,128]{1,0:T(8,128)(2,1)S(1)} %get-tuple-element.98.refs_10_) | copy-start | bytes 221188
  66.4 10.2 %collective-permute-start.14 = (bf16[288,512]{1,0:T(8,128)(2,1)S(1)}, bf16[288,512]{1,0:T(8,128)(2,1)S(1)}, u32[]{:S(2)}, u32[]{:S(2)}) collective-permute-start(bf16[288,512]{1,0:T(8,128)(2,1)S(1)} %get-tuple-element.83.refs_1_.refs_13_), channel_id=1, source_target_pairs={{0,2},{1,3},{2,0},{3,1},{4,6},{5,7},{6,4},{7,5},{8,10},{9,11},{10,... | collective-permute-start | bytes 884744 | tf_op jit(solution)/shard_map/ppermute | solution.py:45
  68.0 9.9 %collective-permute-start.13 = (bf16[288,512]{1,0:T(8,128)(2,1)S(1)}, bf16[288,512]{1,0:T(8,128)(2,1)S(1)}, u32[]{:S(2)}, u32[]{:S(2)}) collective-permute-start(bf16[288,512]{1,0:T(8,128)(2,1)S(1)} %get-tuple-element.83.refs_1_.refs_13_), channel_id=1, source_target_pairs={{0,1},{1,0},{2,3},{3,2},{4,5},{5,4},{6,7},{7,6},{8,9},{9,8},{10,11... | collective-permute-start | bytes 884744 | tf_op jit(solution)/shard_map/ppermute | solution.py:45
  68.6 23.8 %collective-permute-start.17 = (bf16[288,512]{1,0:T(8,128)(2,1)S(1)}, bf16[288,512]{1,0:T(8,128)(2,1)S(1)}, u32[]{:S(2)}, u32[]{:S(2)}) collective-permute-start(bf16[288,512]{1,0:T(8,128)(2,1)S(1)} %get-tuple-element.85.refs_2_.refs_14_), channel_id=1, source_target_pairs={{0,2},{1,3},{2,0},{3,1},{4,6},{5,7},{6,4},{7,5},{8,10},{9,11},{10,... | collective-permute-start | bytes 884744 | tf_op jit(solution)/shard_map/ppermute | solution.py:45
  69.8 22.6 %collective-permute-start.16 = (bf16[288,512]{1,0:T(8,128)(2,1)S(1)}, bf16[288,512]{1,0:T(8,128)(2,1)S(1)}, u32[]{:S(2)}, u32[]{:S(2)}) collective-permute-start(bf16[288,512]{1,0:T(8,128)(2,1)S(1)} %get-tuple-element.85.refs_2_.refs_14_), channel_id=1, source_target_pairs={{0,1},{1,0},{2,3},{3,2},{4,5},{5,4},{6,7},{7,6},{8,9},{9,8},{10,11... | collective-permute-start | bytes 884744 | tf_op jit(solution)/shard_map/ppermute | solution.py:45
  76.6 0.7 copy-start.8
  77.8 26.6 %collective-permute-start.15 = (bf16[288,512]{1,0:T(8,128)(2,1)S(1)}, bf16[288,512]{1,0:T(8,128)(2,1)S(1)}, u32[]{:S(2)}, u32[]{:S(2)}) collective-permute-start(bf16[288,512]{1,0:T(8,128)(2,1)S(1)} %collective-permute-done.13.refs_3_), channel_id=1, source_target_pairs={{0,2},{1,3},{2,0},{3,1},{4,6},{5,7},{6,4},{7,5},{8,10},{9,11},{10,... | collective-permute-start | bytes 884744 | tf_op jit(solution)/shard_map/ppermute | solution.py:45
  78.8 1.0 copy-start.9
  89.3 1.8 %copy-start.4 = (f32[288,3072]{1,0:T(8,128)}, f32[288,3072]{1,0:T(8,128)S(1)}, u32[]{:S(2)}) copy-start(f32[288,3072]{1,0:T(8,128)S(1)} %get-tuple-element.92.refs_7_) | copy-start | bytes 10616836
  91.1 0.7 copy-start.10
  91.7 0.7 copy-start.12
  92.4 0.7 copy-start.6
  93.1 11.4 %collective-permute-start.18 = (bf16[288,512]{1,0:T(8,128)(2,1)S(1)}, bf16[288,512]{1,0:T(8,128)(2,1)}, u32[]{:S(2)}, u32[]{:S(2)}) collective-permute-start(bf16[288,512]{1,0:T(8,128)(2,1)S(1)} %collective-permute-done.17.refs_2_), channel_id=1, source_target_pairs={{0,1},{1,0},{2,3},{3,2},{4,5},{5,4},{6,7},{7,6},{8,9},{9,8},{10,11... | collective-permute-start | bytes 884744 | tf_op jit(solution)/shard_map/ppermute | solution.py:45
  94.1 1.0 copy-start.7
  95.0 0.9 copy-start.11
  95.9 0.9 copy-start.13
  96.8 7.7 %copy-start.15 = (bf16[288,128]{1,0:T(8,128)(2,1)S(1)}, bf16[288,128]{1,0:T(8,128)(2,1)}, u32[]{:S(2)}) copy-start(bf16[288,128]{1,0:T(8,128)(2,1)} %copy-done.14) | copy-start | bytes 221188
Sparse Core Ops, SparseCore 0:
  30.3 23.7 all-gather.1

commit v8 on v6

--- a/solution.py
+++ b/solution.py
@@ -12,10 +12,11 @@
 i32 = jnp.int32
 lane = 128
 kernel_vmem = 46 * 1024 * 1024
-
-
-def params():
-    return pltpu.CompilerParams(vmem_limit_bytes=kernel_vmem)
+whole_vmem = 60 * 1024 * 1024
+
+
+def params(vmem=kernel_vmem):
+    return pltpu.CompilerParams(vmem_limit_bytes=vmem)
 
 
 def cost(flops, nbytes):
@@ -118,7 +119,7 @@
         payload_body,
         out_shape=jax.ShapeDtypeStruct((own, 2 * features + 2 * piece), bf16),
         scratch_shapes=[pltpu.VMEM((own, piece), f32)],
-        compiler_params=params(),
+        compiler_params=params(whole_vmem),
         cost_estimate=cost(own * features, 8 * own * features),
     )(query_emb, passage_emb, gain[None])
 
@@ -339,11 +340,12 @@
     )(wide[None], low)
 
 
-def low_act_body(low_ref, w_hbm, out_ref, weights, sems):
+def low_act_body(part, low_ref, w_hbm, *refs):
+    out_ref, weights, sems = refs[-3:]
     count, tile, _ = weights.shape
 
     def weight_copy(t):
-        rows = pl.ds(pl.multiple_of(t * tile, tile), tile)
+        rows = pl.ds(pl.multiple_of((part * count + t) * tile, tile), tile)
         return pltpu.make_async_copy(w_hbm.at[rows], weights.at[t], sems.at[t])
 
     for t in range(count):
@@ -356,76 +358,74 @@
         out_ref[rows] = dot_t(weights[t], low_ref[...]).astype(bf16)
 
 
-def low_activations(low, features, w_down):
+def low_activations(low, features, w_down, part, parts, filled=()):
     pairs = low.shape[0]
     depth = w_down.shape[0]
-    tile = tile_of(depth, 512)
-    count = depth // tile
-    return pl.pallas_call(
-        low_act_body,
+    some = depth // parts
+    tile = tile_of(some, 512)
+    count = some // tile
+    anywhere = pl.BlockSpec(memory_space=pl.ANY)
+    return pl.pallas_call(
+        lambda *refs: low_act_body(part, *refs),
         grid=(1,),
-        in_specs=[
-            pl.BlockSpec((pairs, features), lambda j: (0, 0)),
-            pl.BlockSpec(memory_space=pl.ANY),
-        ],
-        out_specs=pl.BlockSpec((depth, pairs), lambda j: (0, 0)),
+        in_specs=[pl.BlockSpec((pairs, features), lambda j: (0, 0)), anywhere]
+        + [anywhere] * len(filled),
+        out_specs=pl.BlockSpec((some, pairs), lambda j: (part, 0)),
         out_shape=jax.ShapeDtypeStruct((depth, pairs), bf16),
         scratch_shapes=[
             pltpu.VMEM((count, tile, features), bf16),
             pltpu.SemaphoreType.DMA((count,)),
         ],
+        input_output_aliases={2: 0} if filled else {},
         compiler_params=params(),
-        cost_estimate=cost(2 * pairs * depth * features, 2 * depth * features),
-    )(low, w_down)
+        cost_estimate=cost(2 * pairs * some * features, 2 * some * features),
+    )(low, w_down, *filled)
 
 
 def statistics(hids, lows):
     squares, cross = 0.0, 0.0
-    for hid, low_ref in zip(hids, lows):
-        wide_hid = hid.astype(f32)
-        squares = squares + jnp.sum(wide_hid * wide_hid, axis=1, keepdims=True)
-        cross = cross + dot_t(hid, low_ref[...])
+    for hid_ref, low_ref in zip(hids, lows):
+        hid = hid_ref[...].astype(f32)
+        squares = squares + jnp.sum(hid * hid, axis=1, keepdims=True)
+        cross = cross + dot_t(hid_ref[...], low_ref[...])
     return squares, cross
 
 
 def product(hids, weights):
     total = 0.0
-    for hid, w_ref in zip(hids, weights):
-        total = total + dot_t(hid, w_ref[...])
+    for hid_ref, w_ref in zip(hids, weights):
+        total = total + dot_t(hid_ref[...], w_ref[...])
     return total
 
 
-def group_specs(count, rows_of_block, width, row_step):
-    half = width // 2
+def weight_specs(count, tile, width):
     return [
-        pl.BlockSpec(
-            (rows_of_block, half), lambda j, g, n=n, side=side: (row_step * j, 2 * g[n] + side)
-        )
+        pl.BlockSpec((tile // 2, width), lambda j, g, n=n, side=side: (2 * j + side, g[n]))
         for n in range(count)
         for side in range(2)
     ]
 
 
-def halves_of(ref):
-    half = ref.shape[1] // 2
-    return [ref[:, :half], ref[:, half:]]
+def low_specs(count, pairs, width):
+    return [pl.BlockSpec((pairs, width), lambda j, g, n=n: (0, g[n])) for n in range(count)]
 
 
 def back_body(count, carried, places_ref, *refs):
-    hids, refs = refs[:count], refs[count:]
-    weights, lows, refs = refs[: 2 * count], refs[2 * count : 4 * count], refs[4 * count :]
-    before, (acc_ref, squares_ref, cross_ref) = refs[:carried], refs[carried:]
-    halves = [half for hid in hids for half in halves_of(hid)]
+    hids, weights, refs = refs[:count], refs[count : 3 * count], refs[3 * count :]
+    lows, before, (acc_ref, squares_ref, cross_ref) = refs[:count], refs[count:-3], refs[-3:]
 
     @pl.when(pl.program_id(0) == 0)
     def _():
-        squares, cross = statistics(halves, lows)
+        squares, cross = statistics(hids, lows)
         if carried:
             squares, cross = before[1][...] + squares, before[2][...] + cross
         squares_ref[...], cross_ref[...] = squares, cross
 
-    total = product(halves, weights)
-    acc_ref[...] = before[0][...] + total if carried else total
+    half = acc_ref.shape[1] // 2
+    for side in range(2):
+        at = slice(side * half, (side + 1) * half)
+        total = product(hids, weights[side::2])
+        acc_ref[:, at] = before[0][:, at] + total if carried else total
 
 
 def carried_specs(rows, pairs, tile):
@@ -449,8 +449,8 @@
             num_scalar_prefetch=1,
             grid=(depth // tile,),
             in_specs=[pl.BlockSpec((rows, width), lambda j, g: (0, 0))] * count
-            + group_specs(count, tile, width, 1)
-            + group_specs(count, pairs, width, 0)
+            + weight_specs(count, tile, width)
+            + low_specs(count, pairs, width)
             + totals[: len(before)],
             out_specs=totals,
         ),
@@ -461,35 +461,40 @@
         ],
         compiler_params=params(),
         cost_estimate=cost(2 * rows * depth * width * count, 2 * depth * width * count),
-    )(places, *pieces, *[w_down] * 2 * count, *[low] * 2 * count, *before)
+    )(places, *pieces, *[w_down] * 2 * count, *[low] * count, *before)
 
 
 def finish_body(features, count, places_ref, *refs):
-    hids, weights, lows, refs = refs[:count], refs[count : count + 2], refs[count + 2 : count + 4], refs[count + 4 :]
-    acc_ref, squares_ref, cross_ref, hot_ref, share_ref, low_act_ref = refs[:6]
-    own_ref, own_low_ref, gain_ref, act_out, resid_out, normed_out, hid, lead, pull = refs[6:]
-    rows = own_ref.shape[0]
-    part = rows // count
+    hids, weights, refs = refs[:count], refs[count : count + 2], refs[count + 2 :]
+    low_ref, acc_ref, squares_ref, cross_ref, hot_ref, share_ref, low_act_ref = refs[:7]
+    own_ref, own_low_ref, gain_ref, act_out, resid_out, normed_out = refs[7:13]
+    hid, lead, pull, scale = refs[13:]
+    part = hids[0].shape[0]
+    step = own_ref.shape[0]
 
     @pl.when(pl.program_id(0) == 0)
     def _():
         for n in range(count):
             hid[n * part : (n + 1) * part] = hids[n][...]
-        squares, cross = statistics(halves_of(hid), lows)
-        hot = hot_ref[...]
-        inner = jnp.sum((cross_ref[...] + cross) * hot.astype(f32), axis=1, keepdims=True)
-        inner = inner * share_ref[...]
+        squares, cross = statistics([hid], [low_ref])
+        hot = hot_ref[...].astype(f32)
+        inner = jnp.sum((cross_ref[...] + cross) * hot, axis=1, keepdims=True) * share_ref[...]
         inv_rms = lax.rsqrt((squares_ref[...] + squares) / features + norm_eps)
+        scale[...] = inv_rms
         lead[...] = inv_rms * share_ref[...]
         pull[...] = inv_rms * inv_rms * inv_rms * inner / features
-        own = own_ref[...].astype(f32)
-        own_low = dot(hot, own_low_ref[...])
-        resid_out[...] = (lead[...] * own_low - own * pull[...]).astype(bf16)
-        normed_out[...] = (gain_ref[...] * own * inv_rms).astype(bf16)
-
-    low_act = dot_t(hot_ref[...], low_act_ref[...])
-    hid_act = acc_ref[...] + product(halves_of(hid), weights)
-    act_out[...] = (lead[...] * low_act - pull[...] * hid_act).astype(bf16)
+
+    half = act_out.shape[1] // 2
+    for side in range(2):
+        at = slice(side * half, (side + 1) * half)
+        low_act = dot_t(hot_ref[...], low_act_ref[at])
+        hid_act = acc_ref[:, at] + product([hid], weights[side : side + 1])
+        act_out[:, at] = (lead[...] * low_act - pull[...] * hid_act).astype(bf16)
+    rows = pl.ds(pl.multiple_of(pl.program_id(0) * step, step), step)
+    own = own_ref[...].astype(f32)
+    own_low = dot(hot_ref[rows], own_low_ref[...])
+    resid_out[...] = (lead[rows] * own_low - own * pull[rows]).astype(bf16)
+    normed_out[...] = (gain_ref[...] * own * scale[rows]).astype(bf16)
 
 
 def finish(places, pieces, w_down, low, before, hot, share, low_act, own, gain):
@@ -498,37 +503,32 @@
     depth, features = w_down.shape
     pairs = hot.shape[1]
     tile = tile_of(depth, 512)
+    steps = depth // tile
+    step = rows // steps
 
     def whole(shape):
         return pl.BlockSpec(shape, lambda j, g: (0, 0))
 
+    row_spec = pl.BlockSpec((step, width), lambda j, g: (j, 0))
     return pl.pallas_call(
         lambda *refs: finish_body(features, count, *refs),
         grid_spec=pltpu.PrefetchScalarGridSpec(
             num_scalar_prefetch=1,
-            grid=(depth // tile,),
+            grid=(steps,),
             in_specs=[whole((rows // count, width))] * count
-            + group_specs(1, tile, width, 1)
-            + group_specs(1, pairs, width, 0)
+            + weight_specs(1, tile, width)
+            + low_specs(1, pairs, width)
             + carried_specs(rows, pairs, tile)
             + [
                 whole((rows, pairs)),
                 whole((rows, 1)),
                 pl.BlockSpec((tile, pairs), lambda j, g: (j, 0)),
-                whole((rows, width)),
+                row_spec,
                 pl.BlockSpec((pairs, width), lambda j, g: (0, g[1])),
                 whole((1, width)),
             ],
-            out_specs=[
-                pl.BlockSpec((rows, tile), lambda j, g: (0, j)),
-                whole((rows, width)),
-                whole((rows, width)),
-            ],
-            scratch_shapes=[
-                pltpu.VMEM((rows, width), bf16),
-                pltpu.VMEM((rows, 1), f32),
-                pltpu.VMEM((rows, 1), f32),
-            ],
+            out_specs=[pl.BlockSpec((rows, tile), lambda j, g: (0, j)), row_spec, row_spec],
+            scratch_shapes=[pltpu.VMEM((rows, width), bf16)] + [pltpu.VMEM((rows, 1), f32)] * 3,
         ),
         out_shape=[
             jax.ShapeDtypeStruct((rows, depth), bf16),
@@ -541,7 +541,7 @@
         places,
         *pieces,
         *[w_down] * 2,
-        *[low] * 2,
+        low,
         *before,
         hot,
         share,
@@ -588,14 +588,15 @@
     low = lax.all_gather(low_own, "wide", axis=0, tiled=True)
     packed = pack(wide, destination, own_term, arrived, wide_count, slot_count)
     routed = [packed[k] if k == 0 else swap(packed[k], k, "wide") for k in range(wide_count)]
-    low_act = low_activations(low, features, w_down)
+    low_act = low_activations(low, features, w_down, 0, 2)
     hot, share = slot_passages(wide, low, features, wide_count, slot_count, rows)
     low_act, hot, share, *routed = lax.optimization_barrier((low_act, hot, share, *routed))
     own = assemble(wide, routed)
 
     beside, above = swap(own, 1), swap(own, 2)
     totals = back(blk[None], [own], w_down, low)
-    *totals, beside, above = lax.optimization_barrier((*totals, beside, above))
+    low_act = low_activations(low, features, w_down, 1, 2, [low_act])
+    low_act, *totals, beside, above = lax.optimization_barrier((low_act, *totals, beside, above))
     top = swap(beside[: rows // 2], 2)
     bottom = swap(above[rows // 2 :], 1)
     totals = back(jnp.stack([blk ^ 1, blk ^ 2]), [beside, above], w_down, low, totals)
@@ -710,7 +711,7 @@
         pairs, tok_count = operands[2].shape[0], operands[7].shape[0]
         low_rank = 2 * wide_count * pairs <= 3 * tok_count
         per_pair = tok_count // pairs
-        aligned = operands[9].shape[0] % (lane * operands[0].shape[0]) == 0
+        aligned = operands[9].shape[0] % (lane * operands[0].shape[0]) == 0 and wide_count <= lane
         if low_rank and blk_count == 4 and aligned and per_pair * pairs == tok_count and wide_count & (wide_count - 1) == 0:
             return low_rank_shards(*operands)
         return row_shards(*operands)

time: 111 us -> 106 us (0.955)
  waiting for transfers between devices: 11.6 us -> 6.3 us
  Pallas kernels: 55.8 us -> 58.9 us
  local copies, waits for them, and re-layouts: 6.5 us -> 4.32 us
    ppermute x17, waiting for transfers between devices: 11.6 us -> 6.29 us  [swap(): lax.ppermute(rows, axis, [(i, i ^ k) for i in range(lax.axis_size(axis))])]
    pallas_call x1 -> x2, Pallas kernels: 9.85 us -> 12.1 us  [low_activations(): pl.pallas_call(lambda *refs: low_act_body(part, *refs), grid=(1,), in_spe...]
    unnamed x28 -> x24, local copies, waits for them, and re-layouts: 6.46 us -> 4.28 us
    pallas_call x1, Pallas kernels: 0.02 us -> 1.42 us  [payload(): pl.pallas_call(payload_body, out_shape=jax.ShapeDtypeStruct((own, 2 * fea...]
  transfers between devices with their start and end apart: 18 -> 18, of which waited for: 3 -> 2; matrix products, arithmetic and copies ran while one was open for 0% -> 0% of each run, Pallas kernels for 40% -> 44%
where the time goes in v8:
time: 106 us; the launch traced here: 105 us
  Pallas kernels  58.9 us (56%)
  starting transfers between devices  20.9 us (20%)
  between operations  14.3 us (13%)
  waiting for transfers between devices  6.3 us (6%)
  local copies, waits for them, and re-layouts  4.32 us (4%)
    ppermute x17, starting transfers between devices, swap(): lax.ppermute(rows, axis, [(i, i ^ k) for i in range(lax.axis_size(axis))])  20.9 us
    pallas_call x2, Pallas kernels, back(): pl.pallas_call(lambda *refs: back_body(count, len(before), *refs), grid_s...  16.6 us
    pallas_call x4, Pallas kernels, project(): pl.pallas_call(lambda *refs: project_body(len(own), *refs), in_specs=[pl....  15.6 us
    pallas_call x2, Pallas kernels, low_activations(): pl.pallas_call(lambda *refs: low_act_body(part, *refs), grid=(1,), in_spe...  12.1 us
    pallas_call x1, Pallas kernels, finish(): pl.pallas_call(lambda *refs: finish_body(features, count, *refs), grid_sp...  8.43 us
    ppermute x17, waiting for transfers between devices, swap(): lax.ppermute(rows, axis, [(i, i ^ k) for i in range(lax.axis_size(axis))])  6.29 us
    unnamed x24, local copies, waits for them, and re-layouts  4.28 us
  transfers between devices with their start and end apart: 18, of which 2 were waited for; matrix products, arithmetic and copies ran while one was open for 0% of the time, Pallas kernels for 44%

profile of v8, /device:TPU:0, one launch (start us, length us, event | category | flops | bytes accessed | tf_op | source)
XLA Modules:
  0.0 104.9 jit_solution(14587059128996783987)
XLA Ops:
  7.2 0.0 all-gather.2.cloned.1.call-start
  7.2 1.4 %shard_map.130.refs_1_ = bf16[4,8704]{1,0:T(4,128)(2,1)} custom-call(bf16[4,4096]{1,0:T(4,128)(2,1)} %query_ref.1, bf16[4,4096]{1,0:T(4,128)(2,1)} %passage_ref.1, f32[1,1024]{1,0:T(1,128)} %bitcast.9), custom_call_target="tpu_custom_call" | custom-call | flops 16384 | bytes 131072 | tf_op jit(solution)/shard_map/pallas_call | solution.py:118
  8.6 3.9 %collective-permute-start.2 = (bf16[4,8704]{1,0:T(4,128)(2,1)}, bf16[4,8704]{1,0:T(4,128)(2,1)S(1)}, u32[]{:S(2)}, u32[]{:S(2)}) collective-permute-start(bf16[4,8704]{1,0:T(4,128)(2,1)} %shard_map.130.refs_1_), channel_id=1, source_target_pairs={{0,3},{1,2},{2,1},{3,0},{4,7},{5,6},{6,5},{7,4},{8,11},{9,10},{10,... | collective-permute-start | bytes 208904 | tf_op jit(solution)/shard_map/ppermute | solution.py:46
  12.5 0.5 collective-permute-start.1
  13.0 0.1 collective-permute-start
  13.1 1.3 %copy-done.2 = bf16[192,3072]{1,0:T(8,128)(2,1)S(1)} copy-done((bf16[192,3072]{1,0:T(8,128)(2,1)S(1)}, bf16[192,3072]{1,0:T(8,128)(2,1)}, u32[]{:S(2)}) %copy-start.2) | copy-done | bytes 1179672
  14.4 0.0 copy-start.11
  14.4 3.8 %shard_map.129 = bf16[192,1024]{1,0:T(8,128)(2,1)S(1)} custom-call(s32[1]{0:T(128)} %bitcast.1.refs_0_, bf16[192,3072]{1,0:T(8,128)(2,1)S(1)} %copy-done.2, bf16[3072,4096]{1,0:T(8,128)(2,1)} %refs_4_.3), custom_call_target="tpu_custom_call" | custom-call | flops 1207959552 | bytes 7471104 | tf_op jit(solution)/shard_map/pallas_call | solution.py:84
  18.2 0.0 collective-permute-done.2.refs_4_
  18.2 0.0 collective-permute-done.1.refs_3_
  18.3 1.5 %shard_map.131 = (bf16[4,4096]{1,0:T(4,128)(2,1)}, bf16[16,4224]{1,0:T(8,128)(2,1)}) custom-call(s32[1]{0:T(128)} %bitcast.refs_0_, bf16[4,8704]{1,0:T(4,128)(2,1)S(1)} %copy-done.6, bf16[4,8704]{1,0:T(4,128)(2,1)S(1)} %collective-permute-done.refs_2_, bf16[4,8704]{1,0:T(4,128)(2,1)S(1)} %collective-permute-done.1.refs_3_, ...), custom_call_target="tpu_custom_call" | custom-call | flops 8388608 | bytes 524288 | tf_op jit(solution)/shard_map/pallas_call | solution.py:184
  19.8 0.0 all-gather.2.cloned.1.call-update
  19.9 3.0 %collective-permute-start.3 = (bf16[192,1024]{1,0:T(8,128)(2,1)S(1)}, bf16[192,1024]{1,0:T(8,128)(2,1)S(1)}, u32[]{:S(2)}, u32[]{:S(2)}) collective-permute-start(bf16[192,1024]{1,0:T(8,128)(2,1)S(1)} %shard_map.129), channel_id=1, source_target_pairs={{0,3},{1,2},{2,1},{3,0},{4,7},{5,6},{6,5},{7,4},{8,11},{9,10},{10,... | collective-permute-start | bytes 1179656 | tf_op jit(solution)/shard_map/ppermute | solution.py:46
  22.8 3.6 %shard_map.136 = bf16[192,1024]{1,0:T(8,128)(2,1)S(1)} custom-call(s32[1]{0:T(128)} %bitcast.8.refs_0_, bf16[192,3072]{1,0:T(8,128)(2,1)S(1)} %copy-done.3, bf16[3072,4096]{1,0:T(8,128)(2,1)} %refs_4_.3), custom_call_target="tpu_custom_call" | custom-call | flops 1207959552 | bytes 7471104 | tf_op jit(solution)/shard_map/pallas_call | solution.py:84
  26.5 0.0 copy-start.5
  26.5 4.5 %shard_map.135 = bf16[192,1024]{1,0:T(8,128)(2,1)} custom-call(s32[1]{0:T(128)} %bitcast.7.refs_0_, bf16[192,3072]{1,0:T(8,128)(2,1)S(1)} %copy-done.3, bf16[3072,4096]{1,0:T(8,128)(2,1)} %refs_4_.3), custom_call_target="tpu_custom_call" | custom-call | flops 1207959552 | bytes 7471104 | tf_op jit(solution)/shard_map/pallas_call | solution.py:84
  31.0 0.5 collective-permute-start.4
  31.5 0.0 collective-permute-start.5
  31.6 3.6 %shard_map.134.refs_2_ = f32[192,1024]{1,0:T(8,128)S(1)} custom-call(s32[1]{0:T(128)} %bitcast.refs_0_, bf16[192,3072]{1,0:T(8,128)(2,1)S(1)} %copy-done.3, bf16[3072,4096]{1,0:T(8,128)(2,1)} %refs_4_.3, bf16[192,1024]{1,0:T(8,128)(2,1)S(1)} %copy-done.5), custom_call_target="tpu_custom_call" | custom-call | flops 1207959552 | bytes 7471104 | tf_op jit(solution)/shard_map/pallas_call | solution.py:84
  35.2 0.0 collective-permute-done.3.refs_3_
  35.2 5.7 %collective-permute-done.4.refs_4_ = bf16[192,1024]{1,0:T(8,128)(2,1)S(1)} collective-permute-done((bf16[192,1024]{1,0:T(8,128)(2,1)}, bf16[192,1024]{1,0:T(8,128)(2,1)S(1)}, u32[]{:S(2)}, u32[]{:S(2)}) %collective-permute-start.4) | collective-permute-done | bytes 393248 | tf_op jit(solution)/shard_map/ppermute | solution.py:46
  40.9 0.0 collective-permute-done.5.refs_5_
  41.0 1.1 %shard_map.137 = (bf16[36,1024]{1,0:T(8,128)(2,1)S(1)}, bf16[36,1024]{1,0:T(8,128)(2,1)S(1)}, bf16[36,1024]{1,0:T(8,128)(2,1)S(1)}, bf16[36,1024]{1,0:T(8,128)(2...) custom-call(s32[1]{0:T(128)} %bitcast.6.refs_0_.wide_ref, ...), custom_call_target="tpu_custom_call" | custom-call | flops 226492416 | bytes 1966080 | tf_op jit(solution)/shard_map/pallas_call | solution.py:236
  42.0 0.1 collective-permute-start.6
  42.1 1.6 %collective-permute-start.7 = (bf16[36,1024]{1,0:T(8,128)(2,1)S(1)}, bf16[36,1024]{1,0:T(8,128)(2,1)S(1)}, u32[]{:S(2)}, u32[]{:S(2)}) collective-permute-start(bf16[36,1024]{1,0:T(8,128)(2,1)S(1)} %get-tuple-element.58), channel_id=1, source_target_pairs={{0,8},{4,12},{8,0},{12,4},{16,24},{20,28},{24,16},{28,20},{1,9},{5... | collective-permute-start | bytes 221192 | tf_op jit(solution)/shard_map/ppermute | solution.py:46
  43.7 0.2 collective-permute-start.8
  44.0 2.6 %collective-permute-start.9 = (bf16[36,1024]{1,0:T(8,128)(2,1)S(1)}, bf16[36,1024]{1,0:T(8,128)(2,1)S(1)}, u32[]{:S(2)}, u32[]{:S(2)}) collective-permute-start(bf16[36,1024]{1,0:T(8,128)(2,1)S(1)} %get-tuple-element.60), channel_id=1, source_target_pairs={{0,16},{4,20},{8,24},{12,28},{16,0},{20,4},{24,8},{28,12},{1,17},{... | collective-permute-start | bytes 221192 | tf_op jit(solution)/shard_map/ppermute | solution.py:46
  46.6 0.0 collective-permute-start.10
  46.6 0.0 collective-permute-done.6.refs_1_
  46.6 3.6 %collective-permute-start.11 = (bf16[36,1024]{1,0:T(8,128)(2,1)S(1)}, bf16[36,1024]{1,0:T(8,128)(2,1)S(1)}, u32[]{:S(2)}, u32[]{:S(2)}) collective-permute-start(bf16[36,1024]{1,0:T(8,128)(2,1)S(1)} %get-tuple-element.62), channel_id=1, source_target_pairs={{0,24},{4,28},{8,16},{12,20},{16,8},{20,12},{24,0},{28,4},{1,25},{... | collective-permute-start | bytes 221192 | tf_op jit(solution)/shard_map/ppermute | solution.py:46
  50.2 0.1 collective-permute-start.12
  50.3 1.2 %copy-done = bf16[128,4224]{1,0:T(8,128)(2,1)S(1)} copy-done((bf16[128,4224]{1,0:T(8,128)(2,1)S(1)}, bf16[128,4224]{1,0:T(8,128)(2,1)}, u32[]{:S(2)}) %copy-start) | copy-done | bytes 1081368
  51.5 6.1 %shard_map.132.refs_2_ = bf16[3072,128]{1,0:T(8,128)(2,1)S(1)} custom-call(bf16[128,4224]{1,0:T(8,128)(2,1)S(1)} %copy-done, bf16[3072,4096]{1,0:T(8,128)(2,1)} %refs_4_.3), custom_call_target="tpu_custom_call" | custom-call | flops 1610612736 | bytes 12582912 | tf_op jit(solution)/shard_map/pallas_call | solution.py:368
  57.6 0.9 shard_map.133
  58.5 0.5 collective-permute-done.10.refs_5_
  59.1 1.3 %shard_map.139.refs_1_.refs_12_ = bf16[288,1024]{1,0:T(8,128)(2,1)S(1)} custom-call(s32[1]{0:T(128)} %bitcast.6.refs_0_.wide_ref, bf16[36,1024]{1,0:T(8,128)(2,1)S(1)} %get-tuple-element.65.refs_0_, bf16[36,1024]{1,0:T(8,128)(2,1)S(1)} %collective-permute-done.6.refs_1_, bf16[36,1024]{1,0:T(8,128)(2,1)S(1)} %collective-permute-done.7.refs_2_, ...), custom_call_target="tpu_custom_call" | custom-call | flops 169869312 | bytes 1179648 | tf_op jit(solution)/shard_map/pallas_call | solution.py:267
  60.4 0.6 collective-permute-start.14
  61.0 1.5 %collective-permute-start.13 = (bf16[288,1024]{1,0:T(8,128)(2,1)S(1)}, bf16[288,1024]{1,0:T(8,128)(2,1)S(1)}, u32[]{:S(2)}, u32[]{:S(2)}) collective-permute-start(bf16[288,1024]{1,0:T(8,128)(2,1)S(1)} %shard_map.139.refs_1_.refs_12_), channel_id=1, source_target_pairs={{0,1},{1,0},{2,3},{3,2},{4,5},{5,4},{6,7},{7,6},{8,9},{9,8},{10,11... | collective-permute-start | bytes 1769480 | tf_op jit(solution)/shard_map/ppermute | solution.py:46
  62.5 0.1 pad_add_fusion.refs_0_
  62.6 0.1 pad_add_fusion.1.refs_0_
  62.6 6.0 %shard_map.138.refs_11_ = bf16[3072,128]{1,0:T(8,128)(2,1)S(1)} custom-call(bf16[128,4224]{1,0:T(8,128)(2,1)S(1)} %copy-done.1, bf16[3072,4096]{1,0:T(8,128)(2,1)} %refs_4_.3, bf16[3072,128]{1,0:T(8,128)(2,1)S(1)} %shard_map.132.refs_2_), custom_call_target="tpu_custom_call", output_to_operand_aliasing={{}: (2, {})} | custom-call | flops 1610612736 | bytes 12582912 | tf_op jit(solution)/shard_map/pallas_call | solution.py:368
  68.6 6.4 %shard_map.140 = (f32[288,3072]{1,0:T(8,128)S(1)}, f32[288,1]{1,0:T(8,128)S(1)}, f32[288,128]{1,0:T(8,128)S(1)}) custom-call(s32[1]{0:T(128)} %bitcast.refs_0_, bf16[288,1024]{1,0:T(8,128)(2,1)S(1)} %shard_map.139.refs_1_.refs_12_, bf16[3072,4096]{1,0:T(8,128)(2,1)} %refs_4_.3, bf16[3072,4096]{1,0:T(8,128)(2,1)} %refs_4_.3, bf16[128,4224]{1,0:T(8,128)(2,1)S(1)} %copy-done.1), custom_call_target="tpu_custom_call" | custom-call | flops 1811939328 | bytes 6291456 | tf_op jit(solution)/shard_map/pallas_call | solution.py:446
  75.0 1.7 %copy-done.4 = f32[288,3072]{1,0:T(8,128)} copy-done((f32[288,3072]{1,0:T(8,128)}, f32[288,3072]{1,0:T(8,128)S(1)}, u32[]{:S(2)}) %copy-start.4) | copy-done | bytes 3538968
  76.8 0.0 copy-start.7
  76.8 1.6 %collective-permute-start.15 = (bf16[144,1024]{1,0:T(8,128)(2,1)S(1)}, bf16[144,1024]{1,0:T(8,128)(2,1)S(1)}, u32[]{:S(2)}, u32[]{:S(2)}) collective-permute-start(bf16[144,1024]{1,0:T(8,128)(2,1)S(1)} %slice.6), channel_id=1, source_target_pairs={{0,2},{1,3},{2,0},{3,1},{4,6},{5,7},{6,4},{7,5},{8,10},{9,11},{10,... | collective-permute-start | bytes 884744 | tf_op jit(solution)/shard_map/ppermute | solution.py:46
  78.4 1.0 collective-permute-start.16
  79.4 10.2 %shard_map.141 = (f32[288,3072]{1,0:T(8,128)S(1)}, f32[288,1]{1,0:T(8,128)S(1)}, f32[288,128]{1,0:T(8,128)S(1)}) custom-call(s32[2]{0:T(128)S(1)} %pad_add_fusion.1.refs_0_, bf16[288,1024]{1,0:T(8,128)(2,1)S(1)} %collective-permute-done.13.refs_1_, bf16[288,1024]{1,0:T(8,128)(2,1)S(1)} %collective-permute-done.14.refs_2_, bf16[3072,4096]{1,0:T(8,128)(2,1)} %refs_4_.3, ...), custom_call_target="tpu_custom_call" | custom-call | flops 3623878656 | bytes 12582912 | tf_op jit(solution)/shard_map/pallas_call | solution.py:446
  89.6 8.4 %shard_map.142 = (bf16[288,3072]{1,0:T(8,128)(2,1)}, bf16[288,1024]{1,0:T(8,128)(2,1)}, bf16[288,1024]{1,0:T(8,128)(2,1)}) custom-call(s32[2]{0:T(128)S(1)} %pad_add_fusion.refs_0_, bf16[144,1024]{1,0:T(8,128)(2,1)S(1)} %collective-permute-done.15.refs_1_, bf16[144,1024]{1,0:T(8,128)(2,1)S(1)} %collective-permute-done.16.refs_2_, ...), custom_call_target="tpu_custom_call" | custom-call | flops 1811939328 | bytes 11599872 | tf_op jit(solution)/shard_map/pallas_call | solution.py:513
  (31 shorter events, 0.1 us)
Async XLA Ops:
  7.2 43.1 %all-gather.2.cloned.1.call-start = ((), (), s32[]{:S(2)}) async-start(), calls=%async_computation | async-start | bytes 1216512 | tf_op jit(solution)/shard_map/all_gather | solution.py:588
  8.6 9.6 %collective-permute-start.2 = (bf16[4,8704]{1,0:T(4,128)(2,1)}, bf16[4,8704]{1,0:T(4,128)(2,1)S(1)}, u32[]{:S(2)}, u32[]{:S(2)}) collective-permute-start(bf16[4,8704]{1,0:T(4,128)(2,1)} %shard_map.130.refs_1_), channel_id=1, source_target_pairs={{0,3},{1,2},{2,1},{3,0},{4,7},{5,6},{6,5},{7,4},{8,11},{9,10},{10,... | collective-permute-start | bytes 208904 | tf_op jit(solution)/shard_map/ppermute | solution.py:46
  12.5 5.7 %collective-permute-start.1 = (bf16[4,8704]{1,0:T(4,128)(2,1)}, bf16[4,8704]{1,0:T(4,128)(2,1)S(1)}, u32[]{:S(2)}, u32[]{:S(2)}) collective-permute-start(bf16[4,8704]{1,0:T(4,128)(2,1)} %shard_map.130.refs_1_), channel_id=1, source_target_pairs={{0,2},{1,3},{2,0},{3,1},{4,6},{5,7},{6,4},{7,5},{8,10},{9,11},{10,... | collective-permute-start | bytes 208904 | tf_op jit(solution)/shard_map/ppermute | solution.py:46
  13.0 5.2 %collective-permute-start = (bf16[4,8704]{1,0:T(4,128)(2,1)}, bf16[4,8704]{1,0:T(4,128)(2,1)S(1)}, u32[]{:S(2)}, u32[]{:S(2)}) collective-permute-start(bf16[4,8704]{1,0:T(4,128)(2,1)} %shard_map.130.refs_1_), channel_id=1, source_target_pairs={{0,1},{1,0},{2,3},{3,2},{4,5},{5,4},{6,7},{7,6},{8,9},{9,8},{10,11... | collective-permute-start | bytes 208904 | tf_op jit(solution)/shard_map/ppermute | solution.py:46
  13.1 1.3 %copy-start.2 = (bf16[192,3072]{1,0:T(8,128)(2,1)S(1)}, bf16[192,3072]{1,0:T(8,128)(2,1)}, u32[]{:S(2)}) copy-start(bf16[192,3072]{1,0:T(8,128)(2,1)} %refs_1_.7) | copy-start | bytes 3538948
  14.4 3.9 %copy-start.6 = (bf16[4,8704]{1,0:T(4,128)(2,1)S(1)}, bf16[4,8704]{1,0:T(4,128)(2,1)}, u32[]{:S(2)}) copy-start(bf16[4,8704]{1,0:T(4,128)(2,1)} %shard_map.130.refs_1_) | copy-start | bytes 208900
  14.4 3.9 %copy-start.8 = (s32[192,1]{0,1:T(1,128)S(1)}, s32[192,1]{0,1:T(1,128)}, u32[]{:S(2)}) copy-start(s32[192,1]{0,1:T(1,128)} %param.15) | copy-start | bytes 2308
  14.4 3.9 %copy-start.9 = (f32[16]{0:T(128)S(1)}, f32[16]{0:T(128)}, u32[]{:S(2)}) copy-start(f32[16]{0:T(128)} %param.12) | copy-start | bytes 196
  14.4 3.9 %copy-start.10 = (s32[16]{0:T(128)S(1)}, s32[16]{0:T(128)}, u32[]{:S(2)}) copy-start(s32[16]{0:T(128)} %param.13) | copy-start | bytes 196
  14.4 3.9 %copy-start.11 = (s32[1,16]{1,0:T(1,128)S(1)}, s32[1,16]{1,0:T(1,128)}, u32[]{:S(2)}) copy-start(s32[1,16]{1,0:T(1,128)} %refs_8_.1) | copy-start | bytes 196
  14.4 8.4 %copy-start.3 = (bf16[192,3072]{1,0:T(8,128)(2,1)S(1)}, bf16[192,3072]{1,0:T(8,128)(2,1)}, u32[]{:S(2)}) copy-start(bf16[192,3072]{1,0:T(8,128)(2,1)} %refs_1_.7) | copy-start | bytes 3538948
  19.9 15.4 %collective-permute-start.3 = (bf16[192,1024]{1,0:T(8,128)(2,1)S(1)}, bf16[192,1024]{1,0:T(8,128)(2,1)S(1)}, u32[]{:S(2)}, u32[]{:S(2)}) collective-permute-start(bf16[192,1024]{1,0:T(8,128)(2,1)S(1)} %shard_map.129), channel_id=1, source_target_pairs={{0,3},{1,2},{2,1},{3,0},{4,7},{5,6},{6,5},{7,4},{8,11},{9,10},{10,... | collective-permute-start | bytes 1179656 | tf_op jit(solution)/shard_map/ppermute | solution.py:46
  26.5 5.1 %copy-start.5 = (bf16[192,1024]{1,0:T(8,128)(2,1)S(1)}, bf16[192,1024]{1,0:T(8,128)(2,1)}, u32[]{:S(2)}) copy-start(bf16[192,1024]{1,0:T(8,128)(2,1)} %refs_3_.4) | copy-start | bytes 1179652
  31.0 9.9 %collective-permute-start.4 = (bf16[192,1024]{1,0:T(8,128)(2,1)}, bf16[192,1024]{1,0:T(8,128)(2,1)S(1)}, u32[]{:S(2)}, u32[]{:S(2)}) collective-permute-start(bf16[192,1024]{1,0:T(8,128)(2,1)} %shard_map.135), channel_id=1, source_target_pairs={{0,1},{1,0},{2,3},{3,2},{4,5},{5,4},{6,7},{7,6},{8,9},{9,8},{10,11... | collective-permute-start | bytes 1179656 | tf_op jit(solution)/shard_map/ppermute | solution.py:46
  31.5 9.4 %collective-permute-start.5 = (bf16[192,1024]{1,0:T(8,128)(2,1)S(1)}, bf16[192,1024]{1,0:T(8,128)(2,1)S(1)}, u32[]{:S(2)}, u32[]{:S(2)}) collective-permute-start(bf16[192,1024]{1,0:T(8,128)(2,1)S(1)} %shard_map.136), channel_id=1, source_target_pairs={{0,2},{1,3},{2,0},{3,1},{4,6},{5,7},{6,4},{7,5},{8,10},{9,11},{10,... | collective-permute-start | bytes 1179656 | tf_op jit(solution)/shard_map/ppermute | solution.py:46
  42.0 4.6 %collective-permute-start.6 = (bf16[36,1024]{1,0:T(8,128)(2,1)S(1)}, bf16[36,1024]{1,0:T(8,128)(2,1)S(1)}, u32[]{:S(2)}, u32[]{:S(2)}) collective-permute-start(bf16[36,1024]{1,0:T(8,128)(2,1)S(1)} %get-tuple-element.57), channel_id=1, source_target_pairs={{0,4},{4,0},{8,12},{12,8},{16,20},{20,16},{24,28},{28,24},{1,5},{5... | collective-permute-start | bytes 221192 | tf_op jit(solution)/shard_map/ppermute | solution.py:46
  42.1 8.1 %collective-permute-start.7 = (bf16[36,1024]{1,0:T(8,128)(2,1)S(1)}, bf16[36,1024]{1,0:T(8,128)(2,1)S(1)}, u32[]{:S(2)}, u32[]{:S(2)}) collective-permute-start(bf16[36,1024]{1,0:T(8,128)(2,1)S(1)} %get-tuple-element.58), channel_id=1, source_target_pairs={{0,8},{4,12},{8,0},{12,4},{16,24},{20,28},{24,16},{28,20},{1,9},{5... | collective-permute-start | bytes 221192 | tf_op jit(solution)/shard_map/ppermute | solution.py:46
  43.7 14.8 %collective-permute-start.8 = (bf16[36,1024]{1,0:T(8,128)(2,1)S(1)}, bf16[36,1024]{1,0:T(8,128)(2,1)S(1)}, u32[]{:S(2)}, u32[]{:S(2)}) collective-permute-start(bf16[36,1024]{1,0:T(8,128)(2,1)S(1)} %get-tuple-element.59), channel_id=1, source_target_pairs={{0,12},{4,8},{8,4},{12,0},{16,28},{20,24},{24,20},{28,16},{1,13},{... | collective-permute-start | bytes 221192 | tf_op jit(solution)/shard_map/ppermute | solution.py:46
  44.0 14.6 %collective-permute-start.9 = (bf16[36,1024]{1,0:T(8,128)(2,1)S(1)}, bf16[36,1024]{1,0:T(8,128)(2,1)S(1)}, u32[]{:S(2)}, u32[]{:S(2)}) collective-permute-start(bf16[36,1024]{1,0:T(8,128)(2,1)S(1)} %get-tuple-element.60), channel_id=1, source_target_pairs={{0,16},{4,20},{8,24},{12,28},{16,0},{20,4},{24,8},{28,12},{1,17},{... | collective-permute-start | bytes 221192 | tf_op jit(solution)/shard_map/ppermute | solution.py:46
  46.6 12.5 %collective-permute-start.10 = (bf16[36,1024]{1,0:T(8,128)(2,1)S(1)}, bf16[36,1024]{1,0:T(8,128)(2,1)S(1)}, u32[]{:S(2)}, u32[]{:S(2)}) collective-permute-start(bf16[36,1024]{1,0:T(8,128)(2,1)S(1)} %get-tuple-element.61), channel_id=1, source_target_pairs={{0,20},{4,16},{8,28},{12,24},{16,4},{20,0},{24,12},{28,8},{1,21},{... | collective-permute-start | bytes 221192 | tf_op jit(solution)/shard_map/ppermute | solution.py:46
  46.6 12.5 %collective-permute-start.11 = (bf16[36,1024]{1,0:T(8,128)(2,1)S(1)}, bf16[36,1024]{1,0:T(8,128)(2,1)S(1)}, u32[]{:S(2)}, u32[]{:S(2)}) collective-permute-start(bf16[36,1024]{1,0:T(8,128)(2,1)S(1)} %get-tuple-element.62), channel_id=1, source_target_pairs={{0,24},{4,28},{8,16},{12,20},{16,8},{20,12},{24,0},{28,4},{1,25},{... | collective-permute-start | bytes 221192 | tf_op jit(solution)/shard_map/ppermute | solution.py:46
  50.2 8.9 %collective-permute-start.12 = (bf16[36,1024]{1,0:T(8,128)(2,1)S(1)}, bf16[36,1024]{1,0:T(8,128)(2,1)S(1)}, u32[]{:S(2)}, u32[]{:S(2)}) collective-permute-start(bf16[36,1024]{1,0:T(8,128)(2,1)S(1)} %get-tuple-element.63), channel_id=1, source_target_pairs={{0,28},{4,24},{8,20},{12,16},{16,12},{20,8},{24,4},{28,0},{1,29},{... | collective-permute-start | bytes 221192 | tf_op jit(solution)/shard_map/ppermute | solution.py:46
  50.3 1.2 %copy-start = (bf16[128,4224]{1,0:T(8,128)(2,1)S(1)}, bf16[128,4224]{1,0:T(8,128)(2,1)}, u32[]{:S(2)}) copy-start(bf16[128,4224]{1,0:T(8,128)(2,1)} %all-gather.2.cloned.1.call-done.refs_0_.refs_1_.refs_4_.refs_7_.refs_8_.refs_5_.refs_13_) | copy-start | bytes 3244036
  51.5 6.1 %copy-start.1 = (bf16[128,4224]{1,0:T(8,128)(2,1)S(1)}, bf16[128,4224]{1,0:T(8,128)(2,1)}, u32[]{:S(2)}) copy-start(bf16[128,4224]{1,0:T(8,128)(2,1)} %all-gather.2.cloned.1.call-done.refs_0_.refs_1_.refs_4_.refs_7_.refs_8_.refs_5_.refs_13_) | copy-start | bytes 3244036
  60.4 16.4 %collective-permute-start.14 = (bf16[288,1024]{1,0:T(8,128)(2,1)S(1)}, bf16[288,1024]{1,0:T(8,128)(2,1)S(1)}, u32[]{:S(2)}, u32[]{:S(2)}) collective-permute-start(bf16[288,1024]{1,0:T(8,128)(2,1)S(1)} %shard_map.139.refs_1_.refs_12_), channel_id=1, source_target_pairs={{0,2},{1,3},{2,0},{3,1},{4,6},{5,7},{6,4},{7,5},{8,10},{9,11},{10,... | collective-permute-start | bytes 1769480 | tf_op jit(solution)/shard_map/ppermute | solution.py:46
  61.0 15.8 %collective-permute-start.13 = (bf16[288,1024]{1,0:T(8,128)(2,1)S(1)}, bf16[288,1024]{1,0:T(8,128)(2,1)S(1)}, u32[]{:S(2)}, u32[]{:S(2)}) collective-permute-start(bf16[288,1024]{1,0:T(8,128)(2,1)S(1)} %shard_map.139.refs_1_.refs_12_), channel_id=1, source_target_pairs={{0,1},{1,0},{2,3},{3,2},{4,5},{5,4},{6,7},{7,6},{8,9},{9,8},{10,11... | collective-permute-start | bytes 1769480 | tf_op jit(solution)/shard_map/ppermute | solution.py:46
  75.0 1.7 %copy-start.4 = (f32[288,3072]{1,0:T(8,128)}, f32[288,3072]{1,0:T(8,128)S(1)}, u32[]{:S(2)}) copy-start(f32[288,3072]{1,0:T(8,128)S(1)} %get-tuple-element.78.refs_9_) | copy-start | bytes 10616836
  76.8 12.8 %copy-start.7 = (f32[1024]{0:T(1024)S(1)}, f32[1024]{0:T(1024)}, u32[]{:S(2)}) copy-start(f32[1024]{0:T(1024)} %param.19) | copy-start | bytes 12292
  76.8 12.8 %collective-permute-start.15 = (bf16[144,1024]{1,0:T(8,128)(2,1)S(1)}, bf16[144,1024]{1,0:T(8,128)(2,1)S(1)}, u32[]{:S(2)}, u32[]{:S(2)}) collective-permute-start(bf16[144,1024]{1,0:T(8,128)(2,1)S(1)} %slice.6), channel_id=1, source_target_pairs={{0,2},{1,3},{2,0},{3,1},{4,6},{5,7},{6,4},{7,5},{8,10},{9,11},{10,... | collective-permute-start | bytes 884744 | tf_op jit(solution)/shard_map/ppermute | solution.py:46
  78.4 11.2 %collective-permute-start.16 = (bf16[144,1024]{1,0:T(8,128)(2,1)S(1)}, bf16[144,1024]{1,0:T(8,128)(2,1)S(1)}, u32[]{:S(2)}, u32[]{:S(2)}) collective-permute-start(bf16[144,1024]{1,0:T(8,128)(2,1)S(1)} %slice.7), channel_id=1, source_target_pairs={{0,1},{1,0},{2,3},{3,2},{4,5},{5,4},{6,7},{7,6},{8,9},{9,8},{10,11... | collective-permute-start | bytes 884744 | tf_op jit(solution)/shard_map/ppermute | solution.py:46
Sparse Core Ops, SparseCore 0:
  20.0 23.9 all-gather.1

commit v9 on v8

--- a/solution.py
+++ b/solution.py
@@ -50,14 +50,12 @@
     return lax.optimization_barrier((first, *later))
 
 
-def project_body(has_resid, group_ref, act_hbm, w_hbm, *refs):
-    out_ref, act, weights, act_sem, sems = refs[has_resid:]
-    width = out_ref.shape[1]
+def project_body(tiles_each, has_resid, starts_ref, act_hbm, w_hbm, *refs):
+    outs, (act, weights, act_sem, sems) = refs[has_resid:-4], refs[-4:]
     count, _, tile = weights.shape
-    first = group_ref[0] * width
 
     def weight_copy(i):
-        columns = pl.ds(pl.multiple_of(first + i * tile, lane), tile)
+        columns = pl.ds(pl.multiple_of(starts_ref[i] * tile, lane), tile)
         return pltpu.make_async_copy(w_hbm.at[:, columns], weights.at[i], sems.at[i])
 
     act_copy = pltpu.make_async_copy(act_hbm, act, act_sem)
@@ -65,29 +63,32 @@
     for i in range(count):
         weight_copy(i).start()
     act_copy.wait()
-
-    @pl.loop(0, count)
-    def _(i):
-        weight_copy(i).wait()
-        columns = pl.ds(pl.multiple_of(i * tile, lane), tile)
-        term = dot(act[...], weights[i])
-        if has_resid:
-            term = term + refs[0][:, columns].astype(f32)
-        out_ref[:, columns] = term.astype(out_ref.dtype)
-
-
-def project(group, act, w_down, width, resid=None):
+    for n, out_ref in enumerate(outs):
+
+        @pl.loop(0, tiles_each)
+        def _(i):
+            weight_copy(n * tiles_each + i).wait()
+            columns = pl.ds(pl.multiple_of(i * tile, lane), tile)
+            term = dot(act[...], weights[n * tiles_each + i])
+            if has_resid:
+                term = term + refs[0][:, columns].astype(f32)
+            out_ref[:, columns] = term.astype(out_ref.dtype)
+
+
+def project(pieces, act, w_down, width, resid=None):
     rows, depth = act.shape
     tile = tile_of(width, 256)
-    count = width // tile
+    each = width // tile
+    count = each * len(pieces)
+    starts = jnp.stack([piece * each + i for piece in pieces for i in range(each)])
     own = [] if resid is None else [resid]
     return pl.pallas_call(
-        lambda *refs: project_body(len(own), *refs),
+        lambda *refs: project_body(each, len(own), *refs),
         in_specs=[pl.BlockSpec(memory_space=pltpu.SMEM)]
         + [pl.BlockSpec(memory_space=pl.ANY)] * 2
         + [pl.BlockSpec(memory_space=pltpu.VMEM)] * len(own),
-        out_specs=pl.BlockSpec(memory_space=pltpu.VMEM),
-        out_shape=jax.ShapeDtypeStruct((rows, width), f32 if own else bf16),
+        out_specs=[pl.BlockSpec(memory_space=pltpu.VMEM)] * len(pieces),
+        out_shape=[jax.ShapeDtypeStruct((rows, width), f32 if own else bf16)] * len(pieces),
         scratch_shapes=[
             pltpu.VMEM((rows, depth), bf16),
             pltpu.VMEM((count, depth, tile), bf16),
@@ -95,8 +96,8 @@
             pltpu.SemaphoreType.DMA((count,)),
         ],
         compiler_params=params(),
-        cost_estimate=cost(2 * rows * depth * width, 2 * depth * width + 2 * rows * depth),
-    )(group, act, w_down, *own)
+        cost_estimate=cost(2 * rows * depth * tile * count, 2 * depth * (tile * count + rows)),
+    )(starts, act, w_down, *own)
 
 
 def payload_body(query_ref, passage_ref, gain_ref, out_ref, gains):
@@ -211,14 +212,16 @@
     return (iota((tokens, tokens), 0) < iota((tokens, tokens), 1)).astype(bf16)
 
 
-def pack_body(terms, wide_ref, dest_ref, own_ref, *rest):
-    outs = rest[terms:]
+def pack_body(wide_ref, dest_ref, own_ref, far_ref, *rest):
+    halves, outs = rest[:4], rest[4:]
     groups, slots = len(outs), outs[0].shape[0]
     tokens = dest_ref.shape[1]
     stride = -(-slots // 16) * 16
-    hidden = own_ref[...]
-    for term in rest[:terms]:
-        hidden = hidden + term[...].astype(f32)
+    hidden = own_ref[...] + far_ref[...].astype(f32)
+    for left, right in (halves[:2], halves[2:]):
+        hidden = hidden + jnp.where(
+            pl.program_id(0) == 0, left[...].astype(f32), right[...].astype(f32)
+        )
     partner = dest_ref[...] ^ wide_ref[0]
     hit = (partner == iota((groups, tokens), 0)).astype(f32)
     rank = dot(hit.astype(bf16), earlier_of(tokens))
@@ -229,23 +232,24 @@
         outs[k][...] = packed[k * stride : k * stride + slots]
 
 
-def pack(wide, destination, own, terms, groups, slots):
+def pack(wide, destination, own, far, halves, groups, slots):
     tokens, width = own.shape
-    tile = tile_of(width, 512)
+    tile = width // 2
     column_spec = pl.BlockSpec((tokens, tile), lambda j, g: (0, j))
     return pl.pallas_call(
-        lambda *refs: pack_body(len(terms), *refs),
+        pack_body,
         grid_spec=pltpu.PrefetchScalarGridSpec(
             num_scalar_prefetch=1,
             grid=(width // tile,),
             in_specs=[pl.BlockSpec((1, tokens), lambda j, g: (0, 0))]
-            + [column_spec] * (1 + len(terms)),
+            + [column_spec] * 2
+            + [pl.BlockSpec((tokens, tile), lambda j, g: (0, 0))] * len(halves),
             out_specs=[pl.BlockSpec((slots, tile), lambda j, g: (0, j))] * groups,
         ),
         out_shape=[jax.ShapeDtypeStruct((slots, width), bf16)] * groups,
         compiler_params=params(),
         cost_estimate=cost(4 * groups * slots * tokens * width, 10 * tokens * width),
-    )(wide[None], destination.reshape(1, tokens), own, *terms)
+    )(wide[None], destination.reshape(1, tokens), own, far, *halves)
 
 
 def assemble_body(wide_ref, *refs):
@@ -254,8 +258,8 @@
     rows = out_ref.shape[0]
     row, column = iota((rows, slots), 0), iota((rows, slots), 1)
     total = 0.0
-    for k, part in enumerate(parts):
-        group = wide_ref[0] ^ k
+    for n, part in enumerate(parts):
+        group = wide_ref[0] ^ (len(parts) - 1 - n)
         place = (row == group * slots + column).astype(f32).astype(bf16)
         total = total + dot(place, part[...])
     out_ref[...] = total.astype(bf16)
@@ -340,48 +344,6 @@
     )(wide[None], low)
 
 
-def low_act_body(part, low_ref, w_hbm, *refs):
-    out_ref, weights, sems = refs[-3:]
-    count, tile, _ = weights.shape
-
-    def weight_copy(t):
-        rows = pl.ds(pl.multiple_of((part * count + t) * tile, tile), tile)
-        return pltpu.make_async_copy(w_hbm.at[rows], weights.at[t], sems.at[t])
-
-    for t in range(count):
-        weight_copy(t).start()
-
-    @pl.loop(0, count)
-    def _(t):
-        weight_copy(t).wait()
-        rows = pl.ds(pl.multiple_of(t * tile, tile), tile)
-        out_ref[rows] = dot_t(weights[t], low_ref[...]).astype(bf16)
-
-
-def low_activations(low, features, w_down, part, parts, filled=()):
-    pairs = low.shape[0]
-    depth = w_down.shape[0]
-    some = depth // parts
-    tile = tile_of(some, 512)
-    count = some // tile
-    anywhere = pl.BlockSpec(memory_space=pl.ANY)
-    return pl.pallas_call(
-        lambda *refs: low_act_body(part, *refs),
-        grid=(1,),
-        in_specs=[pl.BlockSpec((pairs, features), lambda j: (0, 0)), anywhere]
-        + [anywhere] * len(filled),
-        out_specs=pl.BlockSpec((some, pairs), lambda j: (part, 0)),
-        out_shape=jax.ShapeDtypeStruct((depth, pairs), bf16),
-        scratch_shapes=[
-            pltpu.VMEM((count, tile, features), bf16),
-            pltpu.SemaphoreType.DMA((count,)),
-        ],
-        input_output_aliases={2: 0} if filled else {},
-        compiler_params=params(),
-        cost_estimate=cost(2 * pairs * some * features, 2 * some * features),
-    )(low, w_down, *filled)
-
-
 def statistics(hids, lows):
     squares, cross = 0.0, 0.0
     for hid_ref, low_ref in zip(hids, lows):
@@ -391,13 +353,6 @@
     return squares, cross
 
 
-def product(hids, weights):
-    total = 0.0
-    for hid_ref, w_ref in zip(hids, weights):
-        total = total + dot_t(hid_ref[...], w_ref[...])
-    return total
-
-
 def weight_specs(count, tile, width):
     return [
         pl.BlockSpec((tile // 2, width), lambda j, g, n=n, side=side: (2 * j + side, g[n]))
@@ -412,10 +367,15 @@
 
 def back_body(count, carried, places_ref, *refs):
     hids, weights, refs = refs[:count], refs[count : 3 * count], refs[3 * count :]
-    lows, before, (acc_ref, squares_ref, cross_ref) = refs[:count], refs[count:-3], refs[-3:]
+    lows, before = refs[:count], refs[count:-4]
+    acc_ref, squares_ref, cross_ref, stack = refs[-4:]
+    rows = hids[0].shape[0]
 
     @pl.when(pl.program_id(0) == 0)
     def _():
+        for n in range(count):
+            stack[n, :rows] = hids[n][...]
+            stack[n, rows:] = lows[n][...]
         squares, cross = statistics(hids, lows)
         if carried:
             squares, cross = before[1][...] + squares, before[2][...] + cross
@@ -424,13 +384,15 @@
     half = acc_ref.shape[1] // 2
     for side in range(2):
         at = slice(side * half, (side + 1) * half)
-        total = product(hids, weights[side::2])
+        total = dot_t(stack[0], weights[side][...])
+        for n in range(1, count):
+            total = total + dot_t(stack[n], weights[2 * n + side][...])
         acc_ref[:, at] = before[0][:, at] + total if carried else total
 
 
 def carried_specs(rows, pairs, tile):
     return [
-        pl.BlockSpec((rows, tile), lambda j, g: (0, j)),
+        pl.BlockSpec((rows + pairs, tile), lambda j, g: (0, j)),
         pl.BlockSpec((rows, 1), lambda j, g: (0, 0)),
         pl.BlockSpec((rows, pairs), lambda j, g: (0, 0)),
     ]
@@ -453,9 +415,10 @@
             + low_specs(count, pairs, width)
             + totals[: len(before)],
             out_specs=totals,
+            scratch_shapes=[pltpu.VMEM((count, rows + pairs, width), bf16)],
         ),
         out_shape=[
-            jax.ShapeDtypeStruct((rows, depth), f32),
+            jax.ShapeDtypeStruct((rows + pairs, depth), f32),
             jax.ShapeDtypeStruct((rows, 1), f32),
             jax.ShapeDtypeStruct((rows, pairs), f32),
         ],
@@ -466,17 +429,19 @@
 
 def finish_body(features, count, places_ref, *refs):
     hids, weights, refs = refs[:count], refs[count : count + 2], refs[count + 2 :]
-    low_ref, acc_ref, squares_ref, cross_ref, hot_ref, share_ref, low_act_ref = refs[:7]
-    own_ref, own_low_ref, gain_ref, act_out, resid_out, normed_out = refs[7:13]
-    hid, lead, pull, scale = refs[13:]
+    low_ref, acc_ref, squares_ref, cross_ref, hot_ref, share_ref = refs[:6]
+    own_ref, own_low_ref, gain_ref, act_out, resid_out, normed_out = refs[6:12]
+    stack, lead, pull, scale = refs[12:]
+    count_rows = hot_ref.shape[0]
     part = hids[0].shape[0]
     step = own_ref.shape[0]
 
     @pl.when(pl.program_id(0) == 0)
     def _():
         for n in range(count):
-            hid[n * part : (n + 1) * part] = hids[n][...]
-        squares, cross = statistics([hid], [low_ref])
+            stack[n * part : (n + 1) * part] = hids[n][...]
+        stack[count_rows:] = low_ref[...]
+        squares, cross = statistics([stack.at[:count_rows]], [low_ref])
         hot = hot_ref[...].astype(f32)
         inner = jnp.sum((cross_ref[...] + cross) * hot, axis=1, keepdims=True) * share_ref[...]
         inv_rms = lax.rsqrt((squares_ref[...] + squares) / features + norm_eps)
@@ -487,9 +452,9 @@
     half = act_out.shape[1] // 2
     for side in range(2):
         at = slice(side * half, (side + 1) * half)
-        low_act = dot_t(hot_ref[...], low_act_ref[at])
-        hid_act = acc_ref[:, at] + product([hid], weights[side : side + 1])
-        act_out[:, at] = (lead[...] * low_act - pull[...] * hid_act).astype(bf16)
+        total = acc_ref[:, at] + dot_t(stack[...], weights[side][...])
+        low_act = dot(hot_ref[...], total[count_rows:].astype(bf16))
+        act_out[:, at] = (lead[...] * low_act - pull[...] * total[:count_rows]).astype(bf16)
     rows = pl.ds(pl.multiple_of(pl.program_id(0) * step, step), step)
     own = own_ref[...].astype(f32)
     own_low = dot(hot_ref[rows], own_low_ref[...])
@@ -497,7 +462,7 @@
     normed_out[...] = (gain_ref[...] * own * scale[rows]).astype(bf16)
 
 
-def finish(places, pieces, w_down, low, before, hot, share, low_act, own, gain):
+def finish(places, pieces, w_down, low, before, hot, share, own, gain):
     count = len(pieces)
     rows, width = own.shape
     depth, features = w_down.shape
@@ -522,13 +487,13 @@
             + [
                 whole((rows, pairs)),
                 whole((rows, 1)),
-                pl.BlockSpec((tile, pairs), lambda j, g: (j, 0)),
                 row_spec,
                 pl.BlockSpec((pairs, width), lambda j, g: (0, g[1])),
                 whole((1, width)),
             ],
             out_specs=[pl.BlockSpec((rows, tile), lambda j, g: (0, j)), row_spec, row_spec],
-            scratch_shapes=[pltpu.VMEM((rows, width), bf16)] + [pltpu.VMEM((rows, 1), f32)] * 3,
+            scratch_shapes=[pltpu.VMEM((rows + pairs, width), bf16)]
+            + [pltpu.VMEM((rows, 1), f32)] * 3,
         ),
         out_shape=[
             jax.ShapeDtypeStruct((rows, depth), bf16),
@@ -545,7 +510,6 @@
         *before,
         hot,
         share,
-        low_act,
         own,
         low,
         gain,
@@ -574,29 +538,31 @@
 
     both = payload(query_emb, passage_emb, gain)
     parts = [both] + [swap(both, k) for k in (1, 2, 3)]
-    first_term = project((blk ^ 3)[None], mlp_act, w_down, width)
-    arrived = [swap(first_term, 3)]
-    parts = after(first_term, *parts)[1:]
+    (first_term,) = project([blk ^ 3], mlp_act, w_down, width)
+    far = swap(first_term, 3)
+    _, *parts = lax.optimization_barrier((first_term, *parts))
     query_grad, low_own = group_part(
         parts, row_lse, positive, token_lengths, destination, features, blk
     )
-    mlp_act = after(low_own, mlp_act)[1]
-    for k in (1, 2):
-        arrived.append(swap(project((blk ^ k)[None], mlp_act, w_down, width), k))
-    own_term = project(blk[None], mlp_act, w_down, width, resid)
+    _, mlp_act = lax.optimization_barrier((low_own, mlp_act))
+    halves = []
+    for side in range(2):
+        places = [(blk ^ k) * 2 + side for k in (1, 2)]
+        terms = project(places, mlp_act, w_down, width // 2)
+        halves += [swap(terms[0], 1), swap(terms[1], 2)]
+    (own_term,) = project([blk], mlp_act, w_down, width, resid)
 
     low = lax.all_gather(low_own, "wide", axis=0, tiled=True)
-    packed = pack(wide, destination, own_term, arrived, wide_count, slot_count)
-    routed = [packed[k] if k == 0 else swap(packed[k], k, "wide") for k in range(wide_count)]
-    low_act = low_activations(low, features, w_down, 0, 2)
+    packed = pack(wide, destination, own_term, far, halves[::2] + halves[1::2], wide_count, slot_count)
+    routed = [swap(packed[k], k, "wide") for k in range(wide_count - 1, 0, -1)] + [packed[0]]
+
     hot, share = slot_passages(wide, low, features, wide_count, slot_count, rows)
-    low_act, hot, share, *routed = lax.optimization_barrier((low_act, hot, share, *routed))
+    hot, share, *routed = lax.optimization_barrier((hot, share, *routed))
     own = assemble(wide, routed)
 
     beside, above = swap(own, 1), swap(own, 2)
     totals = back(blk[None], [own], w_down, low)
-    low_act = low_activations(low, features, w_down, 1, 2, [low_act])
-    low_act, *totals, beside, above = lax.optimization_barrier((low_act, *totals, beside, above))
+    *totals, beside, above = lax.optimization_barrier((*totals, beside, above))
     top = swap(beside[: rows // 2], 2)
     bottom = swap(above[rows // 2 :], 1)
     totals = back(jnp.stack([blk ^ 1, blk ^ 2]), [beside, above], w_down, low, totals)
@@ -608,7 +574,6 @@
         totals,
         hot,
         share,
-        low_act,
         own,
         gain[None],
     )

time: 106 us -> 111 us (1.047)
  starting transfers between devices: 20.9 us -> 27.7 us
  Pallas kernels: 58.9 us -> 54.1 us
  local copies, waits for them, and re-layouts: 4.32 us -> 6.12 us
  waiting for transfers between devices: 6.3 us -> 8.05 us
    pallas_call x7 -> x5, Pallas kernels: 28.7 us -> 17.9 us  [the longest x4 16.9 us: project(): pl.pallas_call(lambda *refs: project_body(each, len(own), *refs), in_spec...]
    ppermute x17 -> x19, starting transfers between devices: 20.9 us -> 27.7 us  [swap(): lax.ppermute(rows, axis, [(i, i ^ k) for i in range(lax.axis_size(axis))])]
    pallas_call x1, Pallas kernels: 8.43 us -> 12.3 us  [finish(): pl.pallas_call(lambda *refs: finish_body(features, count, *refs), grid_sp...]
    pallas_call x2, Pallas kernels: 16.6 us -> 18.7 us  [back(): pl.pallas_call(lambda *refs: back_body(count, len(before), *refs), grid_s...]
    unnamed x24 -> x26, local copies, waits for them, and re-layouts: 4.28 us -> 6.08 us
    ppermute x17 -> x19, waiting for transfers between devices: 6.29 us -> 8.04 us  [swap(): lax.ppermute(rows, axis, [(i, i ^ k) for i in range(lax.axis_size(axis))])]
  transfers between devices with their start and end apart: 18 -> 20, of which waited for: 2 -> 5; matrix products, arithmetic and copies ran while one was open for 0% -> 0% of each run, Pallas kernels for 44% -> 34%
where the time goes in v9:
time: 111 us
  Pallas kernels  54.1 us (49%)
  starting transfers between devices  27.7 us (25%)
  between operations  14.3 us (13%)
  waiting for transfers between devices  8.05 us (7%)
  local copies, waits for them, and re-layouts  6.12 us (6%)
    ppermute x19, starting transfers between devices, swap(): lax.ppermute(rows, axis, [(i, i ^ k) for i in range(lax.axis_size(axis))])  27.7 us
    pallas_call x2, Pallas kernels, back(): pl.pallas_call(lambda *refs: back_body(count, len(before), *refs), grid_s...  18.7 us
    pallas_call x4, Pallas kernels, project(): pl.pallas_call(lambda *refs: project_body(each, len(own), *refs), in_spec...  16.9 us
    pallas_call x1, Pallas kernels, finish(): pl.pallas_call(lambda *refs: finish_body(features, count, *refs), grid_sp...  12.3 us
    ppermute x19, waiting for transfers between devices, swap(): lax.ppermute(rows, axis, [(i, i ^ k) for i in range(lax.axis_size(axis))])  8.04 us
    unnamed x26, local copies, waits for them, and re-layouts  6.08 us
  transfers between devices with their start and end apart: 20, of which 5 were waited for; matrix products, arithmetic and copies ran while one was open for 0% of the time, Pallas kernels for 34%

profile of v9, /device:TPU:0, one launch (start us, length us, event | category | flops | bytes accessed | tf_op | source)
XLA Modules:
  0.0 110.7 jit_solution(8897178323286327522)
XLA Ops:
  7.2 0.0 all-gather.2.cloned.1.call-start
  7.2 1.4 %shard_map.130.refs_1_ = bf16[4,8704]{1,0:T(4,128)(2,1)} custom-call(bf16[4,4096]{1,0:T(4,128)(2,1)} %query_ref.1, bf16[4,4096]{1,0:T(4,128)(2,1)} %passage_ref.1, f32[1,1024]{1,0:T(1,128)} %bitcast.25), custom_call_target="tpu_custom_call" | custom-call | flops 16384 | bytes 131072 | tf_op jit(solution)/shard_map/pallas_call | solution.py:119
  8.6 3.9 %collective-permute-start.2 = (bf16[4,8704]{1,0:T(4,128)(2,1)}, bf16[4,8704]{1,0:T(4,128)(2,1)S(1)}, u32[]{:S(2)}, u32[]{:S(2)}) collective-permute-start(bf16[4,8704]{1,0:T(4,128)(2,1)} %shard_map.130.refs_1_), channel_id=1, source_target_pairs={{0,3},{1,2},{2,1},{3,0},{4,7},{5,6},{6,5},{7,4},{8,11},{9,10},{10,... | collective-permute-start | bytes 208904 | tf_op jit(solution)/shard_map/ppermute | solution.py:46
  12.5 0.5 collective-permute-start.1
  13.0 0.1 collective-permute-start
  13.1 0.1 pad_add_fusion.refs_0_
  13.2 1.3 %copy-done.3 = bf16[192,3072]{1,0:T(8,128)(2,1)S(1)} copy-done((bf16[192,3072]{1,0:T(8,128)(2,1)S(1)}, bf16[192,3072]{1,0:T(8,128)(2,1)}, u32[]{:S(2)}) %copy-start.3) | copy-done | bytes 1179672
  14.5 4.2 %shard_map.129 = bf16[192,1024]{1,0:T(8,128)(2,1)S(1)} custom-call(s32[4]{0:T(128)S(1)} %pad_add_fusion.refs_0_, bf16[192,3072]{1,0:T(8,128)(2,1)S(1)} %copy-done.3, bf16[3072,4096]{1,0:T(8,128)(2,1)} %refs_4_.3), custom_call_target="tpu_custom_call" | custom-call | flops 1207959552 | bytes 7471104 | tf_op jit(solution)/shard_map/pallas_call | solution.py:85
  18.8 1.5 %shard_map.131 = (bf16[4,4096]{1,0:T(4,128)(2,1)}, bf16[16,4224]{1,0:T(8,128)(2,1)}) custom-call(s32[1]{0:T(128)} %bitcast.refs_0_, bf16[4,8704]{1,0:T(4,128)(2,1)S(1)} %copy-done.7, bf16[4,8704]{1,0:T(4,128)(2,1)S(1)} %collective-permute-done.refs_2_, bf16[4,8704]{1,0:T(4,128)(2,1)S(1)} %collective-permute-done.1.refs_3_, ...), custom_call_target="tpu_custom_call" | custom-call | flops 8388608 | bytes 524288 | tf_op jit(solution)/shard_map/pallas_call | solution.py:185
  20.3 0.0 all-gather.2.cloned.1.call-update
  20.3 3.0 %collective-permute-start.3 = (bf16[192,1024]{1,0:T(8,128)(2,1)S(1)}, bf16[192,1024]{1,0:T(8,128)(2,1)S(1)}, u32[]{:S(2)}, u32[]{:S(2)}) collective-permute-start(bf16[192,1024]{1,0:T(8,128)(2,1)S(1)} %shard_map.129), channel_id=1, source_target_pairs={{0,3},{1,2},{2,1},{3,0},{4,7},{5,6},{6,5},{7,4},{8,11},{9,10},{10,... | collective-permute-start | bytes 1179656 | tf_op jit(solution)/shard_map/ppermute | solution.py:46
  23.3 0.1 pad_add_fusion.3.refs_0_
  23.4 0.1 pad_add_fusion.4.refs_0_
  23.4 4.2 %shard_map.135 = (bf16[192,512]{1,0:T(8,128)(2,1)S(1)}, bf16[192,512]{1,0:T(8,128)(2,1)S(1)}) custom-call(s32[4]{0:T(128)S(1)} %pad_add_fusion.4.refs_0_, bf16[192,3072]{1,0:T(8,128)(2,1)S(1)} %copy-done.4, bf16[3072,4096]{1,0:T(8,128)(2,1)} %refs_4_.3), custom_call_target="tpu_custom_call" | custom-call | flops 1207959552 | bytes 7471104 | tf_op jit(solution)/shard_map/pallas_call | solution.py:85
  27.6 0.6 collective-permute-start.5
  28.2 0.1 collective-permute-start.7
  28.3 4.3 %shard_map.134 = (bf16[192,512]{1,0:T(8,128)(2,1)S(1)}, bf16[192,512]{1,0:T(8,128)(2,1)S(1)}) custom-call(s32[4]{0:T(128)S(1)} %pad_add_fusion.3.refs_0_, bf16[192,3072]{1,0:T(8,128)(2,1)S(1)} %copy-done.4, bf16[3072,4096]{1,0:T(8,128)(2,1)} %refs_4_.3), custom_call_target="tpu_custom_call" | custom-call | flops 1207959552 | bytes 7471104 | tf_op jit(solution)/shard_map/pallas_call | solution.py:85
  32.6 2.0 %collective-permute-start.4 = (bf16[192,512]{1,0:T(8,128)(2,1)S(1)}, bf16[192,512]{1,0:T(8,128)(2,1)S(1)}, u32[]{:S(2)}, u32[]{:S(2)}) collective-permute-start(bf16[192,512]{1,0:T(8,128)(2,1)S(1)} %get-tuple-element.58), channel_id=1, source_target_pairs={{0,1},{1,0},{2,3},{3,2},{4,5},{5,4},{6,7},{7,6},{8,9},{9,8},{10,11... | collective-permute-start | bytes 589832 | tf_op jit(solution)/shard_map/ppermute | solution.py:46
  34.6 1.5 %collective-permute-start.6 = (bf16[192,512]{1,0:T(8,128)(2,1)S(1)}, bf16[192,512]{1,0:T(8,128)(2,1)S(1)}, u32[]{:S(2)}, u32[]{:S(2)}) collective-permute-start(bf16[192,512]{1,0:T(8,128)(2,1)S(1)} %get-tuple-element.60), channel_id=1, source_target_pairs={{0,2},{1,3},{2,0},{3,1},{4,6},{5,7},{6,4},{7,5},{8,10},{9,11},{10,... | collective-permute-start | bytes 589832 | tf_op jit(solution)/shard_map/ppermute | solution.py:46
  36.1 0.1 pad_add_fusion.2.refs_0_
  36.2 4.2 %shard_map.133.own_ref = f32[192,1024]{1,0:T(8,128)S(1)} custom-call(s32[4]{0:T(128)S(1)} %pad_add_fusion.2.refs_0_, bf16[192,3072]{1,0:T(8,128)(2,1)S(1)} %copy-done.4, bf16[3072,4096]{1,0:T(8,128)(2,1)} %refs_4_.3, bf16[192,1024]{1,0:T(8,128)(2,1)S(1)} %copy-done.6), custom_call_target="tpu_custom_call" | custom-call | flops 1207959552 | bytes 7471104 | tf_op jit(solution)/shard_map/pallas_call | solution.py:85
  40.5 1.0 shard_map.136
  41.5 1.2 %collective-permute-start.8 = (bf16[36,1024]{1,0:T(8,128)(2,1)S(1)}, bf16[36,1024]{1,0:T(8,128)(2,1)S(1)}, u32[]{:S(2)}, u32[]{:S(2)}) collective-permute-start(bf16[36,1024]{1,0:T(8,128)(2,1)S(1)} %get-tuple-element.62), channel_id=1, source_target_pairs={{0,28},{4,24},{8,20},{12,16},{16,12},{20,8},{24,4},{28,0},{1,29},{... | collective-permute-start | bytes 221192 | tf_op jit(solution)/shard_map/ppermute | solution.py:46
  42.7 2.5 %collective-permute-start.9 = (bf16[36,1024]{1,0:T(8,128)(2,1)S(1)}, bf16[36,1024]{1,0:T(8,128)(2,1)S(1)}, u32[]{:S(2)}, u32[]{:S(2)}) collective-permute-start(bf16[36,1024]{1,0:T(8,128)(2,1)S(1)} %get-tuple-element.63), channel_id=1, source_target_pairs={{0,24},{4,28},{8,16},{12,20},{16,8},{20,12},{24,0},{28,4},{1,25},{... | collective-permute-start | bytes 221192 | tf_op jit(solution)/shard_map/ppermute | solution.py:46
  45.3 0.4 collective-permute-start.10
  45.7 2.2 %collective-permute-start.11 = (bf16[36,1024]{1,0:T(8,128)(2,1)S(1)}, bf16[36,1024]{1,0:T(8,128)(2,1)S(1)}, u32[]{:S(2)}, u32[]{:S(2)}) collective-permute-start(bf16[36,1024]{1,0:T(8,128)(2,1)S(1)} %get-tuple-element.65), channel_id=1, source_target_pairs={{0,16},{4,20},{8,24},{12,28},{16,0},{20,4},{24,8},{28,12},{1,17},{... | collective-permute-start | bytes 221192 | tf_op jit(solution)/shard_map/ppermute | solution.py:46
  47.8 0.9 collective-permute-start.12
  48.8 5.6 %collective-permute-start.13 = (bf16[36,1024]{1,0:T(8,128)(2,1)S(1)}, bf16[36,1024]{1,0:T(8,128)(2,1)S(1)}, u32[]{:S(2)}, u32[]{:S(2)}) collective-permute-start(bf16[36,1024]{1,0:T(8,128)(2,1)S(1)} %get-tuple-element.67), channel_id=1, source_target_pairs={{0,8},{4,12},{8,0},{12,4},{16,24},{20,28},{24,16},{28,20},{1,9},{5... | collective-permute-start | bytes 221192 | tf_op jit(solution)/shard_map/ppermute | solution.py:46
  54.3 0.6 collective-permute-start.14
  54.9 1.2 %copy-done = bf16[128,4224]{1,0:T(8,128)(2,1)S(1)} copy-done((bf16[128,4224]{1,0:T(8,128)(2,1)S(1)}, bf16[128,4224]{1,0:T(8,128)(2,1)}, u32[]{:S(2)}) %copy-start) | copy-done | bytes 1081368
  56.2 0.9 shard_map.132
  57.1 0.8 collective-permute-done.10.refs_2_
  57.9 1.9 %collective-permute-done.11.refs_3_ = bf16[36,1024]{1,0:T(8,128)(2,1)S(1)} collective-permute-done((bf16[36,1024]{1,0:T(8,128)(2,1)S(1)}, bf16[36,1024]{1,0:T(8,128)(2,1)S(1)}, u32[]{:S(2)}, u32[]{:S(2)}) %collective-permute-start.11) | collective-permute-done | bytes 73760 | tf_op jit(solution)/shard_map/ppermute | solution.py:46
  59.8 1.2 %collective-permute-done.13.refs_5_ = bf16[36,1024]{1,0:T(8,128)(2,1)S(1)} collective-permute-done((bf16[36,1024]{1,0:T(8,128)(2,1)S(1)}, bf16[36,1024]{1,0:T(8,128)(2,1)S(1)}, u32[]{:S(2)}, u32[]{:S(2)}) %collective-permute-start.13) | collective-permute-done | bytes 73760 | tf_op jit(solution)/shard_map/ppermute | solution.py:46
  61.0 1.4 %shard_map.137.refs_1_.refs_11_ = bf16[288,1024]{1,0:T(8,128)(2,1)S(1)} custom-call(s32[1]{0:T(128)} %bitcast.10.refs_0_.wide_ref, bf16[36,1024]{1,0:T(8,128)(2,1)S(1)} %collective-permute-done.8.refs_0_, bf16[36,1024]{1,0:T(8,128)(2,1)S(1)} %collective-permute-done.9.refs_1_, bf16[36,1024]{1,0:T(8,128)(2,1)S(1)} %collective-permute-done.10.refs_2_, ...), custom_call_target="tpu_custom_call" | custom-call | flops 169869312 | bytes 1179648 | tf_op jit(solution)/shard_map/pallas_call | solution.py:271
  62.4 1.3 %collective-permute-start.16 = (bf16[288,1024]{1,0:T(8,128)(2,1)S(1)}, bf16[288,1024]{1,0:T(8,128)(2,1)S(1)}, u32[]{:S(2)}, u32[]{:S(2)}) collective-permute-start(bf16[288,1024]{1,0:T(8,128)(2,1)S(1)} %shard_map.137.refs_1_.refs_11_), channel_id=1, source_target_pairs={{0,2},{1,3},{2,0},{3,1},{4,6},{5,7},{6,4},{7,5},{8,10},{9,11},{10,... | collective-permute-start | bytes 1769480 | tf_op jit(solution)/shard_map/ppermute | solution.py:46
  63.6 0.2 collective-permute-start.15
  63.9 0.1 pad_add_fusion.1.refs_0_
  63.9 0.1 pad_add_fusion.5.refs_0_
  64.0 1.2 %copy-done.1 = bf16[128,4224]{1,0:T(8,128)(2,1)S(1)} copy-done((bf16[128,4224]{1,0:T(8,128)(2,1)S(1)}, bf16[128,4224]{1,0:T(8,128)(2,1)}, u32[]{:S(2)}) %copy-start.1) | copy-done | bytes 1081368
  65.3 7.1 %shard_map.138 = (f32[416,3072]{1,0:T(8,128)S(1)}, f32[288,1]{1,0:T(8,128)S(1)}, f32[288,128]{1,0:T(8,128)S(1)}) custom-call(s32[1]{0:T(128)} %bitcast.refs_0_, bf16[288,1024]{1,0:T(8,128)(2,1)S(1)} %shard_map.137.refs_1_.refs_11_, bf16[3072,4096]{1,0:T(8,128)(2,1)} %refs_4_.3, bf16[3072,4096]{1,0:T(8,128)(2,1)} %refs_4_.3, bf16[128,4224]{1,0:T(8,128)(2,1)S(1)} %copy-done.1), custom_call_target="tpu_custom_call" | custom-call | flops 1811939328 | bytes 6291456 | tf_op jit(solution)/shard_map/pallas_call | solution.py:408
  72.3 2.3 %copy-done.5 = f32[416,3072]{1,0:T(8,128)} copy-done((f32[416,3072]{1,0:T(8,128)}, f32[416,3072]{1,0:T(8,128)S(1)}, u32[]{:S(2)}) %copy-start.5) | copy-done | bytes 5111832
  74.6 3.1 %collective-permute-done.16.refs_2_ = bf16[288,1024]{1,0:T(8,128)(2,1)S(1)} collective-permute-done((bf16[288,1024]{1,0:T(8,128)(2,1)S(1)}, bf16[288,1024]{1,0:T(8,128)(2,1)S(1)}, u32[]{:S(2)}, u32[]{:S(2)}) %collective-permute-start.16) | collective-permute-done | bytes 589856 | tf_op jit(solution)/shard_map/ppermute | solution.py:46
  77.8 0.9 collective-permute-done.15.refs_1_
  78.8 0.9 collective-permute-start.17
  79.7 0.3 collective-permute-start.18
  79.9 11.6 %shard_map.139 = (f32[416,3072]{1,0:T(8,128)S(1)}, f32[288,1]{1,0:T(8,128)S(1)}, f32[288,128]{1,0:T(8,128)S(1)}) custom-call(s32[2]{0:T(128)S(1)} %pad_add_fusion.5.refs_0_, bf16[288,1024]{1,0:T(8,128)(2,1)S(1)} %collective-permute-done.15.refs_1_, bf16[288,1024]{1,0:T(8,128)(2,1)S(1)} %collective-permute-done.16.refs_2_, bf16[3072,4096]{1,0:T(8,128)(2,1)} %refs_4_.3, ...), custom_call_target="tpu_custom_call" | custom-call | flops 3623878656 | bytes 12582912 | tf_op jit(solution)/shard_map/pallas_call | solution.py:408
  91.6 12.3 %shard_map.140 = (bf16[288,3072]{1,0:T(8,128)(2,1)}, bf16[288,1024]{1,0:T(8,128)(2,1)}, bf16[288,1024]{1,0:T(8,128)(2,1)}) custom-call(s32[2]{0:T(128)S(1)} %pad_add_fusion.1.refs_0_, bf16[144,1024]{1,0:T(8,128)(2,1)S(1)} %collective-permute-done.17.refs_1_, bf16[144,1024]{1,0:T(8,128)(2,1)S(1)} %collective-permute-done.18.refs_2_, ...), custom_call_target="tpu_custom_call" | custom-call | flops 1811939328 | bytes 11599872 | tf_op jit(solution)/shard_map/pallas_call | solution.py:478
  (39 shorter events, 0.1 us)
Async XLA Ops:
  7.2 47.8 %all-gather.2.cloned.1.call-start = ((), (), s32[]{:S(2)}) async-start(), calls=%async_computation | async-start | bytes 1216512 | tf_op jit(solution)/shard_map/all_gather | solution.py:555
  8.6 10.0 %collective-permute-start.2 = (bf16[4,8704]{1,0:T(4,128)(2,1)}, bf16[4,8704]{1,0:T(4,128)(2,1)S(1)}, u32[]{:S(2)}, u32[]{:S(2)}) collective-permute-start(bf16[4,8704]{1,0:T(4,128)(2,1)} %shard_map.130.refs_1_), channel_id=1, source_target_pairs={{0,3},{1,2},{2,1},{3,0},{4,7},{5,6},{6,5},{7,4},{8,11},{9,10},{10,... | collective-permute-start | bytes 208904 | tf_op jit(solution)/shard_map/ppermute | solution.py:46
  12.5 6.2 %collective-permute-start.1 = (bf16[4,8704]{1,0:T(4,128)(2,1)}, bf16[4,8704]{1,0:T(4,128)(2,1)S(1)}, u32[]{:S(2)}, u32[]{:S(2)}) collective-permute-start(bf16[4,8704]{1,0:T(4,128)(2,1)} %shard_map.130.refs_1_), channel_id=1, source_target_pairs={{0,2},{1,3},{2,0},{3,1},{4,6},{5,7},{6,4},{7,5},{8,10},{9,11},{10,... | collective-permute-start | bytes 208904 | tf_op jit(solution)/shard_map/ppermute | solution.py:46
  13.0 5.7 %collective-permute-start = (bf16[4,8704]{1,0:T(4,128)(2,1)}, bf16[4,8704]{1,0:T(4,128)(2,1)S(1)}, u32[]{:S(2)}, u32[]{:S(2)}) collective-permute-start(bf16[4,8704]{1,0:T(4,128)(2,1)} %shard_map.130.refs_1_), channel_id=1, source_target_pairs={{0,1},{1,0},{2,3},{3,2},{4,5},{5,4},{6,7},{7,6},{8,9},{9,8},{10,11... | collective-permute-start | bytes 208904 | tf_op jit(solution)/shard_map/ppermute | solution.py:46
  13.2 1.3 %copy-start.3 = (bf16[192,3072]{1,0:T(8,128)(2,1)S(1)}, bf16[192,3072]{1,0:T(8,128)(2,1)}, u32[]{:S(2)}) copy-start(bf16[192,3072]{1,0:T(8,128)(2,1)} %refs_1_.4) | copy-start | bytes 3538948
  14.4 4.3 %copy-start.7 = (bf16[4,8704]{1,0:T(4,128)(2,1)S(1)}, bf16[4,8704]{1,0:T(4,128)(2,1)}, u32[]{:S(2)}) copy-start(bf16[4,8704]{1,0:T(4,128)(2,1)} %shard_map.130.refs_1_) | copy-start | bytes 208900
  14.4 4.3 %copy-start.9 = (s32[192,1]{0,1:T(1,128)S(1)}, s32[192,1]{0,1:T(1,128)}, u32[]{:S(2)}) copy-start(s32[192,1]{0,1:T(1,128)} %param.15) | copy-start | bytes 2308
  14.5 4.3 %copy-start.10 = (f32[16]{0:T(128)S(1)}, f32[16]{0:T(128)}, u32[]{:S(2)}) copy-start(f32[16]{0:T(128)} %param.12) | copy-start | bytes 196
  14.5 4.3 %copy-start.11 = (s32[16]{0:T(128)S(1)}, s32[16]{0:T(128)}, u32[]{:S(2)}) copy-start(s32[16]{0:T(128)} %param.13) | copy-start | bytes 196
  14.5 4.3 %copy-start.12 = (s32[1,16]{1,0:T(1,128)S(1)}, s32[1,16]{1,0:T(1,128)}, u32[]{:S(2)}) copy-start(s32[1,16]{1,0:T(1,128)} %refs_8_.1) | copy-start | bytes 196
  14.5 9.0 %copy-start.4 = (bf16[192,3072]{1,0:T(8,128)(2,1)S(1)}, bf16[192,3072]{1,0:T(8,128)(2,1)}, u32[]{:S(2)}) copy-start(bf16[192,3072]{1,0:T(8,128)(2,1)} %refs_1_.4) | copy-start | bytes 3538948
  20.3 20.2 %collective-permute-start.3 = (bf16[192,1024]{1,0:T(8,128)(2,1)S(1)}, bf16[192,1024]{1,0:T(8,128)(2,1)S(1)}, u32[]{:S(2)}, u32[]{:S(2)}) collective-permute-start(bf16[192,1024]{1,0:T(8,128)(2,1)S(1)} %shard_map.129), channel_id=1, source_target_pairs={{0,3},{1,2},{2,1},{3,0},{4,7},{5,6},{6,5},{7,4},{8,11},{9,10},{10,... | collective-permute-start | bytes 1179656 | tf_op jit(solution)/shard_map/ppermute | solution.py:46
  27.6 12.8 %collective-permute-start.5 = (bf16[192,512]{1,0:T(8,128)(2,1)S(1)}, bf16[192,512]{1,0:T(8,128)(2,1)S(1)}, u32[]{:S(2)}, u32[]{:S(2)}) collective-permute-start(bf16[192,512]{1,0:T(8,128)(2,1)S(1)} %get-tuple-element.59), channel_id=1, source_target_pairs={{0,1},{1,0},{2,3},{3,2},{4,5},{5,4},{6,7},{7,6},{8,9},{9,8},{10,11... | collective-permute-start | bytes 589832 | tf_op jit(solution)/shard_map/ppermute | solution.py:46
  28.2 7.9 %copy-start.6 = (bf16[192,1024]{1,0:T(8,128)(2,1)S(1)}, bf16[192,1024]{1,0:T(8,128)(2,1)}, u32[]{:S(2)}) copy-start(bf16[192,1024]{1,0:T(8,128)(2,1)} %refs_3_.4) | copy-start | bytes 1179652
  28.2 12.2 %collective-permute-start.7 = (bf16[192,512]{1,0:T(8,128)(2,1)S(1)}, bf16[192,512]{1,0:T(8,128)(2,1)S(1)}, u32[]{:S(2)}, u32[]{:S(2)}) collective-permute-start(bf16[192,512]{1,0:T(8,128)(2,1)S(1)} %get-tuple-element.61), channel_id=1, source_target_pairs={{0,2},{1,3},{2,0},{3,1},{4,6},{5,7},{6,4},{7,5},{8,10},{9,11},{10,... | collective-permute-start | bytes 589832 | tf_op jit(solution)/shard_map/ppermute | solution.py:46
  32.6 7.8 %collective-permute-start.4 = (bf16[192,512]{1,0:T(8,128)(2,1)S(1)}, bf16[192,512]{1,0:T(8,128)(2,1)S(1)}, u32[]{:S(2)}, u32[]{:S(2)}) collective-permute-start(bf16[192,512]{1,0:T(8,128)(2,1)S(1)} %get-tuple-element.58), channel_id=1, source_target_pairs={{0,1},{1,0},{2,3},{3,2},{4,5},{5,4},{6,7},{7,6},{8,9},{9,8},{10,11... | collective-permute-start | bytes 589832 | tf_op jit(solution)/shard_map/ppermute | solution.py:46
  34.6 5.8 %collective-permute-start.6 = (bf16[192,512]{1,0:T(8,128)(2,1)S(1)}, bf16[192,512]{1,0:T(8,128)(2,1)S(1)}, u32[]{:S(2)}, u32[]{:S(2)}) collective-permute-start(bf16[192,512]{1,0:T(8,128)(2,1)S(1)} %get-tuple-element.60), channel_id=1, source_target_pairs={{0,2},{1,3},{2,0},{3,1},{4,6},{5,7},{6,4},{7,5},{8,10},{9,11},{10,... | collective-permute-start | bytes 589832 | tf_op jit(solution)/shard_map/ppermute | solution.py:46
  41.5 7.3 %collective-permute-start.8 = (bf16[36,1024]{1,0:T(8,128)(2,1)S(1)}, bf16[36,1024]{1,0:T(8,128)(2,1)S(1)}, u32[]{:S(2)}, u32[]{:S(2)}) collective-permute-start(bf16[36,1024]{1,0:T(8,128)(2,1)S(1)} %get-tuple-element.62), channel_id=1, source_target_pairs={{0,28},{4,24},{8,20},{12,16},{16,12},{20,8},{24,4},{28,0},{1,29},{... | collective-permute-start | bytes 221192 | tf_op jit(solution)/shard_map/ppermute | solution.py:46
  42.7 11.6 %collective-permute-start.9 = (bf16[36,1024]{1,0:T(8,128)(2,1)S(1)}, bf16[36,1024]{1,0:T(8,128)(2,1)S(1)}, u32[]{:S(2)}, u32[]{:S(2)}) collective-permute-start(bf16[36,1024]{1,0:T(8,128)(2,1)S(1)} %get-tuple-element.63), channel_id=1, source_target_pairs={{0,24},{4,28},{8,16},{12,20},{16,8},{20,12},{24,0},{28,4},{1,25},{... | collective-permute-start | bytes 221192 | tf_op jit(solution)/shard_map/ppermute | solution.py:46
  45.3 12.6 %collective-permute-start.10 = (bf16[36,1024]{1,0:T(8,128)(2,1)S(1)}, bf16[36,1024]{1,0:T(8,128)(2,1)S(1)}, u32[]{:S(2)}, u32[]{:S(2)}) collective-permute-start(bf16[36,1024]{1,0:T(8,128)(2,1)S(1)} %get-tuple-element.64), channel_id=1, source_target_pairs={{0,20},{4,16},{8,28},{12,24},{16,4},{20,0},{24,12},{28,8},{1,21},{... | collective-permute-start | bytes 221192 | tf_op jit(solution)/shard_map/ppermute | solution.py:46
  45.7 14.1 %collective-permute-start.11 = (bf16[36,1024]{1,0:T(8,128)(2,1)S(1)}, bf16[36,1024]{1,0:T(8,128)(2,1)S(1)}, u32[]{:S(2)}, u32[]{:S(2)}) collective-permute-start(bf16[36,1024]{1,0:T(8,128)(2,1)S(1)} %get-tuple-element.65), channel_id=1, source_target_pairs={{0,16},{4,20},{8,24},{12,28},{16,0},{20,4},{24,8},{28,12},{1,17},{... | collective-permute-start | bytes 221192 | tf_op jit(solution)/shard_map/ppermute | solution.py:46
  47.8 11.9 %collective-permute-start.12 = (bf16[36,1024]{1,0:T(8,128)(2,1)S(1)}, bf16[36,1024]{1,0:T(8,128)(2,1)S(1)}, u32[]{:S(2)}, u32[]{:S(2)}) collective-permute-start(bf16[36,1024]{1,0:T(8,128)(2,1)S(1)} %get-tuple-element.66), channel_id=1, source_target_pairs={{0,12},{4,8},{8,4},{12,0},{16,28},{20,24},{24,20},{28,16},{1,13},{... | collective-permute-start | bytes 221192 | tf_op jit(solution)/shard_map/ppermute | solution.py:46
  48.8 12.2 %collective-permute-start.13 = (bf16[36,1024]{1,0:T(8,128)(2,1)S(1)}, bf16[36,1024]{1,0:T(8,128)(2,1)S(1)}, u32[]{:S(2)}, u32[]{:S(2)}) collective-permute-start(bf16[36,1024]{1,0:T(8,128)(2,1)S(1)} %get-tuple-element.67), channel_id=1, source_target_pairs={{0,8},{4,12},{8,0},{12,4},{16,24},{20,28},{24,16},{28,20},{1,9},{5... | collective-permute-start | bytes 221192 | tf_op jit(solution)/shard_map/ppermute | solution.py:46
  54.3 6.7 %collective-permute-start.14 = (bf16[36,1024]{1,0:T(8,128)(2,1)S(1)}, bf16[36,1024]{1,0:T(8,128)(2,1)S(1)}, u32[]{:S(2)}, u32[]{:S(2)}) collective-permute-start(bf16[36,1024]{1,0:T(8,128)(2,1)S(1)} %get-tuple-element.68), channel_id=1, source_target_pairs={{0,4},{4,0},{8,12},{12,8},{16,20},{20,16},{24,28},{28,24},{1,5},{5... | collective-permute-start | bytes 221192 | tf_op jit(solution)/shard_map/ppermute | solution.py:46
  54.9 1.2 %copy-start = (bf16[128,4224]{1,0:T(8,128)(2,1)S(1)}, bf16[128,4224]{1,0:T(8,128)(2,1)}, u32[]{:S(2)}) copy-start(bf16[128,4224]{1,0:T(8,128)(2,1)} %all-gather.2.cloned.1.call-done.refs_1_.refs_4_.refs_7_.refs_8_.refs_5_.refs_12_) | copy-start | bytes 3244036
  62.4 15.4 %collective-permute-start.16 = (bf16[288,1024]{1,0:T(8,128)(2,1)S(1)}, bf16[288,1024]{1,0:T(8,128)(2,1)S(1)}, u32[]{:S(2)}, u32[]{:S(2)}) collective-permute-start(bf16[288,1024]{1,0:T(8,128)(2,1)S(1)} %shard_map.137.refs_1_.refs_11_), channel_id=1, source_target_pairs={{0,2},{1,3},{2,0},{3,1},{4,6},{5,7},{6,4},{7,5},{8,10},{9,11},{10,... | collective-permute-start | bytes 1769480 | tf_op jit(solution)/shard_map/ppermute | solution.py:46
  63.6 15.1 %collective-permute-start.15 = (bf16[288,1024]{1,0:T(8,128)(2,1)S(1)}, bf16[288,1024]{1,0:T(8,128)(2,1)S(1)}, u32[]{:S(2)}, u32[]{:S(2)}) collective-permute-start(bf16[288,1024]{1,0:T(8,128)(2,1)S(1)} %shard_map.137.refs_1_.refs_11_), channel_id=1, source_target_pairs={{0,1},{1,0},{2,3},{3,2},{4,5},{5,4},{6,7},{7,6},{8,9},{9,8},{10,11... | collective-permute-start | bytes 1769480 | tf_op jit(solution)/shard_map/ppermute | solution.py:46
  64.0 1.2 %copy-start.1 = (bf16[128,4224]{1,0:T(8,128)(2,1)S(1)}, bf16[128,4224]{1,0:T(8,128)(2,1)}, u32[]{:S(2)}) copy-start(bf16[128,4224]{1,0:T(8,128)(2,1)} %all-gather.2.cloned.1.call-done.refs_1_.refs_4_.refs_7_.refs_8_.refs_5_.refs_12_) | copy-start | bytes 3244036
  65.3 14.7 %copy-start.2 = (bf16[128,4224]{1,0:T(8,128)(2,1)S(1)}, bf16[128,4224]{1,0:T(8,128)(2,1)}, u32[]{:S(2)}) copy-start(bf16[128,4224]{1,0:T(8,128)(2,1)} %all-gather.2.cloned.1.call-done.refs_1_.refs_4_.refs_7_.refs_8_.refs_5_.refs_12_) | copy-start | bytes 3244036
  72.3 2.3 %copy-start.5 = (f32[416,3072]{1,0:T(8,128)}, f32[416,3072]{1,0:T(8,128)S(1)}, u32[]{:S(2)}) copy-start(f32[416,3072]{1,0:T(8,128)S(1)} %get-tuple-element.83.refs_9_) | copy-start | bytes 15335428
  78.8 12.8 %copy-start.8 = (f32[1024]{0:T(1024)S(1)}, f32[1024]{0:T(1024)}, u32[]{:S(2)}) copy-start(f32[1024]{0:T(1024)} %param.19) | copy-start | bytes 12292
  78.8 12.8 %collective-permute-start.17 = (bf16[144,1024]{1,0:T(8,128)(2,1)S(1)}, bf16[144,1024]{1,0:T(8,128)(2,1)S(1)}, u32[]{:S(2)}, u32[]{:S(2)}) collective-permute-start(bf16[144,1024]{1,0:T(8,128)(2,1)S(1)} %slice.6), channel_id=1, source_target_pairs={{0,2},{1,3},{2,0},{3,1},{4,6},{5,7},{6,4},{7,5},{8,10},{9,11},{10,... | collective-permute-start | bytes 884744 | tf_op jit(solution)/shard_map/ppermute | solution.py:46
  79.7 11.9 %collective-permute-start.18 = (bf16[144,1024]{1,0:T(8,128)(2,1)S(1)}, bf16[144,1024]{1,0:T(8,128)(2,1)S(1)}, u32[]{:S(2)}, u32[]{:S(2)}) collective-permute-start(bf16[144,1024]{1,0:T(8,128)(2,1)S(1)} %slice.7), channel_id=1, source_target_pairs={{0,1},{1,0},{2,3},{3,2},{4,5},{5,4},{6,7},{7,6},{8,9},{9,8},{10,11... | collective-permute-start | bytes 884744 | tf_op jit(solution)/shard_map/ppermute | solution.py:46
Sparse Core Ops, SparseCore 0:
  20.4 24.1 all-gather.1

commit v10 on v8

--- a/solution.py
+++ b/solution.py
@@ -425,7 +425,9 @@
     for side in range(2):
         at = slice(side * half, (side + 1) * half)
         total = product(hids, weights[side::2])
-        acc_ref[:, at] = before[0][:, at] + total if carried else total
+        if carried:
+            total = total + before[0][:, at].astype(f32)
+        acc_ref[:, at] = total.astype(bf16)
 
 
 def carried_specs(rows, pairs, tile):
@@ -455,7 +457,7 @@
             out_specs=totals,
         ),
         out_shape=[
-            jax.ShapeDtypeStruct((rows, depth), f32),
+            jax.ShapeDtypeStruct((rows, depth), bf16),
             jax.ShapeDtypeStruct((rows, 1), f32),
             jax.ShapeDtypeStruct((rows, pairs), f32),
         ],
@@ -488,7 +490,7 @@
     for side in range(2):
         at = slice(side * half, (side + 1) * half)
         low_act = dot_t(hot_ref[...], low_act_ref[at])
-        hid_act = acc_ref[:, at] + product([hid], weights[side : side + 1])
+        hid_act = acc_ref[:, at].astype(f32) + product([hid], weights[side : side + 1])
         act_out[:, at] = (lead[...] * low_act - pull[...] * hid_act).astype(bf16)
     rows = pl.ds(pl.multiple_of(pl.program_id(0) * step, step), step)
     own = own_ref[...].astype(f32)

time: 106 us -> 106 us (level)
  local copies, waits for them, and re-layouts: 4.32 us -> 2.59 us
  waiting for transfers between devices: 6.3 us -> 7.62 us
    unnamed x24 -> x22, local copies, waits for them, and re-layouts: 4.28 us -> 2.55 us
    ppermute x17, waiting for transfers between devices: 6.29 us -> 7.6 us  [swap(): lax.ppermute(rows, axis, [(i, i ^ k) for i in range(lax.axis_size(axis))])]
  transfers between devices with their start and end apart: 18 -> 18, of which waited for: 2 -> 4; matrix products, arithmetic and copies ran while one was open for 0% -> 0% of each run, Pallas kernels for 44% -> 44%
where the time goes in v10:
time: 106 us; the launch traced here: 104 us
  Pallas kernels  58.1 us (55%)
  starting transfers between devices  21.4 us (20%)
  between operations  14.3 us (13%)
  waiting for transfers between devices  7.62 us (7%)
  local copies, waits for them, and re-layouts  2.59 us (2%)
    ppermute x17, starting transfers between devices, swap(): lax.ppermute(rows, axis, [(i, i ^ k) for i in range(lax.axis_size(axis))])  21.4 us
    pallas_call x2, Pallas kernels, back(): pl.pallas_call(lambda *refs: back_body(count, len(before), *refs), grid_s...  15.8 us
    pallas_call x4, Pallas kernels, project(): pl.pallas_call(lambda *refs: project_body(len(own), *refs), in_specs=[pl....  15.6 us
    pallas_call x2, Pallas kernels, low_activations(): pl.pallas_call(lambda *refs: low_act_body(part, *refs), grid=(1,), in_spe...  12.1 us
    pallas_call x1, Pallas kernels, finish(): pl.pallas_call(lambda *refs: finish_body(features, count, *refs), grid_sp...  8.42 us
    ppermute x17, waiting for transfers between devices, swap(): lax.ppermute(rows, axis, [(i, i ^ k) for i in range(lax.axis_size(axis))])  7.6 us
    unnamed x22, local copies, waits for them, and re-layouts  2.55 us
  transfers between devices with their start and end apart: 18, of which 4 were waited for; matrix products, arithmetic and copies ran while one was open for 0% of the time, Pallas kernels for 44%

profile of v10, /device:TPU:0, one launch (start us, length us, event | category | flops | bytes accessed | tf_op | source)
XLA Modules:
  0.0 104.2 jit_solution(7696158664878694777)
XLA Ops:
  7.2 0.0 all-gather.2.cloned.1.call-start
  7.2 1.4 %shard_map.130.refs_1_ = bf16[4,8704]{1,0:T(4,128)(2,1)} custom-call(bf16[4,4096]{1,0:T(4,128)(2,1)} %query_ref.1, bf16[4,4096]{1,0:T(4,128)(2,1)} %passage_ref.1, f32[1,1024]{1,0:T(1,128)} %bitcast.9), custom_call_target="tpu_custom_call" | custom-call | flops 16384 | bytes 131072 | tf_op jit(solution)/shard_map/pallas_call | solution.py:118
  8.6 3.9 %collective-permute-start.2 = (bf16[4,8704]{1,0:T(4,128)(2,1)}, bf16[4,8704]{1,0:T(4,128)(2,1)S(1)}, u32[]{:S(2)}, u32[]{:S(2)}) collective-permute-start(bf16[4,8704]{1,0:T(4,128)(2,1)} %shard_map.130.refs_1_), channel_id=1, source_target_pairs={{0,3},{1,2},{2,1},{3,0},{4,7},{5,6},{6,5},{7,4},{8,11},{9,10},{10,... | collective-permute-start | bytes 208904 | tf_op jit(solution)/shard_map/ppermute | solution.py:46
  12.5 0.5 collective-permute-start.1
  13.0 0.1 collective-permute-start
  13.1 1.3 %copy-done.2 = bf16[192,3072]{1,0:T(8,128)(2,1)S(1)} copy-done((bf16[192,3072]{1,0:T(8,128)(2,1)S(1)}, bf16[192,3072]{1,0:T(8,128)(2,1)}, u32[]{:S(2)}) %copy-start.2) | copy-done | bytes 1179672
  14.4 0.0 copy-start.10
  14.4 3.8 %shard_map.129 = bf16[192,1024]{1,0:T(8,128)(2,1)S(1)} custom-call(s32[1]{0:T(128)} %bitcast.1.refs_0_, bf16[192,3072]{1,0:T(8,128)(2,1)S(1)} %copy-done.2, bf16[3072,4096]{1,0:T(8,128)(2,1)} %refs_4_.3), custom_call_target="tpu_custom_call" | custom-call | flops 1207959552 | bytes 7471104 | tf_op jit(solution)/shard_map/pallas_call | solution.py:84
  18.2 0.0 collective-permute-done.2.refs_4_
  18.2 0.0 collective-permute-done.1.refs_3_
  18.3 1.5 %shard_map.131 = (bf16[4,4096]{1,0:T(4,128)(2,1)}, bf16[16,4224]{1,0:T(8,128)(2,1)}) custom-call(s32[1]{0:T(128)} %bitcast.refs_0_, bf16[4,8704]{1,0:T(4,128)(2,1)S(1)} %copy-done.5, bf16[4,8704]{1,0:T(4,128)(2,1)S(1)} %collective-permute-done.refs_2_, bf16[4,8704]{1,0:T(4,128)(2,1)S(1)} %collective-permute-done.1.refs_3_, ...), custom_call_target="tpu_custom_call" | custom-call | flops 8388608 | bytes 524288 | tf_op jit(solution)/shard_map/pallas_call | solution.py:184
  19.8 0.0 all-gather.2.cloned.1.call-update
  19.9 3.0 %collective-permute-start.3 = (bf16[192,1024]{1,0:T(8,128)(2,1)S(1)}, bf16[192,1024]{1,0:T(8,128)(2,1)S(1)}, u32[]{:S(2)}, u32[]{:S(2)}) collective-permute-start(bf16[192,1024]{1,0:T(8,128)(2,1)S(1)} %shard_map.129), channel_id=1, source_target_pairs={{0,3},{1,2},{2,1},{3,0},{4,7},{5,6},{6,5},{7,4},{8,11},{9,10},{10,... | collective-permute-start | bytes 1179656 | tf_op jit(solution)/shard_map/ppermute | solution.py:46
  22.8 3.6 %shard_map.136 = bf16[192,1024]{1,0:T(8,128)(2,1)S(1)} custom-call(s32[1]{0:T(128)} %bitcast.8.refs_0_, bf16[192,3072]{1,0:T(8,128)(2,1)S(1)} %copy-done.3, bf16[3072,4096]{1,0:T(8,128)(2,1)} %refs_4_.3), custom_call_target="tpu_custom_call" | custom-call | flops 1207959552 | bytes 7471104 | tf_op jit(solution)/shard_map/pallas_call | solution.py:84
  26.5 0.0 copy-start.4
  26.5 4.5 %shard_map.135 = bf16[192,1024]{1,0:T(8,128)(2,1)} custom-call(s32[1]{0:T(128)} %bitcast.7.refs_0_, bf16[192,3072]{1,0:T(8,128)(2,1)S(1)} %copy-done.3, bf16[3072,4096]{1,0:T(8,128)(2,1)} %refs_4_.3), custom_call_target="tpu_custom_call" | custom-call | flops 1207959552 | bytes 7471104 | tf_op jit(solution)/shard_map/pallas_call | solution.py:84
  31.0 0.5 collective-permute-start.4
  31.5 0.0 collective-permute-start.5
  31.6 3.6 %shard_map.134.refs_2_ = f32[192,1024]{1,0:T(8,128)S(1)} custom-call(s32[1]{0:T(128)} %bitcast.refs_0_, bf16[192,3072]{1,0:T(8,128)(2,1)S(1)} %copy-done.3, bf16[3072,4096]{1,0:T(8,128)(2,1)} %refs_4_.3, bf16[192,1024]{1,0:T(8,128)(2,1)S(1)} %copy-done.4), custom_call_target="tpu_custom_call" | custom-call | flops 1207959552 | bytes 7471104 | tf_op jit(solution)/shard_map/pallas_call | solution.py:84
  35.2 0.0 collective-permute-done.3.refs_3_
  35.2 5.7 %collective-permute-done.4.refs_4_ = bf16[192,1024]{1,0:T(8,128)(2,1)S(1)} collective-permute-done((bf16[192,1024]{1,0:T(8,128)(2,1)}, bf16[192,1024]{1,0:T(8,128)(2,1)S(1)}, u32[]{:S(2)}, u32[]{:S(2)}) %collective-permute-start.4) | collective-permute-done | bytes 393248 | tf_op jit(solution)/shard_map/ppermute | solution.py:46
  40.9 0.0 collective-permute-done.5.refs_5_
  41.0 1.1 %shard_map.137 = (bf16[36,1024]{1,0:T(8,128)(2,1)S(1)}, bf16[36,1024]{1,0:T(8,128)(2,1)S(1)}, bf16[36,1024]{1,0:T(8,128)(2,1)S(1)}, bf16[36,1024]{1,0:T(8,128)(2...) custom-call(s32[1]{0:T(128)} %bitcast.6.refs_0_.wide_ref, ...), custom_call_target="tpu_custom_call" | custom-call | flops 226492416 | bytes 1966080 | tf_op jit(solution)/shard_map/pallas_call | solution.py:236
  42.0 0.1 collective-permute-start.6
  42.1 1.6 %collective-permute-start.7 = (bf16[36,1024]{1,0:T(8,128)(2,1)S(1)}, bf16[36,1024]{1,0:T(8,128)(2,1)S(1)}, u32[]{:S(2)}, u32[]{:S(2)}) collective-permute-start(bf16[36,1024]{1,0:T(8,128)(2,1)S(1)} %get-tuple-element.58), channel_id=1, source_target_pairs={{0,8},{4,12},{8,0},{12,4},{16,24},{20,28},{24,16},{28,20},{1,9},{5... | collective-permute-start | bytes 221192 | tf_op jit(solution)/shard_map/ppermute | solution.py:46
  43.7 0.2 collective-permute-start.8
  44.0 2.6 %collective-permute-start.9 = (bf16[36,1024]{1,0:T(8,128)(2,1)S(1)}, bf16[36,1024]{1,0:T(8,128)(2,1)S(1)}, u32[]{:S(2)}, u32[]{:S(2)}) collective-permute-start(bf16[36,1024]{1,0:T(8,128)(2,1)S(1)} %get-tuple-element.60), channel_id=1, source_target_pairs={{0,16},{4,20},{8,24},{12,28},{16,0},{20,4},{24,8},{28,12},{1,17},{... | collective-permute-start | bytes 221192 | tf_op jit(solution)/shard_map/ppermute | solution.py:46
  46.6 0.0 collective-permute-start.10
  46.6 3.6 %collective-permute-start.11 = (bf16[36,1024]{1,0:T(8,128)(2,1)S(1)}, bf16[36,1024]{1,0:T(8,128)(2,1)S(1)}, u32[]{:S(2)}, u32[]{:S(2)}) collective-permute-start(bf16[36,1024]{1,0:T(8,128)(2,1)S(1)} %get-tuple-element.62), channel_id=1, source_target_pairs={{0,24},{4,28},{8,16},{12,20},{16,8},{20,12},{24,0},{28,4},{1,25},{... | collective-permute-start | bytes 221192 | tf_op jit(solution)/shard_map/ppermute | solution.py:46
  50.2 0.1 collective-permute-start.12
  50.3 1.2 %copy-done = bf16[128,4224]{1,0:T(8,128)(2,1)S(1)} copy-done((bf16[128,4224]{1,0:T(8,128)(2,1)S(1)}, bf16[128,4224]{1,0:T(8,128)(2,1)}, u32[]{:S(2)}) %copy-start) | copy-done | bytes 1081368
  51.5 6.1 %shard_map.132.refs_2_ = bf16[3072,128]{1,0:T(8,128)(2,1)S(1)} custom-call(bf16[128,4224]{1,0:T(8,128)(2,1)S(1)} %copy-done, bf16[3072,4096]{1,0:T(8,128)(2,1)} %refs_4_.3), custom_call_target="tpu_custom_call" | custom-call | flops 1610612736 | bytes 12582912 | tf_op jit(solution)/shard_map/pallas_call | solution.py:368
  57.6 0.9 shard_map.133
  58.5 0.5 collective-permute-done.10.refs_5_
  59.1 1.3 %shard_map.139.refs_1_.refs_12_ = bf16[288,1024]{1,0:T(8,128)(2,1)S(1)} custom-call(s32[1]{0:T(128)} %bitcast.6.refs_0_.wide_ref, bf16[36,1024]{1,0:T(8,128)(2,1)S(1)} %get-tuple-element.65.refs_0_, bf16[36,1024]{1,0:T(8,128)(2,1)S(1)} %collective-permute-done.6.refs_1_, bf16[36,1024]{1,0:T(8,128)(2,1)S(1)} %collective-permute-done.7.refs_2_, ...), custom_call_target="tpu_custom_call" | custom-call | flops 169869312 | bytes 1179648 | tf_op jit(solution)/shard_map/pallas_call | solution.py:267
  60.4 0.6 collective-permute-start.14
  61.0 1.5 %collective-permute-start.13 = (bf16[288,1024]{1,0:T(8,128)(2,1)S(1)}, bf16[288,1024]{1,0:T(8,128)(2,1)S(1)}, u32[]{:S(2)}, u32[]{:S(2)}) collective-permute-start(bf16[288,1024]{1,0:T(8,128)(2,1)S(1)} %shard_map.139.refs_1_.refs_12_), channel_id=1, source_target_pairs={{0,1},{1,0},{2,3},{3,2},{4,5},{5,4},{6,7},{7,6},{8,9},{9,8},{10,11... | collective-permute-start | bytes 1769480 | tf_op jit(solution)/shard_map/ppermute | solution.py:46
  62.5 0.1 pad_add_fusion.refs_0_
  62.6 0.1 pad_add_fusion.1.refs_0_
  62.6 6.0 %shard_map.138.refs_11_ = bf16[3072,128]{1,0:T(8,128)(2,1)S(1)} custom-call(bf16[128,4224]{1,0:T(8,128)(2,1)S(1)} %copy-done.1, bf16[3072,4096]{1,0:T(8,128)(2,1)} %refs_4_.3, bf16[3072,128]{1,0:T(8,128)(2,1)S(1)} %shard_map.132.refs_2_), custom_call_target="tpu_custom_call", output_to_operand_aliasing={{}: (2, {})} | custom-call | flops 1610612736 | bytes 12582912 | tf_op jit(solution)/shard_map/pallas_call | solution.py:368
  68.6 6.3 %shard_map.140 = (bf16[288,3072]{1,0:T(8,128)(2,1)S(1)}, f32[288,1]{1,0:T(8,128)S(1)}, f32[288,128]{1,0:T(8,128)S(1)}) custom-call(s32[1]{0:T(128)} %bitcast.refs_0_, bf16[288,1024]{1,0:T(8,128)(2,1)S(1)} %shard_map.139.refs_1_.refs_12_, bf16[3072,4096]{1,0:T(8,128)(2,1)} %refs_4_.3, bf16[3072,4096]{1,0:T(8,128)(2,1)} %refs_4_.3, bf16[128,4224]{1,0:T(8,128)(2,1)S(1)} %copy-done.1), custom_call_target="tpu_custom_call" | custom-call | flops 1811939328 | bytes 6291456 | tf_op jit(solution)/shard_map/pallas_call | solution.py:448
  75.0 1.1 %collective-permute-done.14.refs_2_ = bf16[288,1024]{1,0:T(8,128)(2,1)S(1)} collective-permute-done((bf16[288,1024]{1,0:T(8,128)(2,1)S(1)}, bf16[288,1024]{1,0:T(8,128)(2,1)S(1)}, u32[]{:S(2)}, u32[]{:S(2)}) %collective-permute-start.14) | collective-permute-done | bytes 589856 | tf_op jit(solution)/shard_map/ppermute | solution.py:46
  76.1 0.2 collective-permute-done.13.refs_1_
  76.3 0.0 copy-start.6
  76.4 1.6 %collective-permute-start.15 = (bf16[144,1024]{1,0:T(8,128)(2,1)S(1)}, bf16[144,1024]{1,0:T(8,128)(2,1)S(1)}, u32[]{:S(2)}, u32[]{:S(2)}) collective-permute-start(bf16[144,1024]{1,0:T(8,128)(2,1)S(1)} %slice.6), channel_id=1, source_target_pairs={{0,2},{1,3},{2,0},{3,1},{4,6},{5,7},{6,4},{7,5},{8,10},{9,11},{10,... | collective-permute-start | bytes 884744 | tf_op jit(solution)/shard_map/ppermute | solution.py:46
  77.9 1.5 %collective-permute-start.16 = (bf16[144,1024]{1,0:T(8,128)(2,1)S(1)}, bf16[144,1024]{1,0:T(8,128)(2,1)S(1)}, u32[]{:S(2)}, u32[]{:S(2)}) collective-permute-start(bf16[144,1024]{1,0:T(8,128)(2,1)S(1)} %slice.7), channel_id=1, source_target_pairs={{0,1},{1,0},{2,3},{3,2},{4,5},{5,4},{6,7},{7,6},{8,9},{9,8},{10,11... | collective-permute-start | bytes 884744 | tf_op jit(solution)/shard_map/ppermute | solution.py:46
  79.4 9.5 %shard_map.141 = (bf16[288,3072]{1,0:T(8,128)(2,1)S(1)}, f32[288,1]{1,0:T(8,128)S(1)}, f32[288,128]{1,0:T(8,128)S(1)}) custom-call(s32[2]{0:T(128)S(1)} %pad_add_fusion.1.refs_0_, bf16[288,1024]{1,0:T(8,128)(2,1)S(1)} %collective-permute-done.13.refs_1_, bf16[288,1024]{1,0:T(8,128)(2,1)S(1)} %collective-permute-done.14.refs_2_, bf16[3072,4096]{1,0:T(8,128)(2,1)} %refs_4_.3, ...), custom_call_target="tpu_custom_call" | custom-call | flops 3623878656 | bytes 12582912 | tf_op jit(solution)/shard_map/pallas_call | solution.py:448
  88.9 8.4 %shard_map.142 = (bf16[288,3072]{1,0:T(8,128)(2,1)}, bf16[288,1024]{1,0:T(8,128)(2,1)}, bf16[288,1024]{1,0:T(8,128)(2,1)}) custom-call(s32[2]{0:T(128)S(1)} %pad_add_fusion.refs_0_, bf16[144,1024]{1,0:T(8,128)(2,1)S(1)} %collective-permute-done.15.refs_1_, bf16[144,1024]{1,0:T(8,128)(2,1)S(1)} %collective-permute-done.16.refs_2_, ...), custom_call_target="tpu_custom_call" | custom-call | flops 1811939328 | bytes 11599872 | tf_op jit(solution)/shard_map/pallas_call | solution.py:515
  (29 shorter events, 0.1 us)
Async XLA Ops:
  7.2 43.1 %all-gather.2.cloned.1.call-start = ((), (), s32[]{:S(2)}) async-start(), calls=%async_computation | async-start | bytes 1216512 | tf_op jit(solution)/shard_map/all_gather | solution.py:590
  8.6 9.6 %collective-permute-start.2 = (bf16[4,8704]{1,0:T(4,128)(2,1)}, bf16[4,8704]{1,0:T(4,128)(2,1)S(1)}, u32[]{:S(2)}, u32[]{:S(2)}) collective-permute-start(bf16[4,8704]{1,0:T(4,128)(2,1)} %shard_map.130.refs_1_), channel_id=1, source_target_pairs={{0,3},{1,2},{2,1},{3,0},{4,7},{5,6},{6,5},{7,4},{8,11},{9,10},{10,... | collective-permute-start | bytes 208904 | tf_op jit(solution)/shard_map/ppermute | solution.py:46
  12.5 5.7 %collective-permute-start.1 = (bf16[4,8704]{1,0:T(4,128)(2,1)}, bf16[4,8704]{1,0:T(4,128)(2,1)S(1)}, u32[]{:S(2)}, u32[]{:S(2)}) collective-permute-start(bf16[4,8704]{1,0:T(4,128)(2,1)} %shard_map.130.refs_1_), channel_id=1, source_target_pairs={{0,2},{1,3},{2,0},{3,1},{4,6},{5,7},{6,4},{7,5},{8,10},{9,11},{10,... | collective-permute-start | bytes 208904 | tf_op jit(solution)/shard_map/ppermute | solution.py:46
  13.0 5.2 %collective-permute-start = (bf16[4,8704]{1,0:T(4,128)(2,1)}, bf16[4,8704]{1,0:T(4,128)(2,1)S(1)}, u32[]{:S(2)}, u32[]{:S(2)}) collective-permute-start(bf16[4,8704]{1,0:T(4,128)(2,1)} %shard_map.130.refs_1_), channel_id=1, source_target_pairs={{0,1},{1,0},{2,3},{3,2},{4,5},{5,4},{6,7},{7,6},{8,9},{9,8},{10,11... | collective-permute-start | bytes 208904 | tf_op jit(solution)/shard_map/ppermute | solution.py:46
  13.1 1.3 %copy-start.2 = (bf16[192,3072]{1,0:T(8,128)(2,1)S(1)}, bf16[192,3072]{1,0:T(8,128)(2,1)}, u32[]{:S(2)}) copy-start(bf16[192,3072]{1,0:T(8,128)(2,1)} %refs_1_.7) | copy-start | bytes 3538948
  14.4 3.9 %copy-start.5 = (bf16[4,8704]{1,0:T(4,128)(2,1)S(1)}, bf16[4,8704]{1,0:T(4,128)(2,1)}, u32[]{:S(2)}) copy-start(bf16[4,8704]{1,0:T(4,128)(2,1)} %shard_map.130.refs_1_) | copy-start | bytes 208900
  14.4 3.9 %copy-start.7 = (s32[192,1]{0,1:T(1,128)S(1)}, s32[192,1]{0,1:T(1,128)}, u32[]{:S(2)}) copy-start(s32[192,1]{0,1:T(1,128)} %param.15) | copy-start | bytes 2308
  14.4 3.9 %copy-start.8 = (f32[16]{0:T(128)S(1)}, f32[16]{0:T(128)}, u32[]{:S(2)}) copy-start(f32[16]{0:T(128)} %param.12) | copy-start | bytes 196
  14.4 3.9 %copy-start.9 = (s32[16]{0:T(128)S(1)}, s32[16]{0:T(128)}, u32[]{:S(2)}) copy-start(s32[16]{0:T(128)} %param.13) | copy-start | bytes 196
  14.4 3.9 %copy-start.10 = (s32[1,16]{1,0:T(1,128)S(1)}, s32[1,16]{1,0:T(1,128)}, u32[]{:S(2)}) copy-start(s32[1,16]{1,0:T(1,128)} %refs_8_.1) | copy-start | bytes 196
  14.4 8.4 %copy-start.3 = (bf16[192,3072]{1,0:T(8,128)(2,1)S(1)}, bf16[192,3072]{1,0:T(8,128)(2,1)}, u32[]{:S(2)}) copy-start(bf16[192,3072]{1,0:T(8,128)(2,1)} %refs_1_.7) | copy-start | bytes 3538948
  19.9 15.4 %collective-permute-start.3 = (bf16[192,1024]{1,0:T(8,128)(2,1)S(1)}, bf16[192,1024]{1,0:T(8,128)(2,1)S(1)}, u32[]{:S(2)}, u32[]{:S(2)}) collective-permute-start(bf16[192,1024]{1,0:T(8,128)(2,1)S(1)} %shard_map.129), channel_id=1, source_target_pairs={{0,3},{1,2},{2,1},{3,0},{4,7},{5,6},{6,5},{7,4},{8,11},{9,10},{10,... | collective-permute-start | bytes 1179656 | tf_op jit(solution)/shard_map/ppermute | solution.py:46
  26.5 5.1 %copy-start.4 = (bf16[192,1024]{1,0:T(8,128)(2,1)S(1)}, bf16[192,1024]{1,0:T(8,128)(2,1)}, u32[]{:S(2)}) copy-start(bf16[192,1024]{1,0:T(8,128)(2,1)} %refs_3_.4) | copy-start | bytes 1179652
  31.0 9.9 %collective-permute-start.4 = (bf16[192,1024]{1,0:T(8,128)(2,1)}, bf16[192,1024]{1,0:T(8,128)(2,1)S(1)}, u32[]{:S(2)}, u32[]{:S(2)}) collective-permute-start(bf16[192,1024]{1,0:T(8,128)(2,1)} %shard_map.135), channel_id=1, source_target_pairs={{0,1},{1,0},{2,3},{3,2},{4,5},{5,4},{6,7},{7,6},{8,9},{9,8},{10,11... | collective-permute-start | bytes 1179656 | tf_op jit(solution)/shard_map/ppermute | solution.py:46
  31.5 9.4 %collective-permute-start.5 = (bf16[192,1024]{1,0:T(8,128)(2,1)S(1)}, bf16[192,1024]{1,0:T(8,128)(2,1)S(1)}, u32[]{:S(2)}, u32[]{:S(2)}) collective-permute-start(bf16[192,1024]{1,0:T(8,128)(2,1)S(1)} %shard_map.136), channel_id=1, source_target_pairs={{0,2},{1,3},{2,0},{3,1},{4,6},{5,7},{6,4},{7,5},{8,10},{9,11},{10,... | collective-permute-start | bytes 1179656 | tf_op jit(solution)/shard_map/ppermute | solution.py:46
  42.0 4.6 %collective-permute-start.6 = (bf16[36,1024]{1,0:T(8,128)(2,1)S(1)}, bf16[36,1024]{1,0:T(8,128)(2,1)S(1)}, u32[]{:S(2)}, u32[]{:S(2)}) collective-permute-start(bf16[36,1024]{1,0:T(8,128)(2,1)S(1)} %get-tuple-element.57), channel_id=1, source_target_pairs={{0,4},{4,0},{8,12},{12,8},{16,20},{20,16},{24,28},{28,24},{1,5},{5... | collective-permute-start | bytes 221192 | tf_op jit(solution)/shard_map/ppermute | solution.py:46
  42.1 8.1 %collective-permute-start.7 = (bf16[36,1024]{1,0:T(8,128)(2,1)S(1)}, bf16[36,1024]{1,0:T(8,128)(2,1)S(1)}, u32[]{:S(2)}, u32[]{:S(2)}) collective-permute-start(bf16[36,1024]{1,0:T(8,128)(2,1)S(1)} %get-tuple-element.58), channel_id=1, source_target_pairs={{0,8},{4,12},{8,0},{12,4},{16,24},{20,28},{24,16},{28,20},{1,9},{5... | collective-permute-start | bytes 221192 | tf_op jit(solution)/shard_map/ppermute | solution.py:46
  43.7 14.8 %collective-permute-start.8 = (bf16[36,1024]{1,0:T(8,128)(2,1)S(1)}, bf16[36,1024]{1,0:T(8,128)(2,1)S(1)}, u32[]{:S(2)}, u32[]{:S(2)}) collective-permute-start(bf16[36,1024]{1,0:T(8,128)(2,1)S(1)} %get-tuple-element.59), channel_id=1, source_target_pairs={{0,12},{4,8},{8,4},{12,0},{16,28},{20,24},{24,20},{28,16},{1,13},{... | collective-permute-start | bytes 221192 | tf_op jit(solution)/shard_map/ppermute | solution.py:46
  44.0 14.6 %collective-permute-start.9 = (bf16[36,1024]{1,0:T(8,128)(2,1)S(1)}, bf16[36,1024]{1,0:T(8,128)(2,1)S(1)}, u32[]{:S(2)}, u32[]{:S(2)}) collective-permute-start(bf16[36,1024]{1,0:T(8,128)(2,1)S(1)} %get-tuple-element.60), channel_id=1, source_target_pairs={{0,16},{4,20},{8,24},{12,28},{16,0},{20,4},{24,8},{28,12},{1,17},{... | collective-permute-start | bytes 221192 | tf_op jit(solution)/shard_map/ppermute | solution.py:46
  46.6 12.5 %collective-permute-start.10 = (bf16[36,1024]{1,0:T(8,128)(2,1)S(1)}, bf16[36,1024]{1,0:T(8,128)(2,1)S(1)}, u32[]{:S(2)}, u32[]{:S(2)}) collective-permute-start(bf16[36,1024]{1,0:T(8,128)(2,1)S(1)} %get-tuple-element.61), channel_id=1, source_target_pairs={{0,20},{4,16},{8,28},{12,24},{16,4},{20,0},{24,12},{28,8},{1,21},{... | collective-permute-start | bytes 221192 | tf_op jit(solution)/shard_map/ppermute | solution.py:46
  46.6 12.5 %collective-permute-start.11 = (bf16[36,1024]{1,0:T(8,128)(2,1)S(1)}, bf16[36,1024]{1,0:T(8,128)(2,1)S(1)}, u32[]{:S(2)}, u32[]{:S(2)}) collective-permute-start(bf16[36,1024]{1,0:T(8,128)(2,1)S(1)} %get-tuple-element.62), channel_id=1, source_target_pairs={{0,24},{4,28},{8,16},{12,20},{16,8},{20,12},{24,0},{28,4},{1,25},{... | collective-permute-start | bytes 221192 | tf_op jit(solution)/shard_map/ppermute | solution.py:46
  50.2 8.9 %collective-permute-start.12 = (bf16[36,1024]{1,0:T(8,128)(2,1)S(1)}, bf16[36,1024]{1,0:T(8,128)(2,1)S(1)}, u32[]{:S(2)}, u32[]{:S(2)}) collective-permute-start(bf16[36,1024]{1,0:T(8,128)(2,1)S(1)} %get-tuple-element.63), channel_id=1, source_target_pairs={{0,28},{4,24},{8,20},{12,16},{16,12},{20,8},{24,4},{28,0},{1,29},{... | collective-permute-start | bytes 221192 | tf_op jit(solution)/shard_map/ppermute | solution.py:46
  50.3 1.2 %copy-start = (bf16[128,4224]{1,0:T(8,128)(2,1)S(1)}, bf16[128,4224]{1,0:T(8,128)(2,1)}, u32[]{:S(2)}) copy-start(bf16[128,4224]{1,0:T(8,128)(2,1)} %all-gather.2.cloned.1.call-done.refs_0_.refs_1_.refs_4_.refs_7_.refs_8_.refs_5_.refs_13_) | copy-start | bytes 3244036
  51.5 6.1 %copy-start.1 = (bf16[128,4224]{1,0:T(8,128)(2,1)S(1)}, bf16[128,4224]{1,0:T(8,128)(2,1)}, u32[]{:S(2)}) copy-start(bf16[128,4224]{1,0:T(8,128)(2,1)} %all-gather.2.cloned.1.call-done.refs_0_.refs_1_.refs_4_.refs_7_.refs_8_.refs_5_.refs_13_) | copy-start | bytes 3244036
  60.4 15.6 %collective-permute-start.14 = (bf16[288,1024]{1,0:T(8,128)(2,1)S(1)}, bf16[288,1024]{1,0:T(8,128)(2,1)S(1)}, u32[]{:S(2)}, u32[]{:S(2)}) collective-permute-start(bf16[288,1024]{1,0:T(8,128)(2,1)S(1)} %shard_map.139.refs_1_.refs_12_), channel_id=1, source_target_pairs={{0,2},{1,3},{2,0},{3,1},{4,6},{5,7},{6,4},{7,5},{8,10},{9,11},{10,... | collective-permute-start | bytes 1769480 | tf_op jit(solution)/shard_map/ppermute | solution.py:46
  61.0 15.3 %collective-permute-start.13 = (bf16[288,1024]{1,0:T(8,128)(2,1)S(1)}, bf16[288,1024]{1,0:T(8,128)(2,1)S(1)}, u32[]{:S(2)}, u32[]{:S(2)}) collective-permute-start(bf16[288,1024]{1,0:T(8,128)(2,1)S(1)} %shard_map.139.refs_1_.refs_12_), channel_id=1, source_target_pairs={{0,1},{1,0},{2,3},{3,2},{4,5},{5,4},{6,7},{7,6},{8,9},{9,8},{10,11... | collective-permute-start | bytes 1769480 | tf_op jit(solution)/shard_map/ppermute | solution.py:46
  76.3 12.6 %copy-start.6 = (f32[1024]{0:T(1024)S(1)}, f32[1024]{0:T(1024)}, u32[]{:S(2)}) copy-start(f32[1024]{0:T(1024)} %param.19) | copy-start | bytes 12292
  76.4 12.6 %collective-permute-start.15 = (bf16[144,1024]{1,0:T(8,128)(2,1)S(1)}, bf16[144,1024]{1,0:T(8,128)(2,1)S(1)}, u32[]{:S(2)}, u32[]{:S(2)}) collective-permute-start(bf16[144,1024]{1,0:T(8,128)(2,1)S(1)} %slice.6), channel_id=1, source_target_pairs={{0,2},{1,3},{2,0},{3,1},{4,6},{5,7},{6,4},{7,5},{8,10},{9,11},{10,... | collective-permute-start | bytes 884744 | tf_op jit(solution)/shard_map/ppermute | solution.py:46
  77.9 11.0 %collective-permute-start.16 = (bf16[144,1024]{1,0:T(8,128)(2,1)S(1)}, bf16[144,1024]{1,0:T(8,128)(2,1)S(1)}, u32[]{:S(2)}, u32[]{:S(2)}) collective-permute-start(bf16[144,1024]{1,0:T(8,128)(2,1)S(1)} %slice.7), channel_id=1, source_target_pairs={{0,1},{1,0},{2,3},{3,2},{4,5},{5,4},{6,7},{7,6},{8,9},{9,8},{10,11... | collective-permute-start | bytes 884744 | tf_op jit(solution)/shard_map/ppermute | solution.py:46
Sparse Core Ops, SparseCore 0:
  20.0 23.9 all-gather.1

commit v11 on v10

--- a/solution.py
+++ b/solution.py
@@ -504,7 +504,7 @@
     rows, width = own.shape
     depth, features = w_down.shape
     pairs = hot.shape[1]
-    tile = tile_of(depth, 512)
+    tile = tile_of(depth, 1024)
     steps = depth // tile
     step = rows // steps
 

time: 106 us -> 105 us (level)
  no operation moved by 1% of the time
where the time goes in v11:
time: 105 us; the launch traced here: 103 us
  Pallas kernels  57.2 us (54%)
  starting transfers between devices  21.4 us (20%)
  between operations  14.3 us (14%)
  waiting for transfers between devices  7.62 us (7%)
  local copies, waits for them, and re-layouts  2.59 us (2%)
    ppermute x17, starting transfers between devices, swap(): lax.ppermute(rows, axis, [(i, i ^ k) for i in range(lax.axis_size(axis))])  21.4 us
    pallas_call x2, Pallas kernels, back(): pl.pallas_call(lambda *refs: back_body(count, len(before), *refs), grid_s...  15.8 us
    pallas_call x4, Pallas kernels, project(): pl.pallas_call(lambda *refs: project_body(len(own), *refs), in_specs=[pl....  15.6 us
    pallas_call x2, Pallas kernels, low_activations(): pl.pallas_call(lambda *refs: low_act_body(part, *refs), grid=(1,), in_spe...  12.1 us
    ppermute x17, waiting for transfers between devices, swap(): lax.ppermute(rows, axis, [(i, i ^ k) for i in range(lax.axis_size(axis))])  7.6 us
    pallas_call x1, Pallas kernels, finish(): pl.pallas_call(lambda *refs: finish_body(features, count, *refs), grid_sp...  7.45 us
    unnamed x22, local copies, waits for them, and re-layouts  2.55 us
  transfers between devices with their start and end apart: 18, of which 4 were waited for; matrix products, arithmetic and copies ran while one was open for 0% of the time, Pallas kernels for 44%

profile of v11, /device:TPU:0, one launch (start us, length us, event | category | flops | bytes accessed | tf_op | source)
XLA Modules:
  0.0 103.2 jit_solution(4915040801282714000)
XLA Ops:
  7.2 0.0 all-gather.2.cloned.1.call-start
  7.2 1.4 %shard_map.130.refs_1_ = bf16[4,8704]{1,0:T(4,128)(2,1)} custom-call(bf16[4,4096]{1,0:T(4,128)(2,1)} %query_ref.1, bf16[4,4096]{1,0:T(4,128)(2,1)} %passage_ref.1, f32[1,1024]{1,0:T(1,128)} %bitcast.9), custom_call_target="tpu_custom_call" | custom-call | flops 16384 | bytes 131072 | tf_op jit(solution)/shard_map/pallas_call | solution.py:118
  8.6 3.9 %collective-permute-start.2 = (bf16[4,8704]{1,0:T(4,128)(2,1)}, bf16[4,8704]{1,0:T(4,128)(2,1)S(1)}, u32[]{:S(2)}, u32[]{:S(2)}) collective-permute-start(bf16[4,8704]{1,0:T(4,128)(2,1)} %shard_map.130.refs_1_), channel_id=1, source_target_pairs={{0,3},{1,2},{2,1},{3,0},{4,7},{5,6},{6,5},{7,4},{8,11},{9,10},{10,... | collective-permute-start | bytes 208904 | tf_op jit(solution)/shard_map/ppermute | solution.py:46
  12.5 0.5 collective-permute-start.1
  13.0 0.1 collective-permute-start
  13.1 1.3 %copy-done.2 = bf16[192,3072]{1,0:T(8,128)(2,1)S(1)} copy-done((bf16[192,3072]{1,0:T(8,128)(2,1)S(1)}, bf16[192,3072]{1,0:T(8,128)(2,1)}, u32[]{:S(2)}) %copy-start.2) | copy-done | bytes 1179672
  14.4 0.0 copy-start.10
  14.4 3.8 %shard_map.129 = bf16[192,1024]{1,0:T(8,128)(2,1)S(1)} custom-call(s32[1]{0:T(128)} %bitcast.1.refs_0_, bf16[192,3072]{1,0:T(8,128)(2,1)S(1)} %copy-done.2, bf16[3072,4096]{1,0:T(8,128)(2,1)} %refs_4_.3), custom_call_target="tpu_custom_call" | custom-call | flops 1207959552 | bytes 7471104 | tf_op jit(solution)/shard_map/pallas_call | solution.py:84
  18.2 0.0 collective-permute-done.2.refs_4_
  18.2 0.0 collective-permute-done.1.refs_3_
  18.3 1.5 %shard_map.131 = (bf16[4,4096]{1,0:T(4,128)(2,1)}, bf16[16,4224]{1,0:T(8,128)(2,1)}) custom-call(s32[1]{0:T(128)} %bitcast.refs_0_, bf16[4,8704]{1,0:T(4,128)(2,1)S(1)} %copy-done.5, bf16[4,8704]{1,0:T(4,128)(2,1)S(1)} %collective-permute-done.refs_2_, bf16[4,8704]{1,0:T(4,128)(2,1)S(1)} %collective-permute-done.1.refs_3_, ...), custom_call_target="tpu_custom_call" | custom-call | flops 8388608 | bytes 524288 | tf_op jit(solution)/shard_map/pallas_call | solution.py:184
  19.8 0.0 all-gather.2.cloned.1.call-update
  19.9 3.0 %collective-permute-start.3 = (bf16[192,1024]{1,0:T(8,128)(2,1)S(1)}, bf16[192,1024]{1,0:T(8,128)(2,1)S(1)}, u32[]{:S(2)}, u32[]{:S(2)}) collective-permute-start(bf16[192,1024]{1,0:T(8,128)(2,1)S(1)} %shard_map.129), channel_id=1, source_target_pairs={{0,3},{1,2},{2,1},{3,0},{4,7},{5,6},{6,5},{7,4},{8,11},{9,10},{10,... | collective-permute-start | bytes 1179656 | tf_op jit(solution)/shard_map/ppermute | solution.py:46
  22.8 3.6 %shard_map.136 = bf16[192,1024]{1,0:T(8,128)(2,1)S(1)} custom-call(s32[1]{0:T(128)} %bitcast.8.refs_0_, bf16[192,3072]{1,0:T(8,128)(2,1)S(1)} %copy-done.3, bf16[3072,4096]{1,0:T(8,128)(2,1)} %refs_4_.3), custom_call_target="tpu_custom_call" | custom-call | flops 1207959552 | bytes 7471104 | tf_op jit(solution)/shard_map/pallas_call | solution.py:84
  26.5 0.0 copy-start.4
  26.5 4.5 %shard_map.135 = bf16[192,1024]{1,0:T(8,128)(2,1)} custom-call(s32[1]{0:T(128)} %bitcast.7.refs_0_, bf16[192,3072]{1,0:T(8,128)(2,1)S(1)} %copy-done.3, bf16[3072,4096]{1,0:T(8,128)(2,1)} %refs_4_.3), custom_call_target="tpu_custom_call" | custom-call | flops 1207959552 | bytes 7471104 | tf_op jit(solution)/shard_map/pallas_call | solution.py:84
  31.0 0.5 collective-permute-start.4
  31.5 0.0 collective-permute-start.5
  31.6 3.6 %shard_map.134.refs_2_ = f32[192,1024]{1,0:T(8,128)S(1)} custom-call(s32[1]{0:T(128)} %bitcast.refs_0_, bf16[192,3072]{1,0:T(8,128)(2,1)S(1)} %copy-done.3, bf16[3072,4096]{1,0:T(8,128)(2,1)} %refs_4_.3, bf16[192,1024]{1,0:T(8,128)(2,1)S(1)} %copy-done.4), custom_call_target="tpu_custom_call" | custom-call | flops 1207959552 | bytes 7471104 | tf_op jit(solution)/shard_map/pallas_call | solution.py:84
  35.2 0.0 collective-permute-done.3.refs_3_
  35.2 5.7 %collective-permute-done.4.refs_4_ = bf16[192,1024]{1,0:T(8,128)(2,1)S(1)} collective-permute-done((bf16[192,1024]{1,0:T(8,128)(2,1)}, bf16[192,1024]{1,0:T(8,128)(2,1)S(1)}, u32[]{:S(2)}, u32[]{:S(2)}) %collective-permute-start.4) | collective-permute-done | bytes 393248 | tf_op jit(solution)/shard_map/ppermute | solution.py:46
  40.9 0.0 collective-permute-done.5.refs_5_
  41.0 1.1 %shard_map.137 = (bf16[36,1024]{1,0:T(8,128)(2,1)S(1)}, bf16[36,1024]{1,0:T(8,128)(2,1)S(1)}, bf16[36,1024]{1,0:T(8,128)(2,1)S(1)}, bf16[36,1024]{1,0:T(8,128)(2...) custom-call(s32[1]{0:T(128)} %bitcast.6.refs_0_.wide_ref, ...), custom_call_target="tpu_custom_call" | custom-call | flops 226492416 | bytes 1966080 | tf_op jit(solution)/shard_map/pallas_call | solution.py:236
  42.0 0.1 collective-permute-start.6
  42.1 1.6 %collective-permute-start.7 = (bf16[36,1024]{1,0:T(8,128)(2,1)S(1)}, bf16[36,1024]{1,0:T(8,128)(2,1)S(1)}, u32[]{:S(2)}, u32[]{:S(2)}) collective-permute-start(bf16[36,1024]{1,0:T(8,128)(2,1)S(1)} %get-tuple-element.58), channel_id=1, source_target_pairs={{0,8},{4,12},{8,0},{12,4},{16,24},{20,28},{24,16},{28,20},{1,9},{5... | collective-permute-start | bytes 221192 | tf_op jit(solution)/shard_map/ppermute | solution.py:46
  43.7 0.2 collective-permute-start.8
  44.0 2.6 %collective-permute-start.9 = (bf16[36,1024]{1,0:T(8,128)(2,1)S(1)}, bf16[36,1024]{1,0:T(8,128)(2,1)S(1)}, u32[]{:S(2)}, u32[]{:S(2)}) collective-permute-start(bf16[36,1024]{1,0:T(8,128)(2,1)S(1)} %get-tuple-element.60), channel_id=1, source_target_pairs={{0,16},{4,20},{8,24},{12,28},{16,0},{20,4},{24,8},{28,12},{1,17},{... | collective-permute-start | bytes 221192 | tf_op jit(solution)/shard_map/ppermute | solution.py:46
  46.6 0.0 collective-permute-start.10
  46.6 3.6 %collective-permute-start.11 = (bf16[36,1024]{1,0:T(8,128)(2,1)S(1)}, bf16[36,1024]{1,0:T(8,128)(2,1)S(1)}, u32[]{:S(2)}, u32[]{:S(2)}) collective-permute-start(bf16[36,1024]{1,0:T(8,128)(2,1)S(1)} %get-tuple-element.62), channel_id=1, source_target_pairs={{0,24},{4,28},{8,16},{12,20},{16,8},{20,12},{24,0},{28,4},{1,25},{... | collective-permute-start | bytes 221192 | tf_op jit(solution)/shard_map/ppermute | solution.py:46
  50.2 0.1 collective-permute-start.12
  50.3 1.2 %copy-done = bf16[128,4224]{1,0:T(8,128)(2,1)S(1)} copy-done((bf16[128,4224]{1,0:T(8,128)(2,1)S(1)}, bf16[128,4224]{1,0:T(8,128)(2,1)}, u32[]{:S(2)}) %copy-start) | copy-done | bytes 1081368
  51.5 6.1 %shard_map.132.refs_2_ = bf16[3072,128]{1,0:T(8,128)(2,1)S(1)} custom-call(bf16[128,4224]{1,0:T(8,128)(2,1)S(1)} %copy-done, bf16[3072,4096]{1,0:T(8,128)(2,1)} %refs_4_.3), custom_call_target="tpu_custom_call" | custom-call | flops 1610612736 | bytes 12582912 | tf_op jit(solution)/shard_map/pallas_call | solution.py:368
  57.6 0.9 shard_map.133
  58.5 0.5 collective-permute-done.10.refs_5_
  59.1 1.3 %shard_map.139.refs_1_.refs_12_ = bf16[288,1024]{1,0:T(8,128)(2,1)S(1)} custom-call(s32[1]{0:T(128)} %bitcast.6.refs_0_.wide_ref, bf16[36,1024]{1,0:T(8,128)(2,1)S(1)} %get-tuple-element.65.refs_0_, bf16[36,1024]{1,0:T(8,128)(2,1)S(1)} %collective-permute-done.6.refs_1_, bf16[36,1024]{1,0:T(8,128)(2,1)S(1)} %collective-permute-done.7.refs_2_, ...), custom_call_target="tpu_custom_call" | custom-call | flops 169869312 | bytes 1179648 | tf_op jit(solution)/shard_map/pallas_call | solution.py:267
  60.4 0.6 collective-permute-start.14
  61.0 1.5 %collective-permute-start.13 = (bf16[288,1024]{1,0:T(8,128)(2,1)S(1)}, bf16[288,1024]{1,0:T(8,128)(2,1)S(1)}, u32[]{:S(2)}, u32[]{:S(2)}) collective-permute-start(bf16[288,1024]{1,0:T(8,128)(2,1)S(1)} %shard_map.139.refs_1_.refs_12_), channel_id=1, source_target_pairs={{0,1},{1,0},{2,3},{3,2},{4,5},{5,4},{6,7},{7,6},{8,9},{9,8},{10,11... | collective-permute-start | bytes 1769480 | tf_op jit(solution)/shard_map/ppermute | solution.py:46
  62.5 0.1 pad_add_fusion.refs_0_
  62.6 0.1 pad_add_fusion.1.refs_0_
  62.6 6.0 %shard_map.138.refs_11_ = bf16[3072,128]{1,0:T(8,128)(2,1)S(1)} custom-call(bf16[128,4224]{1,0:T(8,128)(2,1)S(1)} %copy-done.1, bf16[3072,4096]{1,0:T(8,128)(2,1)} %refs_4_.3, bf16[3072,128]{1,0:T(8,128)(2,1)S(1)} %shard_map.132.refs_2_), custom_call_target="tpu_custom_call", output_to_operand_aliasing={{}: (2, {})} | custom-call | flops 1610612736 | bytes 12582912 | tf_op jit(solution)/shard_map/pallas_call | solution.py:368
  68.6 6.3 %shard_map.140 = (bf16[288,3072]{1,0:T(8,128)(2,1)S(1)}, f32[288,1]{1,0:T(8,128)S(1)}, f32[288,128]{1,0:T(8,128)S(1)}) custom-call(s32[1]{0:T(128)} %bitcast.refs_0_, bf16[288,1024]{1,0:T(8,128)(2,1)S(1)} %shard_map.139.refs_1_.refs_12_, bf16[3072,4096]{1,0:T(8,128)(2,1)} %refs_4_.3, bf16[3072,4096]{1,0:T(8,128)(2,1)} %refs_4_.3, bf16[128,4224]{1,0:T(8,128)(2,1)S(1)} %copy-done.1), custom_call_target="tpu_custom_call" | custom-call | flops 1811939328 | bytes 6291456 | tf_op jit(solution)/shard_map/pallas_call | solution.py:448
  75.0 1.1 %collective-permute-done.14.refs_2_ = bf16[288,1024]{1,0:T(8,128)(2,1)S(1)} collective-permute-done((bf16[288,1024]{1,0:T(8,128)(2,1)S(1)}, bf16[288,1024]{1,0:T(8,128)(2,1)S(1)}, u32[]{:S(2)}, u32[]{:S(2)}) %collective-permute-start.14) | collective-permute-done | bytes 589856 | tf_op jit(solution)/shard_map/ppermute | solution.py:46
  76.1 0.2 collective-permute-done.13.refs_1_
  76.3 0.0 copy-start.6
  76.4 1.6 %collective-permute-start.15 = (bf16[144,1024]{1,0:T(8,128)(2,1)S(1)}, bf16[144,1024]{1,0:T(8,128)(2,1)S(1)}, u32[]{:S(2)}, u32[]{:S(2)}) collective-permute-start(bf16[144,1024]{1,0:T(8,128)(2,1)S(1)} %slice.6), channel_id=1, source_target_pairs={{0,2},{1,3},{2,0},{3,1},{4,6},{5,7},{6,4},{7,5},{8,10},{9,11},{10,... | collective-permute-start | bytes 884744 | tf_op jit(solution)/shard_map/ppermute | solution.py:46
  77.9 1.5 %collective-permute-start.16 = (bf16[144,1024]{1,0:T(8,128)(2,1)S(1)}, bf16[144,1024]{1,0:T(8,128)(2,1)S(1)}, u32[]{:S(2)}, u32[]{:S(2)}) collective-permute-start(bf16[144,1024]{1,0:T(8,128)(2,1)S(1)} %slice.7), channel_id=1, source_target_pairs={{0,1},{1,0},{2,3},{3,2},{4,5},{5,4},{6,7},{7,6},{8,9},{9,8},{10,11... | collective-permute-start | bytes 884744 | tf_op jit(solution)/shard_map/ppermute | solution.py:46
  79.4 9.5 %shard_map.141 = (bf16[288,3072]{1,0:T(8,128)(2,1)S(1)}, f32[288,1]{1,0:T(8,128)S(1)}, f32[288,128]{1,0:T(8,128)S(1)}) custom-call(s32[2]{0:T(128)S(1)} %pad_add_fusion.1.refs_0_, bf16[288,1024]{1,0:T(8,128)(2,1)S(1)} %collective-permute-done.13.refs_1_, bf16[288,1024]{1,0:T(8,128)(2,1)S(1)} %collective-permute-done.14.refs_2_, bf16[3072,4096]{1,0:T(8,128)(2,1)} %refs_4_.3, ...), custom_call_target="tpu_custom_call" | custom-call | flops 3623878656 | bytes 12582912 | tf_op jit(solution)/shard_map/pallas_call | solution.py:448
  88.9 7.5 %shard_map.142 = (bf16[288,3072]{1,0:T(8,128)(2,1)}, bf16[288,1024]{1,0:T(8,128)(2,1)}, bf16[288,1024]{1,0:T(8,128)(2,1)}) custom-call(s32[2]{0:T(128)S(1)} %pad_add_fusion.refs_0_, bf16[144,1024]{1,0:T(8,128)(2,1)S(1)} %collective-permute-done.15.refs_1_, bf16[144,1024]{1,0:T(8,128)(2,1)S(1)} %collective-permute-done.16.refs_2_, ...), custom_call_target="tpu_custom_call" | custom-call | flops 1811939328 | bytes 11599872 | tf_op jit(solution)/shard_map/pallas_call | solution.py:515
  (29 shorter events, 0.1 us)
Async XLA Ops:
  7.2 43.1 %all-gather.2.cloned.1.call-start = ((), (), s32[]{:S(2)}) async-start(), calls=%async_computation | async-start | bytes 1216512 | tf_op jit(solution)/shard_map/all_gather | solution.py:590
  8.6 9.6 %collective-permute-start.2 = (bf16[4,8704]{1,0:T(4,128)(2,1)}, bf16[4,8704]{1,0:T(4,128)(2,1)S(1)}, u32[]{:S(2)}, u32[]{:S(2)}) collective-permute-start(bf16[4,8704]{1,0:T(4,128)(2,1)} %shard_map.130.refs_1_), channel_id=1, source_target_pairs={{0,3},{1,2},{2,1},{3,0},{4,7},{5,6},{6,5},{7,4},{8,11},{9,10},{10,... | collective-permute-start | bytes 208904 | tf_op jit(solution)/shard_map/ppermute | solution.py:46
  12.5 5.7 %collective-permute-start.1 = (bf16[4,8704]{1,0:T(4,128)(2,1)}, bf16[4,8704]{1,0:T(4,128)(2,1)S(1)}, u32[]{:S(2)}, u32[]{:S(2)}) collective-permute-start(bf16[4,8704]{1,0:T(4,128)(2,1)} %shard_map.130.refs_1_), channel_id=1, source_target_pairs={{0,2},{1,3},{2,0},{3,1},{4,6},{5,7},{6,4},{7,5},{8,10},{9,11},{10,... | collective-permute-start | bytes 208904 | tf_op jit(solution)/shard_map/ppermute | solution.py:46
  13.0 5.2 %collective-permute-start = (bf16[4,8704]{1,0:T(4,128)(2,1)}, bf16[4,8704]{1,0:T(4,128)(2,1)S(1)}, u32[]{:S(2)}, u32[]{:S(2)}) collective-permute-start(bf16[4,8704]{1,0:T(4,128)(2,1)} %shard_map.130.refs_1_), channel_id=1, source_target_pairs={{0,1},{1,0},{2,3},{3,2},{4,5},{5,4},{6,7},{7,6},{8,9},{9,8},{10,11... | collective-permute-start | bytes 208904 | tf_op jit(solution)/shard_map/ppermute | solution.py:46
  13.1 1.3 %copy-start.2 = (bf16[192,3072]{1,0:T(8,128)(2,1)S(1)}, bf16[192,3072]{1,0:T(8,128)(2,1)}, u32[]{:S(2)}) copy-start(bf16[192,3072]{1,0:T(8,128)(2,1)} %refs_1_.7) | copy-start | bytes 3538948
  14.4 3.9 %copy-start.5 = (bf16[4,8704]{1,0:T(4,128)(2,1)S(1)}, bf16[4,8704]{1,0:T(4,128)(2,1)}, u32[]{:S(2)}) copy-start(bf16[4,8704]{1,0:T(4,128)(2,1)} %shard_map.130.refs_1_) | copy-start | bytes 208900
  14.4 3.9 %copy-start.7 = (s32[192,1]{0,1:T(1,128)S(1)}, s32[192,1]{0,1:T(1,128)}, u32[]{:S(2)}) copy-start(s32[192,1]{0,1:T(1,128)} %param.15) | copy-start | bytes 2308
  14.4 3.9 %copy-start.8 = (f32[16]{0:T(128)S(1)}, f32[16]{0:T(128)}, u32[]{:S(2)}) copy-start(f32[16]{0:T(128)} %param.12) | copy-start | bytes 196
  14.4 3.9 %copy-start.9 = (s32[16]{0:T(128)S(1)}, s32[16]{0:T(128)}, u32[]{:S(2)}) copy-start(s32[16]{0:T(128)} %param.13) | copy-start | bytes 196
  14.4 3.9 %copy-start.10 = (s32[1,16]{1,0:T(1,128)S(1)}, s32[1,16]{1,0:T(1,128)}, u32[]{:S(2)}) copy-start(s32[1,16]{1,0:T(1,128)} %refs_8_.1) | copy-start | bytes 196
  14.4 8.4 %copy-start.3 = (bf16[192,3072]{1,0:T(8,128)(2,1)S(1)}, bf16[192,3072]{1,0:T(8,128)(2,1)}, u32[]{:S(2)}) copy-start(bf16[192,3072]{1,0:T(8,128)(2,1)} %refs_1_.7) | copy-start | bytes 3538948
  19.9 15.4 %collective-permute-start.3 = (bf16[192,1024]{1,0:T(8,128)(2,1)S(1)}, bf16[192,1024]{1,0:T(8,128)(2,1)S(1)}, u32[]{:S(2)}, u32[]{:S(2)}) collective-permute-start(bf16[192,1024]{1,0:T(8,128)(2,1)S(1)} %shard_map.129), channel_id=1, source_target_pairs={{0,3},{1,2},{2,1},{3,0},{4,7},{5,6},{6,5},{7,4},{8,11},{9,10},{10,... | collective-permute-start | bytes 1179656 | tf_op jit(solution)/shard_map/ppermute | solution.py:46
  26.5 5.1 %copy-start.4 = (bf16[192,1024]{1,0:T(8,128)(2,1)S(1)}, bf16[192,1024]{1,0:T(8,128)(2,1)}, u32[]{:S(2)}) copy-start(bf16[192,1024]{1,0:T(8,128)(2,1)} %refs_3_.4) | copy-start | bytes 1179652
  31.0 9.9 %collective-permute-start.4 = (bf16[192,1024]{1,0:T(8,128)(2,1)}, bf16[192,1024]{1,0:T(8,128)(2,1)S(1)}, u32[]{:S(2)}, u32[]{:S(2)}) collective-permute-start(bf16[192,1024]{1,0:T(8,128)(2,1)} %shard_map.135), channel_id=1, source_target_pairs={{0,1},{1,0},{2,3},{3,2},{4,5},{5,4},{6,7},{7,6},{8,9},{9,8},{10,11... | collective-permute-start | bytes 1179656 | tf_op jit(solution)/shard_map/ppermute | solution.py:46
  31.5 9.4 %collective-permute-start.5 = (bf16[192,1024]{1,0:T(8,128)(2,1)S(1)}, bf16[192,1024]{1,0:T(8,128)(2,1)S(1)}, u32[]{:S(2)}, u32[]{:S(2)}) collective-permute-start(bf16[192,1024]{1,0:T(8,128)(2,1)S(1)} %shard_map.136), channel_id=1, source_target_pairs={{0,2},{1,3},{2,0},{3,1},{4,6},{5,7},{6,4},{7,5},{8,10},{9,11},{10,... | collective-permute-start | bytes 1179656 | tf_op jit(solution)/shard_map/ppermute | solution.py:46
  42.0 4.6 %collective-permute-start.6 = (bf16[36,1024]{1,0:T(8,128)(2,1)S(1)}, bf16[36,1024]{1,0:T(8,128)(2,1)S(1)}, u32[]{:S(2)}, u32[]{:S(2)}) collective-permute-start(bf16[36,1024]{1,0:T(8,128)(2,1)S(1)} %get-tuple-element.57), channel_id=1, source_target_pairs={{0,4},{4,0},{8,12},{12,8},{16,20},{20,16},{24,28},{28,24},{1,5},{5... | collective-permute-start | bytes 221192 | tf_op jit(solution)/shard_map/ppermute | solution.py:46
  42.1 8.1 %collective-permute-start.7 = (bf16[36,1024]{1,0:T(8,128)(2,1)S(1)}, bf16[36,1024]{1,0:T(8,128)(2,1)S(1)}, u32[]{:S(2)}, u32[]{:S(2)}) collective-permute-start(bf16[36,1024]{1,0:T(8,128)(2,1)S(1)} %get-tuple-element.58), channel_id=1, source_target_pairs={{0,8},{4,12},{8,0},{12,4},{16,24},{20,28},{24,16},{28,20},{1,9},{5... | collective-permute-start | bytes 221192 | tf_op jit(solution)/shard_map/ppermute | solution.py:46
  43.7 14.8 %collective-permute-start.8 = (bf16[36,1024]{1,0:T(8,128)(2,1)S(1)}, bf16[36,1024]{1,0:T(8,128)(2,1)S(1)}, u32[]{:S(2)}, u32[]{:S(2)}) collective-permute-start(bf16[36,1024]{1,0:T(8,128)(2,1)S(1)} %get-tuple-element.59), channel_id=1, source_target_pairs={{0,12},{4,8},{8,4},{12,0},{16,28},{20,24},{24,20},{28,16},{1,13},{... | collective-permute-start | bytes 221192 | tf_op jit(solution)/shard_map/ppermute | solution.py:46
  44.0 14.6 %collective-permute-start.9 = (bf16[36,1024]{1,0:T(8,128)(2,1)S(1)}, bf16[36,1024]{1,0:T(8,128)(2,1)S(1)}, u32[]{:S(2)}, u32[]{:S(2)}) collective-permute-start(bf16[36,1024]{1,0:T(8,128)(2,1)S(1)} %get-tuple-element.60), channel_id=1, source_target_pairs={{0,16},{4,20},{8,24},{12,28},{16,0},{20,4},{24,8},{28,12},{1,17},{... | collective-permute-start | bytes 221192 | tf_op jit(solution)/shard_map/ppermute | solution.py:46
  46.6 12.5 %collective-permute-start.10 = (bf16[36,1024]{1,0:T(8,128)(2,1)S(1)}, bf16[36,1024]{1,0:T(8,128)(2,1)S(1)}, u32[]{:S(2)}, u32[]{:S(2)}) collective-permute-start(bf16[36,1024]{1,0:T(8,128)(2,1)S(1)} %get-tuple-element.61), channel_id=1, source_target_pairs={{0,20},{4,16},{8,28},{12,24},{16,4},{20,0},{24,12},{28,8},{1,21},{... | collective-permute-start | bytes 221192 | tf_op jit(solution)/shard_map/ppermute | solution.py:46
  46.6 12.5 %collective-permute-start.11 = (bf16[36,1024]{1,0:T(8,128)(2,1)S(1)}, bf16[36,1024]{1,0:T(8,128)(2,1)S(1)}, u32[]{:S(2)}, u32[]{:S(2)}) collective-permute-start(bf16[36,1024]{1,0:T(8,128)(2,1)S(1)} %get-tuple-element.62), channel_id=1, source_target_pairs={{0,24},{4,28},{8,16},{12,20},{16,8},{20,12},{24,0},{28,4},{1,25},{... | collective-permute-start | bytes 221192 | tf_op jit(solution)/shard_map/ppermute | solution.py:46
  50.2 8.9 %collective-permute-start.12 = (bf16[36,1024]{1,0:T(8,128)(2,1)S(1)}, bf16[36,1024]{1,0:T(8,128)(2,1)S(1)}, u32[]{:S(2)}, u32[]{:S(2)}) collective-permute-start(bf16[36,1024]{1,0:T(8,128)(2,1)S(1)} %get-tuple-element.63), channel_id=1, source_target_pairs={{0,28},{4,24},{8,20},{12,16},{16,12},{20,8},{24,4},{28,0},{1,29},{... | collective-permute-start | bytes 221192 | tf_op jit(solution)/shard_map/ppermute | solution.py:46
  50.3 1.2 %copy-start = (bf16[128,4224]{1,0:T(8,128)(2,1)S(1)}, bf16[128,4224]{1,0:T(8,128)(2,1)}, u32[]{:S(2)}) copy-start(bf16[128,4224]{1,0:T(8,128)(2,1)} %all-gather.2.cloned.1.call-done.refs_0_.refs_1_.refs_4_.refs_7_.refs_8_.refs_5_.refs_13_) | copy-start | bytes 3244036
  51.5 6.1 %copy-start.1 = (bf16[128,4224]{1,0:T(8,128)(2,1)S(1)}, bf16[128,4224]{1,0:T(8,128)(2,1)}, u32[]{:S(2)}) copy-start(bf16[128,4224]{1,0:T(8,128)(2,1)} %all-gather.2.cloned.1.call-done.refs_0_.refs_1_.refs_4_.refs_7_.refs_8_.refs_5_.refs_13_) | copy-start | bytes 3244036
  60.4 15.6 %collective-permute-start.14 = (bf16[288,1024]{1,0:T(8,128)(2,1)S(1)}, bf16[288,1024]{1,0:T(8,128)(2,1)S(1)}, u32[]{:S(2)}, u32[]{:S(2)}) collective-permute-start(bf16[288,1024]{1,0:T(8,128)(2,1)S(1)} %shard_map.139.refs_1_.refs_12_), channel_id=1, source_target_pairs={{0,2},{1,3},{2,0},{3,1},{4,6},{5,7},{6,4},{7,5},{8,10},{9,11},{10,... | collective-permute-start | bytes 1769480 | tf_op jit(solution)/shard_map/ppermute | solution.py:46
  61.0 15.3 %collective-permute-start.13 = (bf16[288,1024]{1,0:T(8,128)(2,1)S(1)}, bf16[288,1024]{1,0:T(8,128)(2,1)S(1)}, u32[]{:S(2)}, u32[]{:S(2)}) collective-permute-start(bf16[288,1024]{1,0:T(8,128)(2,1)S(1)} %shard_map.139.refs_1_.refs_12_), channel_id=1, source_target_pairs={{0,1},{1,0},{2,3},{3,2},{4,5},{5,4},{6,7},{7,6},{8,9},{9,8},{10,11... | collective-permute-start | bytes 1769480 | tf_op jit(solution)/shard_map/ppermute | solution.py:46
  76.3 12.6 %copy-start.6 = (f32[1024]{0:T(1024)S(1)}, f32[1024]{0:T(1024)}, u32[]{:S(2)}) copy-start(f32[1024]{0:T(1024)} %param.19) | copy-start | bytes 12292
  76.4 12.6 %collective-permute-start.15 = (bf16[144,1024]{1,0:T(8,128)(2,1)S(1)}, bf16[144,1024]{1,0:T(8,128)(2,1)S(1)}, u32[]{:S(2)}, u32[]{:S(2)}) collective-permute-start(bf16[144,1024]{1,0:T(8,128)(2,1)S(1)} %slice.6), channel_id=1, source_target_pairs={{0,2},{1,3},{2,0},{3,1},{4,6},{5,7},{6,4},{7,5},{8,10},{9,11},{10,... | collective-permute-start | bytes 884744 | tf_op jit(solution)/shard_map/ppermute | solution.py:46
  77.9 11.0 %collective-permute-start.16 = (bf16[144,1024]{1,0:T(8,128)(2,1)S(1)}, bf16[144,1024]{1,0:T(8,128)(2,1)S(1)}, u32[]{:S(2)}, u32[]{:S(2)}) collective-permute-start(bf16[144,1024]{1,0:T(8,128)(2,1)S(1)} %slice.7), channel_id=1, source_target_pairs={{0,1},{1,0},{2,3},{3,2},{4,5},{5,4},{6,7},{7,6},{8,9},{9,8},{10,11... | collective-permute-start | bytes 884744 | tf_op jit(solution)/shard_map/ppermute | solution.py:46
Sparse Core Ops, SparseCore 0:
  20.0 23.9 all-gather.1

commit v12 on v11

--- a/solution.py
+++ b/solution.py
@@ -443,7 +443,7 @@
     rows, width = pieces[0].shape
     depth = w_down.shape[0]
     pairs = low.shape[0]
-    tile = tile_of(depth, 512)
+    tile = tile_of(depth, 1024)
     totals = carried_specs(rows, pairs, tile)
     return pl.pallas_call(
         lambda *refs: back_body(count, len(before), *refs),

time: 105 us -> 104 us (level)
  Pallas kernels: 57.2 us -> 55 us
  waiting for transfers between devices: 7.62 us -> 8.74 us
    pallas_call x2, Pallas kernels: 15.8 us -> 13.7 us  [back(): pl.pallas_call(lambda *refs: back_body(count, len(before), *refs), grid_s...]
    ppermute x17, waiting for transfers between devices: 7.6 us -> 8.72 us  [swap(): lax.ppermute(rows, axis, [(i, i ^ k) for i in range(lax.axis_size(axis))])]
  transfers between devices with their start and end apart: 18 -> 18, of which waited for: 4 -> 4; matrix products, arithmetic and copies ran while one was open for 0% -> 0% of each run, Pallas kernels for 44% -> 42%
where the time goes in v12:
time: 104 us; the launch traced here: 102 us
  Pallas kernels  55 us (53%)
  starting transfers between devices  21.4 us (21%)
  between operations  14.3 us (14%)
  waiting for transfers between devices  8.74 us (8%)
  local copies, waits for them, and re-layouts  2.59 us (2%)
    ppermute x17, starting transfers between devices, swap(): lax.ppermute(rows, axis, [(i, i ^ k) for i in range(lax.axis_size(axis))])  21.4 us
    pallas_call x4, Pallas kernels, project(): pl.pallas_call(lambda *refs: project_body(len(own), *refs), in_specs=[pl....  15.6 us
    pallas_call x2, Pallas kernels, back(): pl.pallas_call(lambda *refs: back_body(count, len(before), *refs), grid_s...  13.7 us
    pallas_call x2, Pallas kernels, low_activations(): pl.pallas_call(lambda *refs: low_act_body(part, *refs), grid=(1,), in_spe...  12.1 us
    ppermute x17, waiting for transfers between devices, swap(): lax.ppermute(rows, axis, [(i, i ^ k) for i in range(lax.axis_size(axis))])  8.72 us
    pallas_call x1, Pallas kernels, finish(): pl.pallas_call(lambda *refs: finish_body(features, count, *refs), grid_sp...  7.45 us
    unnamed x22, local copies, waits for them, and re-layouts  2.55 us
  transfers between devices with their start and end apart: 18, of which 4 were waited for; matrix products, arithmetic and copies ran while one was open for 0% of the time, Pallas kernels for 42%

profile of v12, /device:TPU:0, one launch (start us, length us, event | category | flops | bytes accessed | tf_op | source)
XLA Modules:
  0.0 102.2 jit_solution(5968929366359665205)
XLA Ops:
  7.2 0.0 all-gather.2.cloned.1.call-start
  7.2 1.4 %shard_map.130.refs_1_ = bf16[4,8704]{1,0:T(4,128)(2,1)} custom-call(bf16[4,4096]{1,0:T(4,128)(2,1)} %query_ref.1, bf16[4,4096]{1,0:T(4,128)(2,1)} %passage_ref.1, f32[1,1024]{1,0:T(1,128)} %bitcast.9), custom_call_target="tpu_custom_call" | custom-call | flops 16384 | bytes 131072 | tf_op jit(solution)/shard_map/pallas_call | solution.py:118
  8.6 3.9 %collective-permute-start.2 = (bf16[4,8704]{1,0:T(4,128)(2,1)}, bf16[4,8704]{1,0:T(4,128)(2,1)S(1)}, u32[]{:S(2)}, u32[]{:S(2)}) collective-permute-start(bf16[4,8704]{1,0:T(4,128)(2,1)} %shard_map.130.refs_1_), channel_id=1, source_target_pairs={{0,3},{1,2},{2,1},{3,0},{4,7},{5,6},{6,5},{7,4},{8,11},{9,10},{10,... | collective-permute-start | bytes 208904 | tf_op jit(solution)/shard_map/ppermute | solution.py:46
  12.5 0.5 collective-permute-start.1
  13.0 0.1 collective-permute-start
  13.1 1.3 %copy-done.2 = bf16[192,3072]{1,0:T(8,128)(2,1)S(1)} copy-done((bf16[192,3072]{1,0:T(8,128)(2,1)S(1)}, bf16[192,3072]{1,0:T(8,128)(2,1)}, u32[]{:S(2)}) %copy-start.2) | copy-done | bytes 1179672
  14.4 0.0 copy-start.10
  14.4 3.8 %shard_map.129 = bf16[192,1024]{1,0:T(8,128)(2,1)S(1)} custom-call(s32[1]{0:T(128)} %bitcast.1.refs_0_, bf16[192,3072]{1,0:T(8,128)(2,1)S(1)} %copy-done.2, bf16[3072,4096]{1,0:T(8,128)(2,1)} %refs_4_.3), custom_call_target="tpu_custom_call" | custom-call | flops 1207959552 | bytes 7471104 | tf_op jit(solution)/shard_map/pallas_call | solution.py:84
  18.2 0.0 collective-permute-done.2.refs_4_
  18.2 0.0 collective-permute-done.1.refs_3_
  18.3 1.5 %shard_map.131 = (bf16[4,4096]{1,0:T(4,128)(2,1)}, bf16[16,4224]{1,0:T(8,128)(2,1)}) custom-call(s32[1]{0:T(128)} %bitcast.refs_0_, bf16[4,8704]{1,0:T(4,128)(2,1)S(1)} %copy-done.5, bf16[4,8704]{1,0:T(4,128)(2,1)S(1)} %collective-permute-done.refs_2_, bf16[4,8704]{1,0:T(4,128)(2,1)S(1)} %collective-permute-done.1.refs_3_, ...), custom_call_target="tpu_custom_call" | custom-call | flops 8388608 | bytes 524288 | tf_op jit(solution)/shard_map/pallas_call | solution.py:184
  19.8 0.0 all-gather.2.cloned.1.call-update
  19.9 3.0 %collective-permute-start.3 = (bf16[192,1024]{1,0:T(8,128)(2,1)S(1)}, bf16[192,1024]{1,0:T(8,128)(2,1)S(1)}, u32[]{:S(2)}, u32[]{:S(2)}) collective-permute-start(bf16[192,1024]{1,0:T(8,128)(2,1)S(1)} %shard_map.129), channel_id=1, source_target_pairs={{0,3},{1,2},{2,1},{3,0},{4,7},{5,6},{6,5},{7,4},{8,11},{9,10},{10,... | collective-permute-start | bytes 1179656 | tf_op jit(solution)/shard_map/ppermute | solution.py:46
  22.8 3.6 %shard_map.136 = bf16[192,1024]{1,0:T(8,128)(2,1)S(1)} custom-call(s32[1]{0:T(128)} %bitcast.8.refs_0_, bf16[192,3072]{1,0:T(8,128)(2,1)S(1)} %copy-done.3, bf16[3072,4096]{1,0:T(8,128)(2,1)} %refs_4_.3), custom_call_target="tpu_custom_call" | custom-call | flops 1207959552 | bytes 7471104 | tf_op jit(solution)/shard_map/pallas_call | solution.py:84
  26.5 0.0 copy-start.4
  26.5 4.5 %shard_map.135 = bf16[192,1024]{1,0:T(8,128)(2,1)} custom-call(s32[1]{0:T(128)} %bitcast.7.refs_0_, bf16[192,3072]{1,0:T(8,128)(2,1)S(1)} %copy-done.3, bf16[3072,4096]{1,0:T(8,128)(2,1)} %refs_4_.3), custom_call_target="tpu_custom_call" | custom-call | flops 1207959552 | bytes 7471104 | tf_op jit(solution)/shard_map/pallas_call | solution.py:84
  31.0 0.5 collective-permute-start.4
  31.5 0.0 collective-permute-start.5
  31.6 3.6 %shard_map.134.refs_2_ = f32[192,1024]{1,0:T(8,128)S(1)} custom-call(s32[1]{0:T(128)} %bitcast.refs_0_, bf16[192,3072]{1,0:T(8,128)(2,1)S(1)} %copy-done.3, bf16[3072,4096]{1,0:T(8,128)(2,1)} %refs_4_.3, bf16[192,1024]{1,0:T(8,128)(2,1)S(1)} %copy-done.4), custom_call_target="tpu_custom_call" | custom-call | flops 1207959552 | bytes 7471104 | tf_op jit(solution)/shard_map/pallas_call | solution.py:84
  35.2 0.0 collective-permute-done.3.refs_3_
  35.2 5.7 %collective-permute-done.4.refs_4_ = bf16[192,1024]{1,0:T(8,128)(2,1)S(1)} collective-permute-done((bf16[192,1024]{1,0:T(8,128)(2,1)}, bf16[192,1024]{1,0:T(8,128)(2,1)S(1)}, u32[]{:S(2)}, u32[]{:S(2)}) %collective-permute-start.4) | collective-permute-done | bytes 393248 | tf_op jit(solution)/shard_map/ppermute | solution.py:46
  40.9 0.0 collective-permute-done.5.refs_5_
  41.0 1.1 %shard_map.137 = (bf16[36,1024]{1,0:T(8,128)(2,1)S(1)}, bf16[36,1024]{1,0:T(8,128)(2,1)S(1)}, bf16[36,1024]{1,0:T(8,128)(2,1)S(1)}, bf16[36,1024]{1,0:T(8,128)(2...) custom-call(s32[1]{0:T(128)} %bitcast.6.refs_0_.wide_ref, ...), custom_call_target="tpu_custom_call" | custom-call | flops 226492416 | bytes 1966080 | tf_op jit(solution)/shard_map/pallas_call | solution.py:236
  42.0 0.1 collective-permute-start.6
  42.1 1.6 %collective-permute-start.7 = (bf16[36,1024]{1,0:T(8,128)(2,1)S(1)}, bf16[36,1024]{1,0:T(8,128)(2,1)S(1)}, u32[]{:S(2)}, u32[]{:S(2)}) collective-permute-start(bf16[36,1024]{1,0:T(8,128)(2,1)S(1)} %get-tuple-element.58), channel_id=1, source_target_pairs={{0,8},{4,12},{8,0},{12,4},{16,24},{20,28},{24,16},{28,20},{1,9},{5... | collective-permute-start | bytes 221192 | tf_op jit(solution)/shard_map/ppermute | solution.py:46
  43.7 0.2 collective-permute-start.8
  44.0 2.6 %collective-permute-start.9 = (bf16[36,1024]{1,0:T(8,128)(2,1)S(1)}, bf16[36,1024]{1,0:T(8,128)(2,1)S(1)}, u32[]{:S(2)}, u32[]{:S(2)}) collective-permute-start(bf16[36,1024]{1,0:T(8,128)(2,1)S(1)} %get-tuple-element.60), channel_id=1, source_target_pairs={{0,16},{4,20},{8,24},{12,28},{16,0},{20,4},{24,8},{28,12},{1,17},{... | collective-permute-start | bytes 221192 | tf_op jit(solution)/shard_map/ppermute | solution.py:46
  46.6 0.0 collective-permute-start.10
  46.6 3.6 %collective-permute-start.11 = (bf16[36,1024]{1,0:T(8,128)(2,1)S(1)}, bf16[36,1024]{1,0:T(8,128)(2,1)S(1)}, u32[]{:S(2)}, u32[]{:S(2)}) collective-permute-start(bf16[36,1024]{1,0:T(8,128)(2,1)S(1)} %get-tuple-element.62), channel_id=1, source_target_pairs={{0,24},{4,28},{8,16},{12,20},{16,8},{20,12},{24,0},{28,4},{1,25},{... | collective-permute-start | bytes 221192 | tf_op jit(solution)/shard_map/ppermute | solution.py:46
  50.2 0.1 collective-permute-start.12
  50.3 1.2 %copy-done = bf16[128,4224]{1,0:T(8,128)(2,1)S(1)} copy-done((bf16[128,4224]{1,0:T(8,128)(2,1)S(1)}, bf16[128,4224]{1,0:T(8,128)(2,1)}, u32[]{:S(2)}) %copy-start) | copy-done | bytes 1081368
  51.5 6.1 %shard_map.132.refs_2_ = bf16[3072,128]{1,0:T(8,128)(2,1)S(1)} custom-call(bf16[128,4224]{1,0:T(8,128)(2,1)S(1)} %copy-done, bf16[3072,4096]{1,0:T(8,128)(2,1)} %refs_4_.3), custom_call_target="tpu_custom_call" | custom-call | flops 1610612736 | bytes 12582912 | tf_op jit(solution)/shard_map/pallas_call | solution.py:368
  57.6 0.9 shard_map.133
  58.5 0.5 collective-permute-done.10.refs_5_
  59.1 1.3 %shard_map.139.refs_1_.refs_12_ = bf16[288,1024]{1,0:T(8,128)(2,1)S(1)} custom-call(s32[1]{0:T(128)} %bitcast.6.refs_0_.wide_ref, bf16[36,1024]{1,0:T(8,128)(2,1)S(1)} %get-tuple-element.65.refs_0_, bf16[36,1024]{1,0:T(8,128)(2,1)S(1)} %collective-permute-done.6.refs_1_, bf16[36,1024]{1,0:T(8,128)(2,1)S(1)} %collective-permute-done.7.refs_2_, ...), custom_call_target="tpu_custom_call" | custom-call | flops 169869312 | bytes 1179648 | tf_op jit(solution)/shard_map/pallas_call | solution.py:267
  60.4 0.6 collective-permute-start.14
  61.0 1.5 %collective-permute-start.13 = (bf16[288,1024]{1,0:T(8,128)(2,1)S(1)}, bf16[288,1024]{1,0:T(8,128)(2,1)S(1)}, u32[]{:S(2)}, u32[]{:S(2)}) collective-permute-start(bf16[288,1024]{1,0:T(8,128)(2,1)S(1)} %shard_map.139.refs_1_.refs_12_), channel_id=1, source_target_pairs={{0,1},{1,0},{2,3},{3,2},{4,5},{5,4},{6,7},{7,6},{8,9},{9,8},{10,11... | collective-permute-start | bytes 1769480 | tf_op jit(solution)/shard_map/ppermute | solution.py:46
  62.5 0.1 pad_add_fusion.refs_0_
  62.6 0.1 pad_add_fusion.1.refs_0_
  62.6 6.0 %shard_map.138.refs_11_ = bf16[3072,128]{1,0:T(8,128)(2,1)S(1)} custom-call(bf16[128,4224]{1,0:T(8,128)(2,1)S(1)} %copy-done.1, bf16[3072,4096]{1,0:T(8,128)(2,1)} %refs_4_.3, bf16[3072,128]{1,0:T(8,128)(2,1)S(1)} %shard_map.132.refs_2_), custom_call_target="tpu_custom_call", output_to_operand_aliasing={{}: (2, {})} | custom-call | flops 1610612736 | bytes 12582912 | tf_op jit(solution)/shard_map/pallas_call | solution.py:368
  68.6 5.2 %shard_map.140 = (bf16[288,3072]{1,0:T(8,128)(2,1)S(1)}, f32[288,1]{1,0:T(8,128)S(1)}, f32[288,128]{1,0:T(8,128)S(1)}) custom-call(s32[1]{0:T(128)} %bitcast.refs_0_, bf16[288,1024]{1,0:T(8,128)(2,1)S(1)} %shard_map.139.refs_1_.refs_12_, bf16[3072,4096]{1,0:T(8,128)(2,1)} %refs_4_.3, bf16[3072,4096]{1,0:T(8,128)(2,1)} %refs_4_.3, bf16[128,4224]{1,0:T(8,128)(2,1)S(1)} %copy-done.1), custom_call_target="tpu_custom_call" | custom-call | flops 1811939328 | bytes 6291456 | tf_op jit(solution)/shard_map/pallas_call | solution.py:448
  73.8 2.2 %collective-permute-done.14.refs_2_ = bf16[288,1024]{1,0:T(8,128)(2,1)S(1)} collective-permute-done((bf16[288,1024]{1,0:T(8,128)(2,1)S(1)}, bf16[288,1024]{1,0:T(8,128)(2,1)S(1)}, u32[]{:S(2)}, u32[]{:S(2)}) %collective-permute-start.14) | collective-permute-done | bytes 589856 | tf_op jit(solution)/shard_map/ppermute | solution.py:46
  76.1 0.2 collective-permute-done.13.refs_1_
  76.3 0.0 copy-start.6
  76.4 1.6 %collective-permute-start.15 = (bf16[144,1024]{1,0:T(8,128)(2,1)S(1)}, bf16[144,1024]{1,0:T(8,128)(2,1)S(1)}, u32[]{:S(2)}, u32[]{:S(2)}) collective-permute-start(bf16[144,1024]{1,0:T(8,128)(2,1)S(1)} %slice.6), channel_id=1, source_target_pairs={{0,2},{1,3},{2,0},{3,1},{4,6},{5,7},{6,4},{7,5},{8,10},{9,11},{10,... | collective-permute-start | bytes 884744 | tf_op jit(solution)/shard_map/ppermute | solution.py:46
  77.9 1.5 %collective-permute-start.16 = (bf16[144,1024]{1,0:T(8,128)(2,1)S(1)}, bf16[144,1024]{1,0:T(8,128)(2,1)S(1)}, u32[]{:S(2)}, u32[]{:S(2)}) collective-permute-start(bf16[144,1024]{1,0:T(8,128)(2,1)S(1)} %slice.7), channel_id=1, source_target_pairs={{0,1},{1,0},{2,3},{3,2},{4,5},{5,4},{6,7},{7,6},{8,9},{9,8},{10,11... | collective-permute-start | bytes 884744 | tf_op jit(solution)/shard_map/ppermute | solution.py:46
  79.4 8.5 %shard_map.141 = (bf16[288,3072]{1,0:T(8,128)(2,1)S(1)}, f32[288,1]{1,0:T(8,128)S(1)}, f32[288,128]{1,0:T(8,128)S(1)}) custom-call(s32[2]{0:T(128)S(1)} %pad_add_fusion.1.refs_0_, bf16[288,1024]{1,0:T(8,128)(2,1)S(1)} %collective-permute-done.13.refs_1_, bf16[288,1024]{1,0:T(8,128)(2,1)S(1)} %collective-permute-done.14.refs_2_, bf16[3072,4096]{1,0:T(8,128)(2,1)} %refs_4_.3, ...), custom_call_target="tpu_custom_call" | custom-call | flops 3623878656 | bytes 12582912 | tf_op jit(solution)/shard_map/pallas_call | solution.py:448
  87.9 7.5 %shard_map.142 = (bf16[288,3072]{1,0:T(8,128)(2,1)}, bf16[288,1024]{1,0:T(8,128)(2,1)}, bf16[288,1024]{1,0:T(8,128)(2,1)}) custom-call(s32[2]{0:T(128)S(1)} %pad_add_fusion.refs_0_, bf16[144,1024]{1,0:T(8,128)(2,1)S(1)} %collective-permute-done.15.refs_1_, bf16[144,1024]{1,0:T(8,128)(2,1)S(1)} %collective-permute-done.16.refs_2_, ...), custom_call_target="tpu_custom_call" | custom-call | flops 1811939328 | bytes 11599872 | tf_op jit(solution)/shard_map/pallas_call | solution.py:515
  (29 shorter events, 0.1 us)
Async XLA Ops:
  7.2 43.1 %all-gather.2.cloned.1.call-start = ((), (), s32[]{:S(2)}) async-start(), calls=%async_computation | async-start | bytes 1216512 | tf_op jit(solution)/shard_map/all_gather | solution.py:590
  8.6 9.6 %collective-permute-start.2 = (bf16[4,8704]{1,0:T(4,128)(2,1)}, bf16[4,8704]{1,0:T(4,128)(2,1)S(1)}, u32[]{:S(2)}, u32[]{:S(2)}) collective-permute-start(bf16[4,8704]{1,0:T(4,128)(2,1)} %shard_map.130.refs_1_), channel_id=1, source_target_pairs={{0,3},{1,2},{2,1},{3,0},{4,7},{5,6},{6,5},{7,4},{8,11},{9,10},{10,... | collective-permute-start | bytes 208904 | tf_op jit(solution)/shard_map/ppermute | solution.py:46
  12.5 5.7 %collective-permute-start.1 = (bf16[4,8704]{1,0:T(4,128)(2,1)}, bf16[4,8704]{1,0:T(4,128)(2,1)S(1)}, u32[]{:S(2)}, u32[]{:S(2)}) collective-permute-start(bf16[4,8704]{1,0:T(4,128)(2,1)} %shard_map.130.refs_1_), channel_id=1, source_target_pairs={{0,2},{1,3},{2,0},{3,1},{4,6},{5,7},{6,4},{7,5},{8,10},{9,11},{10,... | collective-permute-start | bytes 208904 | tf_op jit(solution)/shard_map/ppermute | solution.py:46
  13.0 5.2 %collective-permute-start = (bf16[4,8704]{1,0:T(4,128)(2,1)}, bf16[4,8704]{1,0:T(4,128)(2,1)S(1)}, u32[]{:S(2)}, u32[]{:S(2)}) collective-permute-start(bf16[4,8704]{1,0:T(4,128)(2,1)} %shard_map.130.refs_1_), channel_id=1, source_target_pairs={{0,1},{1,0},{2,3},{3,2},{4,5},{5,4},{6,7},{7,6},{8,9},{9,8},{10,11... | collective-permute-start | bytes 208904 | tf_op jit(solution)/shard_map/ppermute | solution.py:46
  13.1 1.3 %copy-start.2 = (bf16[192,3072]{1,0:T(8,128)(2,1)S(1)}, bf16[192,3072]{1,0:T(8,128)(2,1)}, u32[]{:S(2)}) copy-start(bf16[192,3072]{1,0:T(8,128)(2,1)} %refs_1_.7) | copy-start | bytes 3538948
  14.4 3.9 %copy-start.5 = (bf16[4,8704]{1,0:T(4,128)(2,1)S(1)}, bf16[4,8704]{1,0:T(4,128)(2,1)}, u32[]{:S(2)}) copy-start(bf16[4,8704]{1,0:T(4,128)(2,1)} %shard_map.130.refs_1_) | copy-start | bytes 208900
  14.4 3.9 %copy-start.7 = (s32[192,1]{0,1:T(1,128)S(1)}, s32[192,1]{0,1:T(1,128)}, u32[]{:S(2)}) copy-start(s32[192,1]{0,1:T(1,128)} %param.15) | copy-start | bytes 2308
  14.4 3.9 %copy-start.8 = (f32[16]{0:T(128)S(1)}, f32[16]{0:T(128)}, u32[]{:S(2)}) copy-start(f32[16]{0:T(128)} %param.12) | copy-start | bytes 196
  14.4 3.9 %copy-start.9 = (s32[16]{0:T(128)S(1)}, s32[16]{0:T(128)}, u32[]{:S(2)}) copy-start(s32[16]{0:T(128)} %param.13) | copy-start | bytes 196
  14.4 3.9 %copy-start.10 = (s32[1,16]{1,0:T(1,128)S(1)}, s32[1,16]{1,0:T(1,128)}, u32[]{:S(2)}) copy-start(s32[1,16]{1,0:T(1,128)} %refs_8_.1) | copy-start | bytes 196
  14.4 8.4 %copy-start.3 = (bf16[192,3072]{1,0:T(8,128)(2,1)S(1)}, bf16[192,3072]{1,0:T(8,128)(2,1)}, u32[]{:S(2)}) copy-start(bf16[192,3072]{1,0:T(8,128)(2,1)} %refs_1_.7) | copy-start | bytes 3538948
  19.9 15.4 %collective-permute-start.3 = (bf16[192,1024]{1,0:T(8,128)(2,1)S(1)}, bf16[192,1024]{1,0:T(8,128)(2,1)S(1)}, u32[]{:S(2)}, u32[]{:S(2)}) collective-permute-start(bf16[192,1024]{1,0:T(8,128)(2,1)S(1)} %shard_map.129), channel_id=1, source_target_pairs={{0,3},{1,2},{2,1},{3,0},{4,7},{5,6},{6,5},{7,4},{8,11},{9,10},{10,... | collective-permute-start | bytes 1179656 | tf_op jit(solution)/shard_map/ppermute | solution.py:46
  26.5 5.1 %copy-start.4 = (bf16[192,1024]{1,0:T(8,128)(2,1)S(1)}, bf16[192,1024]{1,0:T(8,128)(2,1)}, u32[]{:S(2)}) copy-start(bf16[192,1024]{1,0:T(8,128)(2,1)} %refs_3_.4) | copy-start | bytes 1179652
  31.0 9.9 %collective-permute-start.4 = (bf16[192,1024]{1,0:T(8,128)(2,1)}, bf16[192,1024]{1,0:T(8,128)(2,1)S(1)}, u32[]{:S(2)}, u32[]{:S(2)}) collective-permute-start(bf16[192,1024]{1,0:T(8,128)(2,1)} %shard_map.135), channel_id=1, source_target_pairs={{0,1},{1,0},{2,3},{3,2},{4,5},{5,4},{6,7},{7,6},{8,9},{9,8},{10,11... | collective-permute-start | bytes 1179656 | tf_op jit(solution)/shard_map/ppermute | solution.py:46
  31.5 9.4 %collective-permute-start.5 = (bf16[192,1024]{1,0:T(8,128)(2,1)S(1)}, bf16[192,1024]{1,0:T(8,128)(2,1)S(1)}, u32[]{:S(2)}, u32[]{:S(2)}) collective-permute-start(bf16[192,1024]{1,0:T(8,128)(2,1)S(1)} %shard_map.136), channel_id=1, source_target_pairs={{0,2},{1,3},{2,0},{3,1},{4,6},{5,7},{6,4},{7,5},{8,10},{9,11},{10,... | collective-permute-start | bytes 1179656 | tf_op jit(solution)/shard_map/ppermute | solution.py:46
  42.0 4.6 %collective-permute-start.6 = (bf16[36,1024]{1,0:T(8,128)(2,1)S(1)}, bf16[36,1024]{1,0:T(8,128)(2,1)S(1)}, u32[]{:S(2)}, u32[]{:S(2)}) collective-permute-start(bf16[36,1024]{1,0:T(8,128)(2,1)S(1)} %get-tuple-element.57), channel_id=1, source_target_pairs={{0,4},{4,0},{8,12},{12,8},{16,20},{20,16},{24,28},{28,24},{1,5},{5... | collective-permute-start | bytes 221192 | tf_op jit(solution)/shard_map/ppermute | solution.py:46
  42.1 8.1 %collective-permute-start.7 = (bf16[36,1024]{1,0:T(8,128)(2,1)S(1)}, bf16[36,1024]{1,0:T(8,128)(2,1)S(1)}, u32[]{:S(2)}, u32[]{:S(2)}) collective-permute-start(bf16[36,1024]{1,0:T(8,128)(2,1)S(1)} %get-tuple-element.58), channel_id=1, source_target_pairs={{0,8},{4,12},{8,0},{12,4},{16,24},{20,28},{24,16},{28,20},{1,9},{5... | collective-permute-start | bytes 221192 | tf_op jit(solution)/shard_map/ppermute | solution.py:46
  43.7 14.8 %collective-permute-start.8 = (bf16[36,1024]{1,0:T(8,128)(2,1)S(1)}, bf16[36,1024]{1,0:T(8,128)(2,1)S(1)}, u32[]{:S(2)}, u32[]{:S(2)}) collective-permute-start(bf16[36,1024]{1,0:T(8,128)(2,1)S(1)} %get-tuple-element.59), channel_id=1, source_target_pairs={{0,12},{4,8},{8,4},{12,0},{16,28},{20,24},{24,20},{28,16},{1,13},{... | collective-permute-start | bytes 221192 | tf_op jit(solution)/shard_map/ppermute | solution.py:46
  44.0 14.6 %collective-permute-start.9 = (bf16[36,1024]{1,0:T(8,128)(2,1)S(1)}, bf16[36,1024]{1,0:T(8,128)(2,1)S(1)}, u32[]{:S(2)}, u32[]{:S(2)}) collective-permute-start(bf16[36,1024]{1,0:T(8,128)(2,1)S(1)} %get-tuple-element.60), channel_id=1, source_target_pairs={{0,16},{4,20},{8,24},{12,28},{16,0},{20,4},{24,8},{28,12},{1,17},{... | collective-permute-start | bytes 221192 | tf_op jit(solution)/shard_map/ppermute | solution.py:46
  46.6 12.5 %collective-permute-start.10 = (bf16[36,1024]{1,0:T(8,128)(2,1)S(1)}, bf16[36,1024]{1,0:T(8,128)(2,1)S(1)}, u32[]{:S(2)}, u32[]{:S(2)}) collective-permute-start(bf16[36,1024]{1,0:T(8,128)(2,1)S(1)} %get-tuple-element.61), channel_id=1, source_target_pairs={{0,20},{4,16},{8,28},{12,24},{16,4},{20,0},{24,12},{28,8},{1,21},{... | collective-permute-start | bytes 221192 | tf_op jit(solution)/shard_map/ppermute | solution.py:46
  46.6 12.5 %collective-permute-start.11 = (bf16[36,1024]{1,0:T(8,128)(2,1)S(1)}, bf16[36,1024]{1,0:T(8,128)(2,1)S(1)}, u32[]{:S(2)}, u32[]{:S(2)}) collective-permute-start(bf16[36,1024]{1,0:T(8,128)(2,1)S(1)} %get-tuple-element.62), channel_id=1, source_target_pairs={{0,24},{4,28},{8,16},{12,20},{16,8},{20,12},{24,0},{28,4},{1,25},{... | collective-permute-start | bytes 221192 | tf_op jit(solution)/shard_map/ppermute | solution.py:46
  50.2 8.9 %collective-permute-start.12 = (bf16[36,1024]{1,0:T(8,128)(2,1)S(1)}, bf16[36,1024]{1,0:T(8,128)(2,1)S(1)}, u32[]{:S(2)}, u32[]{:S(2)}) collective-permute-start(bf16[36,1024]{1,0:T(8,128)(2,1)S(1)} %get-tuple-element.63), channel_id=1, source_target_pairs={{0,28},{4,24},{8,20},{12,16},{16,12},{20,8},{24,4},{28,0},{1,29},{... | collective-permute-start | bytes 221192 | tf_op jit(solution)/shard_map/ppermute | solution.py:46
  50.3 1.2 %copy-start = (bf16[128,4224]{1,0:T(8,128)(2,1)S(1)}, bf16[128,4224]{1,0:T(8,128)(2,1)}, u32[]{:S(2)}) copy-start(bf16[128,4224]{1,0:T(8,128)(2,1)} %all-gather.2.cloned.1.call-done.refs_0_.refs_1_.refs_4_.refs_7_.refs_8_.refs_5_.refs_13_) | copy-start | bytes 3244036
  51.5 6.1 %copy-start.1 = (bf16[128,4224]{1,0:T(8,128)(2,1)S(1)}, bf16[128,4224]{1,0:T(8,128)(2,1)}, u32[]{:S(2)}) copy-start(bf16[128,4224]{1,0:T(8,128)(2,1)} %all-gather.2.cloned.1.call-done.refs_0_.refs_1_.refs_4_.refs_7_.refs_8_.refs_5_.refs_13_) | copy-start | bytes 3244036
  60.4 15.6 %collective-permute-start.14 = (bf16[288,1024]{1,0:T(8,128)(2,1)S(1)}, bf16[288,1024]{1,0:T(8,128)(2,1)S(1)}, u32[]{:S(2)}, u32[]{:S(2)}) collective-permute-start(bf16[288,1024]{1,0:T(8,128)(2,1)S(1)} %shard_map.139.refs_1_.refs_12_), channel_id=1, source_target_pairs={{0,2},{1,3},{2,0},{3,1},{4,6},{5,7},{6,4},{7,5},{8,10},{9,11},{10,... | collective-permute-start | bytes 1769480 | tf_op jit(solution)/shard_map/ppermute | solution.py:46
  61.0 15.3 %collective-permute-start.13 = (bf16[288,1024]{1,0:T(8,128)(2,1)S(1)}, bf16[288,1024]{1,0:T(8,128)(2,1)S(1)}, u32[]{:S(2)}, u32[]{:S(2)}) collective-permute-start(bf16[288,1024]{1,0:T(8,128)(2,1)S(1)} %shard_map.139.refs_1_.refs_12_), channel_id=1, source_target_pairs={{0,1},{1,0},{2,3},{3,2},{4,5},{5,4},{6,7},{7,6},{8,9},{9,8},{10,11... | collective-permute-start | bytes 1769480 | tf_op jit(solution)/shard_map/ppermute | solution.py:46
  76.3 11.6 %copy-start.6 = (f32[1024]{0:T(1024)S(1)}, f32[1024]{0:T(1024)}, u32[]{:S(2)}) copy-start(f32[1024]{0:T(1024)} %param.19) | copy-start | bytes 12292
  76.4 11.6 %collective-permute-start.15 = (bf16[144,1024]{1,0:T(8,128)(2,1)S(1)}, bf16[144,1024]{1,0:T(8,128)(2,1)S(1)}, u32[]{:S(2)}, u32[]{:S(2)}) collective-permute-start(bf16[144,1024]{1,0:T(8,128)(2,1)S(1)} %slice.6), channel_id=1, source_target_pairs={{0,2},{1,3},{2,0},{3,1},{4,6},{5,7},{6,4},{7,5},{8,10},{9,11},{10,... | collective-permute-start | bytes 884744 | tf_op jit(solution)/shard_map/ppermute | solution.py:46
  77.9 10.0 %collective-permute-start.16 = (bf16[144,1024]{1,0:T(8,128)(2,1)S(1)}, bf16[144,1024]{1,0:T(8,128)(2,1)S(1)}, u32[]{:S(2)}, u32[]{:S(2)}) collective-permute-start(bf16[144,1024]{1,0:T(8,128)(2,1)S(1)} %slice.7), channel_id=1, source_target_pairs={{0,1},{1,0},{2,3},{3,2},{4,5},{5,4},{6,7},{7,6},{8,9},{9,8},{10,11... | collective-permute-start | bytes 884744 | tf_op jit(solution)/shard_map/ppermute | solution.py:46
Sparse Core Ops, SparseCore 0:
  20.0 23.9 all-gather.1
